TPU v7x, 32 devices: a whole 2x2x4 slice. The times are simulated.
32 devices in a mesh: dp: 4 (over z), row: 4 (over y, x), col: 2 (over core).
Axes of the slice: x: 2, y: 2, z: 4, core: 2. Of those that a mesh axis runs over, the one named last changes fastest.
Arguments:
- tokens_in: bfloat16 [2048, 4, 384], P('dp', 'row'), may hold values from -6 to 6
- lengths: int32 [16], P(('dp', 'row')), may hold values from 32 to 256, as said below
- joint_weight: float32 [768, 12, 192], P('row', 'col', 'dp'), may hold values from -0.21875 to 0.21875
- joint_first: float32 [768, 12, 192], P('row', 'col', 'dp'), may hold values from -14.08 to 14.08
- joint_second: float32 [768, 12, 192], P('row', 'col', 'dp'), may hold values from 1.024 to 4.096
- output_weight: float32 [768, 4, 192], P('col', 'row', 'dp'), may hold values from -1.75 to 1.75
- output_first: float32 [768, 4, 192], P('col', 'row', 'dp'), may hold values from -2.816 to 2.816
- output_second: float32 [768, 4, 192], P('col', 'row', 'dp'), may hold values from 0.04096 to 0.16384
- up_weight: float32 [768, 2, 1536], P('row', 'col', 'dp'), may hold values from -0.21875 to 0.21875
- up_first: float32 [768, 2, 1536], P('row', 'col', 'dp'), may hold values from -8.448 to 8.448
- up_second: float32 [768, 2, 1536], P('row', 'col', 'dp'), may hold values from 0.36864 to 1.47456
- down_weight: float32 [3072, 4, 192], P('col', 'row', 'dp'), may hold values from -0.109375 to 0.109375
- down_first: float32 [3072, 4, 192], P('col', 'row', 'dp'), may hold values from -14.08 to 14.08
- down_second: float32 [3072, 4, 192], P('col', 'row', 'dp'), may hold values from 1.024 to 4.096
- vectors: float32 [9216], replicated, may hold values from -2.5 to 2.5, as said below
- vector_first: float32 [9216], replicated, may hold values from -19.712 to 19.712
- vector_second: float32 [9216], replicated, may hold values from 2.00704 to 8.02816
- out_grad: bfloat16 [2048, 4, 384], P('dp', 'row'), may hold values from -6 to 6
Outputs:
- layer_out: float32 [2048, 4, 384], P('dp', 'row')
- tokens_grad: float32 [2048, 4, 384], P('dp', 'row')
- joint_first_new: float32 [768, 12, 192], P('row', 'col', 'dp')
- joint_second_new: float32 [768, 12, 192], P('row', 'col', 'dp')
- joint_weight_new: float32 [768, 12, 192], P('row', 'col', 'dp')
- output_first_new: float32 [768, 4, 192], P('col', 'row', 'dp')
- output_second_new: float32 [768, 4, 192], P('col', 'row', 'dp')
- output_weight_new: float32 [768, 4, 192], P('col', 'row', 'dp')
- up_first_new: float32 [768, 2, 1536], P('row', 'col', 'dp')
- up_second_new: float32 [768, 2, 1536], P('row', 'col', 'dp')
- up_weight_new: float32 [768, 2, 1536], P('row', 'col', 'dp')
- down_first_new: float32 [3072, 4, 192], P('col', 'row', 'dp')
- down_second_new: float32 [3072, 4, 192], P('col', 'row', 'dp')
- down_weight_new: float32 [3072, 4, 192], P('col', 'row', 'dp')
- vector_first_new: float32 [9216], replicated
- vector_second_new: float32 [9216], replicated
- vectors_new: float32 [9216], replicated
Inputs may be any that keep to these rules, and one draw needn't show every extreme that they name: `lengths`: at least one sequence has 256 real tokens. `vectors`: the gains g1 and g2 lie in 0.5 to 1.5.
All inputs are finite; a program needn't handle non-finite values.
Results may differ from a plain program's by a relative error of at most 0.01.
Values may be sent and summed in bfloat16 or wider, within the bound.
No kernel may reach another device: no remote copies, remote signals or barrier semaphores. Data moves between devices by JAX's collectives and lax.ppermute only.
A program may use at most 128 MiB of HBM per device.

v0:
```python
from functools import partial

import jax
import jax.numpy as jnp
from jax import lax
from jax.sharding import PartitionSpec as P

D = 768
HD = 64
FF = 3072
LEN = 256
STEP = 10


NORM_EPS = 1e-12
BETA_ONE = 0.9
BETA_TWO = 0.999
ADAM_EPS = 1e-08
DECAY = 0.01
VECTOR_RATE = 0.2


def feature_stats(first, second):
    return lax.psum((jnp.sum(first, axis=1), jnp.sum(second, axis=1)), "row")


def norm_forward(resid, gain, shift):
    total, squares = feature_stats(resid, resid * resid)
    mean = total / D
    var = squares / D - mean * mean
    inverse = lax.rsqrt(var + NORM_EPS)
    normed = (resid - mean[:, None]) * inverse[:, None]
    return (normed * gain + shift, normed, inverse)


def norm_backward(grad, normed, inverse, gain):
    scaled = grad * gain
    total, cross = feature_stats(scaled, scaled * normed)
    return (scaled - (total / D)[:, None] - normed * (cross / D)[:, None]) * inverse[:, None]


def first_forward(value, block):
    flat = block.reshape(block.shape[0], -1)
    return (
        lax.psum_scatter(
            jnp.dot(value, flat, preferred_element_type=jnp.float32),
            "row",
            scatter_dimension=0,
            tiled=True,
        ),
        None,
    )


def first_backward(grad, value, block):
    flat = block.reshape(block.shape[0], -1)
    full = lax.all_gather(grad, "row", axis=0, tiled=True)
    weight_grad = jnp.einsum("tk,tn->kn", value, full, preferred_element_type=jnp.float32)
    partial_sum = jnp.einsum("tn,kn->tk", full, flat, preferred_element_type=jnp.float32)
    return (lax.psum(partial_sum, "col"), weight_grad.reshape(block.shape))


def second_forward(value, block):
    flat = block.reshape(-1, block.shape[2])
    gathered = lax.all_gather(value, "row", axis=0, tiled=True)
    summed = lax.psum(jnp.dot(gathered, flat, preferred_element_type=jnp.float32), "col")
    return (summed, gathered)


def second_backward(grad, gathered, block):
    flat = block.reshape(-1, block.shape[2])
    weight_grad = jnp.einsum("tk,tn->kn", gathered, grad, preferred_element_type=jnp.float32)
    return (
        weight_grad.reshape(block.shape),
        lax.psum_scatter(
            jnp.einsum("tn,kn->tk", grad, flat, preferred_element_type=jnp.float32),
            "row",
            scatter_dimension=0,
            tiled=True,
        ),
    )


def masked_scores(query, keyed, valid):
    scores = jnp.einsum("qhe,khe->hqk", query, keyed, preferred_element_type=jnp.float32) * 0.125
    return jnp.where(valid[None, None, :], scores, -1e30)


def attend_forward(query, keyed, valued, valid):
    scores = masked_scores(query, keyed, valid)
    top = jnp.max(scores, axis=-1, keepdims=True)
    expo = jnp.exp(scores - top)
    total = jnp.sum(expo, axis=-1, keepdims=True)
    probs = (expo / total).astype(jnp.bfloat16)
    attended = jnp.einsum("hqk,khe->qhe", probs, valued, preferred_element_type=jnp.float32)
    return (attended, top + jnp.log(total))


def attend_backward(query, keyed, valued, valid, log_total, grad_out):
    probs = jnp.exp(masked_scores(query, keyed, valid) - log_total)
    grad_value = jnp.einsum(
        "hqk,qhe->khe", probs.astype(jnp.bfloat16), grad_out, preferred_element_type=jnp.float32
    )
    grad_probs = jnp.einsum("qhe,khe->hqk", grad_out, valued, preferred_element_type=jnp.float32)
    inner = jnp.sum(grad_probs * probs, axis=-1, keepdims=True)
    grad_scores = (probs * (grad_probs - inner)).astype(jnp.bfloat16)
    grad_query = (
        jnp.einsum("hqk,khe->qhe", grad_scores, keyed, preferred_element_type=jnp.float32) * 0.125
    )
    grad_key = (
        jnp.einsum("hqk,qhe->khe", grad_scores, query, preferred_element_type=jnp.float32) * 0.125
    )
    return (grad_query, grad_key, grad_value)


def adamw(weight, first, second, grad, rate, decay):
    first_new = BETA_ONE * first + (1.0 - BETA_ONE) * grad
    second_new = BETA_TWO * second + (1.0 - BETA_TWO) * grad * grad
    fix_one = 1.0 - BETA_ONE**STEP
    fix_two = 1.0 - BETA_TWO**STEP
    update = first_new / fix_one / (jnp.sqrt(second_new / fix_two) + ADAM_EPS) + decay * weight
    return (first_new, second_new, weight - rate * update)


def unpack_rows(packed):
    return packed.reshape(packed.shape[0] * 2, packed.shape[2] // 2)


def pack_rows(matrix):
    return matrix.reshape(matrix.shape[0] // 2, 1, matrix.shape[1] * 2)


def per_device(
    tokens_in,
    lengths,
    joint_weight,
    joint_first,
    joint_second,
    output_weight,
    output_first,
    output_second,
    up_weight,
    up_first,
    up_second,
    down_weight,
    down_first,
    down_second,
    vectors,
    vector_first,
    vector_second,
    out_grad,
):
    tokens_rows = unpack_rows(tokens_in)
    row_index = lax.axis_index("row")
    col_index = lax.axis_index("col")
    group_rows, width_row = tokens_rows.shape
    seq_rows = group_rows // lax.axis_size("row")
    joint_block, output_block, up_block, down_block = (
        lax.all_gather(joint_weight.astype(jnp.bfloat16), "dp", axis=2, tiled=True),
        lax.all_gather(output_weight.astype(jnp.bfloat16), "dp", axis=2, tiled=True),
        lax.all_gather(up_weight.astype(jnp.bfloat16), "dp", axis=2, tiled=True),
        lax.all_gather(down_weight.astype(jnp.bfloat16), "dp", axis=2, tiled=True),
    )
    heads_col = joint_block.shape[1]
    head_cols = heads_col * HD
    ff_col = up_block.shape[2]

    def piece(offset, width, index):
        return lax.dynamic_slice_in_dim(vectors, offset + index * width, width, 0)

    bias_query = piece(0, head_cols, col_index).reshape(heads_col, 1, HD)
    bias_value = piece(D, head_cols, col_index).reshape(heads_col, 1, HD)
    bias_out = piece(2 * D, width_row, row_index)
    gain_one = piece(3 * D, width_row, row_index)
    shift_one = piece(4 * D, width_row, row_index)
    bias_down = piece(5 * D, width_row, row_index)
    gain_two = piece(6 * D, width_row, row_index)
    shift_two = piece(7 * D, width_row, row_index)
    bias_up = piece(8 * D, ff_col, col_index)
    mixed, joint_saved = first_forward(tokens_rows, joint_block)
    mixed = mixed.reshape(seq_rows, heads_col, 3, HD)
    bias_mixed = jnp.concatenate([bias_query, jnp.zeros_like(bias_query), bias_value], axis=1)
    mixed = (mixed + bias_mixed).astype(jnp.bfloat16)
    query = mixed[:, :, 0]
    keyed = mixed[:, :, 1]
    valued = mixed[:, :, 2]
    valid = jnp.arange(seq_rows, dtype=jnp.int32) < lengths[0]
    attended, log_total = attend_forward(query, keyed, valued, valid)
    attended = attended.reshape(seq_rows, head_cols).astype(jnp.bfloat16)
    branch, attended_rows = second_forward(attended, output_block)
    hidden, normed_one, inverse_one = norm_forward(
        tokens_rows.astype(jnp.float32) + branch + bias_out, gain_one, shift_one
    )
    hidden_low = hidden.astype(jnp.bfloat16)
    pre, up_saved = first_forward(hidden_low, up_block)
    pre = pre + bias_up
    act = jax.nn.gelu(pre, approximate=False)
    down, act_rows = second_forward(act.astype(jnp.bfloat16), down_block)
    result, normed_two, inverse_two = norm_forward(hidden + down + bias_down, gain_two, shift_two)
    grad_out = unpack_rows(out_grad).astype(jnp.float32)
    grad_two = norm_backward(grad_out, normed_two, inverse_two, gain_two)
    grad_down = grad_two.astype(jnp.bfloat16)
    down_grad, act_grad = second_backward(grad_down, act_rows, down_block)
    unused, gelu_pull = jax.vjp(partial(jax.nn.gelu, approximate=False), pre)
    grad_pre = gelu_pull(act_grad)[0].astype(jnp.bfloat16)
    hidden_back, up_grad = first_backward(grad_pre, hidden_low, up_block)
    grad_hidden = grad_two + hidden_back
    grad_one = norm_backward(grad_hidden, normed_one, inverse_one, gain_one)
    grad_branch = grad_one.astype(jnp.bfloat16)
    output_grad, attended_grad = second_backward(grad_branch, attended_rows, output_block)
    grad_attended = attended_grad.astype(jnp.bfloat16).reshape(seq_rows, heads_col, HD)
    grad_query, grad_key, grad_value = attend_backward(
        query, keyed, valued, valid, log_total, grad_attended
    )
    grad_mixed = jnp.stack([grad_query, grad_key, grad_value], axis=2).astype(jnp.bfloat16)
    token_back, joint_grad = first_backward(
        grad_mixed.reshape(seq_rows, -1), tokens_rows, joint_block
    )
    tokens_grad = grad_one + token_back
    joint_sum, output_sum, up_sum, down_sum = (
        lax.psum_scatter(joint_grad, "dp", scatter_dimension=2, tiled=True),
        lax.psum_scatter(output_grad, "dp", scatter_dimension=2, tiled=True),
        lax.psum_scatter(up_grad, "dp", scatter_dimension=2, tiled=True),
        lax.psum_scatter(down_grad, "dp", scatter_dimension=2, tiled=True),
    )
    keep = (col_index == 0).astype(jnp.float32)
    mixed_sum = jnp.sum(grad_mixed.astype(jnp.float32), axis=0)
    placed = [
        (mixed_sum[:, 0].reshape(-1), col_index * head_cols),
        (mixed_sum[:, 2].reshape(-1), D + col_index * head_cols),
        (keep * jnp.sum(grad_branch.astype(jnp.float32), axis=0), 2 * D + row_index * width_row),
        (keep * jnp.sum(grad_hidden * normed_one, axis=0), 3 * D + row_index * width_row),
        (keep * jnp.sum(grad_hidden, axis=0), 4 * D + row_index * width_row),
        (keep * jnp.sum(grad_down.astype(jnp.float32), axis=0), 5 * D + row_index * width_row),
        (keep * jnp.sum(grad_out * normed_two, axis=0), 6 * D + row_index * width_row),
        (keep * jnp.sum(grad_out, axis=0), 7 * D + row_index * width_row),
        (jnp.sum(grad_pre.astype(jnp.float32), axis=0), 8 * D + col_index * ff_col),
    ]
    vector_local = jnp.zeros((8 * D + FF,), jnp.float32)
    for values, offset in placed:
        vector_local = lax.dynamic_update_slice_in_dim(vector_local, values, offset, 0)
    vector_grad = lax.psum(vector_local, ("dp", "row", "col"))
    joint_new = adamw(joint_weight, joint_first, joint_second, joint_sum, D ** (-0.5), DECAY)
    output_new = adamw(
        output_weight, output_first, output_second, output_sum, (4 * D // LEN) ** (-0.5), DECAY
    )
    up_new = adamw(up_weight, up_first, up_second, up_sum, D ** (-0.5), DECAY)
    down_new = adamw(down_weight, down_first, down_second, down_sum, FF ** (-0.5), DECAY)
    vector_new = adamw(vectors, vector_first, vector_second, vector_grad, VECTOR_RATE, 0.0)
    return (
        pack_rows(result),
        pack_rows(tokens_grad),
        joint_new[0],
        joint_new[1],
        joint_new[2],
        output_new[0],
        output_new[1],
        output_new[2],
        up_new[0],
        up_new[1],
        up_new[2],
        down_new[0],
        down_new[1],
        down_new[2],
        vector_new[0],
        vector_new[1],
        vector_new[2],
    )


def solution(mesh):
    in_specs = (
        P("dp", "row", None),
        P(("dp", "row")),
        P("row", "col", "dp"),
        P("row", "col", "dp"),
        P("row", "col", "dp"),
        P("col", "row", "dp"),
        P("col", "row", "dp"),
        P("col", "row", "dp"),
        P("row", "col", "dp"),
        P("row", "col", "dp"),
        P("row", "col", "dp"),
        P("col", "row", "dp"),
        P("col", "row", "dp"),
        P("col", "row", "dp"),
        P(),
        P(),
        P(),
        P("dp", "row", None),
    )
    out_specs = (
        P("dp", "row", None),
        P("dp", "row", None),
        P("row", "col", "dp"),
        P("row", "col", "dp"),
        P("row", "col", "dp"),
        P("col", "row", "dp"),
        P("col", "row", "dp"),
        P("col", "row", "dp"),
        P("row", "col", "dp"),
        P("row", "col", "dp"),
        P("row", "col", "dp"),
        P("col", "row", "dp"),
        P("col", "row", "dp"),
        P("col", "row", "dp"),
        P(),
        P(),
        P(),
    )
    return jax.shard_map(
        per_device, mesh=mesh, in_specs=in_specs, out_specs=out_specs, check_vma=False
    )
```

profile of v0, /device:TPU:1, one launch (start us, length us, event | category | flops | bytes accessed | tf_op | source)
XLA Modules:
  0.0 700.9 jit_solution(11139704964119375576)
XLA Ops:
  8.2 15.8 %all_gather.24 = bf16[192,6,192]{0,2,1:T(8,128)(2,1)S(1)} all-gather(bf16[192,6,48]{0,2,1:T(8,128)(2,1)S(1)} %convert_element_type.83), channel_id=1, replica_groups=mesh['dp'=4,'row'=4,'col'=2] {'dp'}, dimensions={2}, use_global_device_ids=true | all-gather | bytes 552960 | tf_op jit(solution)/shard_map/all_gather | solution.py:159
  24.0 1.5 reshape.122
  25.5 3.0 fusion.54
  30.4 10.6 %all_gather.26 = bf16[384,1,192]{0,2,1:T(8,128)(2,1)S(1)} all-gather(bf16[384,1,48]{0,2,1:T(8,128)(2,1)S(1)} %convert_element_type.89), channel_id=1, replica_groups=mesh['dp'=4,'row'=4,'col'=2] {'dp'}, dimensions={2}, use_global_device_ids=true | all-gather | bytes 184320 | tf_op jit(solution)/shard_map/all_gather | solution.py:160
  41.1 47.9 %reduce-scatter.9.cloned.1.call-done = f32[256,1152]{1,0:T(8,128)} async-done(((f32[1024,1152]{1,0:T(8,128)}), f32[256,1152]{1,0:T(8,128)}) %reduce-scatter.9.cloned.1.call-update) | async-done | bytes 1179664 | tf_op jit(solution)/shard_map/reduce_scatter | solution.py:45
  89.0 1.6 copy.97
  92.3 16.0 %all_gather.25 = bf16[1024,384]{0,1:T(8,128)(2,1)S(1)} all-gather(bf16[256,384]{0,1:T(8,128)(2,1)S(1)} %bitcast.95), channel_id=1, replica_groups=mesh['dp'=4,'row'=4,'col'=2] {'row'}, dimensions={0}, use_global_device_ids=true | all-gather | bytes 983040 | tf_op jit(solution)/shard_map/all_gather | solution.py:65
  113.2 22.1 %all_gather.27 = bf16[192,1,1536]{2,1,0:T(2,128)(2,1)S(1)} all-gather(bf16[192,1,384]{2,1,0:T(2,128)(2,1)S(1)} %convert_element_type.91), channel_id=1, replica_groups=mesh['dp'=4,'row'=4,'col'=2] {'dp'}, dimensions={2}, use_global_device_ids=true | all-gather | bytes 737280 | tf_op jit(solution)/shard_map/all_gather | solution.py:161
  135.3 1.9 fusion.42
  137.2 7.7 %all-reduce.3 = (f32[1024]{0:T(1024)}, f32[1024]{0:T(1024)}) all-reduce(f32[1024]{0:T(1024)S(1)} %get-tuple-element.95, f32[1024]{0:T(1024)S(1)} %get-tuple-element.94), channel_id=1, replica_groups=mesh['dp'=4,'row'=4,'col'=2] {'row'}, use_global_device_ids=true, to_apply=%region_7.8 | all-reduce | flops 2048 | bytes 16384 | tf_op jit(solution)/shard_map/psum | solution.py:24
  145.6 3.8 fusion.16
  150.2 71.3 %reduce-scatter.11.cloned.1.call-done = f32[256,1536]{1,0:T(8,128)} async-done(((f32[1024,1536]{1,0:T(8,128)}), f32[256,1536]{1,0:T(8,128)}) %reduce-scatter.11.cloned.1.call-update) | async-done | bytes 1572880 | tf_op jit(solution)/shard_map/reduce_scatter | solution.py:45
  221.5 5.6 multiply_convert_fusion.1
  227.1 14.7 %all_gather.29 = bf16[1536,1,192]{0,2,1:T(8,128)(2,1)S(1)} all-gather(bf16[1536,1,48]{0,2,1:T(8,128)(2,1)S(1)} %convert_element_type.93), channel_id=1, replica_groups=mesh['dp'=4,'row'=4,'col'=2] {'dp'}, dimensions={2}, use_global_device_ids=true | all-gather | bytes 737280 | tf_op jit(solution)/shard_map/all_gather | solution.py:162
  241.8 29.4 %all-gather.4.cloned.1.call-done = bf16[1024,1536]{1,0:T(8,128)(2,1)} async-done(((bf16[256,1536]{1,0:T(8,128)(2,1)}), bf16[1024,1536]{1,0:T(8,128)(2,1)}) %all-gather.4.cloned.1.call-update) | async-done | bytes 3145744 | tf_op jit(solution)/shard_map/all_gather | solution.py:65
  271.2 3.9 fusion.20
  277.7 17.2 %all-reduce.11.cloned.1.call-done = f32[1024,192]{0,1:T(8,128)} async-done(((f32[1024,192]{0,1:T(8,128)}), f32[1024,192]{0,1:T(8,128)}) %all-reduce.11.cloned.1.call-update) | async-done | bytes 786448 | tf_op jit(solution)/shard_map/psum | solution.py:66
  294.9 2.3 fusion.41
  297.2 8.3 %all-reduce.2 = (f32[1024]{0:T(1024)S(1)}, f32[1024]{0:T(1024)S(1)}) all-reduce(f32[1024]{0:T(1024)S(1)} %get-tuple-element.93, f32[1024]{0:T(1024)S(1)} %get-tuple-element.92), channel_id=1, replica_groups=mesh['dp'=4,'row'=4,'col'=2] {'row'}, use_global_device_ids=true, to_apply=%region_13.14 | all-reduce | flops 2048 | bytes 16384 | tf_op jit(solution)/shard_map/psum | solution.py:24
  305.5 2.2 multiply_reduce_fusion.1
  307.7 6.0 all-reduce.1
  313.8 3.3 convert_reduce_fusion.2
  317.1 3.7 fusion.18
  321.0 73.8 %reduce-scatter.13.cloned.1.call-done = f32[256,1536]{1,0:T(8,128)} async-done(((f32[1024,1536]{1,0:T(8,128)}), f32[256,1536]{1,0:T(8,128)}) %reduce-scatter.13.cloned.1.call-update) | async-done | bytes 1572880 | tf_op jit(solution)/shard_map/reduce_scatter | solution.py:75
  394.8 4.6 convert_reduce_fusion
  399.4 44.1 %all-gather.6.cloned.1.call-done = bf16[1024,1536]{1,0:T(8,128)(2,1)} async-done(((bf16[256,1536]{1,0:T(8,128)(2,1)}), bf16[1024,1536]{1,0:T(8,128)(2,1)}) %all-gather.6.cloned.1.call-update) | async-done | bytes 3145744 | tf_op jit(solution)/shard_map/all_gather | solution.py:57
  443.5 4.3 fusion.14
  447.9 19.7 %all-reduce.13.cloned.1.call-done = f32[1024,192]{0,1:T(8,128)} async-done(((f32[1024,192]{0,1:T(8,128)}), f32[1024,192]{0,1:T(8,128)}) %all-reduce.13.cloned.1.call-update) | async-done | bytes 786448 | tf_op jit(solution)/shard_map/psum | solution.py:60
  467.6 2.9 multiply_reduce_fusion.2
  470.5 8.4 %all-reduce = (f32[1024]{0:T(1024)S(1)}, f32[1024]{0:T(1024)S(1)}) all-reduce(f32[1024]{0:T(1024)S(1)} %get-tuple-element.88, f32[1024]{0:T(1024)S(1)} %get-tuple-element.89), channel_id=1, replica_groups=mesh['dp'=4,'row'=4,'col'=2] {'row'}, use_global_device_ids=true, to_apply=%region_23.24 | all-reduce | flops 2048 | bytes 16384 | tf_op jit(solution)/shard_map/psum | solution.py:24
  478.9 2.0 convert_reduce_fusion.3
  481.8 1.6 fusion.29
  483.6 3.7 convolution_bitcast_fusion.1
  488.4 2.3 convolution_bitcast_fusion.4
  490.8 24.5 %reduce-scatter.15.cloned.1.call-done = f32[256,384]{1,0:T(8,128)} async-done(((f32[1024,384]{1,0:T(8,128)}), f32[256,384]{1,0:T(8,128)}) %reduce-scatter.15.cloned.1.call-update) | async-done | bytes 393232 | tf_op jit(solution)/shard_map/reduce_scatter | solution.py:75
  521.1 3.8 convolution_bitcast_fusion.2
  526.7 1.9 reshape.138
  528.6 18.0 %reduce-scatter.23.cloned.1.call-done = f32[1536,1,48]{0,2,1:T(8,128)} async-done(((f32[1536,1,192]{0,2,1:T(8,128)}), f32[1536,1,48]{0,2,1:T(8,128)}) %reduce-scatter.23.cloned.1.call-update) | async-done | bytes 294928 | tf_op jit(solution)/shard_map/reduce_scatter | solution.py:224
  546.6 2.1 multiply_subtract_fusion
  548.7 18.0 %reduce-scatter.19.cloned.1.call-done = f32[384,1,48]{0,2,1:T(8,128)} async-done(((f32[384,1,192]{0,2,1:T(8,128)}), f32[384,1,48]{0,2,1:T(8,128)}) %reduce-scatter.19.cloned.1.call-update) | async-done | bytes 73744 | tf_op jit(solution)/shard_map/reduce_scatter | solution.py:222
  566.6 1.6 multiply_subtract_fusion.3
  568.2 37.5 %all-gather.8.cloned.1.call-done = bf16[1024,1152]{0,1:T(8,128)(2,1)} async-done(((bf16[256,1152]{0,1:T(8,128)(2,1)}), bf16[1024,1152]{0,1:T(8,128)(2,1)}) %all-gather.8.cloned.1.call-update) | async-done | bytes 2359312 | tf_op jit(solution)/shard_map/all_gather | solution.py:57
  605.7 3.3 fusion.55
  609.1 28.1 %reduce-scatter.21.cloned.1.call-done = f32[192,1,384]{2,0,1:T(8,128)} async-done(((f32[192,1,1536]{2,0,1:T(8,128)}), f32[192,1,384]{2,0,1:T(8,128)}) %reduce-scatter.21.cloned.1.call-update) | async-done | bytes 294928 | tf_op jit(solution)/shard_map/reduce_scatter | solution.py:223
  642.1 2.5 convolution_bitcast_fusion
  647.3 40.9 %psum.103 = f32[9216]{0:T(1024)S(1)} all-reduce(f32[9216]{0:T(1024)S(1)} %dynamic_update_slice.35), channel_id=1, replica_groups=mesh['dp'=4,'row'=4,'col'=2] {'dp','row','col'}, use_global_device_ids=true, to_apply=%region_39.40 | all-reduce | flops 9216 | bytes 73728 | tf_op jit(solution)/shard_map/psum | solution.py:242
  690.5 1.9 reshape.139
  692.4 2.0 multiply_subtract_fusion.2
  (193 shorter events, 32.8 us)
Async XLA Ops:
  7.2 81.8 %reduce-scatter.9.cloned.1.call-start = ((), (), s32[]{:S(2)}) async-start(), calls=%async_computation.8 | async-start | bytes 5898240 | tf_op jit(solution)/shard_map/reduce_scatter | solution.py:45
  24.0 4.6 copy-start.7
  25.5 85.0 %copy-start.4 = (bf16[1024,192]{1,0:T(8,128)(2,1)}, bf16[1024,192]{1,0:T(8,128)(2,1)S(1)}, u32[]{:S(2)}) copy-start(bf16[1024,192]{1,0:T(8,128)(2,1)S(1)} %reshape.122) | copy-start | bytes 1179652
  28.6 106.7 %all-reduce.9.cloned.1.call-start = ((), (), s32[]{:S(2)}) async-start(), calls=%async_computation.9 | async-start | bytes 1572864 | tf_op jit(solution)/shard_map/psum | solution.py:66
  41.0 67.4 %copy-start.15 = (bf16[384,1,192]{0,2,1:T(8,128)(2,1)}, bf16[384,1,192]{0,2,1:T(8,128)(2,1)S(1)}, u32[]{:S(2)}) copy-start(bf16[384,1,192]{0,2,1:T(8,128)(2,1)S(1)} %all_gather.26) | copy-start | bytes 442372
  109.2 2.3 copy-start.19
  110.5 111.0 %reduce-scatter.11.cloned.1.call-start = ((), (), s32[]{:S(2)}) async-start(), calls=%async_computation.10 | async-start | bytes 7864320 | tf_op jit(solution)/shard_map/reduce_scatter | solution.py:45
  113.2 181.7 %copy-start.41 = (f32[192]{0:T(256)}, f32[192]{0:T(256)S(1)}, u32[]{:S(2)}) copy-start(f32[192]{0:T(256)S(1)} %get-tuple-element.135) | copy-start | bytes 2308
  113.2 365.7 %copy-start.34 = (f32[192]{0:T(256)}, f32[192]{0:T(256)S(1)}, u32[]{:S(2)}) copy-start(f32[192]{0:T(256)S(1)} %get-tuple-element.136) | copy-start | bytes 2308
  135.3 14.0 %copy-start.12 = (bf16[192,1,1536]{2,1,0:T(2,128)(2,1)}, bf16[192,1,1536]{2,1,0:T(2,128)(2,1)S(1)}, u32[]{:S(2)}) copy-start(bf16[192,1,1536]{2,1,0:T(2,128)(2,1)S(1)} %all_gather.27) | copy-start | bytes 1769476
  149.4 121.8 %all-gather.4.cloned.1.call-start = ((), (), s32[]{:S(2)}) async-start(), calls=%async_computation.11 | async-start | bytes 3932160 | tf_op jit(solution)/shard_map/all_gather | solution.py:65
  150.2 76.9 %copy-start.17 = (f32[1536,1,48]{0,2,1:T(8,128)S(1)}, f32[1536,1,48]{0,2,1:T(8,128)}, u32[]{:S(2)}) copy-start(f32[1536,1,48]{0,2,1:T(8,128)} %param.29) | copy-start | bytes 884740
  227.1 67.8 %all-reduce.11.cloned.1.call-start = ((), (), s32[]{:S(2)}) async-start(), calls=%async_computation.12 | async-start | bytes 1572864 | tf_op jit(solution)/shard_map/psum | solution.py:66
  241.8 33.3 %copy-start.13 = (bf16[1536,1,192]{0,2,1:T(8,128)(2,1)}, bf16[1536,1,192]{0,2,1:T(8,128)(2,1)S(1)}, u32[]{:S(2)}) copy-start(bf16[1536,1,192]{0,2,1:T(8,128)(2,1)S(1)} %all_gather.29) | copy-start | bytes 1769476
  275.1 19.8 %copy-start.48 = (f32[192]{0:T(256)S(1)}, f32[192]{0:T(256)}, u32[]{:S(2)}) copy-start(f32[192]{0:T(256)} %get-tuple-element.134) | copy-start | bytes 2308
  275.2 119.6 %reduce-scatter.13.cloned.1.call-start = ((), (), s32[]{:S(2)}) async-start(), calls=%async_computation.13 | async-start | bytes 7864320 | tf_op jit(solution)/shard_map/reduce_scatter | solution.py:75
  276.5 20.7 %copy-start.2 = (f32[1024,192]{1,0:T(8,128)}, f32[1024,192]{1,0:T(8,128)S(1)}, u32[]{:S(2)}) copy-start(f32[1024,192]{1,0:T(8,128)S(1)} %reshape.137) | copy-start | bytes 2359300
  277.7 27.8 %copy-start.43 = (f32[192]{0:T(256)S(1)}, f32[192]{0:T(256)}, u32[]{:S(2)}) copy-start(f32[192]{0:T(256)} %get-tuple-element.133) | copy-start | bytes 2308
  294.9 18.9 %copy-start.47 = (f32[192]{0:T(256)S(1)}, f32[192]{0:T(256)}, u32[]{:S(2)}) copy-start(f32[192]{0:T(256)} %get-tuple-element.138) | copy-start | bytes 2308
  313.8 3.3 copy-start.14
  320.8 122.7 %all-gather.6.cloned.1.call-start = ((), (), s32[]{:S(2)}) async-start(), calls=%async_computation.14 | async-start | bytes 3932160 | tf_op jit(solution)/shard_map/all_gather | solution.py:57
  399.4 68.2 %all-reduce.13.cloned.1.call-start = ((), (), s32[]{:S(2)}) async-start(), calls=%async_computation.15 | async-start | bytes 1572864 | tf_op jit(solution)/shard_map/psum | solution.py:60
  447.8 67.4 %reduce-scatter.15.cloned.1.call-start = ((), (), s32[]{:S(2)}) async-start(), calls=%async_computation.16 | async-start | bytes 1966080 | tf_op jit(solution)/shard_map/reduce_scatter | solution.py:75
  470.5 11.4 %copy-start.16 = (bf16[384,1,192]{0,2,1:T(8,128)(2,1)S(1)}, bf16[384,1,192]{0,2,1:T(8,128)(2,1)}, u32[]{:S(2)}) copy-start(bf16[384,1,192]{0,2,1:T(8,128)(2,1)} %copy-done.15) | copy-start | bytes 442372
  483.5 3.9 copy-start.31
  483.5 3.8 copy-start.39
  483.5 63.1 %reduce-scatter.23.cloned.1.call-start = ((), (), s32[]{:S(2)}) async-start(), calls=%async_computation.22 | async-start | bytes 1474560 | tf_op jit(solution)/shard_map/reduce_scatter | solution.py:224
  487.3 79.3 %reduce-scatter.19.cloned.1.call-start = ((), (), s32[]{:S(2)}) async-start(), calls=%async_computation.20 | async-start | bytes 368640 | tf_op jit(solution)/shard_map/reduce_scatter | solution.py:222
  490.7 115.0 %all-gather.8.cloned.1.call-start = ((), (), s32[]{:S(2)}) async-start(), calls=%async_computation.17 | async-start | bytes 2949120 | tf_op jit(solution)/shard_map/all_gather | solution.py:57
  521.1 116.1 %reduce-scatter.21.cloned.1.call-start = ((), (), s32[]{:S(2)}) async-start(), calls=%async_computation.21 | async-start | bytes 1474560 | tf_op jit(solution)/shard_map/reduce_scatter | solution.py:223
  524.9 163.9 %all-reduce.15.cloned.1.call-start = ((), (), s32[]{:S(2)}) async-start(), calls=%async_computation.18 | async-start | bytes 1572864 | tf_op jit(solution)/shard_map/psum | solution.py:60
  526.4 20.2 %copy-start.18 = (f32[1536,1,48]{0,2,1:T(8,128)S(1)}, f32[1536,1,48]{0,2,1:T(8,128)}, u32[]{:S(2)}) copy-start(f32[1536,1,48]{0,2,1:T(8,128)} %param.29) | copy-start | bytes 884740
  526.4 20.2 %copy-start.24 = (f32[1536,1,48]{0,2,1:T(8,128)S(1)}, f32[1536,1,48]{0,2,1:T(8,128)}, u32[]{:S(2)}) copy-start(f32[1536,1,48]{0,2,1:T(8,128)} %param.31) | copy-start | bytes 884740
  526.7 39.9 %copy-start.23 = (f32[384,1,48]{0,2,1:T(8,128)S(1)}, f32[384,1,48]{0,2,1:T(8,128)}, u32[]{:S(2)}) copy-start(f32[384,1,48]{0,2,1:T(8,128)} %param.23) | copy-start | bytes 221188
  526.7 39.9 %copy-start.32 = (f32[384,1,48]{0,2,1:T(8,128)S(1)}, f32[384,1,48]{0,2,1:T(8,128)}, u32[]{:S(2)}) copy-start(f32[384,1,48]{0,2,1:T(8,128)} %param.25) | copy-start | bytes 221188
  526.7 39.9 %copy-start.33 = (f32[384,1,48]{0,2,1:T(8,128)S(1)}, f32[384,1,48]{0,2,1:T(8,128)}, u32[]{:S(2)}) copy-start(f32[384,1,48]{0,2,1:T(8,128)} %param.24) | copy-start | bytes 221188
  528.6 77.1 %copy-start.8 = (bf16[192,6,192]{0,2,1:T(8,128)(2,1)S(1)}, bf16[192,6,192]{0,2,1:T(8,128)(2,1)}, u32[]{:S(2)}) copy-start(bf16[192,6,192]{0,2,1:T(8,128)(2,1)} %copy-done.7) | copy-start | bytes 1327108
  568.2 69.0 %copy-start.20 = (f32[192,1,384]{2,1,0:T(1,128)S(1)}, f32[192,1,384]{2,1,0:T(1,128)}, u32[]{:S(2)}) copy-start(f32[192,1,384]{2,1,0:T(1,128)} %param.26) | copy-start | bytes 884740
  568.2 69.0 %copy-start.25 = (f32[192,1,384]{2,1,0:T(1,128)S(1)}, f32[192,1,384]{2,1,0:T(1,128)}, u32[]{:S(2)}) copy-start(f32[192,1,384]{2,1,0:T(1,128)} %param.28) | copy-start | bytes 884740
  568.2 69.0 %copy-start.26 = (f32[192,1,384]{2,1,0:T(1,128)S(1)}, f32[192,1,384]{2,1,0:T(1,128)}, u32[]{:S(2)}) copy-start(f32[192,1,384]{2,1,0:T(1,128)} %param.27) | copy-start | bytes 884740
  609.0 33.1 %copy-start.5 = (bf16[1024,192]{1,0:T(8,128)(2,1)S(1)}, bf16[1024,192]{1,0:T(8,128)(2,1)}, u32[]{:S(2)}) copy-start(bf16[1024,192]{1,0:T(8,128)(2,1)} %copy-done.4) | copy-start | bytes 1179652
  609.0 83.3 %reduce-scatter.17.cloned.1.call-start = ((), (), s32[]{:S(2)}) async-start(), calls=%async_computation.19 | async-start | bytes 1474560 | tf_op jit(solution)/shard_map/reduce_scatter | solution.py:221
  644.7 2.4 copy-start.40
  644.7 43.5 %copy-start.29 = (f32[9216]{0:T(1024)S(1)}, f32[9216]{0:T(1024)}, u32[]{:S(2)}) copy-start(f32[9216]{0:T(1024)} %param.32) | copy-start | bytes 110596
  644.7 43.5 %copy-start.36 = (f32[9216]{0:T(1024)S(1)}, f32[9216]{0:T(1024)}, u32[]{:S(2)}) copy-start(f32[9216]{0:T(1024)} %param.34) | copy-start | bytes 110596
  644.7 43.5 %copy-start.37 = (f32[9216]{0:T(1024)S(1)}, f32[9216]{0:T(1024)}, u32[]{:S(2)}) copy-start(f32[9216]{0:T(1024)} %param.33) | copy-start | bytes 110596
  690.1 2.2 copy-start.21
  690.1 2.2 copy-start.27
  (18 other events, 24.9 us)
Sparse Core Ops, SparseCore 0:
  28.7 60.2 reduce-scatter.8
  110.6 21.1 all-reduce.8
  149.5 71.9 reduce-scatter.10
  227.2 43.9 all-gather.3
  275.3 19.5 all-reduce.10
  320.9 73.8 reduce-scatter.12
  399.5 43.9 all-gather.5
  447.9 19.5 all-reduce.12
  483.6 31.6 reduce-scatter.14
  517.5 28.9 reduce-scatter.22
  549.5 17.0 reduce-scatter.18
  568.5 37.2 all-gather.7
  608.1 28.9 reduce-scatter.20
  640.1 18.4 all-reduce.14
  660.7 30.1 reduce-scatter.16
where the time goes:
time: 703 us; the launch traced here: 701 us
  waiting for transfers between devices  430 us (61%)
  blocking collectives  150 us (21%)
  matrix products  40.3 us (6%)
  other arithmetic  38.6 us (5%)
  local copies, waits for them, and re-layouts  25.9 us (4%)
  between operations  15.2 us (2%)
    reduce_scatter x2, waiting for transfers between devices, first_forward(): lax.psum_scatter(jnp.dot(value, flat, preferred_element_type=jnp.float32)...  119 us
    reduce_scatter x2, waiting for transfers between devices, second_backward(): lax.psum_scatter(jnp.einsum('tn,kn->tk', grad, flat, preferred_element_ty...  98.3 us
    all_gather x2, waiting for transfers between devices, first_backward(): full = lax.all_gather(grad, 'row', axis=0, tiled=True)  81.6 us
    psum x1, blocking collectives, per_device(): vector_grad = lax.psum(vector_local, ('dp', 'row', 'col'))  40.9 us
    psum x4, blocking collectives, feature_stats(): return lax.psum((jnp.sum(first, axis=1), jnp.sum(second, axis=1)), 'row')  30.4 us
    all_gather x1, waiting for transfers between devices, second_forward(): gathered = lax.all_gather(value, 'row', axis=0, tiled=True)  29.4 us
    reduce_scatter x1, waiting for transfers between devices, per_device(): lax.psum_scatter(up_grad, 'dp', scatter_dimension=2, tiled=True)  28.1 us
    all_gather x1, blocking collectives, per_device(): lax.all_gather(up_weight.astype(jnp.bfloat16), 'dp', axis=2, tiled=True)  22.1 us
  transfers between devices with their start and end apart: 15, of which 12 were waited for; matrix products, arithmetic and copies ran while one was open for 6% of the time, Pallas kernels for 0%

commit v1 on v0

v1 whole, which is shorter than its diff:
```python
from functools import partial

import jax
import jax.numpy as jnp
from jax import lax
from jax.experimental import pallas as pl
from jax.experimental.pallas import tpu as pltpu
from jax.sharding import PartitionSpec as P

D = 768
H = 12
HD = 64
FF = 3072
LEN = 256
STEP = 10

NORM_EPS = 1e-12
BETA_ONE = 0.9
BETA_TWO = 0.999
ADAM_EPS = 1e-08
DECAY = 0.01
VECTOR_RATE = 0.2

F32 = jnp.float32
BF16 = jnp.bfloat16

ROWS = 4
QUADS = 4
W = D // ROWS
S = W // QUADS
COLS = D // 2
HEADS = COLS // HD
FFC = FF // 2
MIX = HEADS * 3 * HD
PAIRS = LEN // 2
CHUNK = (W, COLS)
MIB = 1024 * 1024


def swap(value, axis, mask):
    n = lax.axis_size(axis)
    return lax.ppermute(value, axis, [(i, i ^ mask) for i in range(n)])


def shape(*dims, dtype=BF16):
    return jax.ShapeDtypeStruct(dims, dtype)


def run(kernel, where, args, outs, scratch=(), limit=8, after=(), fetch=False):
    vmem = pl.BlockSpec(memory_space=pltpu.VMEM)
    first, late = 1 + len(args), len(after)

    def body(*refs):
        kernel(*refs[:first], *refs[first + late :])

    out = pl.pallas_call(
        body,
        out_shape=outs,
        in_specs=[pl.BlockSpec(memory_space=pltpu.SMEM)]
        + [pl.BlockSpec(memory_space=pl.ANY) if fetch else vmem] * len(args)
        + [pl.BlockSpec(memory_space=pl.ANY)] * late,
        out_specs=[vmem] * len(outs),
        scratch_shapes=list(scratch),
        compiler_params=pltpu.CompilerParams(vmem_limit_bytes=limit * MIB),
    )(where, *args, *after)
    return list(out)


def dot(left, right, dims):
    return lax.dot_general(left, right, (dims, ((), ())), preferred_element_type=F32)


NN = ((1,), (0,))
NT = ((1,), (1,))
TN = ((0,), (0,))


def each(count, body):
    def step(i, carry):
        body(i)
        return carry

    lax.fori_loop(0, count, step, 0)


def row_of(vecs, start, count):
    return jnp.concatenate([vecs[start + i : start + i + 1, :] for i in range(count)], axis=1)


def vector_row(vecs, k):
    return row_of(vecs, 6 * k, 6)


def pick_col(where, left, right):
    return jnp.where(where[2] == 0, left, right)


def split_parts(value):
    high = value.astype(BF16)
    return high, (value - high.astype(F32)).astype(BF16)


def opening_kernel(where, tokens, grads, joint, output, *refs):
    outs, first = refs[:ROWS], refs[ROWS]
    tokens_in, grads_in, joint_in, output_in, done = refs[ROWS + 1 :]
    copies = [
        pltpu.make_async_copy(source, target, done.at[i])
        for i, (source, target) in enumerate(
            [(joint, joint_in), (output, output_in), (tokens, tokens_in), (grads, grads_in)]
        )
    ]
    for copy in copies:
        copy.start()
    copies[0].wait()
    copies[1].wait()
    for h in range(HEADS // 2):
        pair = [joint_in[h].astype(BF16), joint_in[h + HEADS // 2].astype(BF16)]
        first[h * S : (h + 1) * S, :] = jnp.concatenate(pair, axis=1)
    first[HEADS // 2 * S :, :] = output_in[...].astype(BF16)
    copies[2].wait()
    copies[3].wait()
    for m, out in enumerate(outs):
        out[0] = tokens_in[where[0] ^ m]
        out[1] = grads_in[where[0] ^ m]


def second_shard_kernel(where, up, second):
    for q in range(3):
        second[:, q * 128 : (q + 1) * 128] = up[pl.ds(q, W, stride=3), :].astype(BF16)


def third_shard_kernel(where, down, third):
    for q in range(4):
        third[q * S : (q + 1) * S, :] = down[:, q * COLS : (q + 1) * COLS].astype(BF16)


def pair_kernel(where, b0, b1, pair):
    pair[0] = b0[...]
    pair[1] = b1[...]


def whole_kernel(where, *refs):
    *pieces, line = refs
    for k in range(QUADS):
        line[k] = pieces[k][...] if len(pieces) == QUADS else pieces[k // 2][k % 2]


def halves_kernel(where, from_x, from_y, near_y, far_x):
    near_y[...] = from_y[0:2]
    far_x[...] = from_x[2:4]


def token_kernel(where, tokens, grads, *outs):
    for m, out in enumerate(outs):
        out[0] = tokens[where[0] ^ m]
        out[1] = grads[where[0] ^ m]


ORDER = (0, 2, 1, 3)


def blocks(where, pieces):
    found = [(piece, i) for piece in pieces for i in range(piece.shape[0])]
    for at, (piece, i) in enumerate(found):
        yield where[0] ^ (at // QUADS), where[1] ^ ORDER[at % QUADS], piece[i]


def unpack_tokens(x):
    parts = [jnp.concatenate([x[r][:, :W], x[r][:, W:]], axis=0) for r in range(ROWS)]
    return jnp.concatenate(parts, axis=1)


def pack_tokens(value, room, k):
    for r in range(ROWS):
        both = value[:, r * W : (r + 1) * W]
        room[r, k] = jnp.concatenate([both[:PAIRS], both[PAIRS:]], axis=1).astype(BF16)


def attend_kernel(where, t0, t1, t2, t3, vecs, *refs):
    pieces, refs = refs[:5], refs[5:]
    tokens, grads, wj, wo, mixed, probs, attended, part, room, mixing, scores, parts = refs
    for m, piece in enumerate([t0, t1, t2, t3]):
        room[where[0] ^ m] = piece[...]
    tokens[...] = unpack_tokens([room[r, 0] for r in range(ROWS)])
    grads[...] = unpack_tokens([room[r, 1] for r in range(ROWS)])
    half = HEADS // 2
    for row, quad, value in blocks(where, pieces):
        for h in range(half):
            rows = value[h * S : (h + 1) * S, :]
            for k, cut in enumerate([rows[:, :W], rows[:, W:]]):
                start = pl.multiple_of((h + k * half) * 3 * HD + quad * S, 16)
                wj[row, pl.ds(start, S), :] = cut
        start = pl.multiple_of(row * W + quad * S, 16)
        wo[pl.ds(start, S), :] = value[half * S :, :]
    total = dot(wj[0], tokens[:, :W], NT)
    for r in range(1, ROWS):
        total = total + dot(wj[r], tokens[:, r * W : (r + 1) * W], NT)
    mixing[...] = total
    query_bias, value_bias = [
        pick_col(where, row_of(vecs, start, 3), row_of(vecs, start + 3, 3)) for start in (0, 6)
    ]
    zero = jnp.zeros((1, HD), F32)
    row = []
    for h in range(HEADS):
        at = slice(h * HD, (h + 1) * HD)
        row += [query_bias[:, at], zero, value_bias[:, at]]
    row = jnp.concatenate(row, axis=1)
    high, low = split_parts(row)
    rest = (row - high.astype(F32) - low.astype(F32)).astype(BF16)
    parts[...] = jnp.zeros_like(parts)
    parts[0:1, :] = high.astype(F32)
    parts[1:2, :] = low.astype(F32)
    parts[2:3, :] = rest.astype(F32)
    bias = dot(parts[...].astype(BF16), jnp.ones((8, LEN), BF16), TN)
    mixed[...] = (mixing[...] + bias).astype(BF16)
    slot = lax.broadcasted_iota(jnp.int32, (LEN, 1), 0)
    slot = jnp.where(slot < PAIRS, 2 * slot, 2 * (slot - PAIRS) + 1)
    valid = slot < where[3]
    for h in range(HEADS):
        base = h * 3 * HD
        query, keyed, valued = [mixed[base + k * HD : base + (k + 1) * HD, :] for k in range(3)]
        scores[...] = dot(keyed, query, TN)
        for q in range(2):
            at = slice(q * 128, (q + 1) * 128)
            score = jnp.where(valid, scores[:, at] * 0.125, -1e30)
            expo = jnp.exp(score - jnp.max(score, axis=0, keepdims=True))
            prob = expo * (1.0 / jnp.sum(expo, axis=0, keepdims=True))
            probs[h, :, at] = prob.astype(BF16)
        attended[h * HD : (h + 1) * HD, :] = dot(valued, probs[h], NN).astype(BF16)
    part[...] = dot(attended[...], wo[...], ((0,), (1,))).astype(BF16)


def norm_rows(resid, gain, shift_by):
    mean = jnp.sum(resid, axis=1, keepdims=True) * (1.0 / D)
    var = jnp.sum(resid * resid, axis=1, keepdims=True) * (1.0 / D) - mean * mean
    inverse = lax.rsqrt(var + NORM_EPS)
    normed = (resid - mean) * inverse
    return normed * gain + shift_by, normed, inverse


def norm_back_rows(grad, normed, inverse, gain):
    scaled = grad * gain
    total = jnp.sum(scaled, axis=1, keepdims=True) * (1.0 / D)
    cross = jnp.sum(scaled * normed, axis=1, keepdims=True) * (1.0 / D)
    return (scaled - total - normed * cross) * inverse


STRIP = 32


def strip(i):
    return pl.ds(pl.multiple_of(i * STRIP, STRIP), STRIP)


def up_kernel(where, tokens, p0, p1, vecs, *refs):
    pieces, refs = refs[:5], refs[5:]
    hidden, low, normed, inverse, act, slope, wu, pre = refs
    for row, quad, value in blocks(where, pieces):
        rows = pl.ds(pl.multiple_of(row * W, W), W)
        wu[rows, pl.ds(pl.multiple_of(quad * COLS, COLS), COLS)] = value

    bias_out, gain, shift_by = [vector_row(vecs, k) for k in (2, 3, 4)]

    def first(i):
        at = strip(i)
        resid = tokens[at, :].astype(F32) + (p0[at, :].astype(F32) + p1[at, :].astype(F32))
        out, unit, scale = norm_rows(resid + bias_out, gain, shift_by)
        hidden[at, :] = out
        low[at, :] = out.astype(BF16)
        normed[at, :] = unit
        inverse[at, :] = scale

    each(LEN // STRIP, first)
    pre[...] = dot(low[...], wu[...], NN)
    bias = pick_col(where, row_of(vecs, 48, 12), row_of(vecs, 60, 12))
    for q in range(4):
        cols = slice(q * COLS, (q + 1) * COLS)
        shift_up = bias[:, cols]

        def second(i, cols=cols, shift_up=shift_up):
            at = (strip(i), cols)
            value = pre[at] + shift_up
            phi = 0.5 * (1.0 + lax.erf(value * (0.5**0.5)))
            density = jnp.exp(-0.5 * value * value) * 0.3989422804014327
            act[at] = (value * phi).astype(BF16)
            slope[at] = phi + value * density

        each(LEN // STRIP, second)


def down_kernel(where, act, *refs):
    pieces, wd, part = refs[:5], refs[5], refs[6]
    for row, quad, value in blocks(where, pieces):
        rows = pl.ds(pl.multiple_of(row * W + quad * S, 16), S)
        for q in range(4):
            wd[rows, q * COLS : (q + 1) * COLS] = value[q * S : (q + 1) * S, :]
    part[...] = dot(act[...], wd[...], NT).astype(BF16)


def hand_out(where, room, outs):
    r = where[0]
    last_x, last_y, own = outs[-3:]
    if len(outs) == 5:
        far_x, far_y = [out.at[0:2] for out in outs[:2]]
        near_x, near_y = [out.at[2:4] for out in outs[:2]]
    else:
        far_x, far_y, near_x, near_y = outs[:4]
    far_x[...] = room[r ^ 3, 0:2]
    far_y[...] = room[r ^ 3, 2:4]
    near_x[...] = room[r ^ 1, 0:2]
    near_y[...] = room[r ^ 2, 2:4]
    last_x[...] = room[r ^ 1, 2:4]
    last_y[...] = room[r ^ 2, 0:2]
    own[...] = room[r]


PAIR = shape(2, *CHUNK)
LINE = shape(4, *CHUNK)
HANDED = [LINE] * 2 + [PAIR] * 2 + [LINE]
SPLIT = [PAIR] * 6 + [LINE]

VROWS = 32
VECTOR = (VROWS, COLS)
CARRIED = (2 * W + 2 * VROWS, COLS)
FIRST = (4 * W + 2 * VROWS, COLS)


def put_vector(out, start, value):
    high, low = split_parts(value)
    out[start : start + VROWS, :] = high
    out[start + VROWS : start + 2 * VROWS, :] = low


def get_vector(value, start):
    high = value[start : start + VROWS, :].astype(F32)
    return high + value[start + VROWS : start + 2 * VROWS, :].astype(F32)


def second_norm_kernel(where, hidden, p0, p1, vecs, grads, act, *refs):
    (result, low, grad_two, sums), handed, room = refs[:4], refs[4:11], refs[11]
    sums[...] = jnp.zeros_like(sums)
    bias_down, gain, shift_by = [vector_row(vecs, k) for k in (5, 6, 7)]

    def body(i):
        at = strip(i)
        resid = hidden[at, :] + (p0[at, :].astype(F32) + p1[at, :].astype(F32)) + bias_down
        out, unit, scale = norm_rows(resid, gain, shift_by)
        result[at, :] = out
        grad = grads[at, :].astype(F32)
        back = norm_back_rows(grad, unit, scale, gain)
        grad_two[at, :] = back
        rounded = back.astype(BF16)
        low[at, :] = rounded
        sums[0:1, :] += jnp.sum(rounded.astype(F32), axis=0, keepdims=True)
        sums[1:2, :] += jnp.sum(grad * unit, axis=0, keepdims=True)
        sums[2:3, :] += jnp.sum(grad, axis=0, keepdims=True)

    each(LEN // STRIP, body)
    for q in range(4):
        cols = slice(q * COLS, (q + 1) * COLS)
        grad = dot(low[...], act[:, cols], TN).astype(BF16)
        for r in range(ROWS):
            for z in range(QUADS):
                start = r * W + z * S
                room[r, z, q * S : (q + 1) * S, :] = grad[start : start + S, :]
    hand_out(where, room, handed)


def hidden_back_kernel(where, low, slope, wd, wu, grad_pre, part, sums, back):
    back[...] = dot(low[...], wd[...], NN)
    sums[...] = jnp.zeros_like(sums)
    for q in range(4):
        cols = slice(q * COLS, (q + 1) * COLS)

        def body(i, cols=cols):
            at = (strip(i), cols)
            value = (back[at] * slope[at]).astype(BF16)
            grad_pre[at] = value
            sums[0:1, cols] += jnp.sum(value.astype(F32), axis=0, keepdims=True)

        each(LEN // STRIP, body)
    part[...] = dot(grad_pre[...], wu[...], NT).astype(BF16)


def up_grad_kernel(where, low, grad_pre, *refs):
    handed, room = refs[:5], refs[5]
    for z in range(QUADS):
        grad = dot(low[...], grad_pre[:, z * COLS : (z + 1) * COLS], TN).astype(BF16)
        for r in range(ROWS):
            room[r, z] = grad[r * W : (r + 1) * W, :]
    hand_out(where, room, handed)


def first_norm_kernel(where, grad_two, p0, p1, normed, inverse, vecs, wo, mixed, probs, attended, tokens, sums_two, sums_up, *refs):
    grad_one, grad_mixed, vector, room, low, back, inner, scores, sums = refs
    sums[...] = jnp.zeros_like(sums)
    gain = vector_row(vecs, 3)

    def body(i):
        at = strip(i)
        grad = grad_two[at, :] + (p0[at, :].astype(F32) + p1[at, :].astype(F32))
        unit = normed[at, :]
        out = norm_back_rows(grad, unit, inverse[at, :], gain)
        grad_one[at, :] = out
        rounded = out.astype(BF16)
        low[at, :] = rounded
        sums[0:1, :] += jnp.sum(rounded.astype(F32), axis=0, keepdims=True)
        sums[1:2, :] += jnp.sum(grad * unit, axis=0, keepdims=True)
        sums[2:3, :] += jnp.sum(grad, axis=0, keepdims=True)

    each(LEN // STRIP, body)
    back[...] = dot(wo[...], low[...], ((0,), (1,))).astype(BF16)
    for h in range(HEADS):
        base = h * 3 * HD
        query, keyed, valued = [mixed[base + k * HD : base + (k + 1) * HD, :] for k in range(3)]
        grad_out = back[h * HD : (h + 1) * HD, :]
        inner[...] = dot(valued, grad_out, TN)
        for q in range(2):
            at = slice(q * 128, (q + 1) * 128)
            prob = probs[h, :, at].astype(F32)
            grad = inner[:, at]
            mean = jnp.sum(grad * prob, axis=0, keepdims=True)
            scores[:, at] = (prob * (grad - mean)).astype(BF16)
        grads = [
            dot(keyed, scores[...], NN) * 0.125,
            dot(query, scores[...], NT) * 0.125,
            dot(grad_out, probs[h], NT),
        ]
        for k, grad in enumerate(grads):
            grad_mixed[base + k * HD : base + (k + 1) * HD, :] = grad.astype(BF16)
    half = HEADS // 2
    for r in range(ROWS):
        cut = tokens[:, r * W : (r + 1) * W]
        grad = dot(grad_mixed[...], cut, NN).astype(BF16)
        for z in range(QUADS):
            for h in range(half):
                starts = [(h + k * half) * 3 * HD + z * S for k in range(2)]
                pair = [grad[start : start + S, :] for start in starts]
                room[r, z, h * S : (h + 1) * S, :] = jnp.concatenate(pair, axis=1)
        grad = dot(low[:, r * W : (r + 1) * W], attended[...], ((0,), (1,))).astype(BF16)
        for z in range(QUADS):
            room[r, z, half * S :, :] = grad[z * S : (z + 1) * S, :]
    left = jnp.where(where[2] == 0, 1.0, 0.0)
    right = 1.0 - left
    total = dot(jnp.ones((8, LEN), BF16), grad_mixed[...], NT)[0:1, :]
    vector[...] = jnp.zeros_like(vector)
    for k, start in enumerate([0, 2 * HD]):
        at = [h * 3 * HD + start for h in range(HEADS)]
        row = jnp.concatenate([total[:, i : i + HD] for i in at], axis=1)
        vector[2 * k : 2 * k + 1, :] = row * left
        vector[2 * k + 1 : 2 * k + 2, :] = row * right
    for k, found in enumerate([sums, sums_two]):
        for i in range(3):
            for j in range(2):
                row = 4 + 6 * k + 2 * i + j
                vector[row : row + 1, :] = found[i : i + 1, j * COLS : (j + 1) * COLS] * left
    for j in range(4):
        row = sums_up[0:1, j * COLS : (j + 1) * COLS]
        vector[16 + j : 17 + j, :] = row * left
        vector[20 + j : 21 + j, :] = row * right


def first_hand_kernel(where, room, vector, carried, *refs):
    handed, first = refs[:-1], refs[-1]
    hand_out(where, room, [first, *handed])
    for k in range(4):
        carried[k * W : (k + 1) * W, :] = first[k]
    put_vector(carried, 4 * W, vector[...])


def token_back_kernel(where, grad_mixed, wj, part):
    for r in range(ROWS):
        part[:, r * W : (r + 1) * W] = dot(grad_mixed[...], wj[r], TN).astype(BF16)


def token_sum_kernel(where, result, grad_one, p0, p1, *refs):
    outs, total, room = refs[:4], refs[4], refs[5]

    def body(i):
        at = strip(i)
        total[at, :] = grad_one[at, :] + (p0[at, :].astype(F32) + p1[at, :].astype(F32))

    each(LEN // STRIP, body)
    pack_tokens(result, room, 0)
    pack_tokens(total, room, 1)
    for m, out in enumerate(outs):
        out[...] = room[where[0] ^ m]


def token_out_kernel(where, t0, t1, t2, t3, result, total):
    for m, piece in enumerate([t0, t1, t2, t3]):
        for k, out in enumerate([result, total]):
            for q in range(3):
                value = piece[k, :, q * 128 : (q + 1) * 128].astype(F32)
                out[where[0] ^ m, pl.ds(q, PAIRS, stride=3), :] = value


def pass_kernel(where, last_x, last_y, from_x, from_y, to_x, to_y):
    to_x[...] = (last_x[...].astype(F32) + from_y[0:2].astype(F32)).astype(BF16)
    to_y[...] = (last_y[...].astype(F32) + from_x[0:2].astype(F32)).astype(BF16)


def carry_pass_kernel(where, last_x, last_y, carried, from_x, from_y, to_x, to_y):
    to_x[...] = (last_x[...].astype(F32) + from_y[0:2].astype(F32)).astype(BF16)
    for k in range(2):
        rows = slice(k * W, (k + 1) * W)
        to_y[rows, :] = (last_y[k].astype(F32) + from_x[rows, :].astype(F32)).astype(BF16)
    put_vector(to_y, 2 * W, get_vector(carried, 4 * W) + get_vector(from_x, 4 * W))


def add_plane(own, from_x, from_y, last_x, last_y, room):
    for k in range(2):
        room[k] = (own[k].astype(F32) + from_x(k)) + last_y(k)
        room[2 + k] = (own[2 + k].astype(F32) + from_y(k)) + last_x(k)


def kept_blocks(ref):
    skip = ref.shape[0] - 2
    return lambda k: ref[skip + k].astype(F32)


def kept_rows(ref, start):
    return lambda k: ref[start + k * W : start + (k + 1) * W, :].astype(F32)


def line_kernel(where, own, from_x, from_y, last_x, last_y, kept, *refs):
    *sends, room = refs
    add_plane(own, *[kept_blocks(v) for v in (from_x, from_y, last_x, last_y)], room)
    if sends:
        kept[...] = room[where[1]]
        for mask, send in zip(ORDER[1:], sends):
            send[...] = room[where[1] ^ mask].astype(BF16)
    else:
        kept[...] = room[...]


def near_line_kernel(where, own, from_x, from_y, last_x, last_y, kept, *refs):
    *sends, room = refs
    add_plane(own, *[kept_blocks(v) for v in (from_x, from_y, last_x, last_y)], room)
    if sends:
        for k, mask in enumerate([0, 2]):
            kept[k] = room[where[1] ^ mask]
            sends[0][k] = room[where[1] ^ mask ^ 1].astype(BF16)
    else:
        kept[...] = room[...]


def far_line_kernel(where, kept, got, total, send):
    total[...] = kept[0] + got[0].astype(F32)
    send[...] = (kept[1] + got[1].astype(F32)).astype(BF16)


def carry_near_kernel(where, own, from_x, near_y, last_x, from_y, passed, kept, *refs):
    *sends, room = refs
    near_x = kept_rows(from_x, 2 * W)
    add_plane(own, near_x, kept_blocks(near_y), kept_blocks(last_x), kept_rows(from_y, 0), room)
    vector = get_vector(passed, 2 * W) + get_vector(from_y, 2 * W)
    if kept.ndim == 2:
        for k, mask in enumerate([0, 2]):
            rows = slice(k * W, (k + 1) * W)
            kept[rows, :] = room[where[1] ^ mask]
            sends[0][rows, :] = room[where[1] ^ mask ^ 1].astype(BF16)
        kept[2 * W :, :] = vector
        put_vector(sends[0], 2 * W, vector)
    else:
        kept[...] = room[...]
        sends[0][...] = vector


def add_vector(own, got, start):
    high, low = split_parts(own)
    return (high.astype(F32) + low.astype(F32)) + get_vector(got, start)


def carry_far_kernel(where, kept, got, total, send):
    total[0:W, :] = kept[0:W, :] + got[0:W, :].astype(F32)
    send[0:W, :] = (kept[W : 2 * W, :] + got[W : 2 * W, :].astype(F32)).astype(BF16)
    vector = add_vector(kept[2 * W :, :], got, 2 * W)
    total[W:, :] = vector
    put_vector(send, W, vector)


def adamw(weight, first, second, grad, rate, decay):
    first_new = BETA_ONE * first + (1.0 - BETA_ONE) * grad
    second_new = BETA_TWO * second + (1.0 - BETA_TWO) * grad * grad
    fix_one = 1.0 - BETA_ONE**STEP
    fix_two = 1.0 - BETA_TWO**STEP
    update = first_new / fix_one / (jnp.sqrt(second_new / fix_two) + ADAM_EPS) + decay * weight
    return (first_new, second_new, weight - rate * update)


JOINT_RATE = D ** (-0.5)
OUTPUT_RATE = (4 * D // LEN) ** (-0.5)
DOWN_RATE = FF ** (-0.5)


def first_adam_kernel(where, kept, got, jw, jf, js, ow, of, os, *refs):
    outs, vector = refs[:6], refs[6]
    grad = kept[0:W, :] + got[0:W, :].astype(F32)
    half = HEADS // 2
    for h in range(HEADS):
        rows = grad[h % half * S : (h % half + 1) * S, :]
        cut = rows[:, :W] if h < half else rows[:, W:]
        new = adamw(jw[h], jf[h], js[h], cut, JOINT_RATE, DECAY)
        for out, value in zip(outs[:3], new):
            out[h] = value
    new = adamw(ow[...], of[...], os[...], grad[half * S :, :], OUTPUT_RATE, DECAY)
    for out, value in zip(outs[3:], new):
        out[...] = value
    vector[...] = add_vector(kept[W:, :], got, W)


def vector_adam_kernel(where, mine, other, weight, first, second, *refs):
    outs, grad = refs[:3], refs[3]
    total = mine[...] + other[...]
    for q in range(3):
        grad[pl.ds(q, 24, stride=3), :] = total[0:24, q * 128 : (q + 1) * 128]
    new = adamw(weight[...], first[...], second[...], grad[...], VECTOR_RATE, 0.0)
    for out, value in zip(outs, new):
        out[...] = value


def up_adam_kernel(where, kept, r2, r1, r3, w, f, s, *outs):
    grad = (kept[...] + r1[...].astype(F32)) + (r2[...].astype(F32) + r3[...].astype(F32))
    for q in range(3):
        at = (pl.ds(q, W, stride=3), slice(None))
        cut = grad[:, q * 128 : (q + 1) * 128]
        for out, value in zip(outs, adamw(w[at], f[at], s[at], cut, JOINT_RATE, DECAY)):
            out[at] = value


def down_adam_kernel(where, kept, got, w, f, s, *outs):
    grad = kept[...] + got[...].astype(F32)
    for q in range(4):
        at = (slice(None), slice(q * COLS, (q + 1) * COLS))
        cut = grad[q * S : (q + 1) * S, :]
        for out, value in zip(outs, adamw(w[at], f[at], s[at], cut, DOWN_RATE, DECAY)):
            out[at] = value


def gather_line(where, shard, steps):
    if steps == 1:
        return [shard] + [swap(shard, "dp", mask) for mask in ORDER[1:]]
    pair = run(pair_kernel, where, [shard, swap(shard, "dp", 2)], [PAIR])[0]
    return [pair, swap(pair, "dp", 1)]


def gather_plane(where, line, after=()):
    line = run(whole_kernel, where, line, [LINE], after=after)[0]
    from_x = swap(line, "row", 1)
    from_y = swap(line, "row", 2)
    near_y, far_x = run(halves_kernel, where, [from_x, from_y], [PAIR] * 2)
    return [line, from_x, from_y, swap(near_y, "row", 1), swap(far_x, "row", 2)]


def scatter_first(handed):
    return [swap(value, "row", 1 + i % 2) for i, value in enumerate(handed[:-3])]


def scatter_pass(where, handed, got, after=()):
    return run(pass_kernel, where, handed[-3:-1] + got[:2], [PAIR] * 2, after=after)


def scatter_second(passed):
    return [swap(passed[0], "row", 1), swap(passed[1], "row", 2)]


def exchange(pieces):
    return [pieces[0]] + [swap(pieces[m], "row", m) for m in range(1, ROWS)]


def wide_lines(joint, output, up, down):
    order = jnp.array(ORDER)
    n = lax.axis_size("dp") // QUADS

    def collect(shard, axis):
        whole = lax.all_gather(shard.astype(BF16), "dp", axis=axis, tiled=True)
        return jnp.stack(jnp.split(whole, QUADS, axis=axis))

    joint = collect(joint, 1)
    half = HEADS // 2
    pair = joint.reshape(QUADS, 2, half, S, W)
    pair = jnp.transpose(pair, (0, 2, 3, 1, 4)).reshape(QUADS, half * S, 2 * W)
    first = jnp.concatenate([pair, collect(output, 0)], axis=1)
    second = collect(up, 1)
    third = collect(down, 0).reshape(QUADS, S, 4, COLS)
    third = jnp.transpose(third, (0, 2, 1, 3)).reshape(QUADS, W, COLS)
    return [jnp.take(value, order, axis=0) for value in (first, second, third)]


def wide_sums(first, second, third):
    def give(value, axis):
        whole = jnp.concatenate(list(value), axis=axis)
        return lax.psum_scatter(whole, "dp", scatter_dimension=axis, tiled=True)

    half = HEADS // 2
    pair = first[:, : half * S].reshape(QUADS, half, S, 2, W)
    joint = jnp.transpose(pair, (0, 3, 1, 2, 4)).reshape(QUADS, HEADS, S, W)
    third = jnp.transpose(third.reshape(QUADS, 4, S, COLS), (0, 2, 1, 3))
    third = third.reshape(QUADS, S, FFC)
    return give(joint, 1), give(first[:, half * S :], 0), give(second, 1), give(third, 0)


def per_device(
    tokens_in,
    lengths,
    joint_weight,
    joint_first,
    joint_second,
    output_weight,
    output_first,
    output_second,
    up_weight,
    up_first,
    up_second,
    down_weight,
    down_first,
    down_second,
    vectors,
    vector_first,
    vector_second,
    out_grad,
):
    r = lax.axis_index("row")
    col = lax.axis_index("col")
    direct = lax.axis_size("dp") == QUADS
    z = lax.axis_index("dp") if direct else jnp.int32(0)
    where = jnp.stack([r, z, col, lengths[0]]).astype(jnp.int32)

    joint = [jnp.transpose(v, (1, 2, 0)) for v in (joint_weight, joint_first, joint_second)]
    output = [v[:, 0].T for v in (output_weight, output_first, output_second)]
    down = [v[:, 0].T for v in (down_weight, down_first, down_second)]
    up = [up_weight, up_first, up_second]
    flat = up_weight.size // 128

    sent = [tokens_in.reshape(ROWS, PAIRS, 2 * W), out_grad.reshape(ROWS, PAIRS, 2 * W)]
    blocks_out = [shape(2, PAIRS, 2 * W)] * ROWS
    if direct:
        up = [v.reshape(flat, 128) for v in up]
        one = [shape(*CHUNK)]
        *pieces, first = run(
            opening_kernel,
            where,
            sent + [joint[0], output[0]],
            blocks_out + one,
            [
                pltpu.VMEM(sent[0].shape, BF16),
                pltpu.VMEM(sent[1].shape, BF16),
                pltpu.VMEM(joint[0].shape, F32),
                pltpu.VMEM(output[0].shape, F32),
                pltpu.SemaphoreType.DMA((4,)),
            ],
            limit=56,
            fetch=True,
        )
        tokens_pieces = exchange(pieces)
        first = gather_line(where, first, 1)
        first_pieces = gather_plane(where, first, tokens_pieces[1:])
        shard = run(second_shard_kernel, where, [up[0]], one, after=first[1:])[0]
        second = gather_line(where, shard, 2)
        second_pieces = gather_plane(where, second)
        shard = run(third_shard_kernel, where, [down[0]], one, after=second[1:])[0]
        third = gather_line(where, shard, 2)
        third_pieces = gather_plane(where, third, first_pieces[3:])
    else:
        tokens_pieces = exchange(run(token_kernel, where, sent, blocks_out))
        lines = wide_lines(joint[0], output[0], up_weight[:, 0], down[0])
        first_pieces, second_pieces, third_pieces = [
            gather_plane(where, list(line)) for line in lines
        ]

    vecs = vectors.reshape(72, 128)
    tokens, grads, wj, wo, mixed, probs, attended, part = run(
        attend_kernel,
        where,
        tokens_pieces + [vecs] + first_pieces,
        [
            shape(LEN, D),
            shape(LEN, D),
            shape(ROWS, MIX, W),
            shape(D, COLS),
            shape(MIX, LEN),
            shape(HEADS, LEN, LEN),
            shape(COLS, LEN),
            shape(LEN, D),
        ],
        [
            pltpu.VMEM((ROWS, 2, PAIRS, 2 * W), BF16),
            pltpu.VMEM((MIX, LEN), F32),
            pltpu.VMEM((LEN, LEN), F32),
            pltpu.VMEM((8, MIX), F32),
        ],
    )
    hidden, hidden_low, normed, inverse, act, slope, wu = run(
        up_kernel,
        where,
        [tokens, part, swap(part, "col", 1), vecs] + second_pieces,
        [
            shape(LEN, D, dtype=F32),
            shape(LEN, D),
            shape(LEN, D, dtype=F32),
            shape(LEN, 1, dtype=F32),
            shape(LEN, FFC),
            shape(LEN, FFC, dtype=F32),
            shape(D, FFC),
        ],
        [pltpu.VMEM((LEN, FFC), F32)],
    )
    wd, part = run(
        down_kernel, where, [act] + third_pieces, [shape(D, FFC), shape(LEN, D)]
    )
    out = run(
        second_norm_kernel,
        where,
        [hidden, part, swap(part, "col", 1), vecs, grads, act],
        [shape(LEN, D, dtype=F32), shape(LEN, D), shape(LEN, D, dtype=F32)]
        + [shape(8, D, dtype=F32)]
        + SPLIT,
        [pltpu.VMEM((ROWS, QUADS) + CHUNK, BF16)],
    )
    (result, grad_low, grad_two, sums_two), third_handed = out[:4], out[4:]
    third_got = scatter_first(third_handed)
    grad_pre, part, sums_up = run(
        hidden_back_kernel,
        where,
        [grad_low, slope, wd, wu],
        [shape(LEN, FFC), shape(LEN, D), shape(8, FFC, dtype=F32)],
        [pltpu.VMEM((LEN, FFC), F32)],
    )
    third_passed = scatter_pass(where, third_handed, third_got, [part])
    third_last = scatter_second(third_passed)
    second_handed = run(
        up_grad_kernel,
        where,
        [hidden_low, grad_pre],
        HANDED,
        [pltpu.VMEM((ROWS, QUADS) + CHUNK, BF16)],
        after=third_last,
    )
    grad_one, grad_mixed, vector, room = run(
        first_norm_kernel,
        where,
        [
            grad_two,
            part,
            swap(part, "col", 1),
            normed,
            inverse,
            vecs,
            wo,
            mixed,
            probs,
            attended,
            tokens,
            sums_two,
            sums_up,
        ],
        [shape(LEN, D, dtype=F32), shape(MIX, LEN), shape(*VECTOR, dtype=F32)]
        + [shape(ROWS, QUADS, *CHUNK)],
        [
            pltpu.VMEM((LEN, D), BF16),
            pltpu.VMEM((COLS, LEN), BF16),
            pltpu.VMEM((LEN, LEN), F32),
            pltpu.VMEM((LEN, LEN), BF16),
            pltpu.VMEM((8, D), F32),
        ],
    )
    first_handed = run(
        first_hand_kernel,
        where,
        [room, vector],
        [shape(*FIRST)] + HANDED[1:],
        [pltpu.VMEM((4,) + CHUNK, BF16)],
        after=third_passed + third_got[2:],
    )
    first_got = scatter_first(first_handed)
    first_passed = run(
        carry_pass_kernel,
        where,
        first_handed[2:4] + first_handed[:1] + first_got,
        [PAIR, shape(*CARRIED)],
    )
    first_last = scatter_second(first_passed)

    def like(values):
        return [shape(*v.shape, dtype=F32) for v in values]

    def sums(dims, split):
        return [shape(*dims, dtype=F32), shape(*split)]

    lines = [pltpu.VMEM((4,) + CHUNK, F32)]
    wide = [shape(4, *CHUNK, dtype=F32)]
    third_sum = run(
        near_line_kernel,
        where,
        third_handed[-1:] + third_got[2:] + third_last,
        sums(PAIR.shape, PAIR.shape) if direct else wide,
        lines,
    )
    if direct:
        got = swap(third_sum[1], "dp", 1)
        third_sum = run(far_line_kernel, where, [third_sum[0], got], sums(CHUNK, CHUNK))
    second_got = scatter_first(second_handed)
    second_passed = scatter_pass(where, second_handed, second_got, third_sum[1:])
    second_last = scatter_second(second_passed)
    first_sum = run(
        carry_near_kernel,
        where,
        first_handed[-1:] + first_got + first_last + first_passed[1:],
        sums((2 * W + VROWS, COLS), CARRIED) if direct else wide + [shape(*VECTOR, dtype=F32)],
        lines,
        after=second_passed,
    )
    second_sum = run(
        line_kernel,
        where,
        second_handed[-1:] + second_got + second_last,
        sums(CHUNK, CHUNK) + [shape(*CHUNK)] * 2 if direct else wide,
        lines,
    )
    ready = []
    if direct:
        got = swap(third_sum[1], "dp", 2)
        down_new = run(down_adam_kernel, where, [third_sum[0], got] + down, like(down))
        ready = down_new[:1]
        got = swap(first_sum[1], "dp", 1)
        first_sum = run(
            carry_far_kernel,
            where,
            [first_sum[0], got],
            sums((W + VROWS, COLS), (W + 2 * VROWS, COLS)),
        )
        got = swap(first_sum[1], "dp", 2)
        state = joint + output
        new = run(
            first_adam_kernel,
            where,
            [first_sum[0], got] + state,
            like(state) + [shape(*VECTOR, dtype=F32)],
        )
        joint_new, output_new, vector = new[:3], new[3:6], new[6]

    (part,) = run(token_back_kernel, where, [grad_mixed, wj], [shape(LEN, D)], after=second_passed)
    pieces = run(
        token_sum_kernel,
        where,
        [result, grad_one, part, swap(part, "col", 1)],
        [shape(2, PAIRS, 2 * W)] * ROWS,
        [pltpu.VMEM((LEN, D), F32), pltpu.VMEM((ROWS, 2, PAIRS, 2 * W), BF16)],
        after=ready,
    )
    flat_out = [shape(ROWS, 3 * PAIRS, 128, dtype=F32)] * 2
    out = run(token_out_kernel, where, exchange(pieces), flat_out)
    layer_out, tokens_grad = [v.reshape(tokens_in.shape) for v in out]

    if direct:
        got = [swap(v, "dp", mask) for v, mask in zip(second_sum[1:], ORDER[1:])]
        up_new = run(up_adam_kernel, where, second_sum[:1] + got + up, like(up), after=out[:1])
        up_new = [v.reshape(up_weight.shape) for v in up_new]
    else:
        grads = wide_sums(first_sum[0], second_sum[0], third_sum[0])
        joint_new = adamw(*joint, grads[0], JOINT_RATE, DECAY)
        output_new = adamw(*output, grads[1], OUTPUT_RATE, DECAY)
        up_new = adamw(*up, grads[2][:, None], JOINT_RATE, DECAY)
        down_new = adamw(*down, grads[3], DOWN_RATE, DECAY)
        vector = lax.psum(first_sum[1], "dp")

    state = [v.reshape(72, 128) for v in (vectors, vector_first, vector_second)]
    vector_new = run(
        vector_adam_kernel,
        where,
        [vector, swap(vector, "col", 1)] + state,
        like(state),
        [pltpu.VMEM((72, 128), F32)],
    )
    vector_new = [v.reshape(vectors.shape) for v in vector_new]

    return (
        layer_out,
        tokens_grad,
        *[jnp.transpose(v, (2, 0, 1)) for v in joint_new],
        *[v.T[:, None] for v in output_new],
        *up_new,
        *[v.T[:, None] for v in down_new],
        *vector_new,
    )


def solution(mesh):
    first = P("row", "col", "dp")
    second = P("col", "row", "dp")
    tokens = P("dp", "row", None)
    weights = (first,) * 3 + (second,) * 3 + (first,) * 3 + (second,) * 3 + (P(),) * 3
    in_specs = (tokens, P(("dp", "row"))) + weights + (tokens,)
    out_specs = (tokens, tokens) + weights
    return jax.shard_map(
        per_device, mesh=mesh, in_specs=in_specs, out_specs=out_specs, check_vma=False
    )
```

time: 703 us -> 211 us (0.30)
  waiting for transfers between devices: 430 us -> 64.4 us
  blocking collectives: 150 us -> 0 us
  starting transfers between devices: 0.8 us -> 86.4 us
  Pallas kernels: 0 us -> 50.6 us
  matrix products: 40.3 us -> 0 us
  other arithmetic: 38.6 us -> 0.59 us
  local copies, waits for them, and re-layouts: 25.9 us -> 4.69 us
  between operations: 15.2 us -> 1.81 us
    reduce_scatter x8 -> x0, waiting for transfers between devices: 282 us -> none  [the longest x2 119 us: first_forward(): lax.psum_scatter(jnp.dot(value, flat, preferred_element_type=jnp.float32)...]
    all_gather x3 -> x0, waiting for transfers between devices: 111 us -> none  [the longest x2 81.6 us: first_backward(): full = lax.all_gather(grad, 'row', axis=0, tiled=True)]
    ppermute x0 -> x51, starting transfers between devices: none -> 86.4 us  [swap(): return lax.ppermute(value, axis, [(i, i ^ mask) for i in range(n)])]
    all_gather x5 -> x0, blocking collectives: 79.1 us -> none  [the longest x1 22.1 us: per_device(): lax.all_gather(up_weight.astype(jnp.bfloat16), 'dp', axis=2, tiled=True)]
    psum x5 -> x0, blocking collectives: 71.3 us -> none  [the longest x1 40.9 us: per_device(): vector_grad = lax.psum(vector_local, ('dp', 'row', 'col'))]
    ppermute x0 -> x51, waiting for transfers between devices: none -> 64.4 us  [swap(): return lax.ppermute(value, axis, [(i, i ^ mask) for i in range(n)])]
    pallas_call x0 -> x34, Pallas kernels: none -> 50.6 us  [run(): pl.pallas_call(body, out_shape=outs, in_specs=[pl.BlockSpec(memory_space=...]
    dot_general x18 -> x0, matrix products: 40.3 us -> none  [the longest x2 7.54 us: first_backward(): jnp.einsum('tn,kn->tk', full, flat, preferred_element_type=jnp.float32)]
  transfers between devices with their start and end apart: 15 -> 51, of which waited for: 12 -> 19; matrix products, arithmetic and copies ran while one was open for 6% -> 0% of each run, Pallas kernels for 0% -> 18%
where the time goes in v1:
time: 211 us; the launch traced here: 208 us
  starting transfers between devices  86.4 us (41%)
  waiting for transfers between devices  64.4 us (31%)
  Pallas kernels  50.6 us (24%)
  local copies, waits for them, and re-layouts  4.69 us (2%)
    ppermute x51, starting transfers between devices, swap(): return lax.ppermute(value, axis, [(i, i ^ mask) for i in range(n)])  86.4 us
    ppermute x51, waiting for transfers between devices, swap(): return lax.ppermute(value, axis, [(i, i ^ mask) for i in range(n)])  64.4 us
    pallas_call x34, Pallas kernels, run(): pl.pallas_call(body, out_shape=outs, in_specs=[pl.BlockSpec(memory_space=...  50.6 us
    unnamed x42, local copies, waits for them, and re-layouts  4.69 us
  transfers between devices with their start and end apart: 51, of which 19 were waited for; matrix products, arithmetic and copies ran while one was open for 0% of the time, Pallas kernels for 18%

profile of v1, /device:TPU:1, one launch (start us, length us, event | category | flops | bytes accessed | tf_op | source)
XLA Modules:
  0.0 208.4 jit_solution(1701114751836679166)
XLA Ops:
  1.9 2.9 %shard_map.305 = (bf16[2,128,384]{2,1,0:T(8,128)(2,1)}, bf16[2,128,384]{2,1,0:T(8,128)(2,1)}, bf16[2,128,384]{2,1,0:T(8,128)(2,1)}, bf16[2,128,384]{2,1,0:T(8,128)(2,1)}, bf16[192,384]{1,0:T(8,128)(2,1)}) custom-call(s32[4]{0:T(128)} %pad_add_fusion.refs_0_, bf16[4,128,384]{2,1,0:T(8,128)(2,1)} %bitcast.86, bf16[4,128,384]{2,1,0:T(8,128)(2,1)} %bitcast.87, ...), custom_call_target="tpu_custom_call" | custom-call | tf_op jit(solution)/shard_map/pallas_call | solution.py:56
  4.9 4.2 %collective-permute-start.5 = (bf16[192,384]{1,0:T(8,128)(2,1)}, bf16[192,384]{1,0:T(8,128)(2,1)S(1)}, u32[]{:S(2)}, u32[]{:S(2)}) collective-permute-start(bf16[192,384]{1,0:T(8,128)(2,1)} %get-tuple-element.117.refs_1_), channel_id=1, source_target_pairs={{0,24},{8,16},{16,8},{24,0},{1,25},{9,17},{17,9},{25,1},{2,26},{10... | collective-permute-start | bytes 442376 | tf_op jit(solution)/shard_map/ppermute | solution.py:42
  9.1 1.2 collective-permute-start
  10.3 1.2 collective-permute-start.1
  12.9 1.5 collective-permute-start.3
  14.4 1.8 collective-permute-done.4.refs_3_
  16.2 1.9 collective-permute-done.3.refs_2_
  20.3 2.6 %collective-permute-start.11 = (bf16[192,384]{1,0:T(8,128)(2,1)S(1)}, bf16[192,384]{1,0:T(8,128)(2,1)S(1)}, u32[]{:S(2)}, u32[]{:S(2)}) collective-permute-start(bf16[192,384]{1,0:T(8,128)(2,1)S(1)} %shard_map.309.refs_1_), channel_id=1, source_target_pairs={{0,16},{8,24},{16,0},{24,8},{1,17},{9,25},{17,1},{25,9},{2,18},{10... | collective-permute-start | bytes 442376 | tf_op jit(solution)/shard_map/ppermute | solution.py:42
  24.4 1.3 collective-permute-start.7
  25.8 1.2 collective-permute-start.6
  27.5 2.6 %collective-permute-start.12 = (bf16[2,192,384]{2,1,0:T(8,128)(2,1)S(1)}, bf16[2,192,384]{2,1,0:T(8,128)(2,1)S(1)}, u32[]{:S(2)}, u32[]{:S(2)}) collective-permute-start(bf16[2,192,384]{2,1,0:T(8,128)(2,1)S(1)} %shard_map.310.refs_1_), channel_id=1, source_target_pairs={{0,8},{8,0},{16,24},{24,16},{1,9},{9,1},{17,25},{25,17},{2,10},{10... | collective-permute-start | bytes 884744 | tf_op jit(solution)/shard_map/ppermute | solution.py:42
  30.1 5.9 %collective-permute-done.12.refs_2_ = bf16[2,192,384]{2,1,0:T(8,128)(2,1)S(1)} collective-permute-done((bf16[2,192,384]{2,1,0:T(8,128)(2,1)S(1)}, bf16[2,192,384]{2,1,0:T(8,128)(2,1)S(1)}, u32[]{:S(2)}, u32[]{:S(2)}) %collective-permute-start.12) | collective-permute-done | bytes 294944 | tf_op jit(solution)/shard_map/ppermute | solution.py:42
  36.7 6.3 %collective-permute-done.17.refs_2_ = bf16[192,384]{1,0:T(8,128)(2,1)S(1)} collective-permute-done((bf16[192,384]{1,0:T(8,128)(2,1)S(1)}, bf16[192,384]{1,0:T(8,128)(2,1)S(1)}, u32[]{:S(2)}, u32[]{:S(2)}) %collective-permute-start.17) | collective-permute-done | bytes 147488 | tf_op jit(solution)/shard_map/ppermute | solution.py:42
  48.0 2.1 %collective-permute-done.18.refs_2_ = bf16[2,192,384]{2,1,0:T(8,128)(2,1)S(1)} collective-permute-done((bf16[2,192,384]{2,1,0:T(8,128)(2,1)S(1)}, bf16[2,192,384]{2,1,0:T(8,128)(2,1)S(1)}, u32[]{:S(2)}, u32[]{:S(2)}) %collective-permute-start.18) | collective-permute-done | bytes 294944 | tf_op jit(solution)/shard_map/ppermute | solution.py:42
  52.7 5.2 %shard_map.308 = (bf16[256,768]{1,0:T(8,128)(2,1)S(1)}, bf16[256,768]{1,0:T(8,128)(2,1)S(1)}, bf16[4,1152,192]{2,1,0:T(8,128)(2,1)S(1)}, bf16[768,384]{1,0:T(8,1...) custom-call(s32[4]{0:T(128)S(1)} %copy-done.6, ...), custom_call_target="tpu_custom_call" | custom-call | tf_op jit(solution)/shard_map/pallas_call | solution.py:56
  57.9 12.9 %collective-permute-start.10 = (bf16[256,768]{1,0:T(8,128)(2,1)S(1)}, bf16[256,768]{1,0:T(8,128)(2,1)S(1)}, u32[]{:S(2)}, u32[]{:S(2)}) collective-permute-start(bf16[256,768]{1,0:T(8,128)(2,1)S(1)} %get-tuple-element.121.refs_2_), channel_id=1, source_target_pairs={{0,1},{1,0},{2,3},{3,2},{4,5},{5,4},{6,7},{7,6},{8,9},{9,8},{10,11... | collective-permute-start | bytes 1179656 | tf_op jit(solution)/shard_map/ppermute | solution.py:42
  71.4 1.4 collective-permute-start.15
  75.0 5.5 %collective-permute-done.15.refs_8_ = bf16[2,192,384]{2,1,0:T(8,128)(2,1)S(1)} collective-permute-done((bf16[2,192,384]{2,1,0:T(8,128)(2,1)S(1)}, bf16[2,192,384]{2,1,0:T(8,128)(2,1)S(1)}, u32[]{:S(2)}, u32[]{:S(2)}) %collective-permute-start.15) | collective-permute-done | bytes 294944 | tf_op jit(solution)/shard_map/ppermute | solution.py:42
  80.5 1.3 collective-permute-done.16.refs_9_
  81.8 3.6 %shard_map.313 = (f32[256,768]{1,0:T(8,128)S(1)}, bf16[256,768]{1,0:T(8,128)(2,1)S(1)}, f32[256,768]{1,0:T(8,128)S(1)}, f32[256,1]{1,0:T(8,128)S(1)}, bf16[256,1...) custom-call(s32[4]{0:T(128)S(1)} %copy-done.6, ...), custom_call_target="tpu_custom_call" | custom-call | tf_op jit(solution)/shard_map/pallas_call | solution.py:56
  85.5 1.4 collective-permute-done.21.refs_5_
  86.8 1.3 collective-permute-done.22.refs_6_
  88.1 1.5 shard_map.318
  89.7 4.7 %collective-permute-start.23 = (bf16[256,768]{1,0:T(8,128)(2,1)S(1)}, bf16[256,768]{1,0:T(8,128)(2,1)S(1)}, u32[]{:S(2)}, u32[]{:S(2)}) collective-permute-start(bf16[256,768]{1,0:T(8,128)(2,1)S(1)} %get-tuple-element.128.refs_2_), channel_id=1, source_target_pairs={{0,1},{1,0},{2,3},{3,2},{4,5},{5,4},{6,7},{7,6},{8,9},{9,8},{10,11... | collective-permute-start | bytes 1179656 | tf_op jit(solution)/shard_map/ppermute | solution.py:42
  94.4 1.3 collective-permute-done.23.refs_3_
  95.7 3.6 %shard_map.319 = (f32[256,768]{1,0:T(8,128)S(1)}, bf16[256,768]{1,0:T(8,128)(2,1)S(1)}, f32[256,768]{1,0:T(8,128)S(1)}, f32[8,768]{1,0:T(8,128)S(1)}, bf16[2,192...) custom-call(s32[4]{0:T(128)S(1)} %copy-done.6, ...), custom_call_target="tpu_custom_call" | custom-call | tf_op jit(solution)/shard_map/pallas_call | solution.py:56
  99.4 3.3 %shard_map.320 = (bf16[256,1536]{1,0:T(8,128)(2,1)S(1)}, bf16[256,768]{1,0:T(8,128)(2,1)S(1)}, f32[8,1536]{1,0:T(8,128)S(1)}) custom-call(s32[4]{0:T(128)S(1)} %copy-done.6, bf16[256,768]{1,0:T(8,128)(2,1)S(1)} %get-tuple-element.132.refs_1_, f32[256,1536]{1,0:T(8,128)S(1)} %get-tuple-element.133.refs_2_, bf16[768,1536]{1,0:T(8,128)(2,1)S(1)} %get-tuple-element.134.refs_3_, ...), custom_call_target="tpu_custom_call" | custom-call | tf_op jit(solution)/shard_map/pallas_call | solution.py:56
  106.0 5.5 %collective-permute-done.25.refs_3_ = bf16[2,192,384]{2,1,0:T(8,128)(2,1)S(1)} collective-permute-done((bf16[2,192,384]{2,1,0:T(8,128)(2,1)S(1)}, bf16[2,192,384]{2,1,0:T(8,128)(2,1)S(1)}, u32[]{:S(2)}, u32[]{:S(2)}) %collective-permute-start.25) | collective-permute-done | bytes 294944 | tf_op jit(solution)/shard_map/ppermute | solution.py:42
  112.9 5.6 %shard_map.321 = (f32[256,768]{1,0:T(8,128)S(1)}, bf16[1152,256]{1,0:T(8,128)(2,1)S(1)}, f32[32,384]{1,0:T(8,128)S(1)}, bf16[4,4,192,384]{3,2,1,0:T(8,128)(2,1)S(1)}) custom-call(s32[4]{0:T(128)S(1)} %copy-done.6, f32[256,768]{1,0:T(8,128)S(1)} %get-tuple-element.131.refs_1_, bf16[256,768]{1,0:T(8,128)(2,1)S(1)} %get-tuple-element.136.refs_2_.refs_5_, ...), custom_call_target="tpu_custom_call" | custom-call | tf_op jit(solution)/shard_map/pallas_call | solution.py:56
  122.4 17.1 %collective-permute-done.27.refs_3_.refs_4_ = bf16[2,192,384]{2,1,0:T(8,128)(2,1)S(1)} collective-permute-done((bf16[2,192,384]{2,1,0:T(8,128)(2,1)S(1)}, bf16[2,192,384]{2,1,0:T(8,128)(2,1)S(1)}, u32[]{:S(2)}, u32[]{:S(2)}) %collective-permute-start.27) | collective-permute-done | bytes 294944 | tf_op jit(solution)/shard_map/ppermute | solution.py:42
  139.5 1.8 shard_map.323
  143.4 1.5 collective-permute-start.33
  147.4 1.9 collective-permute-done.33.refs_2_
  150.0 3.1 %collective-permute-done.29.refs_3_.refs_2_ = bf16[4,192,384]{2,1,0:T(8,128)(2,1)S(1)} collective-permute-done((bf16[4,192,384]{2,1,0:T(8,128)(2,1)S(1)}, bf16[4,192,384]{2,1,0:T(8,128)(2,1)S(1)}, u32[]{:S(2)}, u32[]{:S(2)}) %collective-permute-start.29) | collective-permute-done | bytes 589856 | tf_op jit(solution)/shard_map/ppermute | solution.py:42
  154.0 1.5 shard_map.327.refs_3_
  155.6 8.0 %collective-permute-start.34 = (bf16[256,768]{1,0:T(8,128)(2,1)S(1)}, bf16[256,768]{1,0:T(8,128)(2,1)S(1)}, u32[]{:S(2)}, u32[]{:S(2)}) collective-permute-start(bf16[256,768]{1,0:T(8,128)(2,1)S(1)} %shard_map.327.refs_3_), channel_id=1, source_target_pairs={{0,1},{1,0},{2,3},{3,2},{4,5},{5,4},{6,7},{7,6},{8,9},{9,8},{10,11... | collective-permute-start | bytes 1179656 | tf_op jit(solution)/shard_map/ppermute | solution.py:42
  164.4 1.5 collective-permute-start.43
  165.9 1.8 collective-permute-start.35
  169.7 5.3 %collective-permute-done.35.refs_2_ = bf16[192,384]{1,0:T(8,128)(2,1)S(1)} collective-permute-done((bf16[192,384]{1,0:T(8,128)(2,1)S(1)}, bf16[192,384]{1,0:T(8,128)(2,1)S(1)}, u32[]{:S(2)}, u32[]{:S(2)}) %collective-permute-start.35) | collective-permute-done | bytes 147488 | tf_op jit(solution)/shard_map/ppermute | solution.py:42
  175.1 1.6 shard_map.328
  180.4 2.9 %collective-permute-start.44 = (bf16[256,384]{1,0:T(8,128)(2,1)S(1)}, bf16[256,384]{1,0:T(8,128)(2,1)S(1)}, u32[]{:S(2)}, u32[]{:S(2)}) collective-permute-start(bf16[256,384]{1,0:T(8,128)(2,1)S(1)} %get-tuple-element.188), channel_id=1, source_target_pairs={{0,16},{8,24},{16,0},{24,8},{1,17},{9,25},{17,1},{25,9},{2,18},{10... | collective-permute-start | bytes 589832 | tf_op jit(solution)/shard_map/ppermute | solution.py:42
  185.9 2.7 %collective-permute-start.48 = (bf16[192,384]{1,0:T(8,128)(2,1)S(1)}, bf16[192,384]{1,0:T(8,128)(2,1)S(1)}, u32[]{:S(2)}, u32[]{:S(2)}) collective-permute-start(bf16[192,384]{1,0:T(8,128)(2,1)S(1)} %get-tuple-element.198), channel_id=1, source_target_pairs={{0,8},{8,0},{16,24},{24,16},{1,9},{9,1},{17,25},{25,17},{2,10},{10... | collective-permute-start | bytes 442376 | tf_op jit(solution)/shard_map/ppermute | solution.py:42
  188.6 7.6 %collective-permute-start.49 = (bf16[192,384]{1,0:T(8,128)(2,1)S(1)}, bf16[192,384]{1,0:T(8,128)(2,1)S(1)}, u32[]{:S(2)}, u32[]{:S(2)}) collective-permute-start(bf16[192,384]{1,0:T(8,128)(2,1)S(1)} %get-tuple-element.199), channel_id=1, source_target_pairs={{0,24},{8,16},{16,8},{24,0},{1,25},{9,17},{17,9},{25,1},{2,26},{10... | collective-permute-start | bytes 442376 | tf_op jit(solution)/shard_map/ppermute | solution.py:42
  196.2 1.7 shard_map.335
  198.0 4.6 %collective-permute-start.50 = (f32[32,384]{1,0:T(8,128)S(1)}, f32[32,384]{1,0:T(8,128)S(1)}, u32[]{:S(2)}, u32[]{:S(2)}) collective-permute-start(f32[32,384]{1,0:T(8,128)S(1)} %get-tuple-element.205.refs_1_), channel_id=1, source_target_pairs={{0,1},{1,0},{2,3},{3,2},{4,5},{5,4},{6,7},{7,6},{8,9},{9,8},{10,11... | collective-permute-start | bytes 147464 | tf_op jit(solution)/shard_map/ppermute | solution.py:42
  202.5 1.8 shard_map.330
  205.5 1.7 shard_map.337
  207.2 1.2 shard_map.338
  (131 shorter events, 42.4 us)
Async XLA Ops:
  4.9 8.0 %collective-permute-start.5 = (bf16[192,384]{1,0:T(8,128)(2,1)}, bf16[192,384]{1,0:T(8,128)(2,1)S(1)}, u32[]{:S(2)}, u32[]{:S(2)}) collective-permute-start(bf16[192,384]{1,0:T(8,128)(2,1)} %get-tuple-element.117.refs_1_), channel_id=1, source_target_pairs={{0,24},{8,16},{16,8},{24,0},{1,25},{9,17},{17,9},{25,1},{2,26},{10... | collective-permute-start | bytes 442376 | tf_op jit(solution)/shard_map/ppermute | solution.py:42
  9.1 13.8 %collective-permute-start = (bf16[2,128,384]{2,1,0:T(8,128)(2,1)}, bf16[2,128,384]{2,1,0:T(8,128)(2,1)S(1)}, u32[]{:S(2)}, u32[]{:S(2)}) collective-permute-start(bf16[2,128,384]{2,1,0:T(8,128)(2,1)} %get-tuple-element.114), channel_id=1, source_target_pairs={{0,2},{2,0},{4,6},{6,4},{1,3},{3,1},{5,7},{7,5},{8,10},{10,8},{12,... | collective-permute-start | bytes 589832 | tf_op jit(solution)/shard_map/ppermute | solution.py:42
  10.3 12.6 %collective-permute-start.1 = (bf16[2,128,384]{2,1,0:T(8,128)(2,1)}, bf16[2,128,384]{2,1,0:T(8,128)(2,1)S(1)}, u32[]{:S(2)}, u32[]{:S(2)}) collective-permute-start(bf16[2,128,384]{2,1,0:T(8,128)(2,1)} %get-tuple-element.115), channel_id=1, source_target_pairs={{0,4},{2,6},{4,0},{6,2},{1,5},{3,7},{5,1},{7,3},{8,12},{10,14},{12... | collective-permute-start | bytes 589832 | tf_op jit(solution)/shard_map/ppermute | solution.py:42
  11.5 11.4 %collective-permute-start.2 = (bf16[2,128,384]{2,1,0:T(8,128)(2,1)}, bf16[2,128,384]{2,1,0:T(8,128)(2,1)S(1)}, u32[]{:S(2)}, u32[]{:S(2)}) collective-permute-start(bf16[2,128,384]{2,1,0:T(8,128)(2,1)} %get-tuple-element.116), channel_id=1, source_target_pairs={{0,6},{2,4},{4,2},{6,0},{1,7},{3,5},{5,3},{7,1},{8,14},{10,12},{12... | collective-permute-start | bytes 589832 | tf_op jit(solution)/shard_map/ppermute | solution.py:42
  20.3 6.6 %collective-permute-start.11 = (bf16[192,384]{1,0:T(8,128)(2,1)S(1)}, bf16[192,384]{1,0:T(8,128)(2,1)S(1)}, u32[]{:S(2)}, u32[]{:S(2)}) collective-permute-start(bf16[192,384]{1,0:T(8,128)(2,1)S(1)} %shard_map.309.refs_1_), channel_id=1, source_target_pairs={{0,16},{8,24},{16,0},{24,8},{1,17},{9,25},{17,1},{25,9},{2,18},{10... | collective-permute-start | bytes 442376 | tf_op jit(solution)/shard_map/ppermute | solution.py:42
  24.4 19.3 %collective-permute-start.7 = (bf16[4,192,384]{2,1,0:T(8,128)(2,1)S(1)}, bf16[4,192,384]{2,1,0:T(8,128)(2,1)S(1)}, u32[]{:S(2)}, u32[]{:S(2)}) collective-permute-start(bf16[4,192,384]{2,1,0:T(8,128)(2,1)S(1)} %shard_map.306.refs_6_), channel_id=1, source_target_pairs={{0,4},{2,6},{4,0},{6,2},{1,5},{3,7},{5,1},{7,3},{8,12},{10,14},{12... | collective-permute-start | bytes 1769480 | tf_op jit(solution)/shard_map/ppermute | solution.py:42
  25.8 18.0 %collective-permute-start.6 = (bf16[4,192,384]{2,1,0:T(8,128)(2,1)S(1)}, bf16[4,192,384]{2,1,0:T(8,128)(2,1)S(1)}, u32[]{:S(2)}, u32[]{:S(2)}) collective-permute-start(bf16[4,192,384]{2,1,0:T(8,128)(2,1)S(1)} %shard_map.306.refs_6_), channel_id=1, source_target_pairs={{0,2},{2,0},{4,6},{6,4},{1,3},{3,1},{5,7},{7,5},{8,10},{10,8},{12,... | collective-permute-start | bytes 1769480 | tf_op jit(solution)/shard_map/ppermute | solution.py:42
  27.5 8.5 %collective-permute-start.12 = (bf16[2,192,384]{2,1,0:T(8,128)(2,1)S(1)}, bf16[2,192,384]{2,1,0:T(8,128)(2,1)S(1)}, u32[]{:S(2)}, u32[]{:S(2)}) collective-permute-start(bf16[2,192,384]{2,1,0:T(8,128)(2,1)S(1)} %shard_map.310.refs_1_), channel_id=1, source_target_pairs={{0,8},{8,0},{16,24},{24,16},{1,9},{9,1},{17,25},{25,17},{2,10},{10... | collective-permute-start | bytes 884744 | tf_op jit(solution)/shard_map/ppermute | solution.py:42
  36.6 6.4 %collective-permute-start.17 = (bf16[192,384]{1,0:T(8,128)(2,1)S(1)}, bf16[192,384]{1,0:T(8,128)(2,1)S(1)}, u32[]{:S(2)}, u32[]{:S(2)}) collective-permute-start(bf16[192,384]{1,0:T(8,128)(2,1)S(1)} %shard_map.314.refs_1_), channel_id=1, source_target_pairs={{0,16},{8,24},{16,0},{24,8},{1,17},{9,25},{17,1},{25,9},{2,18},{10... | collective-permute-start | bytes 442376 | tf_op jit(solution)/shard_map/ppermute | solution.py:42
  43.6 6.5 %collective-permute-start.18 = (bf16[2,192,384]{2,1,0:T(8,128)(2,1)S(1)}, bf16[2,192,384]{2,1,0:T(8,128)(2,1)S(1)}, u32[]{:S(2)}, u32[]{:S(2)}) collective-permute-start(bf16[2,192,384]{2,1,0:T(8,128)(2,1)S(1)} %shard_map.315.refs_1_), channel_id=1, source_target_pairs={{0,8},{8,0},{16,24},{24,16},{1,9},{9,1},{17,25},{25,17},{2,10},{10... | collective-permute-start | bytes 884744 | tf_op jit(solution)/shard_map/ppermute | solution.py:42
  44.3 5.8 %collective-permute-start.8 = (bf16[2,192,384]{2,1,0:T(8,128)(2,1)S(1)}, bf16[2,192,384]{2,1,0:T(8,128)(2,1)S(1)}, u32[]{:S(2)}, u32[]{:S(2)}) collective-permute-start(bf16[2,192,384]{2,1,0:T(8,128)(2,1)S(1)} %get-tuple-element.118), channel_id=1, source_target_pairs={{0,2},{2,0},{4,6},{6,4},{1,3},{3,1},{5,7},{7,5},{8,10},{10,8},{12,... | collective-permute-start | bytes 884744 | tf_op jit(solution)/shard_map/ppermute | solution.py:42
  46.2 24.6 %collective-permute-start.14 = (bf16[4,192,384]{2,1,0:T(8,128)(2,1)S(1)}, bf16[4,192,384]{2,1,0:T(8,128)(2,1)S(1)}, u32[]{:S(2)}, u32[]{:S(2)}) collective-permute-start(bf16[4,192,384]{2,1,0:T(8,128)(2,1)S(1)} %shard_map.311.refs_5_), channel_id=1, source_target_pairs={{0,4},{2,6},{4,0},{6,2},{1,5},{3,7},{5,1},{7,3},{8,12},{10,14},{12... | collective-permute-start | bytes 1769480 | tf_op jit(solution)/shard_map/ppermute | solution.py:42
  47.0 23.8 %collective-permute-start.13 = (bf16[4,192,384]{2,1,0:T(8,128)(2,1)S(1)}, bf16[4,192,384]{2,1,0:T(8,128)(2,1)S(1)}, u32[]{:S(2)}, u32[]{:S(2)}) collective-permute-start(bf16[4,192,384]{2,1,0:T(8,128)(2,1)S(1)} %shard_map.311.refs_5_), channel_id=1, source_target_pairs={{0,2},{2,0},{4,6},{6,4},{1,3},{3,1},{5,7},{7,5},{8,10},{10,8},{12,... | collective-permute-start | bytes 1769480 | tf_op jit(solution)/shard_map/ppermute | solution.py:42
  51.0 21.9 %collective-permute-start.20 = (bf16[4,192,384]{2,1,0:T(8,128)(2,1)S(1)}, bf16[4,192,384]{2,1,0:T(8,128)(2,1)S(1)}, u32[]{:S(2)}, u32[]{:S(2)}) collective-permute-start(bf16[4,192,384]{2,1,0:T(8,128)(2,1)S(1)} %shard_map.316.refs_2_), channel_id=1, source_target_pairs={{0,4},{2,6},{4,0},{6,2},{1,5},{3,7},{5,1},{7,3},{8,12},{10,14},{12... | collective-permute-start | bytes 1769480 | tf_op jit(solution)/shard_map/ppermute | solution.py:42
  52.0 20.9 %collective-permute-start.19 = (bf16[4,192,384]{2,1,0:T(8,128)(2,1)S(1)}, bf16[4,192,384]{2,1,0:T(8,128)(2,1)S(1)}, u32[]{:S(2)}, u32[]{:S(2)}) collective-permute-start(bf16[4,192,384]{2,1,0:T(8,128)(2,1)S(1)} %shard_map.316.refs_2_), channel_id=1, source_target_pairs={{0,2},{2,0},{4,6},{6,4},{1,3},{3,1},{5,7},{7,5},{8,10},{10,8},{12,... | collective-permute-start | bytes 1769480 | tf_op jit(solution)/shard_map/ppermute | solution.py:42
  57.9 17.1 %collective-permute-start.10 = (bf16[256,768]{1,0:T(8,128)(2,1)S(1)}, bf16[256,768]{1,0:T(8,128)(2,1)S(1)}, u32[]{:S(2)}, u32[]{:S(2)}) collective-permute-start(bf16[256,768]{1,0:T(8,128)(2,1)S(1)} %get-tuple-element.121.refs_2_), channel_id=1, source_target_pairs={{0,1},{1,0},{2,3},{3,2},{4,5},{5,4},{6,7},{7,6},{8,9},{9,8},{10,11... | collective-permute-start | bytes 1179656 | tf_op jit(solution)/shard_map/ppermute | solution.py:42
  71.4 9.2 %collective-permute-start.15 = (bf16[2,192,384]{2,1,0:T(8,128)(2,1)S(1)}, bf16[2,192,384]{2,1,0:T(8,128)(2,1)S(1)}, u32[]{:S(2)}, u32[]{:S(2)}) collective-permute-start(bf16[2,192,384]{2,1,0:T(8,128)(2,1)S(1)} %get-tuple-element.122), channel_id=1, source_target_pairs={{0,2},{2,0},{4,6},{6,4},{1,3},{3,1},{5,7},{7,5},{8,10},{10,8},{12,... | collective-permute-start | bytes 884744 | tf_op jit(solution)/shard_map/ppermute | solution.py:42
  72.7 9.1 %collective-permute-start.16 = (bf16[2,192,384]{2,1,0:T(8,128)(2,1)S(1)}, bf16[2,192,384]{2,1,0:T(8,128)(2,1)S(1)}, u32[]{:S(2)}, u32[]{:S(2)}) collective-permute-start(bf16[2,192,384]{2,1,0:T(8,128)(2,1)S(1)} %get-tuple-element.123), channel_id=1, source_target_pairs={{0,4},{2,6},{4,0},{6,2},{1,5},{3,7},{5,1},{7,3},{8,12},{10,14},{12... | collective-permute-start | bytes 884744 | tf_op jit(solution)/shard_map/ppermute | solution.py:42
  73.5 13.3 %collective-permute-start.21 = (bf16[2,192,384]{2,1,0:T(8,128)(2,1)S(1)}, bf16[2,192,384]{2,1,0:T(8,128)(2,1)S(1)}, u32[]{:S(2)}, u32[]{:S(2)}) collective-permute-start(bf16[2,192,384]{2,1,0:T(8,128)(2,1)S(1)} %get-tuple-element.126), channel_id=1, source_target_pairs={{0,2},{2,0},{4,6},{6,4},{1,3},{3,1},{5,7},{7,5},{8,10},{10,8},{12,... | collective-permute-start | bytes 884744 | tf_op jit(solution)/shard_map/ppermute | solution.py:42
  74.3 13.9 %collective-permute-start.22 = (bf16[2,192,384]{2,1,0:T(8,128)(2,1)S(1)}, bf16[2,192,384]{2,1,0:T(8,128)(2,1)S(1)}, u32[]{:S(2)}, u32[]{:S(2)}) collective-permute-start(bf16[2,192,384]{2,1,0:T(8,128)(2,1)S(1)} %get-tuple-element.127), channel_id=1, source_target_pairs={{0,4},{2,6},{4,0},{6,2},{1,5},{3,7},{5,1},{7,3},{8,12},{10,14},{12... | collective-permute-start | bytes 884744 | tf_op jit(solution)/shard_map/ppermute | solution.py:42
  89.7 6.0 %collective-permute-start.23 = (bf16[256,768]{1,0:T(8,128)(2,1)S(1)}, bf16[256,768]{1,0:T(8,128)(2,1)S(1)}, u32[]{:S(2)}, u32[]{:S(2)}) collective-permute-start(bf16[256,768]{1,0:T(8,128)(2,1)S(1)} %get-tuple-element.128.refs_2_), channel_id=1, source_target_pairs={{0,1},{1,0},{2,3},{3,2},{4,5},{5,4},{6,7},{7,6},{8,9},{9,8},{10,11... | collective-permute-start | bytes 1179656 | tf_op jit(solution)/shard_map/ppermute | solution.py:42
  102.7 10.3 %collective-permute-start.24 = (bf16[256,768]{1,0:T(8,128)(2,1)S(1)}, bf16[256,768]{1,0:T(8,128)(2,1)S(1)}, u32[]{:S(2)}, u32[]{:S(2)}) collective-permute-start(bf16[256,768]{1,0:T(8,128)(2,1)S(1)} %get-tuple-element.136.refs_2_.refs_5_), channel_id=1, source_target_pairs={{0,1},{1,0},{2,3},{3,2},{4,5},{5,4},{6,7},{7,6},{8,9},{9,8},{10,11... | collective-permute-start | bytes 1179656 | tf_op jit(solution)/shard_map/ppermute | solution.py:42
  103.1 8.5 %collective-permute-start.25 = (bf16[2,192,384]{2,1,0:T(8,128)(2,1)S(1)}, bf16[2,192,384]{2,1,0:T(8,128)(2,1)S(1)}, u32[]{:S(2)}, u32[]{:S(2)}) collective-permute-start(bf16[2,192,384]{2,1,0:T(8,128)(2,1)S(1)} %get-tuple-element.152), channel_id=1, source_target_pairs={{0,2},{2,0},{4,6},{6,4},{1,3},{3,1},{5,7},{7,5},{8,10},{10,8},{12,... | collective-permute-start | bytes 884744 | tf_op jit(solution)/shard_map/ppermute | solution.py:42
  104.1 8.1 %collective-permute-start.26 = (bf16[2,192,384]{2,1,0:T(8,128)(2,1)S(1)}, bf16[2,192,384]{2,1,0:T(8,128)(2,1)S(1)}, u32[]{:S(2)}, u32[]{:S(2)}) collective-permute-start(bf16[2,192,384]{2,1,0:T(8,128)(2,1)S(1)} %get-tuple-element.153), channel_id=1, source_target_pairs={{0,4},{2,6},{4,0},{6,2},{1,5},{3,7},{5,1},{7,3},{8,12},{10,14},{12... | collective-permute-start | bytes 884744 | tf_op jit(solution)/shard_map/ppermute | solution.py:42
  104.5 14.0 %collective-permute-start.31 = (bf16[2,192,384]{2,1,0:T(8,128)(2,1)S(1)}, bf16[2,192,384]{2,1,0:T(8,128)(2,1)S(1)}, u32[]{:S(2)}, u32[]{:S(2)}) collective-permute-start(bf16[2,192,384]{2,1,0:T(8,128)(2,1)S(1)} %get-tuple-element.161), channel_id=1, source_target_pairs={{0,2},{2,0},{4,6},{6,4},{1,3},{3,1},{5,7},{7,5},{8,10},{10,8},{12,... | collective-permute-start | bytes 884744 | tf_op jit(solution)/shard_map/ppermute | solution.py:42
  105.3 13.3 %collective-permute-start.32 = (bf16[2,192,384]{2,1,0:T(8,128)(2,1)S(1)}, bf16[2,192,384]{2,1,0:T(8,128)(2,1)S(1)}, u32[]{:S(2)}, u32[]{:S(2)}) collective-permute-start(bf16[2,192,384]{2,1,0:T(8,128)(2,1)S(1)} %get-tuple-element.162), channel_id=1, source_target_pairs={{0,4},{2,6},{4,0},{6,2},{1,5},{3,7},{5,1},{7,3},{8,12},{10,14},{12... | collective-permute-start | bytes 884744 | tf_op jit(solution)/shard_map/ppermute | solution.py:42
  119.4 25.6 %collective-permute-start.39 = (bf16[832,384]{1,0:T(8,128)(2,1)S(1)}, bf16[832,384]{1,0:T(8,128)(2,1)S(1)}, u32[]{:S(2)}, u32[]{:S(2)}) collective-permute-start(bf16[832,384]{1,0:T(8,128)(2,1)S(1)} %get-tuple-element.179.refs_3_), channel_id=1, source_target_pairs={{0,2},{2,0},{4,6},{6,4},{1,3},{3,1},{5,7},{7,5},{8,10},{10,8},{12,... | collective-permute-start | bytes 1916936 | tf_op jit(solution)/shard_map/ppermute | solution.py:42
  119.9 19.6 %collective-permute-start.27 = (bf16[2,192,384]{2,1,0:T(8,128)(2,1)S(1)}, bf16[2,192,384]{2,1,0:T(8,128)(2,1)S(1)}, u32[]{:S(2)}, u32[]{:S(2)}) collective-permute-start(bf16[2,192,384]{2,1,0:T(8,128)(2,1)S(1)} %get-tuple-element.154.refs_3_), channel_id=1, source_target_pairs={{0,2},{2,0},{4,6},{6,4},{1,3},{3,1},{5,7},{7,5},{8,10},{10,8},{12,... | collective-permute-start | bytes 884744 | tf_op jit(solution)/shard_map/ppermute | solution.py:42
  120.9 18.6 %collective-permute-start.28 = (bf16[2,192,384]{2,1,0:T(8,128)(2,1)S(1)}, bf16[2,192,384]{2,1,0:T(8,128)(2,1)S(1)}, u32[]{:S(2)}, u32[]{:S(2)}) collective-permute-start(bf16[2,192,384]{2,1,0:T(8,128)(2,1)S(1)} %get-tuple-element.155.refs_4_), channel_id=1, source_target_pairs={{0,4},{2,6},{4,0},{6,2},{1,5},{3,7},{5,1},{7,3},{8,12},{10,14},{12... | collective-permute-start | bytes 884744 | tf_op jit(solution)/shard_map/ppermute | solution.py:42
  121.4 23.6 %collective-permute-start.40 = (bf16[4,192,384]{2,1,0:T(8,128)(2,1)S(1)}, bf16[4,192,384]{2,1,0:T(8,128)(2,1)S(1)}, u32[]{:S(2)}, u32[]{:S(2)}) collective-permute-start(bf16[4,192,384]{2,1,0:T(8,128)(2,1)S(1)} %get-tuple-element.180), channel_id=1, source_target_pairs={{0,4},{2,6},{4,0},{6,2},{1,5},{3,7},{5,1},{7,3},{8,12},{10,14},{12... | collective-permute-start | bytes 1769480 | tf_op jit(solution)/shard_map/ppermute | solution.py:42
  141.3 11.8 %collective-permute-start.29 = (bf16[4,192,384]{2,1,0:T(8,128)(2,1)S(1)}, bf16[4,192,384]{2,1,0:T(8,128)(2,1)S(1)}, u32[]{:S(2)}, u32[]{:S(2)}) collective-permute-start(bf16[4,192,384]{2,1,0:T(8,128)(2,1)S(1)} %get-tuple-element.158), channel_id=1, source_target_pairs={{0,2},{2,0},{4,6},{6,4},{1,3},{3,1},{5,7},{7,5},{8,10},{10,8},{12,... | collective-permute-start | bytes 1769480 | tf_op jit(solution)/shard_map/ppermute | solution.py:42
  141.8 11.5 %collective-permute-start.30 = (bf16[4,192,384]{2,1,0:T(8,128)(2,1)S(1)}, bf16[4,192,384]{2,1,0:T(8,128)(2,1)S(1)}, u32[]{:S(2)}, u32[]{:S(2)}) collective-permute-start(bf16[4,192,384]{2,1,0:T(8,128)(2,1)S(1)} %get-tuple-element.159), channel_id=1, source_target_pairs={{0,4},{2,6},{4,0},{6,2},{1,5},{3,7},{5,1},{7,3},{8,12},{10,14},{12... | collective-permute-start | bytes 1769480 | tf_op jit(solution)/shard_map/ppermute | solution.py:42
  143.4 5.9 %collective-permute-start.33 = (bf16[2,192,384]{2,1,0:T(8,128)(2,1)S(1)}, bf16[2,192,384]{2,1,0:T(8,128)(2,1)S(1)}, u32[]{:S(2)}, u32[]{:S(2)}) collective-permute-start(bf16[2,192,384]{2,1,0:T(8,128)(2,1)S(1)} %get-tuple-element.164), channel_id=1, source_target_pairs={{0,8},{8,0},{16,24},{24,16},{1,9},{9,1},{17,25},{25,17},{2,10},{10... | collective-permute-start | bytes 884744 | tf_op jit(solution)/shard_map/ppermute | solution.py:42
  145.6 17.9 %collective-permute-start.42 = (bf16[448,384]{1,0:T(8,128)(2,1)S(1)}, bf16[448,384]{1,0:T(8,128)(2,1)S(1)}, u32[]{:S(2)}, u32[]{:S(2)}) collective-permute-start(bf16[448,384]{1,0:T(8,128)(2,1)S(1)} %get-tuple-element.184.refs_6_), channel_id=1, source_target_pairs={{0,4},{2,6},{4,0},{6,2},{1,5},{3,7},{5,1},{7,3},{8,12},{10,14},{12... | collective-permute-start | bytes 1032200 | tf_op jit(solution)/shard_map/ppermute | solution.py:42
  146.4 17.1 %collective-permute-start.41 = (bf16[2,192,384]{2,1,0:T(8,128)(2,1)S(1)}, bf16[2,192,384]{2,1,0:T(8,128)(2,1)S(1)}, u32[]{:S(2)}, u32[]{:S(2)}) collective-permute-start(bf16[2,192,384]{2,1,0:T(8,128)(2,1)S(1)} %get-tuple-element.183), channel_id=1, source_target_pairs={{0,2},{2,0},{4,6},{6,4},{1,3},{3,1},{5,7},{7,5},{8,10},{10,8},{12,... | collective-permute-start | bytes 884744 | tf_op jit(solution)/shard_map/ppermute | solution.py:42
  155.6 21.1 %collective-permute-start.34 = (bf16[256,768]{1,0:T(8,128)(2,1)S(1)}, bf16[256,768]{1,0:T(8,128)(2,1)S(1)}, u32[]{:S(2)}, u32[]{:S(2)}) collective-permute-start(bf16[256,768]{1,0:T(8,128)(2,1)S(1)} %shard_map.327.refs_3_), channel_id=1, source_target_pairs={{0,1},{1,0},{2,3},{3,2},{4,5},{5,4},{6,7},{7,6},{8,9},{9,8},{10,11... | collective-permute-start | bytes 1179656 | tf_op jit(solution)/shard_map/ppermute | solution.py:42
  164.4 15.3 %collective-permute-start.43 = (bf16[448,384]{1,0:T(8,128)(2,1)S(1)}, bf16[448,384]{1,0:T(8,128)(2,1)S(1)}, u32[]{:S(2)}, u32[]{:S(2)}) collective-permute-start(bf16[448,384]{1,0:T(8,128)(2,1)S(1)} %get-tuple-element.186), channel_id=1, source_target_pairs={{0,8},{8,0},{16,24},{24,16},{1,9},{9,1},{17,25},{25,17},{2,10},{10... | collective-permute-start | bytes 1032200 | tf_op jit(solution)/shard_map/ppermute | solution.py:42
  165.9 9.1 %collective-permute-start.35 = (bf16[192,384]{1,0:T(8,128)(2,1)S(1)}, bf16[192,384]{1,0:T(8,128)(2,1)S(1)}, u32[]{:S(2)}, u32[]{:S(2)}) collective-permute-start(bf16[192,384]{1,0:T(8,128)(2,1)S(1)} %get-tuple-element.165.refs_5_), channel_id=1, source_target_pairs={{0,16},{8,24},{16,0},{24,8},{1,17},{9,25},{17,1},{25,9},{2,18},{10... | collective-permute-start | bytes 442376 | tf_op jit(solution)/shard_map/ppermute | solution.py:42
  167.8 15.9 %collective-permute-start.45 = (bf16[2,192,384]{2,1,0:T(8,128)(2,1)S(1)}, bf16[2,192,384]{2,1,0:T(8,128)(2,1)S(1)}, u32[]{:S(2)}, u32[]{:S(2)}) collective-permute-start(bf16[2,192,384]{2,1,0:T(8,128)(2,1)S(1)} %get-tuple-element.166.refs_3_.refs_7_), channel_id=1, source_target_pairs={{0,2},{2,0},{4,6},{6,4},{1,3},{3,1},{5,7},{7,5},{8,10},{10,8},{12,... | collective-permute-start | bytes 884744 | tf_op jit(solution)/shard_map/ppermute | solution.py:42
  168.7 16.2 %collective-permute-start.46 = (bf16[2,192,384]{2,1,0:T(8,128)(2,1)S(1)}, bf16[2,192,384]{2,1,0:T(8,128)(2,1)S(1)}, u32[]{:S(2)}, u32[]{:S(2)}) collective-permute-start(bf16[2,192,384]{2,1,0:T(8,128)(2,1)S(1)} %get-tuple-element.167.refs_4_.refs_8_), channel_id=1, source_target_pairs={{0,4},{2,6},{4,0},{6,2},{1,5},{3,7},{5,1},{7,3},{8,12},{10,14},{12... | collective-permute-start | bytes 884744 | tf_op jit(solution)/shard_map/ppermute | solution.py:42
  178.7 7.3 %collective-permute-start.36 = (bf16[2,128,384]{2,1,0:T(8,128)(2,1)S(1)}, bf16[2,128,384]{2,1,0:T(8,128)(2,1)S(1)}, u32[]{:S(2)}, u32[]{:S(2)}) collective-permute-start(bf16[2,128,384]{2,1,0:T(8,128)(2,1)S(1)} %get-tuple-element.171), channel_id=1, source_target_pairs={{0,2},{2,0},{4,6},{6,4},{1,3},{3,1},{5,7},{7,5},{8,10},{10,8},{12,... | collective-permute-start | bytes 589832 | tf_op jit(solution)/shard_map/ppermute | solution.py:42
  180.4 8.2 %collective-permute-start.44 = (bf16[256,384]{1,0:T(8,128)(2,1)S(1)}, bf16[256,384]{1,0:T(8,128)(2,1)S(1)}, u32[]{:S(2)}, u32[]{:S(2)}) collective-permute-start(bf16[256,384]{1,0:T(8,128)(2,1)S(1)} %get-tuple-element.188), channel_id=1, source_target_pairs={{0,16},{8,24},{16,0},{24,8},{1,17},{9,25},{17,1},{25,9},{2,18},{10... | collective-permute-start | bytes 589832 | tf_op jit(solution)/shard_map/ppermute | solution.py:42
  183.2 14.7 %collective-permute-start.37 = (bf16[2,128,384]{2,1,0:T(8,128)(2,1)S(1)}, bf16[2,128,384]{2,1,0:T(8,128)(2,1)S(1)}, u32[]{:S(2)}, u32[]{:S(2)}) collective-permute-start(bf16[2,128,384]{2,1,0:T(8,128)(2,1)S(1)} %get-tuple-element.172), channel_id=1, source_target_pairs={{0,4},{2,6},{4,0},{6,2},{1,5},{3,7},{5,1},{7,3},{8,12},{10,14},{12... | collective-permute-start | bytes 589832 | tf_op jit(solution)/shard_map/ppermute | solution.py:42
  183.7 18.9 %collective-permute-start.38 = (bf16[2,128,384]{2,1,0:T(8,128)(2,1)S(1)}, bf16[2,128,384]{2,1,0:T(8,128)(2,1)S(1)}, u32[]{:S(2)}, u32[]{:S(2)}) collective-permute-start(bf16[2,128,384]{2,1,0:T(8,128)(2,1)S(1)} %get-tuple-element.173), channel_id=1, source_target_pairs={{0,6},{2,4},{4,2},{6,0},{1,7},{3,5},{5,3},{7,1},{8,14},{10,12},{12... | collective-permute-start | bytes 589832 | tf_op jit(solution)/shard_map/ppermute | solution.py:42
  185.8 18.5 %collective-permute-start.47 = (bf16[192,384]{1,0:T(8,128)(2,1)S(1)}, bf16[192,384]{1,0:T(8,128)(2,1)S(1)}, u32[]{:S(2)}, u32[]{:S(2)}) collective-permute-start(bf16[192,384]{1,0:T(8,128)(2,1)S(1)} %get-tuple-element.197), channel_id=1, source_target_pairs={{0,16},{8,24},{16,0},{24,8},{1,17},{9,25},{17,1},{25,9},{2,18},{10... | collective-permute-start | bytes 442376 | tf_op jit(solution)/shard_map/ppermute | solution.py:42
  185.9 18.4 %collective-permute-start.48 = (bf16[192,384]{1,0:T(8,128)(2,1)S(1)}, bf16[192,384]{1,0:T(8,128)(2,1)S(1)}, u32[]{:S(2)}, u32[]{:S(2)}) collective-permute-start(bf16[192,384]{1,0:T(8,128)(2,1)S(1)} %get-tuple-element.198), channel_id=1, source_target_pairs={{0,8},{8,0},{16,24},{24,16},{1,9},{9,1},{17,25},{25,17},{2,10},{10... | collective-permute-start | bytes 442376 | tf_op jit(solution)/shard_map/ppermute | solution.py:42
  188.6 15.7 %collective-permute-start.49 = (bf16[192,384]{1,0:T(8,128)(2,1)S(1)}, bf16[192,384]{1,0:T(8,128)(2,1)S(1)}, u32[]{:S(2)}, u32[]{:S(2)}) collective-permute-start(bf16[192,384]{1,0:T(8,128)(2,1)S(1)} %get-tuple-element.199), channel_id=1, source_target_pairs={{0,24},{8,16},{16,8},{24,0},{1,25},{9,17},{17,9},{25,1},{2,26},{10... | collective-permute-start | bytes 442376 | tf_op jit(solution)/shard_map/ppermute | solution.py:42
  198.0 9.2 %collective-permute-start.50 = (f32[32,384]{1,0:T(8,128)S(1)}, f32[32,384]{1,0:T(8,128)S(1)}, u32[]{:S(2)}, u32[]{:S(2)}) collective-permute-start(f32[32,384]{1,0:T(8,128)S(1)} %get-tuple-element.205.refs_1_), channel_id=1, source_target_pairs={{0,1},{1,0},{2,3},{3,2},{4,5},{5,4},{6,7},{7,6},{8,9},{9,8},{10,11... | collective-permute-start | bytes 147464 | tf_op jit(solution)/shard_map/ppermute | solution.py:42
  (24 other events, 318.0 us)

commit v2 on v1

--- a/solution.py
+++ b/solution.py
@@ -759,7 +759,8 @@
         shard = run(second_shard_kernel, where, [up[0]], one, after=first[1:])[0]
         second = gather_line(where, shard, 2)
         second_pieces = gather_plane(where, second)
-        shard = run(third_shard_kernel, where, [down[0]], one, after=second[1:])[0]
+        after = second_pieces[:1] + first_pieces[1:3]
+        shard = run(third_shard_kernel, where, [down[0]], one, after=after)[0]
         third = gather_line(where, shard, 2)
         third_pieces = gather_plane(where, third, first_pieces[3:])
     else:
@@ -827,7 +828,7 @@
         [shape(LEN, FFC), shape(LEN, D), shape(8, FFC, dtype=F32)],
         [pltpu.VMEM((LEN, FFC), F32)],
     )
-    third_passed = scatter_pass(where, third_handed, third_got, [part])
+    third_passed = scatter_pass(where, third_handed, third_got)
     third_last = scatter_second(third_passed)
     second_handed = run(
         up_grad_kernel,
@@ -874,11 +875,20 @@
         after=third_passed + third_got[2:],
     )
     first_got = scatter_first(first_handed)
+    (part,) = run(token_back_kernel, where, [grad_mixed, wj], [shape(LEN, D)], after=first_handed[:1])
+    pieces = run(
+        token_sum_kernel,
+        where,
+        [result, grad_one, part, swap(part, "col", 1)],
+        [shape(2, PAIRS, 2 * W)] * ROWS,
+        [pltpu.VMEM((LEN, D), F32), pltpu.VMEM((ROWS, 2, PAIRS, 2 * W), BF16)],
+    )
     first_passed = run(
         carry_pass_kernel,
         where,
         first_handed[2:4] + first_handed[:1] + first_got,
         [PAIR, shape(*CARRIED)],
+        after=pieces[:1],
     )
     first_last = scatter_second(first_passed)
 
@@ -900,8 +910,13 @@
     if direct:
         got = swap(third_sum[1], "dp", 1)
         third_sum = run(far_line_kernel, where, [third_sum[0], got], sums(CHUNK, CHUNK))
+        got = swap(third_sum[1], "dp", 2)
+        down_new = run(down_adam_kernel, where, [third_sum[0], got] + down, like(down))
+        ready = down_new[:1]
+    else:
+        ready = []
     second_got = scatter_first(second_handed)
-    second_passed = scatter_pass(where, second_handed, second_got, third_sum[1:])
+    second_passed = scatter_pass(where, second_handed, second_got, ready)
     second_last = scatter_second(second_passed)
     first_sum = run(
         carry_near_kernel,
@@ -918,11 +933,7 @@
         sums(CHUNK, CHUNK) + [shape(*CHUNK)] * 2 if direct else wide,
         lines,
     )
-    ready = []
     if direct:
-        got = swap(third_sum[1], "dp", 2)
-        down_new = run(down_adam_kernel, where, [third_sum[0], got] + down, like(down))
-        ready = down_new[:1]
         got = swap(first_sum[1], "dp", 1)
         first_sum = run(
             carry_far_kernel,
@@ -940,15 +951,6 @@
         )
         joint_new, output_new, vector = new[:3], new[3:6], new[6]
 
-    (part,) = run(token_back_kernel, where, [grad_mixed, wj], [shape(LEN, D)], after=second_passed)
-    pieces = run(
-        token_sum_kernel,
-        where,
-        [result, grad_one, part, swap(part, "col", 1)],
-        [shape(2, PAIRS, 2 * W)] * ROWS,
-        [pltpu.VMEM((LEN, D), F32), pltpu.VMEM((ROWS, 2, PAIRS, 2 * W), BF16)],
-        after=ready,
-    )
     flat_out = [shape(ROWS, 3 * PAIRS, 128, dtype=F32)] * 2
     out = run(token_out_kernel, where, exchange(pieces), flat_out)
     layer_out, tokens_grad = [v.reshape(tokens_in.shape) for v in out]

time: 211 us -> 201 us (0.953)
  starting transfers between devices: 86.4 us -> 79.2 us
    ppermute x51, starting transfers between devices: 86.4 us -> 79.2 us  [swap(): return lax.ppermute(value, axis, [(i, i ^ mask) for i in range(n)])]
    unnamed x42 -> x40, local copies, waits for them, and re-layouts: 4.69 us -> 3.74 us
  transfers between devices with their start and end apart: 51 -> 51, of which waited for: 19 -> 20; matrix products, arithmetic and copies ran while one was open for 0% -> 0% of each run, Pallas kernels for 18% -> 18%
where the time goes in v2:
time: 201 us; the launch traced here: 200 us
  starting transfers between devices  79.2 us (39%)
  waiting for transfers between devices  63.5 us (32%)
  Pallas kernels  50.8 us (25%)
  local copies, waits for them, and re-layouts  3.74 us (2%)
    ppermute x51, starting transfers between devices, swap(): return lax.ppermute(value, axis, [(i, i ^ mask) for i in range(n)])  79.2 us
    ppermute x51, waiting for transfers between devices, swap(): return lax.ppermute(value, axis, [(i, i ^ mask) for i in range(n)])  63.5 us
    pallas_call x34, Pallas kernels, run(): pl.pallas_call(body, out_shape=outs, in_specs=[pl.BlockSpec(memory_space=...  50.8 us
  transfers between devices with their start and end apart: 51, of which 20 were waited for; matrix products, arithmetic and copies ran while one was open for 0% of the time, Pallas kernels for 18%

profile of v2, /device:TPU:1, one launch (start us, length us, event | category | flops | bytes accessed | tf_op | source)
XLA Modules:
  0.0 199.7 jit_solution(2145718749882704389)
XLA Ops:
  1.9 2.9 %shard_map.305 = (bf16[2,128,384]{2,1,0:T(8,128)(2,1)}, bf16[2,128,384]{2,1,0:T(8,128)(2,1)}, bf16[2,128,384]{2,1,0:T(8,128)(2,1)}, bf16[2,128,384]{2,1,0:T(8,128)(2,1)}, bf16[192,384]{1,0:T(8,128)(2,1)}) custom-call(s32[4]{0:T(128)} %pad_add_fusion.refs_0_, bf16[4,128,384]{2,1,0:T(8,128)(2,1)} %bitcast.86, bf16[4,128,384]{2,1,0:T(8,128)(2,1)} %bitcast.87, ...), custom_call_target="tpu_custom_call" | custom-call | tf_op jit(solution)/shard_map/pallas_call | solution.py:56
  4.9 4.2 %collective-permute-start.5 = (bf16[192,384]{1,0:T(8,128)(2,1)}, bf16[192,384]{1,0:T(8,128)(2,1)S(1)}, u32[]{:S(2)}, u32[]{:S(2)}) collective-permute-start(bf16[192,384]{1,0:T(8,128)(2,1)} %get-tuple-element.117.refs_1_), channel_id=1, source_target_pairs={{0,24},{8,16},{16,8},{24,0},{1,25},{9,17},{17,9},{25,1},{2,26},{10... | collective-permute-start | bytes 442376 | tf_op jit(solution)/shard_map/ppermute | solution.py:42
  12.9 1.5 collective-permute-start.3
  14.4 1.8 collective-permute-done.4.refs_3_
  16.3 1.9 collective-permute-done.3.refs_2_
  18.2 1.8 collective-permute-done.2.refs_7_.refs_4_
  24.2 1.8 collective-permute-start.11
  26.0 3.2 %collective-permute-done.11.refs_2_ = bf16[192,384]{1,0:T(8,128)(2,1)S(1)} collective-permute-done((bf16[192,384]{1,0:T(8,128)(2,1)S(1)}, bf16[192,384]{1,0:T(8,128)(2,1)S(1)}, u32[]{:S(2)}, u32[]{:S(2)}) %collective-permute-start.11) | collective-permute-done | bytes 147488 | tf_op jit(solution)/shard_map/ppermute | solution.py:42
  29.8 2.0 collective-permute-start.12
  31.7 6.0 %collective-permute-done.12.refs_2_ = bf16[2,192,384]{2,1,0:T(8,128)(2,1)S(1)} collective-permute-done((bf16[2,192,384]{2,1,0:T(8,128)(2,1)S(1)}, bf16[2,192,384]{2,1,0:T(8,128)(2,1)S(1)}, u32[]{:S(2)}, u32[]{:S(2)}) %collective-permute-start.12) | collective-permute-done | bytes 294944 | tf_op jit(solution)/shard_map/ppermute | solution.py:42
  38.9 1.7 collective-permute-start.17
  42.2 3.4 %collective-permute-done.17.refs_2_ = bf16[192,384]{1,0:T(8,128)(2,1)S(1)} collective-permute-done((bf16[192,384]{1,0:T(8,128)(2,1)S(1)}, bf16[192,384]{1,0:T(8,128)(2,1)S(1)}, u32[]{:S(2)}, u32[]{:S(2)}) %collective-permute-start.17) | collective-permute-done | bytes 147488 | tf_op jit(solution)/shard_map/ppermute | solution.py:42
  47.9 5.0 %collective-permute-done.18.refs_2_ = bf16[2,192,384]{2,1,0:T(8,128)(2,1)S(1)} collective-permute-done((bf16[2,192,384]{2,1,0:T(8,128)(2,1)S(1)}, bf16[2,192,384]{2,1,0:T(8,128)(2,1)S(1)}, u32[]{:S(2)}, u32[]{:S(2)}) %collective-permute-start.18) | collective-permute-done | bytes 294944 | tf_op jit(solution)/shard_map/ppermute | solution.py:42
  53.5 2.1 %collective-permute-start.20 = (bf16[4,192,384]{2,1,0:T(8,128)(2,1)S(1)}, bf16[4,192,384]{2,1,0:T(8,128)(2,1)S(1)}, u32[]{:S(2)}, u32[]{:S(2)}) collective-permute-start(bf16[4,192,384]{2,1,0:T(8,128)(2,1)S(1)} %shard_map.316.refs_2_), channel_id=1, source_target_pairs={{0,4},{2,6},{4,0},{6,2},{1,5},{3,7},{5,1},{7,3},{8,12},{10,14},{12... | collective-permute-start | bytes 1769480 | tf_op jit(solution)/shard_map/ppermute | solution.py:42
  55.9 5.2 %shard_map.308 = (bf16[256,768]{1,0:T(8,128)(2,1)S(1)}, bf16[256,768]{1,0:T(8,128)(2,1)S(1)}, bf16[4,1152,192]{2,1,0:T(8,128)(2,1)S(1)}, bf16[768,384]{1,0:T(8,1...) custom-call(s32[4]{0:T(128)S(1)} %copy-done.5, ...), custom_call_target="tpu_custom_call" | custom-call | tf_op jit(solution)/shard_map/pallas_call | solution.py:56
  61.1 6.8 %collective-permute-start.10 = (bf16[256,768]{1,0:T(8,128)(2,1)S(1)}, bf16[256,768]{1,0:T(8,128)(2,1)S(1)}, u32[]{:S(2)}, u32[]{:S(2)}) collective-permute-start(bf16[256,768]{1,0:T(8,128)(2,1)S(1)} %get-tuple-element.121.refs_2_), channel_id=1, source_target_pairs={{0,1},{1,0},{2,3},{3,2},{4,5},{5,4},{6,7},{7,6},{8,9},{9,8},{10,11... | collective-permute-start | bytes 1179656 | tf_op jit(solution)/shard_map/ppermute | solution.py:42
  69.8 1.7 collective-permute-start.16
  72.4 1.9 collective-permute-done.19.refs_1_.refs_3_
  75.3 5.2 %collective-permute-done.15.refs_8_ = bf16[2,192,384]{2,1,0:T(8,128)(2,1)S(1)} collective-permute-done((bf16[2,192,384]{2,1,0:T(8,128)(2,1)S(1)}, bf16[2,192,384]{2,1,0:T(8,128)(2,1)S(1)}, u32[]{:S(2)}, u32[]{:S(2)}) %collective-permute-start.15) | collective-permute-done | bytes 294944 | tf_op jit(solution)/shard_map/ppermute | solution.py:42
  80.6 3.8 %shard_map.313 = (f32[256,768]{1,0:T(8,128)S(1)}, bf16[256,768]{1,0:T(8,128)(2,1)S(1)}, f32[256,768]{1,0:T(8,128)S(1)}, f32[256,1]{1,0:T(8,128)S(1)}, bf16[256,1...) custom-call(s32[4]{0:T(128)S(1)} %copy-done.5, ...), custom_call_target="tpu_custom_call" | custom-call | tf_op jit(solution)/shard_map/pallas_call | solution.py:56
  84.4 2.5 %collective-permute-done.21.refs_5_ = bf16[2,192,384]{2,1,0:T(8,128)(2,1)S(1)} collective-permute-done((bf16[2,192,384]{2,1,0:T(8,128)(2,1)S(1)}, bf16[2,192,384]{2,1,0:T(8,128)(2,1)S(1)}, u32[]{:S(2)}, u32[]{:S(2)}) %collective-permute-start.21) | collective-permute-done | bytes 294944 | tf_op jit(solution)/shard_map/ppermute | solution.py:42
  86.9 1.6 shard_map.318
  88.5 5.7 %collective-permute-start.23 = (bf16[256,768]{1,0:T(8,128)(2,1)S(1)}, bf16[256,768]{1,0:T(8,128)(2,1)S(1)}, u32[]{:S(2)}, u32[]{:S(2)}) collective-permute-start(bf16[256,768]{1,0:T(8,128)(2,1)S(1)} %get-tuple-element.128.refs_2_), channel_id=1, source_target_pairs={{0,1},{1,0},{2,3},{3,2},{4,5},{5,4},{6,7},{7,6},{8,9},{9,8},{10,11... | collective-permute-start | bytes 1179656 | tf_op jit(solution)/shard_map/ppermute | solution.py:42
  94.2 1.3 collective-permute-done.23.refs_3_
  95.5 3.6 %shard_map.319 = (f32[256,768]{1,0:T(8,128)S(1)}, bf16[256,768]{1,0:T(8,128)(2,1)S(1)}, f32[256,768]{1,0:T(8,128)S(1)}, f32[8,768]{1,0:T(8,128)S(1)}, bf16[2,192...) custom-call(s32[4]{0:T(128)S(1)} %copy-done.5, ...), custom_call_target="tpu_custom_call" | custom-call | tf_op jit(solution)/shard_map/pallas_call | solution.py:56
  99.2 3.3 %shard_map.320 = (bf16[256,1536]{1,0:T(8,128)(2,1)S(1)}, bf16[256,768]{1,0:T(8,128)(2,1)S(1)}, f32[8,1536]{1,0:T(8,128)S(1)}) custom-call(s32[4]{0:T(128)S(1)} %copy-done.5, bf16[256,768]{1,0:T(8,128)(2,1)S(1)} %get-tuple-element.132.refs_1_, f32[256,1536]{1,0:T(8,128)S(1)} %get-tuple-element.133.refs_2_, bf16[768,1536]{1,0:T(8,128)(2,1)S(1)} %get-tuple-element.134.refs_3_, ...), custom_call_target="tpu_custom_call" | custom-call | tf_op jit(solution)/shard_map/pallas_call | solution.py:56
  104.4 1.5 collective-permute-start.28
  105.9 5.5 %collective-permute-done.25.refs_3_ = bf16[2,192,384]{2,1,0:T(8,128)(2,1)S(1)} collective-permute-done((bf16[2,192,384]{2,1,0:T(8,128)(2,1)S(1)}, bf16[2,192,384]{2,1,0:T(8,128)(2,1)S(1)}, u32[]{:S(2)}, u32[]{:S(2)}) %collective-permute-start.25) | collective-permute-done | bytes 294944 | tf_op jit(solution)/shard_map/ppermute | solution.py:42
  112.1 5.4 %shard_map.321 = (f32[256,768]{1,0:T(8,128)S(1)}, bf16[1152,256]{1,0:T(8,128)(2,1)S(1)}, f32[32,384]{1,0:T(8,128)S(1)}, bf16[4,4,192,384]{3,2,1,0:T(8,128)(2,1)S(1)}) custom-call(s32[4]{0:T(128)S(1)} %copy-done.5, f32[256,768]{1,0:T(8,128)S(1)} %get-tuple-element.131.refs_1_, bf16[256,768]{1,0:T(8,128)(2,1)S(1)} %get-tuple-element.136.refs_2_, ...), custom_call_target="tpu_custom_call" | custom-call | tf_op jit(solution)/shard_map/pallas_call | solution.py:56
  121.5 1.5 shard_map.324.refs_3_
  123.0 3.1 %collective-permute-start.29 = (bf16[256,768]{1,0:T(8,128)(2,1)S(1)}, bf16[256,768]{1,0:T(8,128)(2,1)S(1)}, u32[]{:S(2)}, u32[]{:S(2)}) collective-permute-start(bf16[256,768]{1,0:T(8,128)(2,1)S(1)} %shard_map.324.refs_3_), channel_id=1, source_target_pairs={{0,1},{1,0},{2,3},{3,2},{4,5},{5,4},{6,7},{7,6},{8,9},{9,8},{10,11... | collective-permute-start | bytes 1179656 | tf_op jit(solution)/shard_map/ppermute | solution.py:42
  126.2 12.7 %collective-permute-done.37.refs_3_.refs_4_ = bf16[2,192,384]{2,1,0:T(8,128)(2,1)S(1)} collective-permute-done((bf16[2,192,384]{2,1,0:T(8,128)(2,1)S(1)}, bf16[2,192,384]{2,1,0:T(8,128)(2,1)S(1)}, u32[]{:S(2)}, u32[]{:S(2)}) %collective-permute-start.37) | collective-permute-done | bytes 294944 | tf_op jit(solution)/shard_map/ppermute | solution.py:42
  138.8 1.8 shard_map.328
  142.8 2.5 %collective-permute-start.41 = (bf16[2,192,384]{2,1,0:T(8,128)(2,1)S(1)}, bf16[2,192,384]{2,1,0:T(8,128)(2,1)S(1)}, u32[]{:S(2)}, u32[]{:S(2)}) collective-permute-start(bf16[2,192,384]{2,1,0:T(8,128)(2,1)S(1)} %get-tuple-element.179), channel_id=1, source_target_pairs={{0,8},{8,0},{16,24},{24,16},{1,9},{9,1},{17,25},{25,17},{2,10},{10... | collective-permute-start | bytes 884744 | tf_op jit(solution)/shard_map/ppermute | solution.py:42
  151.5 5.3 %collective-permute-done.42.refs_2_ = bf16[192,384]{1,0:T(8,128)(2,1)S(1)} collective-permute-done((bf16[192,384]{1,0:T(8,128)(2,1)S(1)}, bf16[192,384]{1,0:T(8,128)(2,1)S(1)}, u32[]{:S(2)}, u32[]{:S(2)}) %collective-permute-start.42) | collective-permute-done | bytes 147488 | tf_op jit(solution)/shard_map/ppermute | solution.py:42
  156.8 1.6 shard_map.331
  161.8 1.5 collective-permute-start.43
  163.3 1.7 collective-permute-start.45
  165.8 2.2 %collective-permute-done.43.refs_2_ = bf16[448,384]{1,0:T(8,128)(2,1)S(1)} collective-permute-done((bf16[448,384]{1,0:T(8,128)(2,1)S(1)}, bf16[448,384]{1,0:T(8,128)(2,1)S(1)}, u32[]{:S(2)}, u32[]{:S(2)}) %collective-permute-start.43) | collective-permute-done | bytes 344096 | tf_op jit(solution)/shard_map/ppermute | solution.py:42
  168.6 2.3 %collective-permute-start.44 = (bf16[256,384]{1,0:T(8,128)(2,1)S(1)}, bf16[256,384]{1,0:T(8,128)(2,1)S(1)}, u32[]{:S(2)}, u32[]{:S(2)}) collective-permute-start(bf16[256,384]{1,0:T(8,128)(2,1)S(1)} %get-tuple-element.188), channel_id=1, source_target_pairs={{0,16},{8,24},{16,0},{24,8},{1,17},{9,25},{17,1},{25,9},{2,18},{10... | collective-permute-start | bytes 589832 | tf_op jit(solution)/shard_map/ppermute | solution.py:42
  170.9 1.6 collective-permute-start.32
  173.4 1.4 collective-permute-start.47
  174.8 1.5 collective-permute-start.48
  176.3 1.9 collective-permute-start.49
  178.2 1.7 shard_map.335
  179.9 14.0 %collective-permute-start.50 = (f32[32,384]{1,0:T(8,128)S(1)}, f32[32,384]{1,0:T(8,128)S(1)}, u32[]{:S(2)}, u32[]{:S(2)}) collective-permute-start(f32[32,384]{1,0:T(8,128)S(1)} %get-tuple-element.205.refs_1_), channel_id=1, source_target_pairs={{0,1},{1,0},{2,3},{3,2},{4,5},{5,4},{6,7},{7,6},{8,9},{9,8},{10,11... | collective-permute-start | bytes 147464 | tf_op jit(solution)/shard_map/ppermute | solution.py:42
  193.9 1.8 shard_map.326
  196.9 1.7 shard_map.337
  (129 shorter events, 42.1 us)
Async XLA Ops:
  4.9 8.0 %collective-permute-start.5 = (bf16[192,384]{1,0:T(8,128)(2,1)}, bf16[192,384]{1,0:T(8,128)(2,1)S(1)}, u32[]{:S(2)}, u32[]{:S(2)}) collective-permute-start(bf16[192,384]{1,0:T(8,128)(2,1)} %get-tuple-element.117.refs_1_), channel_id=1, source_target_pairs={{0,24},{8,16},{16,8},{24,0},{1,25},{9,17},{17,9},{25,1},{2,26},{10... | collective-permute-start | bytes 442376 | tf_op jit(solution)/shard_map/ppermute | solution.py:42
  9.1 9.0 %collective-permute-start = (bf16[2,128,384]{2,1,0:T(8,128)(2,1)}, bf16[2,128,384]{2,1,0:T(8,128)(2,1)S(1)}, u32[]{:S(2)}, u32[]{:S(2)}) collective-permute-start(bf16[2,128,384]{2,1,0:T(8,128)(2,1)} %get-tuple-element.114), channel_id=1, source_target_pairs={{0,2},{2,0},{4,6},{6,4},{1,3},{3,1},{5,7},{7,5},{8,10},{10,8},{12,... | collective-permute-start | bytes 589832 | tf_op jit(solution)/shard_map/ppermute | solution.py:42
  10.3 7.8 %collective-permute-start.1 = (bf16[2,128,384]{2,1,0:T(8,128)(2,1)}, bf16[2,128,384]{2,1,0:T(8,128)(2,1)S(1)}, u32[]{:S(2)}, u32[]{:S(2)}) collective-permute-start(bf16[2,128,384]{2,1,0:T(8,128)(2,1)} %get-tuple-element.115), channel_id=1, source_target_pairs={{0,4},{2,6},{4,0},{6,2},{1,5},{3,7},{5,1},{7,3},{8,12},{10,14},{12... | collective-permute-start | bytes 589832 | tf_op jit(solution)/shard_map/ppermute | solution.py:42
  11.6 8.4 %collective-permute-start.2 = (bf16[2,128,384]{2,1,0:T(8,128)(2,1)}, bf16[2,128,384]{2,1,0:T(8,128)(2,1)S(1)}, u32[]{:S(2)}, u32[]{:S(2)}) collective-permute-start(bf16[2,128,384]{2,1,0:T(8,128)(2,1)} %get-tuple-element.116), channel_id=1, source_target_pairs={{0,6},{2,4},{4,2},{6,0},{1,7},{3,5},{5,3},{7,1},{8,14},{10,12},{12... | collective-permute-start | bytes 589832 | tf_op jit(solution)/shard_map/ppermute | solution.py:42
  22.2 16.2 %collective-permute-start.7 = (bf16[4,192,384]{2,1,0:T(8,128)(2,1)S(1)}, bf16[4,192,384]{2,1,0:T(8,128)(2,1)S(1)}, u32[]{:S(2)}, u32[]{:S(2)}) collective-permute-start(bf16[4,192,384]{2,1,0:T(8,128)(2,1)S(1)} %shard_map.306.refs_6_), channel_id=1, source_target_pairs={{0,4},{2,6},{4,0},{6,2},{1,5},{3,7},{5,1},{7,3},{8,12},{10,14},{12... | collective-permute-start | bytes 1769480 | tf_op jit(solution)/shard_map/ppermute | solution.py:42
  22.4 15.9 %collective-permute-start.6 = (bf16[4,192,384]{2,1,0:T(8,128)(2,1)S(1)}, bf16[4,192,384]{2,1,0:T(8,128)(2,1)S(1)}, u32[]{:S(2)}, u32[]{:S(2)}) collective-permute-start(bf16[4,192,384]{2,1,0:T(8,128)(2,1)S(1)} %shard_map.306.refs_6_), channel_id=1, source_target_pairs={{0,2},{2,0},{4,6},{6,4},{1,3},{3,1},{5,7},{7,5},{8,10},{10,8},{12,... | collective-permute-start | bytes 1769480 | tf_op jit(solution)/shard_map/ppermute | solution.py:42
  29.8 8.0 %collective-permute-start.12 = (bf16[2,192,384]{2,1,0:T(8,128)(2,1)S(1)}, bf16[2,192,384]{2,1,0:T(8,128)(2,1)S(1)}, u32[]{:S(2)}, u32[]{:S(2)}) collective-permute-start(bf16[2,192,384]{2,1,0:T(8,128)(2,1)S(1)} %shard_map.310.refs_1_), channel_id=1, source_target_pairs={{0,8},{8,0},{16,24},{24,16},{1,9},{9,1},{17,25},{25,17},{2,10},{10... | collective-permute-start | bytes 884744 | tf_op jit(solution)/shard_map/ppermute | solution.py:42
  38.9 6.6 %collective-permute-start.17 = (bf16[192,384]{1,0:T(8,128)(2,1)S(1)}, bf16[192,384]{1,0:T(8,128)(2,1)S(1)}, u32[]{:S(2)}, u32[]{:S(2)}) collective-permute-start(bf16[192,384]{1,0:T(8,128)(2,1)S(1)} %shard_map.314.refs_1_), channel_id=1, source_target_pairs={{0,16},{8,24},{16,0},{24,8},{1,17},{9,25},{17,1},{25,9},{2,18},{10... | collective-permute-start | bytes 442376 | tf_op jit(solution)/shard_map/ppermute | solution.py:42
  41.2 6.7 %collective-permute-start.8 = (bf16[2,192,384]{2,1,0:T(8,128)(2,1)S(1)}, bf16[2,192,384]{2,1,0:T(8,128)(2,1)S(1)}, u32[]{:S(2)}, u32[]{:S(2)}) collective-permute-start(bf16[2,192,384]{2,1,0:T(8,128)(2,1)S(1)} %get-tuple-element.118), channel_id=1, source_target_pairs={{0,2},{2,0},{4,6},{6,4},{1,3},{3,1},{5,7},{7,5},{8,10},{10,8},{12,... | collective-permute-start | bytes 884744 | tf_op jit(solution)/shard_map/ppermute | solution.py:42
  41.5 6.4 %collective-permute-start.9 = (bf16[2,192,384]{2,1,0:T(8,128)(2,1)S(1)}, bf16[2,192,384]{2,1,0:T(8,128)(2,1)S(1)}, u32[]{:S(2)}, u32[]{:S(2)}) collective-permute-start(bf16[2,192,384]{2,1,0:T(8,128)(2,1)S(1)} %get-tuple-element.119), channel_id=1, source_target_pairs={{0,4},{2,6},{4,0},{6,2},{1,5},{3,7},{5,1},{7,3},{8,12},{10,14},{12... | collective-permute-start | bytes 884744 | tf_op jit(solution)/shard_map/ppermute | solution.py:42
  46.1 6.8 %collective-permute-start.18 = (bf16[2,192,384]{2,1,0:T(8,128)(2,1)S(1)}, bf16[2,192,384]{2,1,0:T(8,128)(2,1)S(1)}, u32[]{:S(2)}, u32[]{:S(2)}) collective-permute-start(bf16[2,192,384]{2,1,0:T(8,128)(2,1)S(1)} %shard_map.315.refs_1_), channel_id=1, source_target_pairs={{0,8},{8,0},{16,24},{24,16},{1,9},{9,1},{17,25},{25,17},{2,10},{10... | collective-permute-start | bytes 884744 | tf_op jit(solution)/shard_map/ppermute | solution.py:42
  46.6 21.3 %collective-permute-start.14 = (bf16[4,192,384]{2,1,0:T(8,128)(2,1)S(1)}, bf16[4,192,384]{2,1,0:T(8,128)(2,1)S(1)}, u32[]{:S(2)}, u32[]{:S(2)}) collective-permute-start(bf16[4,192,384]{2,1,0:T(8,128)(2,1)S(1)} %shard_map.311.refs_5_.refs_2_), channel_id=1, source_target_pairs={{0,4},{2,6},{4,0},{6,2},{1,5},{3,7},{5,1},{7,3},{8,12},{10,14},{12... | collective-permute-start | bytes 1769480 | tf_op jit(solution)/shard_map/ppermute | solution.py:42
  47.6 20.3 %collective-permute-start.13 = (bf16[4,192,384]{2,1,0:T(8,128)(2,1)S(1)}, bf16[4,192,384]{2,1,0:T(8,128)(2,1)S(1)}, u32[]{:S(2)}, u32[]{:S(2)}) collective-permute-start(bf16[4,192,384]{2,1,0:T(8,128)(2,1)S(1)} %shard_map.311.refs_5_.refs_2_), channel_id=1, source_target_pairs={{0,2},{2,0},{4,6},{6,4},{1,3},{3,1},{5,7},{7,5},{8,10},{10,8},{12,... | collective-permute-start | bytes 1769480 | tf_op jit(solution)/shard_map/ppermute | solution.py:42
  53.5 18.8 %collective-permute-start.20 = (bf16[4,192,384]{2,1,0:T(8,128)(2,1)S(1)}, bf16[4,192,384]{2,1,0:T(8,128)(2,1)S(1)}, u32[]{:S(2)}, u32[]{:S(2)}) collective-permute-start(bf16[4,192,384]{2,1,0:T(8,128)(2,1)S(1)} %shard_map.316.refs_2_), channel_id=1, source_target_pairs={{0,4},{2,6},{4,0},{6,2},{1,5},{3,7},{5,1},{7,3},{8,12},{10,14},{12... | collective-permute-start | bytes 1769480 | tf_op jit(solution)/shard_map/ppermute | solution.py:42
  55.7 18.6 %collective-permute-start.19 = (bf16[4,192,384]{2,1,0:T(8,128)(2,1)S(1)}, bf16[4,192,384]{2,1,0:T(8,128)(2,1)S(1)}, u32[]{:S(2)}, u32[]{:S(2)}) collective-permute-start(bf16[4,192,384]{2,1,0:T(8,128)(2,1)S(1)} %shard_map.316.refs_2_), channel_id=1, source_target_pairs={{0,2},{2,0},{4,6},{6,4},{1,3},{3,1},{5,7},{7,5},{8,10},{10,8},{12,... | collective-permute-start | bytes 1769480 | tf_op jit(solution)/shard_map/ppermute | solution.py:42
  61.1 14.3 %collective-permute-start.10 = (bf16[256,768]{1,0:T(8,128)(2,1)S(1)}, bf16[256,768]{1,0:T(8,128)(2,1)S(1)}, u32[]{:S(2)}, u32[]{:S(2)}) collective-permute-start(bf16[256,768]{1,0:T(8,128)(2,1)S(1)} %get-tuple-element.121.refs_2_), channel_id=1, source_target_pairs={{0,1},{1,0},{2,3},{3,2},{4,5},{5,4},{6,7},{7,6},{8,9},{9,8},{10,11... | collective-permute-start | bytes 1179656 | tf_op jit(solution)/shard_map/ppermute | solution.py:42
  68.5 12.1 %collective-permute-start.15 = (bf16[2,192,384]{2,1,0:T(8,128)(2,1)S(1)}, bf16[2,192,384]{2,1,0:T(8,128)(2,1)S(1)}, u32[]{:S(2)}, u32[]{:S(2)}) collective-permute-start(bf16[2,192,384]{2,1,0:T(8,128)(2,1)S(1)} %get-tuple-element.122), channel_id=1, source_target_pairs={{0,2},{2,0},{4,6},{6,4},{1,3},{3,1},{5,7},{7,5},{8,10},{10,8},{12,... | collective-permute-start | bytes 884744 | tf_op jit(solution)/shard_map/ppermute | solution.py:42
  69.8 10.8 %collective-permute-start.16 = (bf16[2,192,384]{2,1,0:T(8,128)(2,1)S(1)}, bf16[2,192,384]{2,1,0:T(8,128)(2,1)S(1)}, u32[]{:S(2)}, u32[]{:S(2)}) collective-permute-start(bf16[2,192,384]{2,1,0:T(8,128)(2,1)S(1)} %get-tuple-element.123), channel_id=1, source_target_pairs={{0,4},{2,6},{4,0},{6,2},{1,5},{3,7},{5,1},{7,3},{8,12},{10,14},{12... | collective-permute-start | bytes 884744 | tf_op jit(solution)/shard_map/ppermute | solution.py:42
  74.9 12.0 %collective-permute-start.21 = (bf16[2,192,384]{2,1,0:T(8,128)(2,1)S(1)}, bf16[2,192,384]{2,1,0:T(8,128)(2,1)S(1)}, u32[]{:S(2)}, u32[]{:S(2)}) collective-permute-start(bf16[2,192,384]{2,1,0:T(8,128)(2,1)S(1)} %get-tuple-element.126), channel_id=1, source_target_pairs={{0,2},{2,0},{4,6},{6,4},{1,3},{3,1},{5,7},{7,5},{8,10},{10,8},{12,... | collective-permute-start | bytes 884744 | tf_op jit(solution)/shard_map/ppermute | solution.py:42
  75.2 11.7 %collective-permute-start.22 = (bf16[2,192,384]{2,1,0:T(8,128)(2,1)S(1)}, bf16[2,192,384]{2,1,0:T(8,128)(2,1)S(1)}, u32[]{:S(2)}, u32[]{:S(2)}) collective-permute-start(bf16[2,192,384]{2,1,0:T(8,128)(2,1)S(1)} %get-tuple-element.127), channel_id=1, source_target_pairs={{0,4},{2,6},{4,0},{6,2},{1,5},{3,7},{5,1},{7,3},{8,12},{10,14},{12... | collective-permute-start | bytes 884744 | tf_op jit(solution)/shard_map/ppermute | solution.py:42
  88.5 7.0 %collective-permute-start.23 = (bf16[256,768]{1,0:T(8,128)(2,1)S(1)}, bf16[256,768]{1,0:T(8,128)(2,1)S(1)}, u32[]{:S(2)}, u32[]{:S(2)}) collective-permute-start(bf16[256,768]{1,0:T(8,128)(2,1)S(1)} %get-tuple-element.128.refs_2_), channel_id=1, source_target_pairs={{0,1},{1,0},{2,3},{3,2},{4,5},{5,4},{6,7},{7,6},{8,9},{9,8},{10,11... | collective-permute-start | bytes 1179656 | tf_op jit(solution)/shard_map/ppermute | solution.py:42
  102.5 9.6 %collective-permute-start.24 = (bf16[256,768]{1,0:T(8,128)(2,1)S(1)}, bf16[256,768]{1,0:T(8,128)(2,1)S(1)}, u32[]{:S(2)}, u32[]{:S(2)}) collective-permute-start(bf16[256,768]{1,0:T(8,128)(2,1)S(1)} %get-tuple-element.136.refs_2_), channel_id=1, source_target_pairs={{0,1},{1,0},{2,3},{3,2},{4,5},{5,4},{6,7},{7,6},{8,9},{9,8},{10,11... | collective-permute-start | bytes 1179656 | tf_op jit(solution)/shard_map/ppermute | solution.py:42
  102.9 8.5 %collective-permute-start.25 = (bf16[2,192,384]{2,1,0:T(8,128)(2,1)S(1)}, bf16[2,192,384]{2,1,0:T(8,128)(2,1)S(1)}, u32[]{:S(2)}, u32[]{:S(2)}) collective-permute-start(bf16[2,192,384]{2,1,0:T(8,128)(2,1)S(1)} %get-tuple-element.152), channel_id=1, source_target_pairs={{0,2},{2,0},{4,6},{6,4},{1,3},{3,1},{5,7},{7,5},{8,10},{10,8},{12,... | collective-permute-start | bytes 884744 | tf_op jit(solution)/shard_map/ppermute | solution.py:42
  103.2 8.2 %collective-permute-start.26 = (bf16[2,192,384]{2,1,0:T(8,128)(2,1)S(1)}, bf16[2,192,384]{2,1,0:T(8,128)(2,1)S(1)}, u32[]{:S(2)}, u32[]{:S(2)}) collective-permute-start(bf16[2,192,384]{2,1,0:T(8,128)(2,1)S(1)} %get-tuple-element.153), channel_id=1, source_target_pairs={{0,4},{2,6},{4,0},{6,2},{1,5},{3,7},{5,1},{7,3},{8,12},{10,14},{12... | collective-permute-start | bytes 884744 | tf_op jit(solution)/shard_map/ppermute | solution.py:42
  104.0 13.7 %collective-permute-start.27 = (bf16[2,192,384]{2,1,0:T(8,128)(2,1)S(1)}, bf16[2,192,384]{2,1,0:T(8,128)(2,1)S(1)}, u32[]{:S(2)}, u32[]{:S(2)}) collective-permute-start(bf16[2,192,384]{2,1,0:T(8,128)(2,1)S(1)} %get-tuple-element.156), channel_id=1, source_target_pairs={{0,2},{2,0},{4,6},{6,4},{1,3},{3,1},{5,7},{7,5},{8,10},{10,8},{12,... | collective-permute-start | bytes 884744 | tf_op jit(solution)/shard_map/ppermute | solution.py:42
  104.4 13.3 %collective-permute-start.28 = (bf16[2,192,384]{2,1,0:T(8,128)(2,1)S(1)}, bf16[2,192,384]{2,1,0:T(8,128)(2,1)S(1)}, u32[]{:S(2)}, u32[]{:S(2)}) collective-permute-start(bf16[2,192,384]{2,1,0:T(8,128)(2,1)S(1)} %get-tuple-element.157), channel_id=1, source_target_pairs={{0,4},{2,6},{4,0},{6,2},{1,5},{3,7},{5,1},{7,3},{8,12},{10,14},{12... | collective-permute-start | bytes 884744 | tf_op jit(solution)/shard_map/ppermute | solution.py:42
  118.5 27.9 %collective-permute-start.33 = (bf16[832,384]{1,0:T(8,128)(2,1)S(1)}, bf16[832,384]{1,0:T(8,128)(2,1)S(1)}, u32[]{:S(2)}, u32[]{:S(2)}) collective-permute-start(bf16[832,384]{1,0:T(8,128)(2,1)S(1)} %get-tuple-element.158.refs_3_), channel_id=1, source_target_pairs={{0,2},{2,0},{4,6},{6,4},{1,3},{3,1},{5,7},{7,5},{8,10},{10,8},{12,... | collective-permute-start | bytes 1916936 | tf_op jit(solution)/shard_map/ppermute | solution.py:42
  119.7 26.7 %collective-permute-start.34 = (bf16[4,192,384]{2,1,0:T(8,128)(2,1)S(1)}, bf16[4,192,384]{2,1,0:T(8,128)(2,1)S(1)}, u32[]{:S(2)}, u32[]{:S(2)}) collective-permute-start(bf16[4,192,384]{2,1,0:T(8,128)(2,1)S(1)} %get-tuple-element.166), channel_id=1, source_target_pairs={{0,4},{2,6},{4,0},{6,2},{1,5},{3,7},{5,1},{7,3},{8,12},{10,14},{12... | collective-permute-start | bytes 1769480 | tf_op jit(solution)/shard_map/ppermute | solution.py:42
  119.8 19.1 %collective-permute-start.37 = (bf16[2,192,384]{2,1,0:T(8,128)(2,1)S(1)}, bf16[2,192,384]{2,1,0:T(8,128)(2,1)S(1)}, u32[]{:S(2)}, u32[]{:S(2)}) collective-permute-start(bf16[2,192,384]{2,1,0:T(8,128)(2,1)S(1)} %get-tuple-element.154.refs_3_), channel_id=1, source_target_pairs={{0,2},{2,0},{4,6},{6,4},{1,3},{3,1},{5,7},{7,5},{8,10},{10,8},{12,... | collective-permute-start | bytes 884744 | tf_op jit(solution)/shard_map/ppermute | solution.py:42
  120.9 18.0 %collective-permute-start.38 = (bf16[2,192,384]{2,1,0:T(8,128)(2,1)S(1)}, bf16[2,192,384]{2,1,0:T(8,128)(2,1)S(1)}, u32[]{:S(2)}, u32[]{:S(2)}) collective-permute-start(bf16[2,192,384]{2,1,0:T(8,128)(2,1)S(1)} %get-tuple-element.155.refs_4_), channel_id=1, source_target_pairs={{0,4},{2,6},{4,0},{6,2},{1,5},{3,7},{5,1},{7,3},{8,12},{10,14},{12... | collective-permute-start | bytes 884744 | tf_op jit(solution)/shard_map/ppermute | solution.py:42
  123.0 19.8 %collective-permute-start.29 = (bf16[256,768]{1,0:T(8,128)(2,1)S(1)}, bf16[256,768]{1,0:T(8,128)(2,1)S(1)}, u32[]{:S(2)}, u32[]{:S(2)}) collective-permute-start(bf16[256,768]{1,0:T(8,128)(2,1)S(1)} %shard_map.324.refs_3_), channel_id=1, source_target_pairs={{0,1},{1,0},{2,3},{3,2},{4,5},{5,4},{6,7},{7,6},{8,9},{9,8},{10,11... | collective-permute-start | bytes 1179656 | tf_op jit(solution)/shard_map/ppermute | solution.py:42
  140.6 17.8 %collective-permute-start.39 = (bf16[4,192,384]{2,1,0:T(8,128)(2,1)S(1)}, bf16[4,192,384]{2,1,0:T(8,128)(2,1)S(1)}, u32[]{:S(2)}, u32[]{:S(2)}) collective-permute-start(bf16[4,192,384]{2,1,0:T(8,128)(2,1)S(1)} %get-tuple-element.175), channel_id=1, source_target_pairs={{0,2},{2,0},{4,6},{6,4},{1,3},{3,1},{5,7},{7,5},{8,10},{10,8},{12,... | collective-permute-start | bytes 1769480 | tf_op jit(solution)/shard_map/ppermute | solution.py:42
  141.8 16.6 %collective-permute-start.40 = (bf16[4,192,384]{2,1,0:T(8,128)(2,1)S(1)}, bf16[4,192,384]{2,1,0:T(8,128)(2,1)S(1)}, u32[]{:S(2)}, u32[]{:S(2)}) collective-permute-start(bf16[4,192,384]{2,1,0:T(8,128)(2,1)S(1)} %get-tuple-element.176), channel_id=1, source_target_pairs={{0,4},{2,6},{4,0},{6,2},{1,5},{3,7},{5,1},{7,3},{8,12},{10,14},{12... | collective-permute-start | bytes 1769480 | tf_op jit(solution)/shard_map/ppermute | solution.py:42
  142.8 6.9 %collective-permute-start.41 = (bf16[2,192,384]{2,1,0:T(8,128)(2,1)S(1)}, bf16[2,192,384]{2,1,0:T(8,128)(2,1)S(1)}, u32[]{:S(2)}, u32[]{:S(2)}) collective-permute-start(bf16[2,192,384]{2,1,0:T(8,128)(2,1)S(1)} %get-tuple-element.179), channel_id=1, source_target_pairs={{0,8},{8,0},{16,24},{24,16},{1,9},{9,1},{17,25},{25,17},{2,10},{10... | collective-permute-start | bytes 884744 | tf_op jit(solution)/shard_map/ppermute | solution.py:42
  147.2 13.7 %collective-permute-start.36 = (bf16[448,384]{1,0:T(8,128)(2,1)S(1)}, bf16[448,384]{1,0:T(8,128)(2,1)S(1)}, u32[]{:S(2)}, u32[]{:S(2)}) collective-permute-start(bf16[448,384]{1,0:T(8,128)(2,1)S(1)} %get-tuple-element.170.refs_6_), channel_id=1, source_target_pairs={{0,4},{2,6},{4,0},{6,2},{1,5},{3,7},{5,1},{7,3},{8,12},{10,14},{12... | collective-permute-start | bytes 1032200 | tf_op jit(solution)/shard_map/ppermute | solution.py:42
  147.6 12.5 %collective-permute-start.35 = (bf16[2,192,384]{2,1,0:T(8,128)(2,1)S(1)}, bf16[2,192,384]{2,1,0:T(8,128)(2,1)S(1)}, u32[]{:S(2)}, u32[]{:S(2)}) collective-permute-start(bf16[2,192,384]{2,1,0:T(8,128)(2,1)S(1)} %get-tuple-element.169), channel_id=1, source_target_pairs={{0,2},{2,0},{4,6},{6,4},{1,3},{3,1},{5,7},{7,5},{8,10},{10,8},{12,... | collective-permute-start | bytes 884744 | tf_op jit(solution)/shard_map/ppermute | solution.py:42
  150.3 6.5 %collective-permute-start.42 = (bf16[192,384]{1,0:T(8,128)(2,1)S(1)}, bf16[192,384]{1,0:T(8,128)(2,1)S(1)}, u32[]{:S(2)}, u32[]{:S(2)}) collective-permute-start(bf16[192,384]{1,0:T(8,128)(2,1)S(1)} %get-tuple-element.181), channel_id=1, source_target_pairs={{0,16},{8,24},{16,0},{24,8},{1,17},{9,25},{17,1},{25,9},{2,18},{10... | collective-permute-start | bytes 442376 | tf_op jit(solution)/shard_map/ppermute | solution.py:42
  161.8 6.2 %collective-permute-start.43 = (bf16[448,384]{1,0:T(8,128)(2,1)S(1)}, bf16[448,384]{1,0:T(8,128)(2,1)S(1)}, u32[]{:S(2)}, u32[]{:S(2)}) collective-permute-start(bf16[448,384]{1,0:T(8,128)(2,1)S(1)} %get-tuple-element.186), channel_id=1, source_target_pairs={{0,8},{8,0},{16,24},{24,16},{1,9},{9,1},{17,25},{25,17},{2,10},{10... | collective-permute-start | bytes 1032200 | tf_op jit(solution)/shard_map/ppermute | solution.py:42
  163.3 7.6 %collective-permute-start.45 = (bf16[2,192,384]{2,1,0:T(8,128)(2,1)S(1)}, bf16[2,192,384]{2,1,0:T(8,128)(2,1)S(1)}, u32[]{:S(2)}, u32[]{:S(2)}) collective-permute-start(bf16[2,192,384]{2,1,0:T(8,128)(2,1)S(1)} %get-tuple-element.183.refs_7_), channel_id=1, source_target_pairs={{0,2},{2,0},{4,6},{6,4},{1,3},{3,1},{5,7},{7,5},{8,10},{10,8},{12,... | collective-permute-start | bytes 884744 | tf_op jit(solution)/shard_map/ppermute | solution.py:42
  165.0 7.5 %collective-permute-start.46 = (bf16[2,192,384]{2,1,0:T(8,128)(2,1)S(1)}, bf16[2,192,384]{2,1,0:T(8,128)(2,1)S(1)}, u32[]{:S(2)}, u32[]{:S(2)}) collective-permute-start(bf16[2,192,384]{2,1,0:T(8,128)(2,1)S(1)} %get-tuple-element.184.refs_8_), channel_id=1, source_target_pairs={{0,4},{2,6},{4,0},{6,2},{1,5},{3,7},{5,1},{7,3},{8,12},{10,14},{12... | collective-permute-start | bytes 884744 | tf_op jit(solution)/shard_map/ppermute | solution.py:42
  165.4 9.4 %collective-permute-start.30 = (bf16[2,128,384]{2,1,0:T(8,128)(2,1)S(1)}, bf16[2,128,384]{2,1,0:T(8,128)(2,1)S(1)}, u32[]{:S(2)}, u32[]{:S(2)}) collective-permute-start(bf16[2,128,384]{2,1,0:T(8,128)(2,1)S(1)} %get-tuple-element.160), channel_id=1, source_target_pairs={{0,2},{2,0},{4,6},{6,4},{1,3},{3,1},{5,7},{7,5},{8,10},{10,8},{12,... | collective-permute-start | bytes 589832 | tf_op jit(solution)/shard_map/ppermute | solution.py:42
  168.6 7.7 %collective-permute-start.44 = (bf16[256,384]{1,0:T(8,128)(2,1)S(1)}, bf16[256,384]{1,0:T(8,128)(2,1)S(1)}, u32[]{:S(2)}, u32[]{:S(2)}) collective-permute-start(bf16[256,384]{1,0:T(8,128)(2,1)S(1)} %get-tuple-element.188), channel_id=1, source_target_pairs={{0,16},{8,24},{16,0},{24,8},{1,17},{9,25},{17,1},{25,9},{2,18},{10... | collective-permute-start | bytes 589832 | tf_op jit(solution)/shard_map/ppermute | solution.py:42
  170.9 9.1 %collective-permute-start.31 = (bf16[2,128,384]{2,1,0:T(8,128)(2,1)S(1)}, bf16[2,128,384]{2,1,0:T(8,128)(2,1)S(1)}, u32[]{:S(2)}, u32[]{:S(2)}) collective-permute-start(bf16[2,128,384]{2,1,0:T(8,128)(2,1)S(1)} %get-tuple-element.161), channel_id=1, source_target_pairs={{0,4},{2,6},{4,0},{6,2},{1,5},{3,7},{5,1},{7,3},{8,12},{10,14},{12... | collective-permute-start | bytes 589832 | tf_op jit(solution)/shard_map/ppermute | solution.py:42
  170.9 23.0 %collective-permute-start.32 = (bf16[2,128,384]{2,1,0:T(8,128)(2,1)S(1)}, bf16[2,128,384]{2,1,0:T(8,128)(2,1)S(1)}, u32[]{:S(2)}, u32[]{:S(2)}) collective-permute-start(bf16[2,128,384]{2,1,0:T(8,128)(2,1)S(1)} %get-tuple-element.162), channel_id=1, source_target_pairs={{0,6},{2,4},{4,2},{6,0},{1,7},{3,5},{5,3},{7,1},{8,14},{10,12},{12... | collective-permute-start | bytes 589832 | tf_op jit(solution)/shard_map/ppermute | solution.py:42
  173.4 22.3 %collective-permute-start.47 = (bf16[192,384]{1,0:T(8,128)(2,1)S(1)}, bf16[192,384]{1,0:T(8,128)(2,1)S(1)}, u32[]{:S(2)}, u32[]{:S(2)}) collective-permute-start(bf16[192,384]{1,0:T(8,128)(2,1)S(1)} %get-tuple-element.197), channel_id=1, source_target_pairs={{0,16},{8,24},{16,0},{24,8},{1,17},{9,25},{17,1},{25,9},{2,18},{10... | collective-permute-start | bytes 442376 | tf_op jit(solution)/shard_map/ppermute | solution.py:42
  174.8 20.9 %collective-permute-start.48 = (bf16[192,384]{1,0:T(8,128)(2,1)S(1)}, bf16[192,384]{1,0:T(8,128)(2,1)S(1)}, u32[]{:S(2)}, u32[]{:S(2)}) collective-permute-start(bf16[192,384]{1,0:T(8,128)(2,1)S(1)} %get-tuple-element.198), channel_id=1, source_target_pairs={{0,8},{8,0},{16,24},{24,16},{1,9},{9,1},{17,25},{25,17},{2,10},{10... | collective-permute-start | bytes 442376 | tf_op jit(solution)/shard_map/ppermute | solution.py:42
  176.3 19.4 %collective-permute-start.49 = (bf16[192,384]{1,0:T(8,128)(2,1)S(1)}, bf16[192,384]{1,0:T(8,128)(2,1)S(1)}, u32[]{:S(2)}, u32[]{:S(2)}) collective-permute-start(bf16[192,384]{1,0:T(8,128)(2,1)S(1)} %get-tuple-element.199), channel_id=1, source_target_pairs={{0,24},{8,16},{16,8},{24,0},{1,25},{9,17},{17,9},{25,1},{2,26},{10... | collective-permute-start | bytes 442376 | tf_op jit(solution)/shard_map/ppermute | solution.py:42
  179.9 18.6 %collective-permute-start.50 = (f32[32,384]{1,0:T(8,128)S(1)}, f32[32,384]{1,0:T(8,128)S(1)}, u32[]{:S(2)}, u32[]{:S(2)}) collective-permute-start(f32[32,384]{1,0:T(8,128)S(1)} %get-tuple-element.205.refs_1_), channel_id=1, source_target_pairs={{0,1},{1,0},{2,3},{3,2},{4,5},{5,4},{6,7},{7,6},{8,9},{9,8},{10,11... | collective-permute-start | bytes 147464 | tf_op jit(solution)/shard_map/ppermute | solution.py:42
  (23 other events, 316.2 us)

commit v3 on v2

--- a/solution.py
+++ b/solution.py
@@ -34,6 +34,8 @@
 MIX = HEADS * 3 * HD
 PAIRS = LEN // 2
 CHUNK = (W, COLS)
+PART = (3 * S, COLS)
+CROSS = (S, COLS)
 MIB = 1024 * 1024
 
 
@@ -100,13 +102,19 @@
     return high, (value - high.astype(F32)).astype(BF16)
 
 
-def opening_kernel(where, tokens, grads, joint, output, *refs):
+def opening_kernel(where, tokens, grads, joint, output, down, *refs):
     outs, first = refs[:ROWS], refs[ROWS]
-    tokens_in, grads_in, joint_in, output_in, done = refs[ROWS + 1 :]
+    tokens_in, grads_in, joint_in, output_in, down_in, done = refs[ROWS + 1 :]
     copies = [
         pltpu.make_async_copy(source, target, done.at[i])
         for i, (source, target) in enumerate(
-            [(joint, joint_in), (output, output_in), (tokens, tokens_in), (grads, grads_in)]
+            [
+                (joint, joint_in),
+                (output, output_in),
+                (tokens, tokens_in),
+                (grads, grads_in),
+                (down.at[:, 3 * COLS :], down_in),
+            ]
         )
     ]
     for copy in copies:
@@ -119,9 +127,11 @@
     first[HEADS // 2 * S :, :] = output_in[...].astype(BF16)
     copies[2].wait()
     copies[3].wait()
+    copies[4].wait()
     for m, out in enumerate(outs):
-        out[0] = tokens_in[where[0] ^ m]
-        out[1] = grads_in[where[0] ^ m]
+        out[0:PAIRS, :] = tokens_in[where[0] ^ m]
+        out[PAIRS:LEN, :] = grads_in[where[0] ^ m]
+        out[LEN:, :] = down_in[...].astype(BF16)
 
 
 def second_shard_kernel(where, up, second):
@@ -130,13 +140,23 @@
 
 
 def third_shard_kernel(where, down, third):
-    for q in range(4):
+    for q in range(3):
         third[q * S : (q + 1) * S, :] = down[:, q * COLS : (q + 1) * COLS].astype(BF16)
 
 
 def pair_kernel(where, b0, b1, pair):
     pair[0] = b0[...]
     pair[1] = b1[...]
+
+
+def cross_kernel(where, t0, t1, t2, t3, plane):
+    for m, piece in enumerate([t0, t1, t2, t3]):
+        plane[m] = piece[LEN:, :]
+
+
+def planes_kernel(where, b0, b1, planes):
+    planes[0:ROWS] = b0[...]
+    planes[ROWS:] = b1[...]
 
 
 def whole_kernel(where, *refs):
@@ -152,8 +172,8 @@
 
 def token_kernel(where, tokens, grads, *outs):
     for m, out in enumerate(outs):
-        out[0] = tokens[where[0] ^ m]
-        out[1] = grads[where[0] ^ m]
+        out[0:PAIRS, :] = tokens[where[0] ^ m]
+        out[PAIRS:LEN, :] = grads[where[0] ^ m]
 
 
 ORDER = (0, 2, 1, 3)
@@ -165,6 +185,12 @@
         yield where[0] ^ (at // QUADS), where[1] ^ ORDER[at % QUADS], piece[i]
 
 
+def cross_blocks(where, pieces):
+    for j, piece in enumerate(pieces):
+        for i in range(2 * ROWS):
+            yield where[0] ^ (i % ROWS), where[1] ^ ORDER[2 * j + i // ROWS], piece[i]
+
+
 def unpack_tokens(x):
     parts = [jnp.concatenate([x[r][:, :W], x[r][:, W:]], axis=0) for r in range(ROWS)]
     return jnp.concatenate(parts, axis=1)
@@ -173,16 +199,17 @@
 def pack_tokens(value, room, k):
     for r in range(ROWS):
         both = value[:, r * W : (r + 1) * W]
-        room[r, k] = jnp.concatenate([both[:PAIRS], both[PAIRS:]], axis=1).astype(BF16)
+        packed = jnp.concatenate([both[:PAIRS], both[PAIRS:]], axis=1).astype(BF16)
+        room[r, k * PAIRS : (k + 1) * PAIRS, :] = packed
 
 
 def attend_kernel(where, t0, t1, t2, t3, vecs, *refs):
     pieces, refs = refs[:5], refs[5:]
     tokens, grads, wj, wo, mixed, probs, attended, part, room, mixing, scores, parts = refs
     for m, piece in enumerate([t0, t1, t2, t3]):
-        room[where[0] ^ m] = piece[...]
-    tokens[...] = unpack_tokens([room[r, 0] for r in range(ROWS)])
-    grads[...] = unpack_tokens([room[r, 1] for r in range(ROWS)])
+        room[where[0] ^ m] = piece[0:LEN, :]
+    tokens[...] = unpack_tokens([room[r, 0:PAIRS, :] for r in range(ROWS)])
+    grads[...] = unpack_tokens([room[r, PAIRS:, :] for r in range(ROWS)])
     half = HEADS // 2
     for row, quad, value in blocks(where, pieces):
         for h in range(half):
@@ -289,40 +316,46 @@
 
 
 def down_kernel(where, act, *refs):
-    pieces, wd, part = refs[:5], refs[5], refs[6]
+    pieces, cross, wd, part = refs[:5], refs[5:7], refs[7], refs[8]
     for row, quad, value in blocks(where, pieces):
         rows = pl.ds(pl.multiple_of(row * W + quad * S, 16), S)
-        for q in range(4):
+        for q in range(3):
             wd[rows, q * COLS : (q + 1) * COLS] = value[q * S : (q + 1) * S, :]
+    for row, quad, value in cross_blocks(where, cross):
+        rows = pl.ds(pl.multiple_of(row * W + quad * S, 16), S)
+        wd[rows, 3 * COLS :] = value
     part[...] = dot(act[...], wd[...], NT).astype(BF16)
 
 
 def hand_out(where, room, outs):
     r = where[0]
-    last_x, last_y, own = outs[-3:]
-    if len(outs) == 5:
-        far_x, far_y = [out.at[0:2] for out in outs[:2]]
-        near_x, near_y = [out.at[2:4] for out in outs[:2]]
-    else:
-        far_x, far_y, near_x, near_y = outs[:4]
-    far_x[...] = room[r ^ 3, 0:2]
-    far_y[...] = room[r ^ 3, 2:4]
-    near_x[...] = room[r ^ 1, 0:2]
-    near_y[...] = room[r ^ 2, 2:4]
+    to_x, to_y, last_x, last_y, own = outs
+    to_x[0:2] = room[r ^ 3, 0:2]
+    to_x[2:4] = room[r ^ 1, 0:2]
+    to_y[0:2] = room[r ^ 3, 2:4]
+    to_y[2:4] = room[r ^ 2, 2:4]
     last_x[...] = room[r ^ 1, 2:4]
     last_y[...] = room[r ^ 2, 0:2]
     own[...] = room[r]
 
 
+def handed_shapes(block):
+    pair, line = shape(2, *block), shape(4, *block)
+    return [line] * 2 + [pair] * 2 + [line]
+
+
+HANDED = handed_shapes(CHUNK)
 PAIR = shape(2, *CHUNK)
-LINE = shape(4, *CHUNK)
-HANDED = [LINE] * 2 + [PAIR] * 2 + [LINE]
-SPLIT = [PAIR] * 6 + [LINE]
+PLANES = shape(2 * ROWS, *CROSS)
 
 VROWS = 32
 VECTOR = (VROWS, COLS)
 CARRIED = (2 * W + 2 * VROWS, COLS)
-FIRST = (4 * W + 2 * VROWS, COLS)
+
+LATE_X = 4 * W + 2 * VROWS
+LATE_Y = 4 * W
+FIRST_X = (LATE_X + 2 * PART[0], COLS)
+FIRST_Y = (LATE_Y + 2 * PART[0], COLS)
 
 
 def put_vector(out, start, value):
@@ -337,7 +370,8 @@
 
 
 def second_norm_kernel(where, hidden, p0, p1, vecs, grads, act, *refs):
-    (result, low, grad_two, sums), handed, room = refs[:4], refs[4:11], refs[11]
+    (result, low, grad_two, sums), handed = refs[:4], refs[4:9]
+    cross_own, cross_send, room, cross = refs[9:]
     sums[...] = jnp.zeros_like(sums)
     bias_down, gain, shift_by = [vector_row(vecs, k) for k in (5, 6, 7)]
 
@@ -362,8 +396,15 @@
         for r in range(ROWS):
             for z in range(QUADS):
                 start = r * W + z * S
-                room[r, z, q * S : (q + 1) * S, :] = grad[start : start + S, :]
+                if q < 3:
+                    room[r, z, q * S : (q + 1) * S, :] = grad[start : start + S, :]
+                else:
+                    cross[z, r] = grad[start : start + S, :]
     hand_out(where, room, handed)
+    for k, mask in enumerate([0, 2]):
+        rows = slice(k * ROWS, (k + 1) * ROWS)
+        cross_own[rows] = cross[where[1] ^ mask]
+        cross_send[rows] = cross[where[1] ^ mask ^ 1]
 
 
 def hidden_back_kernel(where, low, slope, wd, wu, grad_pre, part, sums, back):
@@ -460,12 +501,21 @@
         vector[20 + j : 21 + j, :] = row * right
 
 
-def first_hand_kernel(where, room, vector, carried, *refs):
-    handed, first = refs[:-1], refs[-1]
-    hand_out(where, room, [first, *handed])
-    for k in range(4):
-        carried[k * W : (k + 1) * W, :] = first[k]
-    put_vector(carried, 4 * W, vector[...])
+def first_hand_kernel(where, room, vector, late_x, late_y, to_x, to_y, last_x, last_y, own):
+    r = where[0]
+    for k in range(2):
+        far, near = slice(k * W, (k + 1) * W), slice((2 + k) * W, (3 + k) * W)
+        to_x[far, :] = room[r ^ 3, k]
+        to_x[near, :] = room[r ^ 1, k]
+        to_y[far, :] = room[r ^ 3, 2 + k]
+        to_y[near, :] = room[r ^ 2, 2 + k]
+        for start, out, late in [(LATE_X, to_x, late_x), (LATE_Y, to_y, late_y)]:
+            at = start + k * PART[0]
+            out[at : at + PART[0], :] = late[k]
+    last_x[...] = room[r ^ 1, 2:4]
+    last_y[...] = room[r ^ 2, 0:2]
+    own[...] = room[r]
+    put_vector(to_x, 4 * W, vector[...])
 
 
 def token_back_kernel(where, grad_mixed, wj, part):
@@ -474,7 +524,9 @@
 
 
 def token_sum_kernel(where, result, grad_one, p0, p1, *refs):
-    outs, total, room = refs[:4], refs[4], refs[5]
+    total, room = refs[-2:]
+    cross = [*refs[:2], refs[6]] if len(refs) > 6 else []
+    outs = refs[2:6] if cross else refs[:4]
 
     def body(i):
         at = strip(i)
@@ -484,14 +536,21 @@
     pack_tokens(result, room, 0)
     pack_tokens(total, room, 1)
     for m, out in enumerate(outs):
-        out[...] = room[where[0] ^ m]
+        row = where[0] ^ m
+        out[0:LEN, :] = room[row]
+        if cross:
+            kept, got, own = cross
+            sums = kept[row] + got[row].astype(F32)
+            out[LEN:, :] = sums.astype(BF16)
+            if m == 0:
+                own[...] = sums
 
 
 def token_out_kernel(where, t0, t1, t2, t3, result, total):
     for m, piece in enumerate([t0, t1, t2, t3]):
         for k, out in enumerate([result, total]):
             for q in range(3):
-                value = piece[k, :, q * 128 : (q + 1) * 128].astype(F32)
+                value = piece[k * PAIRS : (k + 1) * PAIRS, q * 128 : (q + 1) * 128].astype(F32)
                 out[where[0] ^ m, pl.ds(q, PAIRS, stride=3), :] = value
 
 
@@ -501,9 +560,9 @@
 
 
 def carry_pass_kernel(where, last_x, last_y, carried, from_x, from_y, to_x, to_y):
-    to_x[...] = (last_x[...].astype(F32) + from_y[0:2].astype(F32)).astype(BF16)
     for k in range(2):
         rows = slice(k * W, (k + 1) * W)
+        to_x[k] = (last_x[k].astype(F32) + from_y[rows, :].astype(F32)).astype(BF16)
         to_y[rows, :] = (last_y[k].astype(F32) + from_x[rows, :].astype(F32)).astype(BF16)
     put_vector(to_y, 2 * W, get_vector(carried, 4 * W) + get_vector(from_x, 4 * W))
 
@@ -519,8 +578,8 @@
     return lambda k: ref[skip + k].astype(F32)
 
 
-def kept_rows(ref, start):
-    return lambda k: ref[start + k * W : start + (k + 1) * W, :].astype(F32)
+def kept_rows(ref, start, rows=W):
+    return lambda k: ref[start + k * rows : start + (k + 1) * rows, :].astype(F32)
 
 
 def line_kernel(where, own, from_x, from_y, last_x, last_y, kept, *refs):
@@ -534,9 +593,10 @@
         kept[...] = room[...]
 
 
-def near_line_kernel(where, own, from_x, from_y, last_x, last_y, kept, *refs):
+def near_line_kernel(where, own, from_x, from_y, late_x, late_y, kept, *refs):
     *sends, room = refs
-    add_plane(own, *[kept_blocks(v) for v in (from_x, from_y, last_x, last_y)], room)
+    late = [kept_rows(late_x, LATE_X, PART[0]), kept_rows(late_y, LATE_Y, PART[0])]
+    add_plane(own, kept_blocks(from_x), kept_blocks(from_y), *late, room)
     if sends:
         for k, mask in enumerate([0, 2]):
             kept[k] = room[where[1] ^ mask]
@@ -550,10 +610,15 @@
     send[...] = (kept[1] + got[1].astype(F32)).astype(BF16)
 
 
-def carry_near_kernel(where, own, from_x, near_y, last_x, from_y, passed, kept, *refs):
+def cross_far_kernel(where, own, got, kept, send):
+    kept[...] = own[0:ROWS].astype(F32) + got[0:ROWS].astype(F32)
+    send[...] = (own[ROWS:].astype(F32) + got[ROWS:].astype(F32)).astype(BF16)
+
+
+def carry_near_kernel(where, own, first_x, first_y, last_x, from_y, passed, kept, *refs):
     *sends, room = refs
-    near_x = kept_rows(from_x, 2 * W)
-    add_plane(own, near_x, kept_blocks(near_y), kept_blocks(last_x), kept_rows(from_y, 0), room)
+    near = [kept_rows(first_x, 2 * W), kept_rows(first_y, 2 * W)]
+    add_plane(own, *near, kept_blocks(last_x), kept_rows(from_y, 0), room)
     vector = get_vector(passed, 2 * W) + get_vector(from_y, 2 * W)
     if kept.ndim == 2:
         for k, mask in enumerate([0, 2]):
@@ -629,11 +694,13 @@
             out[at] = value
 
 
-def down_adam_kernel(where, kept, got, w, f, s, *outs):
-    grad = kept[...] + got[...].astype(F32)
+def down_adam_kernel(where, kept, got, own, r1, r2, r3, w, f, s, *outs):
+    far = r2[LEN:, :].astype(F32) + r3[LEN:, :].astype(F32)
+    cross = (own[...] + r1[LEN:, :].astype(F32)) + far
+    most = kept[...] + got[...].astype(F32)
     for q in range(4):
         at = (slice(None), slice(q * COLS, (q + 1) * COLS))
-        cut = grad[q * S : (q + 1) * S, :]
+        cut = most[q * S : (q + 1) * S, :] if q < 3 else cross
         for out, value in zip(outs, adamw(w[at], f[at], s[at], cut, DOWN_RATE, DECAY)):
             out[at] = value
 
@@ -641,16 +708,23 @@
 def gather_line(where, shard, steps):
     if steps == 1:
         return [shard] + [swap(shard, "dp", mask) for mask in ORDER[1:]]
-    pair = run(pair_kernel, where, [shard, swap(shard, "dp", 2)], [PAIR])[0]
+    pair = [shape(2, *shard.shape)]
+    pair = run(pair_kernel, where, [shard, swap(shard, "dp", 2)], pair)[0]
     return [pair, swap(pair, "dp", 1)]
 
 
 def gather_plane(where, line, after=()):
-    line = run(whole_kernel, where, line, [LINE], after=after)[0]
+    block = line[0].shape[-2:]
+    line = run(whole_kernel, where, line, [shape(4, *block)], after=after)[0]
     from_x = swap(line, "row", 1)
     from_y = swap(line, "row", 2)
-    near_y, far_x = run(halves_kernel, where, [from_x, from_y], [PAIR] * 2)
+    near_y, far_x = run(halves_kernel, where, [from_x, from_y], [shape(2, *block)] * 2)
     return [line, from_x, from_y, swap(near_y, "row", 1), swap(far_x, "row", 2)]
+
+
+def gather_cross(where, plane):
+    planes = run(planes_kernel, where, [plane, swap(plane, "dp", 2)], [PLANES])[0]
+    return [planes, swap(planes, "dp", 1)]
 
 
 def scatter_first(handed):
@@ -658,7 +732,8 @@
 
 
 def scatter_pass(where, handed, got, after=()):
-    return run(pass_kernel, where, handed[-3:-1] + got[:2], [PAIR] * 2, after=after)
+    pair = [shape(*handed[2].shape)] * 2
+    return run(pass_kernel, where, handed[2:4] + got, pair, after=after)
 
 
 def scatter_second(passed):
@@ -734,21 +809,22 @@
     flat = up_weight.size // 128
 
     sent = [tokens_in.reshape(ROWS, PAIRS, 2 * W), out_grad.reshape(ROWS, PAIRS, 2 * W)]
-    blocks_out = [shape(2, PAIRS, 2 * W)] * ROWS
+    blocks_out = [shape(LEN + S if direct else LEN, 2 * W)] * ROWS
     if direct:
         up = [v.reshape(flat, 128) for v in up]
         one = [shape(*CHUNK)]
         *pieces, first = run(
             opening_kernel,
             where,
-            sent + [joint[0], output[0]],
+            sent + [joint[0], output[0], down[0]],
             blocks_out + one,
             [
                 pltpu.VMEM(sent[0].shape, BF16),
                 pltpu.VMEM(sent[1].shape, BF16),
                 pltpu.VMEM(joint[0].shape, F32),
                 pltpu.VMEM(output[0].shape, F32),
-                pltpu.SemaphoreType.DMA((4,)),
+                pltpu.VMEM(CROSS, F32),
+                pltpu.SemaphoreType.DMA((5,)),
             ],
             limit=56,
             fetch=True,
@@ -758,17 +834,24 @@
         first_pieces = gather_plane(where, first, tokens_pieces[1:])
         shard = run(second_shard_kernel, where, [up[0]], one, after=first[1:])[0]
         second = gather_line(where, shard, 2)
+        plane = run(cross_kernel, where, tokens_pieces, [shape(ROWS, *CROSS)])[0]
+        cross = gather_cross(where, plane)
         second_pieces = gather_plane(where, second)
-        after = second_pieces[:1] + first_pieces[1:3]
-        shard = run(third_shard_kernel, where, [down[0]], one, after=after)[0]
+        after = second_pieces[:1] + cross[:1]
+        shard = run(third_shard_kernel, where, [down[0]], [shape(*PART)], after=after)[0]
         third = gather_line(where, shard, 2)
         third_pieces = gather_plane(where, third, first_pieces[3:])
+        third_pieces += cross
     else:
         tokens_pieces = exchange(run(token_kernel, where, sent, blocks_out))
         lines = wide_lines(joint[0], output[0], up_weight[:, 0], down[0])
+        cross = lines[2][:, 3 * S :]
+        lines[2] = lines[2][:, : 3 * S]
         first_pieces, second_pieces, third_pieces = [
             gather_plane(where, list(line)) for line in lines
         ]
+        cross = jnp.stack([cross] + [swap(cross, "row", m) for m in range(1, ROWS)], axis=1)
+        third_pieces += list(cross.reshape(2, *PLANES.shape))
 
     vecs = vectors.reshape(72, 128)
     tokens, grads, wj, wo, mixed, probs, attended, part = run(
@@ -786,7 +869,7 @@
             shape(LEN, D),
         ],
         [
-            pltpu.VMEM((ROWS, 2, PAIRS, 2 * W), BF16),
+            pltpu.VMEM((ROWS, LEN, 2 * W), BF16),
             pltpu.VMEM((MIX, LEN), F32),
             pltpu.VMEM((LEN, LEN), F32),
             pltpu.VMEM((8, MIX), F32),
@@ -806,6 +889,7 @@
             shape(D, FFC),
         ],
         [pltpu.VMEM((LEN, FFC), F32)],
+        after=third_pieces[6:],
     )
     wd, part = run(
         down_kernel, where, [act] + third_pieces, [shape(D, FFC), shape(LEN, D)]
@@ -816,10 +900,14 @@
         [hidden, part, swap(part, "col", 1), vecs, grads, act],
         [shape(LEN, D, dtype=F32), shape(LEN, D), shape(LEN, D, dtype=F32)]
         + [shape(8, D, dtype=F32)]
-        + SPLIT,
-        [pltpu.VMEM((ROWS, QUADS) + CHUNK, BF16)],
-    )
-    (result, grad_low, grad_two, sums_two), third_handed = out[:4], out[4:]
+        + handed_shapes(PART)
+        + [PLANES] * 2,
+        [
+            pltpu.VMEM((ROWS, QUADS) + PART, BF16),
+            pltpu.VMEM((QUADS, ROWS) + CROSS, BF16),
+        ],
+    )
+    (result, grad_low, grad_two, sums_two), third_handed, cross = out[:4], out[4:9], out[9:]
     third_got = scatter_first(third_handed)
     grad_pre, part, sums_up = run(
         hidden_back_kernel,
@@ -829,14 +917,12 @@
         [pltpu.VMEM((LEN, FFC), F32)],
     )
     third_passed = scatter_pass(where, third_handed, third_got)
-    third_last = scatter_second(third_passed)
     second_handed = run(
         up_grad_kernel,
         where,
         [hidden_low, grad_pre],
         HANDED,
         [pltpu.VMEM((ROWS, QUADS) + CHUNK, BF16)],
-        after=third_last,
     )
     grad_one, grad_mixed, vector, room = run(
         first_norm_kernel,
@@ -865,23 +951,40 @@
             pltpu.VMEM((LEN, LEN), BF16),
             pltpu.VMEM((8, D), F32),
         ],
-    )
+        after=third_got,
+    )
+    cross_got = [swap(cross[1], "dp", 1)] if direct else []
     first_handed = run(
         first_hand_kernel,
         where,
-        [room, vector],
-        [shape(*FIRST)] + HANDED[1:],
-        [pltpu.VMEM((4,) + CHUNK, BF16)],
-        after=third_passed + third_got[2:],
+        [room, vector] + third_passed,
+        [shape(*FIRST_X), shape(*FIRST_Y)] + HANDED[2:],
+        after=cross_got,
     )
     first_got = scatter_first(first_handed)
-    (part,) = run(token_back_kernel, where, [grad_mixed, wj], [shape(LEN, D)], after=first_handed[:1])
+
+    def like(values):
+        return [shape(*v.shape, dtype=F32) for v in values]
+
+    def sums(dims, split):
+        return [shape(*dims, dtype=F32), shape(*split)]
+
+    if direct:
+        plane = (ROWS,) + CROSS
+        cross = run(cross_far_kernel, where, cross[:1] + cross_got, sums(plane, plane))
+        cross_sum = [cross[0], swap(cross[1], "dp", 2)]
+    else:
+        cross_sum = []
+    (part,) = run(
+        token_back_kernel, where, [grad_mixed, wj], [shape(LEN, D)], after=first_handed[:1]
+    )
+    own = [shape(*CROSS, dtype=F32)] if direct else []
     pieces = run(
         token_sum_kernel,
         where,
-        [result, grad_one, part, swap(part, "col", 1)],
-        [shape(2, PAIRS, 2 * W)] * ROWS,
-        [pltpu.VMEM((LEN, D), F32), pltpu.VMEM((ROWS, 2, PAIRS, 2 * W), BF16)],
+        [result, grad_one, part, swap(part, "col", 1)] + cross_sum,
+        blocks_out + own,
+        [pltpu.VMEM((LEN, D), F32), pltpu.VMEM((ROWS, LEN, 2 * W), BF16)],
     )
     first_passed = run(
         carry_pass_kernel,
@@ -892,29 +995,22 @@
     )
     first_last = scatter_second(first_passed)
 
-    def like(values):
-        return [shape(*v.shape, dtype=F32) for v in values]
-
-    def sums(dims, split):
-        return [shape(*dims, dtype=F32), shape(*split)]
-
     lines = [pltpu.VMEM((4,) + CHUNK, F32)]
     wide = [shape(4, *CHUNK, dtype=F32)]
     third_sum = run(
         near_line_kernel,
         where,
-        third_handed[-1:] + third_got[2:] + third_last,
-        sums(PAIR.shape, PAIR.shape) if direct else wide,
-        lines,
+        third_handed[-1:] + third_got + first_got,
+        sums((2,) + PART, (2,) + PART) if direct else [shape(4, *PART, dtype=F32)],
+        [pltpu.VMEM((4,) + PART, F32)],
     )
     if direct:
         got = swap(third_sum[1], "dp", 1)
-        third_sum = run(far_line_kernel, where, [third_sum[0], got], sums(CHUNK, CHUNK))
-        got = swap(third_sum[1], "dp", 2)
-        down_new = run(down_adam_kernel, where, [third_sum[0], got] + down, like(down))
-        ready = down_new[:1]
+        third_sum = run(far_line_kernel, where, [third_sum[0], got], sums(PART, PART))
+        third_sum[1] = swap(third_sum[1], "dp", 2)
+        ready = third_sum[1:] + pieces[:1]
     else:
-        ready = []
+        ready = pieces[:1]
     second_got = scatter_first(second_handed)
     second_passed = scatter_pass(where, second_handed, second_got, ready)
     second_last = scatter_second(second_passed)
@@ -952,30 +1048,41 @@
         joint_new, output_new, vector = new[:3], new[3:6], new[6]
 
     flat_out = [shape(ROWS, 3 * PAIRS, 128, dtype=F32)] * 2
-    out = run(token_out_kernel, where, exchange(pieces), flat_out)
+    got = exchange(pieces[:ROWS])
+    out = run(token_out_kernel, where, got, flat_out)
     layer_out, tokens_grad = [v.reshape(tokens_in.shape) for v in out]
 
+    def step_vectors(vector):
+        state = [v.reshape(72, 128) for v in (vectors, vector_first, vector_second)]
+        new = run(
+            vector_adam_kernel,
+            where,
+            [vector, swap(vector, "col", 1)] + state,
+            like(state),
+            [pltpu.VMEM((72, 128), F32)],
+        )
+        return [v.reshape(vectors.shape) for v in new]
+
     if direct:
+        down_new = run(
+            down_adam_kernel, where, third_sum + pieces[ROWS:] + got[1:] + down, like(down)
+        )
+        vector_new = step_vectors(vector)
         got = [swap(v, "dp", mask) for v, mask in zip(second_sum[1:], ORDER[1:])]
-        up_new = run(up_adam_kernel, where, second_sum[:1] + got + up, like(up), after=out[:1])
+        after = out[:1] + vector_new[:1] + down_new[:1]
+        up_new = run(up_adam_kernel, where, second_sum[:1] + got + up, like(up), after=after)
         up_new = [v.reshape(up_weight.shape) for v in up_new]
     else:
-        grads = wide_sums(first_sum[0], second_sum[0], third_sum[0])
+        kept, sent = [v.reshape(2, ROWS, *CROSS) for v in cross]
+        cross = jnp.stack([kept, sent], axis=1).reshape(QUADS, ROWS, *CROSS)
+        cross = lax.psum_scatter(cross.astype(F32), "row", scatter_dimension=1)
+        third = jnp.concatenate([third_sum[0], cross], axis=1)
+        grads = wide_sums(first_sum[0], second_sum[0], third)
         joint_new = adamw(*joint, grads[0], JOINT_RATE, DECAY)
         output_new = adamw(*output, grads[1], OUTPUT_RATE, DECAY)
         up_new = adamw(*up, grads[2][:, None], JOINT_RATE, DECAY)
         down_new = adamw(*down, grads[3], DOWN_RATE, DECAY)
-        vector = lax.psum(first_sum[1], "dp")
-
-    state = [v.reshape(72, 128) for v in (vectors, vector_first, vector_second)]
-    vector_new = run(
-        vector_adam_kernel,
-        where,
-        [vector, swap(vector, "col", 1)] + state,
-        like(state),
-        [pltpu.VMEM((72, 128), F32)],
-    )
-    vector_new = [v.reshape(vectors.shape) for v in vector_new]
+        vector_new = step_vectors(lax.psum(first_sum[1], "dp"))
 
     return (
         layer_out,

time: 201 us -> 194 us (0.965)
  starting transfers between devices: 79.2 us -> 68.2 us
  waiting for transfers between devices: 63.5 us -> 66.8 us
    ppermute x51, starting transfers between devices: 79.2 us -> 68.2 us  [swap(): return lax.ppermute(value, axis, [(i, i ^ mask) for i in range(n)])]
    ppermute x51, waiting for transfers between devices: 63.5 us -> 66.8 us  [swap(): return lax.ppermute(value, axis, [(i, i ^ mask) for i in range(n)])]
    pallas_call x34 -> x37, Pallas kernels: 50.8 us -> 52.5 us  [run(): pl.pallas_call(body, out_shape=outs, in_specs=[pl.BlockSpec(memory_space=...]
  transfers between devices with their start and end apart: 51 -> 51, of which waited for: 20 -> 22; matrix products, arithmetic and copies ran while one was open for 0% -> 0% of each run, Pallas kernels for 18% -> 21%
where the time goes in v3:
time: 194 us; the launch traced here: 193 us
  starting transfers between devices  68.2 us (35%)
  waiting for transfers between devices  66.8 us (34%)
  Pallas kernels  52.5 us (27%)
  local copies, waits for them, and re-layouts  3.39 us (2%)
    ppermute x51, starting transfers between devices, swap(): return lax.ppermute(value, axis, [(i, i ^ mask) for i in range(n)])  68.2 us
    ppermute x51, waiting for transfers between devices, swap(): return lax.ppermute(value, axis, [(i, i ^ mask) for i in range(n)])  66.8 us
    pallas_call x37, Pallas kernels, run(): pl.pallas_call(body, out_shape=outs, in_specs=[pl.BlockSpec(memory_space=...  52.5 us
  transfers between devices with their start and end apart: 51, of which 22 were waited for; matrix products, arithmetic and copies ran while one was open for 0% of the time, Pallas kernels for 21%

profile of v3, /device:TPU:1, one launch (start us, length us, event | category | flops | bytes accessed | tf_op | source)
XLA Modules:
  0.0 193.3 jit_solution(777071397230492361)
XLA Ops:
  1.9 3.0 %shard_map.305 = (bf16[304,384]{1,0:T(8,128)(2,1)}, bf16[304,384]{1,0:T(8,128)(2,1)}, bf16[304,384]{1,0:T(8,128)(2,1)}, bf16[304,384]{1,0:T(8,128)(2,1)}, bf16[192,384]{1,0:T(8,128)(2,1)}) custom-call(s32[4]{0:T(128)} %pad_add_fusion.refs_0_, bf16[4,128,384]{2,1,0:T(8,128)(2,1)} %bitcast.89, bf16[4,128,384]{2,1,0:T(8,128)(2,1)} %bitcast.90, ...), custom_call_target="tpu_custom_call" | custom-call | tf_op jit(solution)/shard_map/pallas_call | solution.py:58
  5.0 4.2 %collective-permute-start.5 = (bf16[192,384]{1,0:T(8,128)(2,1)}, bf16[192,384]{1,0:T(8,128)(2,1)S(1)}, u32[]{:S(2)}, u32[]{:S(2)}) collective-permute-start(bf16[192,384]{1,0:T(8,128)(2,1)} %get-tuple-element.120.refs_1_), channel_id=1, source_target_pairs={{0,24},{8,16},{16,8},{24,0},{1,25},{9,17},{17,9},{25,1},{2,26},{10... | collective-permute-start | bytes 442376 | tf_op jit(solution)/shard_map/ppermute | solution.py:44
  10.4 1.2 collective-permute-start.1
  13.0 1.5 collective-permute-start.3
  14.5 1.8 collective-permute-done.4.refs_3_
  16.3 1.9 collective-permute-done.3.refs_2_
  18.2 3.4 %collective-permute-done.2.refs_7_.refs_4_ = bf16[304,384]{1,0:T(8,128)(2,1)S(1)} collective-permute-done((bf16[304,384]{1,0:T(8,128)(2,1)}, bf16[304,384]{1,0:T(8,128)(2,1)S(1)}, u32[]{:S(2)}, u32[]{:S(2)}) %collective-permute-start.2) | collective-permute-done | bytes 233504 | tf_op jit(solution)/shard_map/ppermute | solution.py:44
  26.3 6.1 %collective-permute-done.11.refs_2_ = bf16[192,384]{1,0:T(8,128)(2,1)S(1)} collective-permute-done((bf16[192,384]{1,0:T(8,128)(2,1)S(1)}, bf16[192,384]{1,0:T(8,128)(2,1)S(1)}, u32[]{:S(2)}, u32[]{:S(2)}) %collective-permute-start.11) | collective-permute-done | bytes 147488 | tf_op jit(solution)/shard_map/ppermute | solution.py:44
  33.7 1.6 collective-permute-start.17
  35.2 5.1 %collective-permute-done.17.refs_2_ = bf16[4,48,384]{2,1,0:T(8,128)(2,1)S(1)} collective-permute-done((bf16[4,48,384]{2,1,0:T(8,128)(2,1)S(1)}, bf16[4,48,384]{2,1,0:T(8,128)(2,1)S(1)}, u32[]{:S(2)}, u32[]{:S(2)}) %collective-permute-start.17) | collective-permute-done | bytes 147488 | tf_op jit(solution)/shard_map/ppermute | solution.py:44
  44.3 1.2 collective-permute-start.14
  45.5 2.4 %collective-permute-done.19.refs_2_ = bf16[144,384]{1,0:T(8,128)(2,1)S(1)} collective-permute-done((bf16[144,384]{1,0:T(8,128)(2,1)S(1)}, bf16[144,384]{1,0:T(8,128)(2,1)S(1)}, u32[]{:S(2)}, u32[]{:S(2)}) %collective-permute-start.19) | collective-permute-done | bytes 110624 | tf_op jit(solution)/shard_map/ppermute | solution.py:44
  49.1 5.7 %collective-permute-done.20.refs_2_ = bf16[2,144,384]{2,1,0:T(8,128)(2,1)S(1)} collective-permute-done((bf16[2,144,384]{2,1,0:T(8,128)(2,1)S(1)}, bf16[2,144,384]{2,1,0:T(8,128)(2,1)S(1)}, u32[]{:S(2)}, u32[]{:S(2)}) %collective-permute-start.20) | collective-permute-done | bytes 221216 | tf_op jit(solution)/shard_map/ppermute | solution.py:44
  56.5 5.2 %shard_map.308 = (bf16[256,768]{1,0:T(8,128)(2,1)S(1)}, bf16[256,768]{1,0:T(8,128)(2,1)S(1)}, bf16[4,1152,192]{2,1,0:T(8,128)(2,1)S(1)}, bf16[768,384]{1,0:T(8,1...) custom-call(s32[4]{0:T(128)S(1)} %copy-done.6, ...), custom_call_target="tpu_custom_call" | custom-call | tf_op jit(solution)/shard_map/pallas_call | solution.py:58
  61.6 9.2 %collective-permute-start.10 = (bf16[256,768]{1,0:T(8,128)(2,1)S(1)}, bf16[256,768]{1,0:T(8,128)(2,1)S(1)}, u32[]{:S(2)}, u32[]{:S(2)}) collective-permute-start(bf16[256,768]{1,0:T(8,128)(2,1)S(1)} %get-tuple-element.124.refs_2_), channel_id=1, source_target_pairs={{0,1},{1,0},{2,3},{3,2},{4,5},{5,4},{6,7},{7,6},{8,9},{9,8},{10,11... | collective-permute-start | bytes 1179656 | tf_op jit(solution)/shard_map/ppermute | solution.py:44
  71.4 1.3 collective-permute-start.15
  75.1 5.5 %collective-permute-done.15.refs_8_ = bf16[2,192,384]{2,1,0:T(8,128)(2,1)S(1)} collective-permute-done((bf16[2,192,384]{2,1,0:T(8,128)(2,1)S(1)}, bf16[2,192,384]{2,1,0:T(8,128)(2,1)S(1)}, u32[]{:S(2)}, u32[]{:S(2)}) %collective-permute-start.15) | collective-permute-done | bytes 294944 | tf_op jit(solution)/shard_map/ppermute | solution.py:44
  80.6 3.8 %shard_map.315 = (f32[256,768]{1,0:T(8,128)S(1)}, bf16[256,768]{1,0:T(8,128)(2,1)S(1)}, f32[256,768]{1,0:T(8,128)S(1)}, f32[256,1]{1,0:T(8,128)S(1)}, bf16[256,1...) custom-call(s32[4]{0:T(128)S(1)} %copy-done.6, ...), custom_call_target="tpu_custom_call" | custom-call | tf_op jit(solution)/shard_map/pallas_call | solution.py:58
  85.3 1.6 shard_map.320
  86.9 4.2 %collective-permute-start.25 = (bf16[256,768]{1,0:T(8,128)(2,1)S(1)}, bf16[256,768]{1,0:T(8,128)(2,1)S(1)}, u32[]{:S(2)}, u32[]{:S(2)}) collective-permute-start(bf16[256,768]{1,0:T(8,128)(2,1)S(1)} %get-tuple-element.131.refs_2_), channel_id=1, source_target_pairs={{0,1},{1,0},{2,3},{3,2},{4,5},{5,4},{6,7},{7,6},{8,9},{9,8},{10,11... | collective-permute-start | bytes 1179656 | tf_op jit(solution)/shard_map/ppermute | solution.py:44
  91.1 1.3 collective-permute-done.25.refs_3_
  92.4 3.7 %shard_map.321 = (f32[256,768]{1,0:T(8,128)S(1)}, bf16[256,768]{1,0:T(8,128)(2,1)S(1)}, f32[256,768]{1,0:T(8,128)S(1)}, f32[8,768]{1,0:T(8,128)S(1)}, bf16[4,144...) custom-call(s32[4]{0:T(128)S(1)} %copy-done.6, ...), custom_call_target="tpu_custom_call" | custom-call | tf_op jit(solution)/shard_map/pallas_call | solution.py:58
  96.6 3.3 %shard_map.322 = (bf16[256,1536]{1,0:T(8,128)(2,1)S(1)}, bf16[256,768]{1,0:T(8,128)(2,1)S(1)}, f32[8,1536]{1,0:T(8,128)S(1)}) custom-call(s32[4]{0:T(128)S(1)} %copy-done.6, bf16[256,768]{1,0:T(8,128)(2,1)S(1)} %get-tuple-element.135.refs_1_, f32[256,1536]{1,0:T(8,128)S(1)} %get-tuple-element.136.refs_2_, bf16[768,1536]{1,0:T(8,128)(2,1)S(1)} %get-tuple-element.137.refs_3_, ...), custom_call_target="tpu_custom_call" | custom-call | tf_op jit(solution)/shard_map/pallas_call | solution.py:58
  100.7 1.7 collective-permute-start.29
  102.4 5.2 %collective-permute-done.27.refs_14_.refs_3_.refs_2_ = bf16[4,144,384]{2,1,0:T(8,128)(2,1)S(1)} collective-permute-done((bf16[4,144,384]{2,1,0:T(8,128)(2,1)S(1)}, bf16[4,144,384]{2,1,0:T(8,128)(2,1)S(1)}, u32[]{:S(2)}, u32[]{:S(2)}) %collective-permute-start.27) | collective-permute-done | bytes 442400 | tf_op jit(solution)/shard_map/ppermute | solution.py:44
  108.2 5.4 %shard_map.323 = (f32[256,768]{1,0:T(8,128)S(1)}, bf16[1152,256]{1,0:T(8,128)(2,1)S(1)}, f32[32,384]{1,0:T(8,128)S(1)}, bf16[4,4,192,384]{3,2,1,0:T(8,128)(2,1)S(1)}) custom-call(s32[4]{0:T(128)S(1)} %copy-done.6, f32[256,768]{1,0:T(8,128)S(1)} %get-tuple-element.134.refs_1_, bf16[256,768]{1,0:T(8,128)(2,1)S(1)} %get-tuple-element.139.refs_2_, ...), custom_call_target="tpu_custom_call" | custom-call | tf_op jit(solution)/shard_map/pallas_call | solution.py:58
  114.4 1.2 collective-permute-start.35
  116.0 1.5 shard_map.326.refs_3_
  117.5 2.1 %collective-permute-start.30 = (bf16[256,768]{1,0:T(8,128)(2,1)S(1)}, bf16[256,768]{1,0:T(8,128)(2,1)S(1)}, u32[]{:S(2)}, u32[]{:S(2)}) collective-permute-start(bf16[256,768]{1,0:T(8,128)(2,1)S(1)} %shard_map.326.refs_3_), channel_id=1, source_target_pairs={{0,1},{1,0},{2,3},{3,2},{4,5},{5,4},{6,7},{7,6},{8,9},{9,8},{10,11... | collective-permute-start | bytes 1179656 | tf_op jit(solution)/shard_map/ppermute | solution.py:44
  120.3 1.6 collective-permute-start.31
  121.8 1.8 shard_map.331
  124.2 5.6 %collective-permute-done.31.refs_6_ = bf16[4,48,384]{2,1,0:T(8,128)(2,1)S(1)} collective-permute-done((bf16[4,48,384]{2,1,0:T(8,128)(2,1)S(1)}, bf16[4,48,384]{2,1,0:T(8,128)(2,1)S(1)}, u32[]{:S(2)}, u32[]{:S(2)}) %collective-permute-start.31) | collective-permute-done | bytes 147488 | tf_op jit(solution)/shard_map/ppermute | solution.py:44
  132.1 1.3 collective-permute-done.36.refs_5_.refs_3_
  135.9 1.3 collective-permute-start.41
  138.1 2.9 %collective-permute-done.41.refs_2_ = bf16[2,144,384]{2,1,0:T(8,128)(2,1)S(1)} collective-permute-done((bf16[2,144,384]{2,1,0:T(8,128)(2,1)S(1)}, bf16[2,144,384]{2,1,0:T(8,128)(2,1)S(1)}, u32[]{:S(2)}, u32[]{:S(2)}) %collective-permute-start.41) | collective-permute-done | bytes 221216 | tf_op jit(solution)/shard_map/ppermute | solution.py:44
  141.7 1.4 collective-permute-start.42
  143.1 3.4 %collective-permute-done.39.refs_3_.refs_2_ = bf16[4,192,384]{2,1,0:T(8,128)(2,1)S(1)} collective-permute-done((bf16[4,192,384]{2,1,0:T(8,128)(2,1)S(1)}, bf16[4,192,384]{2,1,0:T(8,128)(2,1)S(1)}, u32[]{:S(2)}, u32[]{:S(2)}) %collective-permute-start.39) | collective-permute-done | bytes 589856 | tf_op jit(solution)/shard_map/ppermute | solution.py:44
  147.2 5.6 %collective-permute-done.37.refs_4_ = bf16[2,192,384]{2,1,0:T(8,128)(2,1)S(1)} collective-permute-done((bf16[2,192,384]{2,1,0:T(8,128)(2,1)S(1)}, bf16[2,192,384]{2,1,0:T(8,128)(2,1)S(1)}, u32[]{:S(2)}, u32[]{:S(2)}) %collective-permute-start.37) | collective-permute-done | bytes 294944 | tf_op jit(solution)/shard_map/ppermute | solution.py:44
  157.7 3.6 %collective-permute-done.43.refs_2_ = bf16[448,384]{1,0:T(8,128)(2,1)S(1)} collective-permute-done((bf16[448,384]{1,0:T(8,128)(2,1)S(1)}, bf16[448,384]{1,0:T(8,128)(2,1)S(1)}, u32[]{:S(2)}, u32[]{:S(2)}) %collective-permute-start.43) | collective-permute-done | bytes 344096 | tf_op jit(solution)/shard_map/ppermute | solution.py:44
  161.9 1.7 collective-permute-start.44
  163.8 1.5 collective-permute-start.34
  168.1 1.8 collective-permute-done.44.refs_2_
  169.9 1.9 collective-permute-start.49
  171.8 1.7 shard_map.337
  173.5 11.7 %collective-permute-start.50 = (f32[32,384]{1,0:T(8,128)S(1)}, f32[32,384]{1,0:T(8,128)S(1)}, u32[]{:S(2)}, u32[]{:S(2)}) collective-permute-start(f32[32,384]{1,0:T(8,128)S(1)} %get-tuple-element.203.refs_1_), channel_id=1, source_target_pairs={{0,1},{1,0},{2,3},{3,2},{4,5},{5,4},{6,7},{7,6},{8,9},{9,8},{10,11... | collective-permute-start | bytes 147464 | tf_op jit(solution)/shard_map/ppermute | solution.py:44
  185.2 1.8 shard_map.329
  187.0 1.6 shard_map.340
  191.6 1.7 shard_map.341
  (134 shorter events, 42.4 us)
Async XLA Ops:
  5.0 8.0 %collective-permute-start.5 = (bf16[192,384]{1,0:T(8,128)(2,1)}, bf16[192,384]{1,0:T(8,128)(2,1)S(1)}, u32[]{:S(2)}, u32[]{:S(2)}) collective-permute-start(bf16[192,384]{1,0:T(8,128)(2,1)} %get-tuple-element.120.refs_1_), channel_id=1, source_target_pairs={{0,24},{8,16},{16,8},{24,0},{1,25},{9,17},{17,9},{25,1},{2,26},{10... | collective-permute-start | bytes 442376 | tf_op jit(solution)/shard_map/ppermute | solution.py:44
  9.2 9.0 %collective-permute-start = (bf16[304,384]{1,0:T(8,128)(2,1)}, bf16[304,384]{1,0:T(8,128)(2,1)S(1)}, u32[]{:S(2)}, u32[]{:S(2)}) collective-permute-start(bf16[304,384]{1,0:T(8,128)(2,1)} %get-tuple-element.117), channel_id=1, source_target_pairs={{0,2},{2,0},{4,6},{6,4},{1,3},{3,1},{5,7},{7,5},{8,10},{10,8},{12,... | collective-permute-start | bytes 700424 | tf_op jit(solution)/shard_map/ppermute | solution.py:44
  10.4 7.8 %collective-permute-start.1 = (bf16[304,384]{1,0:T(8,128)(2,1)}, bf16[304,384]{1,0:T(8,128)(2,1)S(1)}, u32[]{:S(2)}, u32[]{:S(2)}) collective-permute-start(bf16[304,384]{1,0:T(8,128)(2,1)} %get-tuple-element.118), channel_id=1, source_target_pairs={{0,4},{2,6},{4,0},{6,2},{1,5},{3,7},{5,1},{7,3},{8,12},{10,14},{12... | collective-permute-start | bytes 700424 | tf_op jit(solution)/shard_map/ppermute | solution.py:44
  11.6 10.0 %collective-permute-start.2 = (bf16[304,384]{1,0:T(8,128)(2,1)}, bf16[304,384]{1,0:T(8,128)(2,1)S(1)}, u32[]{:S(2)}, u32[]{:S(2)}) collective-permute-start(bf16[304,384]{1,0:T(8,128)(2,1)} %get-tuple-element.119), channel_id=1, source_target_pairs={{0,6},{2,4},{4,2},{6,0},{1,7},{3,5},{5,3},{7,1},{8,14},{10,12},{12... | collective-permute-start | bytes 700424 | tf_op jit(solution)/shard_map/ppermute | solution.py:44
  13.0 5.2 %collective-permute-start.3 = (bf16[192,384]{1,0:T(8,128)(2,1)}, bf16[192,384]{1,0:T(8,128)(2,1)S(1)}, u32[]{:S(2)}, u32[]{:S(2)}) collective-permute-start(bf16[192,384]{1,0:T(8,128)(2,1)} %get-tuple-element.120.refs_1_), channel_id=1, source_target_pairs={{0,16},{8,24},{16,0},{24,8},{1,17},{9,25},{17,1},{25,9},{2,18},{10... | collective-permute-start | bytes 442376 | tf_op jit(solution)/shard_map/ppermute | solution.py:44
  23.8 19.3 %collective-permute-start.7 = (bf16[4,192,384]{2,1,0:T(8,128)(2,1)S(1)}, bf16[4,192,384]{2,1,0:T(8,128)(2,1)S(1)}, u32[]{:S(2)}, u32[]{:S(2)}) collective-permute-start(bf16[4,192,384]{2,1,0:T(8,128)(2,1)S(1)} %shard_map.306.refs_6_), channel_id=1, source_target_pairs={{0,4},{2,6},{4,0},{6,2},{1,5},{3,7},{5,1},{7,3},{8,12},{10,14},{12... | collective-permute-start | bytes 1769480 | tf_op jit(solution)/shard_map/ppermute | solution.py:44
  24.1 19.0 %collective-permute-start.6 = (bf16[4,192,384]{2,1,0:T(8,128)(2,1)S(1)}, bf16[4,192,384]{2,1,0:T(8,128)(2,1)S(1)}, u32[]{:S(2)}, u32[]{:S(2)}) collective-permute-start(bf16[4,192,384]{2,1,0:T(8,128)(2,1)S(1)} %shard_map.306.refs_6_), channel_id=1, source_target_pairs={{0,2},{2,0},{4,6},{6,4},{1,3},{3,1},{5,7},{7,5},{8,10},{10,8},{12,... | collective-permute-start | bytes 1769480 | tf_op jit(solution)/shard_map/ppermute | solution.py:44
  25.9 6.5 %collective-permute-start.11 = (bf16[192,384]{1,0:T(8,128)(2,1)S(1)}, bf16[192,384]{1,0:T(8,128)(2,1)S(1)}, u32[]{:S(2)}, u32[]{:S(2)}) collective-permute-start(bf16[192,384]{1,0:T(8,128)(2,1)S(1)} %shard_map.309.refs_1_), channel_id=1, source_target_pairs={{0,16},{8,24},{16,0},{24,8},{1,17},{9,25},{17,1},{25,9},{2,18},{10... | collective-permute-start | bytes 442376 | tf_op jit(solution)/shard_map/ppermute | solution.py:44
  33.0 8.8 %collective-permute-start.12 = (bf16[2,192,384]{2,1,0:T(8,128)(2,1)S(1)}, bf16[2,192,384]{2,1,0:T(8,128)(2,1)S(1)}, u32[]{:S(2)}, u32[]{:S(2)}) collective-permute-start(bf16[2,192,384]{2,1,0:T(8,128)(2,1)S(1)} %shard_map.310.refs_1_), channel_id=1, source_target_pairs={{0,8},{8,0},{16,24},{24,16},{1,9},{9,1},{17,25},{25,17},{2,10},{10... | collective-permute-start | bytes 884744 | tf_op jit(solution)/shard_map/ppermute | solution.py:44
  33.7 6.7 %collective-permute-start.17 = (bf16[4,48,384]{2,1,0:T(8,128)(2,1)S(1)}, bf16[4,48,384]{2,1,0:T(8,128)(2,1)S(1)}, u32[]{:S(2)}, u32[]{:S(2)}) collective-permute-start(bf16[4,48,384]{2,1,0:T(8,128)(2,1)S(1)} %shard_map.313.refs_1_), channel_id=1, source_target_pairs={{0,16},{8,24},{16,0},{24,8},{1,17},{9,25},{17,1},{25,9},{2,18},{10... | collective-permute-start | bytes 442376 | tf_op jit(solution)/shard_map/ppermute | solution.py:44
  43.7 11.1 %collective-permute-start.8 = (bf16[2,192,384]{2,1,0:T(8,128)(2,1)S(1)}, bf16[2,192,384]{2,1,0:T(8,128)(2,1)S(1)}, u32[]{:S(2)}, u32[]{:S(2)}) collective-permute-start(bf16[2,192,384]{2,1,0:T(8,128)(2,1)S(1)} %get-tuple-element.121), channel_id=1, source_target_pairs={{0,2},{2,0},{4,6},{6,4},{1,3},{3,1},{5,7},{7,5},{8,10},{10,8},{12,... | collective-permute-start | bytes 884744 | tf_op jit(solution)/shard_map/ppermute | solution.py:44
  44.0 10.7 %collective-permute-start.9 = (bf16[2,192,384]{2,1,0:T(8,128)(2,1)S(1)}, bf16[2,192,384]{2,1,0:T(8,128)(2,1)S(1)}, u32[]{:S(2)}, u32[]{:S(2)}) collective-permute-start(bf16[2,192,384]{2,1,0:T(8,128)(2,1)S(1)} %get-tuple-element.122), channel_id=1, source_target_pairs={{0,4},{2,6},{4,0},{6,2},{1,5},{3,7},{5,1},{7,3},{8,12},{10,14},{12... | collective-permute-start | bytes 884744 | tf_op jit(solution)/shard_map/ppermute | solution.py:44
  44.3 17.4 %collective-permute-start.14 = (bf16[4,192,384]{2,1,0:T(8,128)(2,1)S(1)}, bf16[4,192,384]{2,1,0:T(8,128)(2,1)S(1)}, u32[]{:S(2)}, u32[]{:S(2)}) collective-permute-start(bf16[4,192,384]{2,1,0:T(8,128)(2,1)S(1)} %shard_map.311.refs_5_.refs_2_), channel_id=1, source_target_pairs={{0,4},{2,6},{4,0},{6,2},{1,5},{3,7},{5,1},{7,3},{8,12},{10,14},{12... | collective-permute-start | bytes 1769480 | tf_op jit(solution)/shard_map/ppermute | solution.py:44
  48.4 6.3 %collective-permute-start.20 = (bf16[2,144,384]{2,1,0:T(8,128)(2,1)S(1)}, bf16[2,144,384]{2,1,0:T(8,128)(2,1)S(1)}, u32[]{:S(2)}, u32[]{:S(2)}) collective-permute-start(bf16[2,144,384]{2,1,0:T(8,128)(2,1)S(1)} %shard_map.317.refs_1_), channel_id=1, source_target_pairs={{0,8},{8,0},{16,24},{24,16},{1,9},{9,1},{17,25},{25,17},{2,10},{10... | collective-permute-start | bytes 663560 | tf_op jit(solution)/shard_map/ppermute | solution.py:44
  48.5 22.3 %collective-permute-start.13 = (bf16[4,192,384]{2,1,0:T(8,128)(2,1)S(1)}, bf16[4,192,384]{2,1,0:T(8,128)(2,1)S(1)}, u32[]{:S(2)}, u32[]{:S(2)}) collective-permute-start(bf16[4,192,384]{2,1,0:T(8,128)(2,1)S(1)} %shard_map.311.refs_5_.refs_2_), channel_id=1, source_target_pairs={{0,2},{2,0},{4,6},{6,4},{1,3},{3,1},{5,7},{7,5},{8,10},{10,8},{12,... | collective-permute-start | bytes 1769480 | tf_op jit(solution)/shard_map/ppermute | solution.py:44
  55.4 17.4 %collective-permute-start.22 = (bf16[4,144,384]{2,1,0:T(8,128)(2,1)S(1)}, bf16[4,144,384]{2,1,0:T(8,128)(2,1)S(1)}, u32[]{:S(2)}, u32[]{:S(2)}) collective-permute-start(bf16[4,144,384]{2,1,0:T(8,128)(2,1)S(1)} %shard_map.318.refs_2_), channel_id=1, source_target_pairs={{0,4},{2,6},{4,0},{6,2},{1,5},{3,7},{5,1},{7,3},{8,12},{10,14},{12... | collective-permute-start | bytes 1327112 | tf_op jit(solution)/shard_map/ppermute | solution.py:44
  56.1 17.8 %collective-permute-start.21 = (bf16[4,144,384]{2,1,0:T(8,128)(2,1)S(1)}, bf16[4,144,384]{2,1,0:T(8,128)(2,1)S(1)}, u32[]{:S(2)}, u32[]{:S(2)}) collective-permute-start(bf16[4,144,384]{2,1,0:T(8,128)(2,1)S(1)} %shard_map.318.refs_2_), channel_id=1, source_target_pairs={{0,2},{2,0},{4,6},{6,4},{1,3},{3,1},{5,7},{7,5},{8,10},{10,8},{12,... | collective-permute-start | bytes 1327112 | tf_op jit(solution)/shard_map/ppermute | solution.py:44
  56.5 18.2 %collective-permute-start.18 = (bf16[8,48,384]{2,1,0:T(8,128)(2,1)S(1)}, bf16[8,48,384]{2,1,0:T(8,128)(2,1)S(1)}, u32[]{:S(2)}, u32[]{:S(2)}) collective-permute-start(bf16[8,48,384]{2,1,0:T(8,128)(2,1)S(1)} %shard_map.314.refs_3_.refs_7_), channel_id=1, source_target_pairs={{0,8},{8,0},{16,24},{24,16},{1,9},{9,1},{17,25},{25,17},{2,10},{10... | collective-permute-start | bytes 884744 | tf_op jit(solution)/shard_map/ppermute | solution.py:44
  61.6 19.0 %collective-permute-start.10 = (bf16[256,768]{1,0:T(8,128)(2,1)S(1)}, bf16[256,768]{1,0:T(8,128)(2,1)S(1)}, u32[]{:S(2)}, u32[]{:S(2)}) collective-permute-start(bf16[256,768]{1,0:T(8,128)(2,1)S(1)} %get-tuple-element.124.refs_2_), channel_id=1, source_target_pairs={{0,1},{1,0},{2,3},{3,2},{4,5},{5,4},{6,7},{7,6},{8,9},{9,8},{10,11... | collective-permute-start | bytes 1179656 | tf_op jit(solution)/shard_map/ppermute | solution.py:44
  71.4 9.2 %collective-permute-start.15 = (bf16[2,192,384]{2,1,0:T(8,128)(2,1)S(1)}, bf16[2,192,384]{2,1,0:T(8,128)(2,1)S(1)}, u32[]{:S(2)}, u32[]{:S(2)}) collective-permute-start(bf16[2,192,384]{2,1,0:T(8,128)(2,1)S(1)} %get-tuple-element.125), channel_id=1, source_target_pairs={{0,2},{2,0},{4,6},{6,4},{1,3},{3,1},{5,7},{7,5},{8,10},{10,8},{12,... | collective-permute-start | bytes 884744 | tf_op jit(solution)/shard_map/ppermute | solution.py:44
  72.7 7.9 %collective-permute-start.16 = (bf16[2,192,384]{2,1,0:T(8,128)(2,1)S(1)}, bf16[2,192,384]{2,1,0:T(8,128)(2,1)S(1)}, u32[]{:S(2)}, u32[]{:S(2)}) collective-permute-start(bf16[2,192,384]{2,1,0:T(8,128)(2,1)S(1)} %get-tuple-element.126), channel_id=1, source_target_pairs={{0,4},{2,6},{4,0},{6,2},{1,5},{3,7},{5,1},{7,3},{8,12},{10,14},{12... | collective-permute-start | bytes 884744 | tf_op jit(solution)/shard_map/ppermute | solution.py:44
  74.5 10.8 %collective-permute-start.23 = (bf16[2,144,384]{2,1,0:T(8,128)(2,1)S(1)}, bf16[2,144,384]{2,1,0:T(8,128)(2,1)S(1)}, u32[]{:S(2)}, u32[]{:S(2)}) collective-permute-start(bf16[2,144,384]{2,1,0:T(8,128)(2,1)S(1)} %get-tuple-element.129), channel_id=1, source_target_pairs={{0,2},{2,0},{4,6},{6,4},{1,3},{3,1},{5,7},{7,5},{8,10},{10,8},{12,... | collective-permute-start | bytes 663560 | tf_op jit(solution)/shard_map/ppermute | solution.py:44
  74.6 10.7 %collective-permute-start.24 = (bf16[2,144,384]{2,1,0:T(8,128)(2,1)S(1)}, bf16[2,144,384]{2,1,0:T(8,128)(2,1)S(1)}, u32[]{:S(2)}, u32[]{:S(2)}) collective-permute-start(bf16[2,144,384]{2,1,0:T(8,128)(2,1)S(1)} %get-tuple-element.130), channel_id=1, source_target_pairs={{0,4},{2,6},{4,0},{6,2},{1,5},{3,7},{5,1},{7,3},{8,12},{10,14},{12... | collective-permute-start | bytes 663560 | tf_op jit(solution)/shard_map/ppermute | solution.py:44
  86.9 5.5 %collective-permute-start.25 = (bf16[256,768]{1,0:T(8,128)(2,1)S(1)}, bf16[256,768]{1,0:T(8,128)(2,1)S(1)}, u32[]{:S(2)}, u32[]{:S(2)}) collective-permute-start(bf16[256,768]{1,0:T(8,128)(2,1)S(1)} %get-tuple-element.131.refs_2_), channel_id=1, source_target_pairs={{0,1},{1,0},{2,3},{3,2},{4,5},{5,4},{6,7},{7,6},{8,9},{9,8},{10,11... | collective-permute-start | bytes 1179656 | tf_op jit(solution)/shard_map/ppermute | solution.py:44
  96.1 11.5 %collective-permute-start.27 = (bf16[4,144,384]{2,1,0:T(8,128)(2,1)S(1)}, bf16[4,144,384]{2,1,0:T(8,128)(2,1)S(1)}, u32[]{:S(2)}, u32[]{:S(2)}) collective-permute-start(bf16[4,144,384]{2,1,0:T(8,128)(2,1)S(1)} %get-tuple-element.148), channel_id=1, source_target_pairs={{0,2},{2,0},{4,6},{6,4},{1,3},{3,1},{5,7},{7,5},{8,10},{10,8},{12,... | collective-permute-start | bytes 1327112 | tf_op jit(solution)/shard_map/ppermute | solution.py:44
  96.2 11.4 %collective-permute-start.28 = (bf16[4,144,384]{2,1,0:T(8,128)(2,1)S(1)}, bf16[4,144,384]{2,1,0:T(8,128)(2,1)S(1)}, u32[]{:S(2)}, u32[]{:S(2)}) collective-permute-start(bf16[4,144,384]{2,1,0:T(8,128)(2,1)S(1)} %get-tuple-element.149), channel_id=1, source_target_pairs={{0,4},{2,6},{4,0},{6,2},{1,5},{3,7},{5,1},{7,3},{8,12},{10,14},{12... | collective-permute-start | bytes 1327112 | tf_op jit(solution)/shard_map/ppermute | solution.py:44
  99.9 8.3 %collective-permute-start.26 = (bf16[256,768]{1,0:T(8,128)(2,1)S(1)}, bf16[256,768]{1,0:T(8,128)(2,1)S(1)}, u32[]{:S(2)}, u32[]{:S(2)}) collective-permute-start(bf16[256,768]{1,0:T(8,128)(2,1)S(1)} %get-tuple-element.139.refs_2_), channel_id=1, source_target_pairs={{0,1},{1,0},{2,3},{3,2},{4,5},{5,4},{6,7},{7,6},{8,9},{9,8},{10,11... | collective-permute-start | bytes 1179656 | tf_op jit(solution)/shard_map/ppermute | solution.py:44
  100.7 12.9 %collective-permute-start.29 = (bf16[8,48,384]{2,1,0:T(8,128)(2,1)S(1)}, bf16[8,48,384]{2,1,0:T(8,128)(2,1)S(1)}, u32[]{:S(2)}, u32[]{:S(2)}) collective-permute-start(bf16[8,48,384]{2,1,0:T(8,128)(2,1)S(1)} %get-tuple-element.159), channel_id=1, source_target_pairs={{0,8},{8,0},{16,24},{24,16},{1,9},{9,1},{17,25},{25,17},{2,10},{10... | collective-permute-start | bytes 884744 | tf_op jit(solution)/shard_map/ppermute | solution.py:44
  114.4 19.4 %collective-permute-start.35 = (bf16[1120,384]{1,0:T(8,128)(2,1)S(1)}, bf16[1120,384]{1,0:T(8,128)(2,1)S(1)}, u32[]{:S(2)}, u32[]{:S(2)}) collective-permute-start(bf16[1120,384]{1,0:T(8,128)(2,1)S(1)} %get-tuple-element.160.refs_3_), channel_id=1, source_target_pairs={{0,2},{2,0},{4,6},{6,4},{1,3},{3,1},{5,7},{7,5},{8,10},{10,8},{12,... | collective-permute-start | bytes 2580488 | tf_op jit(solution)/shard_map/ppermute | solution.py:44
  115.6 17.8 %collective-permute-start.36 = (bf16[1056,384]{1,0:T(8,128)(2,1)S(1)}, bf16[1056,384]{1,0:T(8,128)(2,1)S(1)}, u32[]{:S(2)}, u32[]{:S(2)}) collective-permute-start(bf16[1056,384]{1,0:T(8,128)(2,1)S(1)} %get-tuple-element.171), channel_id=1, source_target_pairs={{0,4},{2,6},{4,0},{6,2},{1,5},{3,7},{5,1},{7,3},{8,12},{10,14},{12... | collective-permute-start | bytes 2433032 | tf_op jit(solution)/shard_map/ppermute | solution.py:44
  117.5 13.4 %collective-permute-start.30 = (bf16[256,768]{1,0:T(8,128)(2,1)S(1)}, bf16[256,768]{1,0:T(8,128)(2,1)S(1)}, u32[]{:S(2)}, u32[]{:S(2)}) collective-permute-start(bf16[256,768]{1,0:T(8,128)(2,1)S(1)} %shard_map.326.refs_3_), channel_id=1, source_target_pairs={{0,1},{1,0},{2,3},{3,2},{4,5},{5,4},{6,7},{7,6},{8,9},{9,8},{10,11... | collective-permute-start | bytes 1179656 | tf_op jit(solution)/shard_map/ppermute | solution.py:44
  120.3 9.6 %collective-permute-start.31 = (bf16[4,48,384]{2,1,0:T(8,128)(2,1)S(1)}, bf16[4,48,384]{2,1,0:T(8,128)(2,1)S(1)}, u32[]{:S(2)}, u32[]{:S(2)}) collective-permute-start(bf16[4,48,384]{2,1,0:T(8,128)(2,1)S(1)} %get-tuple-element.163), channel_id=1, source_target_pairs={{0,16},{8,24},{16,0},{24,8},{1,17},{9,25},{17,1},{25,9},{2,18},{10... | collective-permute-start | bytes 442376 | tf_op jit(solution)/shard_map/ppermute | solution.py:44
  123.6 22.9 %collective-permute-start.39 = (bf16[4,192,384]{2,1,0:T(8,128)(2,1)S(1)}, bf16[4,192,384]{2,1,0:T(8,128)(2,1)S(1)}, u32[]{:S(2)}, u32[]{:S(2)}) collective-permute-start(bf16[4,192,384]{2,1,0:T(8,128)(2,1)S(1)} %get-tuple-element.180), channel_id=1, source_target_pairs={{0,2},{2,0},{4,6},{6,4},{1,3},{3,1},{5,7},{7,5},{8,10},{10,8},{12,... | collective-permute-start | bytes 1769480 | tf_op jit(solution)/shard_map/ppermute | solution.py:44
  129.9 16.6 %collective-permute-start.40 = (bf16[4,192,384]{2,1,0:T(8,128)(2,1)S(1)}, bf16[4,192,384]{2,1,0:T(8,128)(2,1)S(1)}, u32[]{:S(2)}, u32[]{:S(2)}) collective-permute-start(bf16[4,192,384]{2,1,0:T(8,128)(2,1)S(1)} %get-tuple-element.181), channel_id=1, source_target_pairs={{0,4},{2,6},{4,0},{6,2},{1,5},{3,7},{5,1},{7,3},{8,12},{10,14},{12... | collective-permute-start | bytes 1769480 | tf_op jit(solution)/shard_map/ppermute | solution.py:44
  134.5 18.9 %collective-permute-start.38 = (bf16[448,384]{1,0:T(8,128)(2,1)S(1)}, bf16[448,384]{1,0:T(8,128)(2,1)S(1)}, u32[]{:S(2)}, u32[]{:S(2)}) collective-permute-start(bf16[448,384]{1,0:T(8,128)(2,1)S(1)} %get-tuple-element.175.refs_6_), channel_id=1, source_target_pairs={{0,4},{2,6},{4,0},{6,2},{1,5},{3,7},{5,1},{7,3},{8,12},{10,14},{12... | collective-permute-start | bytes 1032200 | tf_op jit(solution)/shard_map/ppermute | solution.py:44
  135.9 5.1 %collective-permute-start.41 = (bf16[2,144,384]{2,1,0:T(8,128)(2,1)S(1)}, bf16[2,144,384]{2,1,0:T(8,128)(2,1)S(1)}, u32[]{:S(2)}, u32[]{:S(2)}) collective-permute-start(bf16[2,144,384]{2,1,0:T(8,128)(2,1)S(1)} %get-tuple-element.184), channel_id=1, source_target_pairs={{0,8},{8,0},{16,24},{24,16},{1,9},{9,1},{17,25},{25,17},{2,10},{10... | collective-permute-start | bytes 663560 | tf_op jit(solution)/shard_map/ppermute | solution.py:44
  137.2 15.6 %collective-permute-start.37 = (bf16[2,192,384]{2,1,0:T(8,128)(2,1)S(1)}, bf16[2,192,384]{2,1,0:T(8,128)(2,1)S(1)}, u32[]{:S(2)}, u32[]{:S(2)}) collective-permute-start(bf16[2,192,384]{2,1,0:T(8,128)(2,1)S(1)} %get-tuple-element.174), channel_id=1, source_target_pairs={{0,2},{2,0},{4,6},{6,4},{1,3},{3,1},{5,7},{7,5},{8,10},{10,8},{12,... | collective-permute-start | bytes 884744 | tf_op jit(solution)/shard_map/ppermute | solution.py:44
  154.4 6.9 %collective-permute-start.43 = (bf16[448,384]{1,0:T(8,128)(2,1)S(1)}, bf16[448,384]{1,0:T(8,128)(2,1)S(1)}, u32[]{:S(2)}, u32[]{:S(2)}) collective-permute-start(bf16[448,384]{1,0:T(8,128)(2,1)S(1)} %get-tuple-element.189), channel_id=1, source_target_pairs={{0,8},{8,0},{16,24},{24,16},{1,9},{9,1},{17,25},{25,17},{2,10},{10... | collective-permute-start | bytes 1032200 | tf_op jit(solution)/shard_map/ppermute | solution.py:44
  155.5 8.4 %collective-permute-start.45 = (bf16[2,192,384]{2,1,0:T(8,128)(2,1)S(1)}, bf16[2,192,384]{2,1,0:T(8,128)(2,1)S(1)}, u32[]{:S(2)}, u32[]{:S(2)}) collective-permute-start(bf16[2,192,384]{2,1,0:T(8,128)(2,1)S(1)} %get-tuple-element.186.refs_7_), channel_id=1, source_target_pairs={{0,2},{2,0},{4,6},{6,4},{1,3},{3,1},{5,7},{7,5},{8,10},{10,8},{12,... | collective-permute-start | bytes 884744 | tf_op jit(solution)/shard_map/ppermute | solution.py:44
  156.1 9.3 %collective-permute-start.46 = (bf16[2,192,384]{2,1,0:T(8,128)(2,1)S(1)}, bf16[2,192,384]{2,1,0:T(8,128)(2,1)S(1)}, u32[]{:S(2)}, u32[]{:S(2)}) collective-permute-start(bf16[2,192,384]{2,1,0:T(8,128)(2,1)S(1)} %get-tuple-element.187.refs_8_), channel_id=1, source_target_pairs={{0,4},{2,6},{4,0},{6,2},{1,5},{3,7},{5,1},{7,3},{8,12},{10,14},{12... | collective-permute-start | bytes 884744 | tf_op jit(solution)/shard_map/ppermute | solution.py:44
  156.7 10.6 %collective-permute-start.32 = (bf16[304,384]{1,0:T(8,128)(2,1)S(1)}, bf16[304,384]{1,0:T(8,128)(2,1)S(1)}, u32[]{:S(2)}, u32[]{:S(2)}) collective-permute-start(bf16[304,384]{1,0:T(8,128)(2,1)S(1)} %get-tuple-element.165), channel_id=1, source_target_pairs={{0,2},{2,0},{4,6},{6,4},{1,3},{3,1},{5,7},{7,5},{8,10},{10,8},{12,... | collective-permute-start | bytes 700424 | tf_op jit(solution)/shard_map/ppermute | solution.py:44
  161.9 7.9 %collective-permute-start.44 = (bf16[256,384]{1,0:T(8,128)(2,1)S(1)}, bf16[256,384]{1,0:T(8,128)(2,1)S(1)}, u32[]{:S(2)}, u32[]{:S(2)}) collective-permute-start(bf16[256,384]{1,0:T(8,128)(2,1)S(1)} %get-tuple-element.191), channel_id=1, source_target_pairs={{0,16},{8,24},{16,0},{24,8},{1,17},{9,25},{17,1},{25,9},{2,18},{10... | collective-permute-start | bytes 589832 | tf_op jit(solution)/shard_map/ppermute | solution.py:44
  163.6 9.9 %collective-permute-start.33 = (bf16[304,384]{1,0:T(8,128)(2,1)S(1)}, bf16[304,384]{1,0:T(8,128)(2,1)S(1)}, u32[]{:S(2)}, u32[]{:S(2)}) collective-permute-start(bf16[304,384]{1,0:T(8,128)(2,1)S(1)} %get-tuple-element.166), channel_id=1, source_target_pairs={{0,4},{2,6},{4,0},{6,2},{1,5},{3,7},{5,1},{7,3},{8,12},{10,14},{12... | collective-permute-start | bytes 700424 | tf_op jit(solution)/shard_map/ppermute | solution.py:44
  163.8 21.4 %collective-permute-start.34 = (bf16[304,384]{1,0:T(8,128)(2,1)S(1)}, bf16[304,384]{1,0:T(8,128)(2,1)S(1)}, u32[]{:S(2)}, u32[]{:S(2)}) collective-permute-start(bf16[304,384]{1,0:T(8,128)(2,1)S(1)} %get-tuple-element.167), channel_id=1, source_target_pairs={{0,6},{2,4},{4,2},{6,0},{1,7},{3,5},{5,3},{7,1},{8,14},{10,12},{12... | collective-permute-start | bytes 700424 | tf_op jit(solution)/shard_map/ppermute | solution.py:44
  166.3 23.6 %collective-permute-start.47 = (bf16[192,384]{1,0:T(8,128)(2,1)S(1)}, bf16[192,384]{1,0:T(8,128)(2,1)S(1)}, u32[]{:S(2)}, u32[]{:S(2)}) collective-permute-start(bf16[192,384]{1,0:T(8,128)(2,1)S(1)} %get-tuple-element.200), channel_id=1, source_target_pairs={{0,16},{8,24},{16,0},{24,8},{1,17},{9,25},{17,1},{25,9},{2,18},{10... | collective-permute-start | bytes 442376 | tf_op jit(solution)/shard_map/ppermute | solution.py:44
  167.3 22.5 %collective-permute-start.48 = (bf16[192,384]{1,0:T(8,128)(2,1)S(1)}, bf16[192,384]{1,0:T(8,128)(2,1)S(1)}, u32[]{:S(2)}, u32[]{:S(2)}) collective-permute-start(bf16[192,384]{1,0:T(8,128)(2,1)S(1)} %get-tuple-element.201), channel_id=1, source_target_pairs={{0,8},{8,0},{16,24},{24,16},{1,9},{9,1},{17,25},{25,17},{2,10},{10... | collective-permute-start | bytes 442376 | tf_op jit(solution)/shard_map/ppermute | solution.py:44
  169.9 20.0 %collective-permute-start.49 = (bf16[192,384]{1,0:T(8,128)(2,1)S(1)}, bf16[192,384]{1,0:T(8,128)(2,1)S(1)}, u32[]{:S(2)}, u32[]{:S(2)}) collective-permute-start(bf16[192,384]{1,0:T(8,128)(2,1)S(1)} %get-tuple-element.202), channel_id=1, source_target_pairs={{0,24},{8,16},{16,8},{24,0},{1,25},{9,17},{17,9},{25,1},{2,26},{10... | collective-permute-start | bytes 442376 | tf_op jit(solution)/shard_map/ppermute | solution.py:44
  173.5 15.1 %collective-permute-start.50 = (f32[32,384]{1,0:T(8,128)S(1)}, f32[32,384]{1,0:T(8,128)S(1)}, u32[]{:S(2)}, u32[]{:S(2)}) collective-permute-start(f32[32,384]{1,0:T(8,128)S(1)} %get-tuple-element.203.refs_1_), channel_id=1, source_target_pairs={{0,1},{1,0},{2,3},{3,2},{4,5},{5,4},{6,7},{7,6},{8,9},{9,8},{10,11... | collective-permute-start | bytes 147464 | tf_op jit(solution)/shard_map/ppermute | solution.py:44
  (24 other events, 334.4 us)

commit v4 on v3

--- a/solution.py
+++ b/solution.py
@@ -432,8 +432,10 @@
     hand_out(where, room, handed)
 
 
-def first_norm_kernel(where, grad_two, p0, p1, normed, inverse, vecs, wo, mixed, probs, attended, tokens, sums_two, sums_up, *refs):
-    grad_one, grad_mixed, vector, room, low, back, inner, scores, sums = refs
+def first_norm_kernel(
+    where, grad_two, p0, p1, normed, inverse, vecs, wo, mixed, probs, *refs
+):
+    grad_one, grad_mixed, low, sums, back, inner, scores = refs
     sums[...] = jnp.zeros_like(sums)
     gain = vector_row(vecs, 3)
 
@@ -469,6 +471,10 @@
         ]
         for k, grad in enumerate(grads):
             grad_mixed[base + k * HD : base + (k + 1) * HD, :] = grad.astype(BF16)
+
+
+def first_grad_kernel(where, grad_mixed, low, sums, attended, tokens, sums_two, sums_up, *refs):
+    vector, room = refs
     half = HEADS // 2
     for r in range(ROWS):
         cut = tokens[:, r * W : (r + 1) * W]
@@ -924,7 +930,7 @@
         HANDED,
         [pltpu.VMEM((ROWS, QUADS) + CHUNK, BF16)],
     )
-    grad_one, grad_mixed, vector, room = run(
+    grad_one, grad_mixed, low, sums_one = run(
         first_norm_kernel,
         where,
         [
@@ -937,21 +943,24 @@
             wo,
             mixed,
             probs,
-            attended,
-            tokens,
-            sums_two,
-            sums_up,
         ],
-        [shape(LEN, D, dtype=F32), shape(MIX, LEN), shape(*VECTOR, dtype=F32)]
-        + [shape(ROWS, QUADS, *CHUNK)],
         [
-            pltpu.VMEM((LEN, D), BF16),
+            shape(LEN, D, dtype=F32),
+            shape(MIX, LEN),
+            shape(LEN, D),
+            shape(8, D, dtype=F32),
+        ],
+        [
             pltpu.VMEM((COLS, LEN), BF16),
             pltpu.VMEM((LEN, LEN), F32),
             pltpu.VMEM((LEN, LEN), BF16),
-            pltpu.VMEM((8, D), F32),
         ],
-        after=third_got,
+    )
+    vector, room = run(
+        first_grad_kernel,
+        where,
+        [grad_mixed, low, sums_one, attended, tokens, sums_two, sums_up],
+        [shape(*VECTOR, dtype=F32), shape(ROWS, QUADS, *CHUNK)],
     )
     cross_got = [swap(cross[1], "dp", 1)] if direct else []
     first_handed = run(

time: 194 us -> 189 us (0.974)
  starting transfers between devices: 68.2 us -> 62.8 us
    ppermute x51, starting transfers between devices: 68.2 us -> 62.8 us  [swap(): return lax.ppermute(value, axis, [(i, i ^ mask) for i in range(n)])]
    pallas_call x37 -> x38, Pallas kernels: 52.5 us -> 53.2 us  [run(): pl.pallas_call(body, out_shape=outs, in_specs=[pl.BlockSpec(memory_space=...]
  transfers between devices with their start and end apart: 51 -> 51, of which waited for: 22 -> 23; matrix products, arithmetic and copies ran while one was open for 0% -> 0% of each run, Pallas kernels for 21% -> 22%
where the time goes in v4:
time: 189 us; the launch traced here: 188 us
  waiting for transfers between devices  66.4 us (35%)
  starting transfers between devices  62.8 us (33%)
  Pallas kernels  53.2 us (28%)
  local copies, waits for them, and re-layouts  3.39 us (2%)
    ppermute x51, waiting for transfers between devices, swap(): return lax.ppermute(value, axis, [(i, i ^ mask) for i in range(n)])  66.4 us
    ppermute x51, starting transfers between devices, swap(): return lax.ppermute(value, axis, [(i, i ^ mask) for i in range(n)])  62.8 us
    pallas_call x38, Pallas kernels, run(): pl.pallas_call(body, out_shape=outs, in_specs=[pl.BlockSpec(memory_space=...  53.2 us
  transfers between devices with their start and end apart: 51, of which 23 were waited for; matrix products, arithmetic and copies ran while one was open for 0% of the time, Pallas kernels for 22%

profile of v4, /device:TPU:1, one launch (start us, length us, event | category | flops | bytes accessed | tf_op | source)
XLA Modules:
  0.0 188.2 jit_solution(8042988292325991117)
XLA Ops:
  1.9 3.0 %shard_map.305 = (bf16[304,384]{1,0:T(8,128)(2,1)}, bf16[304,384]{1,0:T(8,128)(2,1)}, bf16[304,384]{1,0:T(8,128)(2,1)}, bf16[304,384]{1,0:T(8,128)(2,1)}, bf16[192,384]{1,0:T(8,128)(2,1)}) custom-call(s32[4]{0:T(128)} %pad_add_fusion.refs_0_, bf16[4,128,384]{2,1,0:T(8,128)(2,1)} %bitcast.89, bf16[4,128,384]{2,1,0:T(8,128)(2,1)} %bitcast.90, ...), custom_call_target="tpu_custom_call" | custom-call | tf_op jit(solution)/shard_map/pallas_call | solution.py:58
  5.0 4.2 %collective-permute-start.5 = (bf16[192,384]{1,0:T(8,128)(2,1)}, bf16[192,384]{1,0:T(8,128)(2,1)S(1)}, u32[]{:S(2)}, u32[]{:S(2)}) collective-permute-start(bf16[192,384]{1,0:T(8,128)(2,1)} %get-tuple-element.122.refs_1_), channel_id=1, source_target_pairs={{0,24},{8,16},{16,8},{24,0},{1,25},{9,17},{17,9},{25,1},{2,26},{10... | collective-permute-start | bytes 442376 | tf_op jit(solution)/shard_map/ppermute | solution.py:44
  10.4 1.2 collective-permute-start.1
  13.0 1.5 collective-permute-start.3
  14.5 1.8 collective-permute-done.4.refs_3_
  16.3 1.9 %collective-permute-done.3.refs_2_ = bf16[192,384]{1,0:T(8,128)(2,1)S(1)} collective-permute-done((bf16[192,384]{1,0:T(8,128)(2,1)}, bf16[192,384]{1,0:T(8,128)(2,1)S(1)}, u32[]{:S(2)}, u32[]{:S(2)}) %collective-permute-start.3) | collective-permute-done | bytes 147488 | tf_op jit(solution)/shard_map/ppermute | solution.py:44
  18.2 3.4 %collective-permute-done.2.refs_7_.refs_4_ = bf16[304,384]{1,0:T(8,128)(2,1)S(1)} collective-permute-done((bf16[304,384]{1,0:T(8,128)(2,1)}, bf16[304,384]{1,0:T(8,128)(2,1)S(1)}, u32[]{:S(2)}, u32[]{:S(2)}) %collective-permute-start.2) | collective-permute-done | bytes 233504 | tf_op jit(solution)/shard_map/ppermute | solution.py:44
  26.3 6.1 %collective-permute-done.11.refs_2_ = bf16[192,384]{1,0:T(8,128)(2,1)S(1)} collective-permute-done((bf16[192,384]{1,0:T(8,128)(2,1)S(1)}, bf16[192,384]{1,0:T(8,128)(2,1)S(1)}, u32[]{:S(2)}, u32[]{:S(2)}) %collective-permute-start.11) | collective-permute-done | bytes 147488 | tf_op jit(solution)/shard_map/ppermute | solution.py:44
  33.7 1.6 collective-permute-start.17
  35.2 5.1 %collective-permute-done.17.refs_2_ = bf16[4,48,384]{2,1,0:T(8,128)(2,1)S(1)} collective-permute-done((bf16[4,48,384]{2,1,0:T(8,128)(2,1)S(1)}, bf16[4,48,384]{2,1,0:T(8,128)(2,1)S(1)}, u32[]{:S(2)}, u32[]{:S(2)}) %collective-permute-start.17) | collective-permute-done | bytes 147488 | tf_op jit(solution)/shard_map/ppermute | solution.py:44
  45.5 2.4 %collective-permute-done.19.refs_2_ = bf16[144,384]{1,0:T(8,128)(2,1)S(1)} collective-permute-done((bf16[144,384]{1,0:T(8,128)(2,1)S(1)}, bf16[144,384]{1,0:T(8,128)(2,1)S(1)}, u32[]{:S(2)}, u32[]{:S(2)}) %collective-permute-start.19) | collective-permute-done | bytes 110624 | tf_op jit(solution)/shard_map/ppermute | solution.py:44
  49.1 5.7 %collective-permute-done.20.refs_2_ = bf16[2,144,384]{2,1,0:T(8,128)(2,1)S(1)} collective-permute-done((bf16[2,144,384]{2,1,0:T(8,128)(2,1)S(1)}, bf16[2,144,384]{2,1,0:T(8,128)(2,1)S(1)}, u32[]{:S(2)}, u32[]{:S(2)}) %collective-permute-start.20) | collective-permute-done | bytes 221216 | tf_op jit(solution)/shard_map/ppermute | solution.py:44
  56.5 5.2 %shard_map.308 = (bf16[256,768]{1,0:T(8,128)(2,1)S(1)}, bf16[256,768]{1,0:T(8,128)(2,1)S(1)}, bf16[4,1152,192]{2,1,0:T(8,128)(2,1)S(1)}, bf16[768,384]{1,0:T(8,1...) custom-call(s32[4]{0:T(128)S(1)} %copy-done.6, ...), custom_call_target="tpu_custom_call" | custom-call | tf_op jit(solution)/shard_map/pallas_call | solution.py:58
  61.6 9.2 %collective-permute-start.10 = (bf16[256,768]{1,0:T(8,128)(2,1)S(1)}, bf16[256,768]{1,0:T(8,128)(2,1)S(1)}, u32[]{:S(2)}, u32[]{:S(2)}) collective-permute-start(bf16[256,768]{1,0:T(8,128)(2,1)S(1)} %get-tuple-element.126.refs_2_), channel_id=1, source_target_pairs={{0,1},{1,0},{2,3},{3,2},{4,5},{5,4},{6,7},{7,6},{8,9},{9,8},{10,11... | collective-permute-start | bytes 1179656 | tf_op jit(solution)/shard_map/ppermute | solution.py:44
  71.4 1.3 collective-permute-start.15
  75.1 5.5 %collective-permute-done.15.refs_8_ = bf16[2,192,384]{2,1,0:T(8,128)(2,1)S(1)} collective-permute-done((bf16[2,192,384]{2,1,0:T(8,128)(2,1)S(1)}, bf16[2,192,384]{2,1,0:T(8,128)(2,1)S(1)}, u32[]{:S(2)}, u32[]{:S(2)}) %collective-permute-start.15) | collective-permute-done | bytes 294944 | tf_op jit(solution)/shard_map/ppermute | solution.py:44
  80.6 3.8 %shard_map.315 = (f32[256,768]{1,0:T(8,128)S(1)}, bf16[256,768]{1,0:T(8,128)(2,1)S(1)}, f32[256,768]{1,0:T(8,128)S(1)}, f32[256,1]{1,0:T(8,128)S(1)}, bf16[256,1...) custom-call(s32[4]{0:T(128)S(1)} %copy-done.6, ...), custom_call_target="tpu_custom_call" | custom-call | tf_op jit(solution)/shard_map/pallas_call | solution.py:58
  85.3 1.5 shard_map.320
  86.9 4.2 %collective-permute-start.25 = (bf16[256,768]{1,0:T(8,128)(2,1)S(1)}, bf16[256,768]{1,0:T(8,128)(2,1)S(1)}, u32[]{:S(2)}, u32[]{:S(2)}) collective-permute-start(bf16[256,768]{1,0:T(8,128)(2,1)S(1)} %get-tuple-element.133.refs_2_), channel_id=1, source_target_pairs={{0,1},{1,0},{2,3},{3,2},{4,5},{5,4},{6,7},{7,6},{8,9},{9,8},{10,11... | collective-permute-start | bytes 1179656 | tf_op jit(solution)/shard_map/ppermute | solution.py:44
  91.1 1.3 collective-permute-done.25.refs_3_
  92.4 3.7 %shard_map.321 = (f32[256,768]{1,0:T(8,128)S(1)}, bf16[256,768]{1,0:T(8,128)(2,1)S(1)}, f32[256,768]{1,0:T(8,128)S(1)}, f32[8,768]{1,0:T(8,128)S(1)}, bf16[4,144...) custom-call(s32[4]{0:T(128)S(1)} %copy-done.6, ...), custom_call_target="tpu_custom_call" | custom-call | tf_op jit(solution)/shard_map/pallas_call | solution.py:58
  96.6 3.3 %shard_map.322 = (bf16[256,1536]{1,0:T(8,128)(2,1)S(1)}, bf16[256,768]{1,0:T(8,128)(2,1)S(1)}, f32[8,1536]{1,0:T(8,128)S(1)}) custom-call(s32[4]{0:T(128)S(1)} %copy-done.6, bf16[256,768]{1,0:T(8,128)(2,1)S(1)} %get-tuple-element.137.refs_1_, f32[256,1536]{1,0:T(8,128)S(1)} %get-tuple-element.138.refs_2_, bf16[768,1536]{1,0:T(8,128)(2,1)S(1)} %get-tuple-element.139.refs_3_, ...), custom_call_target="tpu_custom_call" | custom-call | tf_op jit(solution)/shard_map/pallas_call | solution.py:58
  100.7 1.7 collective-permute-start.29
  102.4 4.4 %shard_map.323 = (f32[256,768]{1,0:T(8,128)S(1)}, bf16[1152,256]{1,0:T(8,128)(2,1)S(1)}, bf16[256,768]{1,0:T(8,128)(2,1)S(1)}, f32[8,768]{1,0:T(8,128)S(1)}) custom-call(s32[4]{0:T(128)S(1)} %copy-done.6, f32[256,768]{1,0:T(8,128)S(1)} %get-tuple-element.136.refs_1_, bf16[256,768]{1,0:T(8,128)(2,1)S(1)} %get-tuple-element.141.refs_2_, ...), custom_call_target="tpu_custom_call" | custom-call | tf_op jit(solution)/shard_map/pallas_call | solution.py:58
  106.8 1.7 shard_map.324
  110.4 1.4 collective-permute-start.35
  112.8 1.5 shard_map.327.refs_3_
  114.3 1.5 collective-permute-start.30
  116.4 1.7 collective-permute-start.31
  118.2 1.8 shard_map.332
  120.6 5.5 %collective-permute-done.31.refs_6_ = bf16[4,48,384]{2,1,0:T(8,128)(2,1)S(1)} collective-permute-done((bf16[4,48,384]{2,1,0:T(8,128)(2,1)S(1)}, bf16[4,48,384]{2,1,0:T(8,128)(2,1)S(1)}, u32[]{:S(2)}, u32[]{:S(2)}) %collective-permute-start.31) | collective-permute-done | bytes 147488 | tf_op jit(solution)/shard_map/ppermute | solution.py:44
  127.7 2.6 %collective-permute-done.36.refs_5_.refs_3_ = bf16[1056,384]{1,0:T(8,128)(2,1)S(1)} collective-permute-done((bf16[1056,384]{1,0:T(8,128)(2,1)S(1)}, bf16[1056,384]{1,0:T(8,128)(2,1)S(1)}, u32[]{:S(2)}, u32[]{:S(2)}) %collective-permute-start.36) | collective-permute-done | bytes 811040 | tf_op jit(solution)/shard_map/ppermute | solution.py:44
  131.2 1.3 collective-permute-start.38
  135.3 3.1 %collective-permute-done.41.refs_2_ = bf16[2,144,384]{2,1,0:T(8,128)(2,1)S(1)} collective-permute-done((bf16[2,144,384]{2,1,0:T(8,128)(2,1)S(1)}, bf16[2,144,384]{2,1,0:T(8,128)(2,1)S(1)}, u32[]{:S(2)}, u32[]{:S(2)}) %collective-permute-start.41) | collective-permute-done | bytes 221216 | tf_op jit(solution)/shard_map/ppermute | solution.py:44
  139.0 1.8 collective-permute-start.42
  140.8 2.3 %collective-permute-done.39.refs_3_.refs_2_ = bf16[4,192,384]{2,1,0:T(8,128)(2,1)S(1)} collective-permute-done((bf16[4,192,384]{2,1,0:T(8,128)(2,1)S(1)}, bf16[4,192,384]{2,1,0:T(8,128)(2,1)S(1)}, u32[]{:S(2)}, u32[]{:S(2)}) %collective-permute-start.39) | collective-permute-done | bytes 589856 | tf_op jit(solution)/shard_map/ppermute | solution.py:44
  144.5 4.9 %collective-permute-done.37.refs_4_ = bf16[2,192,384]{2,1,0:T(8,128)(2,1)S(1)} collective-permute-done((bf16[2,192,384]{2,1,0:T(8,128)(2,1)S(1)}, bf16[2,192,384]{2,1,0:T(8,128)(2,1)S(1)}, u32[]{:S(2)}, u32[]{:S(2)}) %collective-permute-start.37) | collective-permute-done | bytes 294944 | tf_op jit(solution)/shard_map/ppermute | solution.py:44
  151.2 1.4 collective-permute-start.43
  154.8 3.9 %collective-permute-done.43.refs_2_ = bf16[448,384]{1,0:T(8,128)(2,1)S(1)} collective-permute-done((bf16[448,384]{1,0:T(8,128)(2,1)S(1)}, bf16[448,384]{1,0:T(8,128)(2,1)S(1)}, u32[]{:S(2)}, u32[]{:S(2)}) %collective-permute-start.43) | collective-permute-done | bytes 344096 | tf_op jit(solution)/shard_map/ppermute | solution.py:44
  159.4 1.6 collective-permute-start.44
  164.5 1.4 collective-permute-start.48
  165.9 5.6 %collective-permute-done.44.refs_2_ = bf16[256,384]{1,0:T(8,128)(2,1)S(1)} collective-permute-done((bf16[256,384]{1,0:T(8,128)(2,1)S(1)}, bf16[256,384]{1,0:T(8,128)(2,1)S(1)}, u32[]{:S(2)}, u32[]{:S(2)}) %collective-permute-start.44) | collective-permute-done | bytes 196640 | tf_op jit(solution)/shard_map/ppermute | solution.py:44
  171.5 2.0 %collective-permute-start.49 = (bf16[192,384]{1,0:T(8,128)(2,1)S(1)}, bf16[192,384]{1,0:T(8,128)(2,1)S(1)}, u32[]{:S(2)}, u32[]{:S(2)}) collective-permute-start(bf16[192,384]{1,0:T(8,128)(2,1)S(1)} %get-tuple-element.206), channel_id=1, source_target_pairs={{0,24},{8,16},{16,8},{24,0},{1,25},{9,17},{17,9},{25,1},{2,26},{10... | collective-permute-start | bytes 442376 | tf_op jit(solution)/shard_map/ppermute | solution.py:44
  173.6 1.7 shard_map.338
  175.3 4.8 %collective-permute-start.50 = (f32[32,384]{1,0:T(8,128)S(1)}, f32[32,384]{1,0:T(8,128)S(1)}, u32[]{:S(2)}, u32[]{:S(2)}) collective-permute-start(f32[32,384]{1,0:T(8,128)S(1)} %get-tuple-element.207.refs_1_), channel_id=1, source_target_pairs={{0,1},{1,0},{2,3},{3,2},{4,5},{5,4},{6,7},{7,6},{8,9},{9,8},{10,11... | collective-permute-start | bytes 147464 | tf_op jit(solution)/shard_map/ppermute | solution.py:44
  180.1 1.8 shard_map.330
  181.9 1.6 shard_map.341
  186.6 1.7 shard_map.342
  (135 shorter events, 44.8 us)
Async XLA Ops:
  5.0 8.0 %collective-permute-start.5 = (bf16[192,384]{1,0:T(8,128)(2,1)}, bf16[192,384]{1,0:T(8,128)(2,1)S(1)}, u32[]{:S(2)}, u32[]{:S(2)}) collective-permute-start(bf16[192,384]{1,0:T(8,128)(2,1)} %get-tuple-element.122.refs_1_), channel_id=1, source_target_pairs={{0,24},{8,16},{16,8},{24,0},{1,25},{9,17},{17,9},{25,1},{2,26},{10... | collective-permute-start | bytes 442376 | tf_op jit(solution)/shard_map/ppermute | solution.py:44
  9.2 9.0 %collective-permute-start = (bf16[304,384]{1,0:T(8,128)(2,1)}, bf16[304,384]{1,0:T(8,128)(2,1)S(1)}, u32[]{:S(2)}, u32[]{:S(2)}) collective-permute-start(bf16[304,384]{1,0:T(8,128)(2,1)} %get-tuple-element.119), channel_id=1, source_target_pairs={{0,2},{2,0},{4,6},{6,4},{1,3},{3,1},{5,7},{7,5},{8,10},{10,8},{12,... | collective-permute-start | bytes 700424 | tf_op jit(solution)/shard_map/ppermute | solution.py:44
  10.4 7.8 %collective-permute-start.1 = (bf16[304,384]{1,0:T(8,128)(2,1)}, bf16[304,384]{1,0:T(8,128)(2,1)S(1)}, u32[]{:S(2)}, u32[]{:S(2)}) collective-permute-start(bf16[304,384]{1,0:T(8,128)(2,1)} %get-tuple-element.120), channel_id=1, source_target_pairs={{0,4},{2,6},{4,0},{6,2},{1,5},{3,7},{5,1},{7,3},{8,12},{10,14},{12... | collective-permute-start | bytes 700424 | tf_op jit(solution)/shard_map/ppermute | solution.py:44
  11.6 10.0 %collective-permute-start.2 = (bf16[304,384]{1,0:T(8,128)(2,1)}, bf16[304,384]{1,0:T(8,128)(2,1)S(1)}, u32[]{:S(2)}, u32[]{:S(2)}) collective-permute-start(bf16[304,384]{1,0:T(8,128)(2,1)} %get-tuple-element.121), channel_id=1, source_target_pairs={{0,6},{2,4},{4,2},{6,0},{1,7},{3,5},{5,3},{7,1},{8,14},{10,12},{12... | collective-permute-start | bytes 700424 | tf_op jit(solution)/shard_map/ppermute | solution.py:44
  13.0 5.2 %collective-permute-start.3 = (bf16[192,384]{1,0:T(8,128)(2,1)}, bf16[192,384]{1,0:T(8,128)(2,1)S(1)}, u32[]{:S(2)}, u32[]{:S(2)}) collective-permute-start(bf16[192,384]{1,0:T(8,128)(2,1)} %get-tuple-element.122.refs_1_), channel_id=1, source_target_pairs={{0,16},{8,24},{16,0},{24,8},{1,17},{9,25},{17,1},{25,9},{2,18},{10... | collective-permute-start | bytes 442376 | tf_op jit(solution)/shard_map/ppermute | solution.py:44
  23.8 19.3 %collective-permute-start.7 = (bf16[4,192,384]{2,1,0:T(8,128)(2,1)S(1)}, bf16[4,192,384]{2,1,0:T(8,128)(2,1)S(1)}, u32[]{:S(2)}, u32[]{:S(2)}) collective-permute-start(bf16[4,192,384]{2,1,0:T(8,128)(2,1)S(1)} %shard_map.306.refs_6_), channel_id=1, source_target_pairs={{0,4},{2,6},{4,0},{6,2},{1,5},{3,7},{5,1},{7,3},{8,12},{10,14},{12... | collective-permute-start | bytes 1769480 | tf_op jit(solution)/shard_map/ppermute | solution.py:44
  24.1 19.0 %collective-permute-start.6 = (bf16[4,192,384]{2,1,0:T(8,128)(2,1)S(1)}, bf16[4,192,384]{2,1,0:T(8,128)(2,1)S(1)}, u32[]{:S(2)}, u32[]{:S(2)}) collective-permute-start(bf16[4,192,384]{2,1,0:T(8,128)(2,1)S(1)} %shard_map.306.refs_6_), channel_id=1, source_target_pairs={{0,2},{2,0},{4,6},{6,4},{1,3},{3,1},{5,7},{7,5},{8,10},{10,8},{12,... | collective-permute-start | bytes 1769480 | tf_op jit(solution)/shard_map/ppermute | solution.py:44
  25.9 6.5 %collective-permute-start.11 = (bf16[192,384]{1,0:T(8,128)(2,1)S(1)}, bf16[192,384]{1,0:T(8,128)(2,1)S(1)}, u32[]{:S(2)}, u32[]{:S(2)}) collective-permute-start(bf16[192,384]{1,0:T(8,128)(2,1)S(1)} %shard_map.309.refs_1_), channel_id=1, source_target_pairs={{0,16},{8,24},{16,0},{24,8},{1,17},{9,25},{17,1},{25,9},{2,18},{10... | collective-permute-start | bytes 442376 | tf_op jit(solution)/shard_map/ppermute | solution.py:44
  33.0 8.8 %collective-permute-start.12 = (bf16[2,192,384]{2,1,0:T(8,128)(2,1)S(1)}, bf16[2,192,384]{2,1,0:T(8,128)(2,1)S(1)}, u32[]{:S(2)}, u32[]{:S(2)}) collective-permute-start(bf16[2,192,384]{2,1,0:T(8,128)(2,1)S(1)} %shard_map.310.refs_1_), channel_id=1, source_target_pairs={{0,8},{8,0},{16,24},{24,16},{1,9},{9,1},{17,25},{25,17},{2,10},{10... | collective-permute-start | bytes 884744 | tf_op jit(solution)/shard_map/ppermute | solution.py:44
  33.7 6.7 %collective-permute-start.17 = (bf16[4,48,384]{2,1,0:T(8,128)(2,1)S(1)}, bf16[4,48,384]{2,1,0:T(8,128)(2,1)S(1)}, u32[]{:S(2)}, u32[]{:S(2)}) collective-permute-start(bf16[4,48,384]{2,1,0:T(8,128)(2,1)S(1)} %shard_map.313.refs_1_), channel_id=1, source_target_pairs={{0,16},{8,24},{16,0},{24,8},{1,17},{9,25},{17,1},{25,9},{2,18},{10... | collective-permute-start | bytes 442376 | tf_op jit(solution)/shard_map/ppermute | solution.py:44
  43.0 4.9 %collective-permute-start.19 = (bf16[144,384]{1,0:T(8,128)(2,1)S(1)}, bf16[144,384]{1,0:T(8,128)(2,1)S(1)}, u32[]{:S(2)}, u32[]{:S(2)}) collective-permute-start(bf16[144,384]{1,0:T(8,128)(2,1)S(1)} %shard_map.316.refs_1_), channel_id=1, source_target_pairs={{0,16},{8,24},{16,0},{24,8},{1,17},{9,25},{17,1},{25,9},{2,18},{10... | collective-permute-start | bytes 331784 | tf_op jit(solution)/shard_map/ppermute | solution.py:44
  43.7 11.1 %collective-permute-start.8 = (bf16[2,192,384]{2,1,0:T(8,128)(2,1)S(1)}, bf16[2,192,384]{2,1,0:T(8,128)(2,1)S(1)}, u32[]{:S(2)}, u32[]{:S(2)}) collective-permute-start(bf16[2,192,384]{2,1,0:T(8,128)(2,1)S(1)} %get-tuple-element.123), channel_id=1, source_target_pairs={{0,2},{2,0},{4,6},{6,4},{1,3},{3,1},{5,7},{7,5},{8,10},{10,8},{12,... | collective-permute-start | bytes 884744 | tf_op jit(solution)/shard_map/ppermute | solution.py:44
  44.0 10.7 %collective-permute-start.9 = (bf16[2,192,384]{2,1,0:T(8,128)(2,1)S(1)}, bf16[2,192,384]{2,1,0:T(8,128)(2,1)S(1)}, u32[]{:S(2)}, u32[]{:S(2)}) collective-permute-start(bf16[2,192,384]{2,1,0:T(8,128)(2,1)S(1)} %get-tuple-element.124), channel_id=1, source_target_pairs={{0,4},{2,6},{4,0},{6,2},{1,5},{3,7},{5,1},{7,3},{8,12},{10,14},{12... | collective-permute-start | bytes 884744 | tf_op jit(solution)/shard_map/ppermute | solution.py:44
  44.3 17.4 %collective-permute-start.14 = (bf16[4,192,384]{2,1,0:T(8,128)(2,1)S(1)}, bf16[4,192,384]{2,1,0:T(8,128)(2,1)S(1)}, u32[]{:S(2)}, u32[]{:S(2)}) collective-permute-start(bf16[4,192,384]{2,1,0:T(8,128)(2,1)S(1)} %shard_map.311.refs_5_.refs_2_), channel_id=1, source_target_pairs={{0,4},{2,6},{4,0},{6,2},{1,5},{3,7},{5,1},{7,3},{8,12},{10,14},{12... | collective-permute-start | bytes 1769480 | tf_op jit(solution)/shard_map/ppermute | solution.py:44
  48.4 6.3 %collective-permute-start.20 = (bf16[2,144,384]{2,1,0:T(8,128)(2,1)S(1)}, bf16[2,144,384]{2,1,0:T(8,128)(2,1)S(1)}, u32[]{:S(2)}, u32[]{:S(2)}) collective-permute-start(bf16[2,144,384]{2,1,0:T(8,128)(2,1)S(1)} %shard_map.317.refs_1_), channel_id=1, source_target_pairs={{0,8},{8,0},{16,24},{24,16},{1,9},{9,1},{17,25},{25,17},{2,10},{10... | collective-permute-start | bytes 663560 | tf_op jit(solution)/shard_map/ppermute | solution.py:44
  48.5 22.3 %collective-permute-start.13 = (bf16[4,192,384]{2,1,0:T(8,128)(2,1)S(1)}, bf16[4,192,384]{2,1,0:T(8,128)(2,1)S(1)}, u32[]{:S(2)}, u32[]{:S(2)}) collective-permute-start(bf16[4,192,384]{2,1,0:T(8,128)(2,1)S(1)} %shard_map.311.refs_5_.refs_2_), channel_id=1, source_target_pairs={{0,2},{2,0},{4,6},{6,4},{1,3},{3,1},{5,7},{7,5},{8,10},{10,8},{12,... | collective-permute-start | bytes 1769480 | tf_op jit(solution)/shard_map/ppermute | solution.py:44
  55.4 17.4 %collective-permute-start.22 = (bf16[4,144,384]{2,1,0:T(8,128)(2,1)S(1)}, bf16[4,144,384]{2,1,0:T(8,128)(2,1)S(1)}, u32[]{:S(2)}, u32[]{:S(2)}) collective-permute-start(bf16[4,144,384]{2,1,0:T(8,128)(2,1)S(1)} %shard_map.318.refs_2_), channel_id=1, source_target_pairs={{0,4},{2,6},{4,0},{6,2},{1,5},{3,7},{5,1},{7,3},{8,12},{10,14},{12... | collective-permute-start | bytes 1327112 | tf_op jit(solution)/shard_map/ppermute | solution.py:44
  56.1 17.8 %collective-permute-start.21 = (bf16[4,144,384]{2,1,0:T(8,128)(2,1)S(1)}, bf16[4,144,384]{2,1,0:T(8,128)(2,1)S(1)}, u32[]{:S(2)}, u32[]{:S(2)}) collective-permute-start(bf16[4,144,384]{2,1,0:T(8,128)(2,1)S(1)} %shard_map.318.refs_2_), channel_id=1, source_target_pairs={{0,2},{2,0},{4,6},{6,4},{1,3},{3,1},{5,7},{7,5},{8,10},{10,8},{12,... | collective-permute-start | bytes 1327112 | tf_op jit(solution)/shard_map/ppermute | solution.py:44
  56.5 18.2 %collective-permute-start.18 = (bf16[8,48,384]{2,1,0:T(8,128)(2,1)S(1)}, bf16[8,48,384]{2,1,0:T(8,128)(2,1)S(1)}, u32[]{:S(2)}, u32[]{:S(2)}) collective-permute-start(bf16[8,48,384]{2,1,0:T(8,128)(2,1)S(1)} %shard_map.314.refs_3_.refs_7_), channel_id=1, source_target_pairs={{0,8},{8,0},{16,24},{24,16},{1,9},{9,1},{17,25},{25,17},{2,10},{10... | collective-permute-start | bytes 884744 | tf_op jit(solution)/shard_map/ppermute | solution.py:44
  61.6 19.0 %collective-permute-start.10 = (bf16[256,768]{1,0:T(8,128)(2,1)S(1)}, bf16[256,768]{1,0:T(8,128)(2,1)S(1)}, u32[]{:S(2)}, u32[]{:S(2)}) collective-permute-start(bf16[256,768]{1,0:T(8,128)(2,1)S(1)} %get-tuple-element.126.refs_2_), channel_id=1, source_target_pairs={{0,1},{1,0},{2,3},{3,2},{4,5},{5,4},{6,7},{7,6},{8,9},{9,8},{10,11... | collective-permute-start | bytes 1179656 | tf_op jit(solution)/shard_map/ppermute | solution.py:44
  71.4 9.2 %collective-permute-start.15 = (bf16[2,192,384]{2,1,0:T(8,128)(2,1)S(1)}, bf16[2,192,384]{2,1,0:T(8,128)(2,1)S(1)}, u32[]{:S(2)}, u32[]{:S(2)}) collective-permute-start(bf16[2,192,384]{2,1,0:T(8,128)(2,1)S(1)} %get-tuple-element.127), channel_id=1, source_target_pairs={{0,2},{2,0},{4,6},{6,4},{1,3},{3,1},{5,7},{7,5},{8,10},{10,8},{12,... | collective-permute-start | bytes 884744 | tf_op jit(solution)/shard_map/ppermute | solution.py:44
  72.7 7.9 %collective-permute-start.16 = (bf16[2,192,384]{2,1,0:T(8,128)(2,1)S(1)}, bf16[2,192,384]{2,1,0:T(8,128)(2,1)S(1)}, u32[]{:S(2)}, u32[]{:S(2)}) collective-permute-start(bf16[2,192,384]{2,1,0:T(8,128)(2,1)S(1)} %get-tuple-element.128), channel_id=1, source_target_pairs={{0,4},{2,6},{4,0},{6,2},{1,5},{3,7},{5,1},{7,3},{8,12},{10,14},{12... | collective-permute-start | bytes 884744 | tf_op jit(solution)/shard_map/ppermute | solution.py:44
  74.5 10.8 %collective-permute-start.23 = (bf16[2,144,384]{2,1,0:T(8,128)(2,1)S(1)}, bf16[2,144,384]{2,1,0:T(8,128)(2,1)S(1)}, u32[]{:S(2)}, u32[]{:S(2)}) collective-permute-start(bf16[2,144,384]{2,1,0:T(8,128)(2,1)S(1)} %get-tuple-element.131), channel_id=1, source_target_pairs={{0,2},{2,0},{4,6},{6,4},{1,3},{3,1},{5,7},{7,5},{8,10},{10,8},{12,... | collective-permute-start | bytes 663560 | tf_op jit(solution)/shard_map/ppermute | solution.py:44
  74.6 10.7 %collective-permute-start.24 = (bf16[2,144,384]{2,1,0:T(8,128)(2,1)S(1)}, bf16[2,144,384]{2,1,0:T(8,128)(2,1)S(1)}, u32[]{:S(2)}, u32[]{:S(2)}) collective-permute-start(bf16[2,144,384]{2,1,0:T(8,128)(2,1)S(1)} %get-tuple-element.132), channel_id=1, source_target_pairs={{0,4},{2,6},{4,0},{6,2},{1,5},{3,7},{5,1},{7,3},{8,12},{10,14},{12... | collective-permute-start | bytes 663560 | tf_op jit(solution)/shard_map/ppermute | solution.py:44
  86.9 5.5 %collective-permute-start.25 = (bf16[256,768]{1,0:T(8,128)(2,1)S(1)}, bf16[256,768]{1,0:T(8,128)(2,1)S(1)}, u32[]{:S(2)}, u32[]{:S(2)}) collective-permute-start(bf16[256,768]{1,0:T(8,128)(2,1)S(1)} %get-tuple-element.133.refs_2_), channel_id=1, source_target_pairs={{0,1},{1,0},{2,3},{3,2},{4,5},{5,4},{6,7},{7,6},{8,9},{9,8},{10,11... | collective-permute-start | bytes 1179656 | tf_op jit(solution)/shard_map/ppermute | solution.py:44
  96.1 12.4 %collective-permute-start.27 = (bf16[4,144,384]{2,1,0:T(8,128)(2,1)S(1)}, bf16[4,144,384]{2,1,0:T(8,128)(2,1)S(1)}, u32[]{:S(2)}, u32[]{:S(2)}) collective-permute-start(bf16[4,144,384]{2,1,0:T(8,128)(2,1)S(1)} %get-tuple-element.159), channel_id=1, source_target_pairs={{0,2},{2,0},{4,6},{6,4},{1,3},{3,1},{5,7},{7,5},{8,10},{10,8},{12,... | collective-permute-start | bytes 1327112 | tf_op jit(solution)/shard_map/ppermute | solution.py:44
  96.2 12.3 %collective-permute-start.28 = (bf16[4,144,384]{2,1,0:T(8,128)(2,1)S(1)}, bf16[4,144,384]{2,1,0:T(8,128)(2,1)S(1)}, u32[]{:S(2)}, u32[]{:S(2)}) collective-permute-start(bf16[4,144,384]{2,1,0:T(8,128)(2,1)S(1)} %get-tuple-element.160), channel_id=1, source_target_pairs={{0,4},{2,6},{4,0},{6,2},{1,5},{3,7},{5,1},{7,3},{8,12},{10,14},{12... | collective-permute-start | bytes 1327112 | tf_op jit(solution)/shard_map/ppermute | solution.py:44
  100.7 9.0 %collective-permute-start.29 = (bf16[8,48,384]{2,1,0:T(8,128)(2,1)S(1)}, bf16[8,48,384]{2,1,0:T(8,128)(2,1)S(1)}, u32[]{:S(2)}, u32[]{:S(2)}) collective-permute-start(bf16[8,48,384]{2,1,0:T(8,128)(2,1)S(1)} %get-tuple-element.163), channel_id=1, source_target_pairs={{0,8},{8,0},{16,24},{24,16},{1,9},{9,1},{17,25},{25,17},{2,10},{10... | collective-permute-start | bytes 884744 | tf_op jit(solution)/shard_map/ppermute | solution.py:44
  110.4 20.0 %collective-permute-start.35 = (bf16[1120,384]{1,0:T(8,128)(2,1)S(1)}, bf16[1120,384]{1,0:T(8,128)(2,1)S(1)}, u32[]{:S(2)}, u32[]{:S(2)}) collective-permute-start(bf16[1120,384]{1,0:T(8,128)(2,1)S(1)} %get-tuple-element.164.refs_3_), channel_id=1, source_target_pairs={{0,2},{2,0},{4,6},{6,4},{1,3},{3,1},{5,7},{7,5},{8,10},{10,8},{12,... | collective-permute-start | bytes 2580488 | tf_op jit(solution)/shard_map/ppermute | solution.py:44
  111.8 18.4 %collective-permute-start.36 = (bf16[1056,384]{1,0:T(8,128)(2,1)S(1)}, bf16[1056,384]{1,0:T(8,128)(2,1)S(1)}, u32[]{:S(2)}, u32[]{:S(2)}) collective-permute-start(bf16[1056,384]{1,0:T(8,128)(2,1)S(1)} %get-tuple-element.175), channel_id=1, source_target_pairs={{0,4},{2,6},{4,0},{6,2},{1,5},{3,7},{5,1},{7,3},{8,12},{10,14},{12... | collective-permute-start | bytes 2433032 | tf_op jit(solution)/shard_map/ppermute | solution.py:44
  114.3 12.1 %collective-permute-start.30 = (bf16[256,768]{1,0:T(8,128)(2,1)S(1)}, bf16[256,768]{1,0:T(8,128)(2,1)S(1)}, u32[]{:S(2)}, u32[]{:S(2)}) collective-permute-start(bf16[256,768]{1,0:T(8,128)(2,1)S(1)} %shard_map.327.refs_3_), channel_id=1, source_target_pairs={{0,1},{1,0},{2,3},{3,2},{4,5},{5,4},{6,7},{7,6},{8,9},{9,8},{10,11... | collective-permute-start | bytes 1179656 | tf_op jit(solution)/shard_map/ppermute | solution.py:44
  116.4 9.6 %collective-permute-start.31 = (bf16[4,48,384]{2,1,0:T(8,128)(2,1)S(1)}, bf16[4,48,384]{2,1,0:T(8,128)(2,1)S(1)}, u32[]{:S(2)}, u32[]{:S(2)}) collective-permute-start(bf16[4,48,384]{2,1,0:T(8,128)(2,1)S(1)} %get-tuple-element.167), channel_id=1, source_target_pairs={{0,16},{8,24},{16,0},{24,8},{1,17},{9,25},{17,1},{25,9},{2,18},{10... | collective-permute-start | bytes 442376 | tf_op jit(solution)/shard_map/ppermute | solution.py:44
  119.9 23.2 %collective-permute-start.39 = (bf16[4,192,384]{2,1,0:T(8,128)(2,1)S(1)}, bf16[4,192,384]{2,1,0:T(8,128)(2,1)S(1)}, u32[]{:S(2)}, u32[]{:S(2)}) collective-permute-start(bf16[4,192,384]{2,1,0:T(8,128)(2,1)S(1)} %get-tuple-element.184), channel_id=1, source_target_pairs={{0,2},{2,0},{4,6},{6,4},{1,3},{3,1},{5,7},{7,5},{8,10},{10,8},{12,... | collective-permute-start | bytes 1769480 | tf_op jit(solution)/shard_map/ppermute | solution.py:44
  126.0 17.1 %collective-permute-start.40 = (bf16[4,192,384]{2,1,0:T(8,128)(2,1)S(1)}, bf16[4,192,384]{2,1,0:T(8,128)(2,1)S(1)}, u32[]{:S(2)}, u32[]{:S(2)}) collective-permute-start(bf16[4,192,384]{2,1,0:T(8,128)(2,1)S(1)} %get-tuple-element.185), channel_id=1, source_target_pairs={{0,4},{2,6},{4,0},{6,2},{1,5},{3,7},{5,1},{7,3},{8,12},{10,14},{12... | collective-permute-start | bytes 1769480 | tf_op jit(solution)/shard_map/ppermute | solution.py:44
  131.2 19.0 %collective-permute-start.38 = (bf16[448,384]{1,0:T(8,128)(2,1)S(1)}, bf16[448,384]{1,0:T(8,128)(2,1)S(1)}, u32[]{:S(2)}, u32[]{:S(2)}) collective-permute-start(bf16[448,384]{1,0:T(8,128)(2,1)S(1)} %get-tuple-element.179.refs_6_), channel_id=1, source_target_pairs={{0,4},{2,6},{4,0},{6,2},{1,5},{3,7},{5,1},{7,3},{8,12},{10,14},{12... | collective-permute-start | bytes 1032200 | tf_op jit(solution)/shard_map/ppermute | solution.py:44
  133.2 5.1 %collective-permute-start.41 = (bf16[2,144,384]{2,1,0:T(8,128)(2,1)S(1)}, bf16[2,144,384]{2,1,0:T(8,128)(2,1)S(1)}, u32[]{:S(2)}, u32[]{:S(2)}) collective-permute-start(bf16[2,144,384]{2,1,0:T(8,128)(2,1)S(1)} %get-tuple-element.188), channel_id=1, source_target_pairs={{0,8},{8,0},{16,24},{24,16},{1,9},{9,1},{17,25},{25,17},{2,10},{10... | collective-permute-start | bytes 663560 | tf_op jit(solution)/shard_map/ppermute | solution.py:44
  134.4 15.0 %collective-permute-start.37 = (bf16[2,192,384]{2,1,0:T(8,128)(2,1)S(1)}, bf16[2,192,384]{2,1,0:T(8,128)(2,1)S(1)}, u32[]{:S(2)}, u32[]{:S(2)}) collective-permute-start(bf16[2,192,384]{2,1,0:T(8,128)(2,1)S(1)} %get-tuple-element.178), channel_id=1, source_target_pairs={{0,2},{2,0},{4,6},{6,4},{1,3},{3,1},{5,7},{7,5},{8,10},{10,8},{12,... | collective-permute-start | bytes 884744 | tf_op jit(solution)/shard_map/ppermute | solution.py:44
  151.2 7.6 %collective-permute-start.43 = (bf16[448,384]{1,0:T(8,128)(2,1)S(1)}, bf16[448,384]{1,0:T(8,128)(2,1)S(1)}, u32[]{:S(2)}, u32[]{:S(2)}) collective-permute-start(bf16[448,384]{1,0:T(8,128)(2,1)S(1)} %get-tuple-element.193), channel_id=1, source_target_pairs={{0,8},{8,0},{16,24},{24,16},{1,9},{9,1},{17,25},{25,17},{2,10},{10... | collective-permute-start | bytes 1032200 | tf_op jit(solution)/shard_map/ppermute | solution.py:44
  152.6 9.5 %collective-permute-start.45 = (bf16[2,192,384]{2,1,0:T(8,128)(2,1)S(1)}, bf16[2,192,384]{2,1,0:T(8,128)(2,1)S(1)}, u32[]{:S(2)}, u32[]{:S(2)}) collective-permute-start(bf16[2,192,384]{2,1,0:T(8,128)(2,1)S(1)} %get-tuple-element.190.refs_7_), channel_id=1, source_target_pairs={{0,2},{2,0},{4,6},{6,4},{1,3},{3,1},{5,7},{7,5},{8,10},{10,8},{12,... | collective-permute-start | bytes 884744 | tf_op jit(solution)/shard_map/ppermute | solution.py:44
  152.9 9.7 %collective-permute-start.46 = (bf16[2,192,384]{2,1,0:T(8,128)(2,1)S(1)}, bf16[2,192,384]{2,1,0:T(8,128)(2,1)S(1)}, u32[]{:S(2)}, u32[]{:S(2)}) collective-permute-start(bf16[2,192,384]{2,1,0:T(8,128)(2,1)S(1)} %get-tuple-element.191.refs_8_), channel_id=1, source_target_pairs={{0,4},{2,6},{4,0},{6,2},{1,5},{3,7},{5,1},{7,3},{8,12},{10,14},{12... | collective-permute-start | bytes 884744 | tf_op jit(solution)/shard_map/ppermute | solution.py:44
  153.9 10.5 %collective-permute-start.32 = (bf16[304,384]{1,0:T(8,128)(2,1)S(1)}, bf16[304,384]{1,0:T(8,128)(2,1)S(1)}, u32[]{:S(2)}, u32[]{:S(2)}) collective-permute-start(bf16[304,384]{1,0:T(8,128)(2,1)S(1)} %get-tuple-element.169), channel_id=1, source_target_pairs={{0,2},{2,0},{4,6},{6,4},{1,3},{3,1},{5,7},{7,5},{8,10},{10,8},{12,... | collective-permute-start | bytes 700424 | tf_op jit(solution)/shard_map/ppermute | solution.py:44
  159.4 12.1 %collective-permute-start.44 = (bf16[256,384]{1,0:T(8,128)(2,1)S(1)}, bf16[256,384]{1,0:T(8,128)(2,1)S(1)}, u32[]{:S(2)}, u32[]{:S(2)}) collective-permute-start(bf16[256,384]{1,0:T(8,128)(2,1)S(1)} %get-tuple-element.195), channel_id=1, source_target_pairs={{0,16},{8,24},{16,0},{24,8},{1,17},{9,25},{17,1},{25,9},{2,18},{10... | collective-permute-start | bytes 589832 | tf_op jit(solution)/shard_map/ppermute | solution.py:44
  160.9 14.4 %collective-permute-start.33 = (bf16[304,384]{1,0:T(8,128)(2,1)S(1)}, bf16[304,384]{1,0:T(8,128)(2,1)S(1)}, u32[]{:S(2)}, u32[]{:S(2)}) collective-permute-start(bf16[304,384]{1,0:T(8,128)(2,1)S(1)} %get-tuple-element.170), channel_id=1, source_target_pairs={{0,4},{2,6},{4,0},{6,2},{1,5},{3,7},{5,1},{7,3},{8,12},{10,14},{12... | collective-permute-start | bytes 700424 | tf_op jit(solution)/shard_map/ppermute | solution.py:44
  162.2 18.0 %collective-permute-start.34 = (bf16[304,384]{1,0:T(8,128)(2,1)S(1)}, bf16[304,384]{1,0:T(8,128)(2,1)S(1)}, u32[]{:S(2)}, u32[]{:S(2)}) collective-permute-start(bf16[304,384]{1,0:T(8,128)(2,1)S(1)} %get-tuple-element.171), channel_id=1, source_target_pairs={{0,6},{2,4},{4,2},{6,0},{1,7},{3,5},{5,3},{7,1},{8,14},{10,12},{12... | collective-permute-start | bytes 700424 | tf_op jit(solution)/shard_map/ppermute | solution.py:44
  163.6 21.2 %collective-permute-start.47 = (bf16[192,384]{1,0:T(8,128)(2,1)S(1)}, bf16[192,384]{1,0:T(8,128)(2,1)S(1)}, u32[]{:S(2)}, u32[]{:S(2)}) collective-permute-start(bf16[192,384]{1,0:T(8,128)(2,1)S(1)} %get-tuple-element.204), channel_id=1, source_target_pairs={{0,16},{8,24},{16,0},{24,8},{1,17},{9,25},{17,1},{25,9},{2,18},{10... | collective-permute-start | bytes 442376 | tf_op jit(solution)/shard_map/ppermute | solution.py:44
  164.5 20.3 %collective-permute-start.48 = (bf16[192,384]{1,0:T(8,128)(2,1)S(1)}, bf16[192,384]{1,0:T(8,128)(2,1)S(1)}, u32[]{:S(2)}, u32[]{:S(2)}) collective-permute-start(bf16[192,384]{1,0:T(8,128)(2,1)S(1)} %get-tuple-element.205), channel_id=1, source_target_pairs={{0,8},{8,0},{16,24},{24,16},{1,9},{9,1},{17,25},{25,17},{2,10},{10... | collective-permute-start | bytes 442376 | tf_op jit(solution)/shard_map/ppermute | solution.py:44
  171.5 13.3 %collective-permute-start.49 = (bf16[192,384]{1,0:T(8,128)(2,1)S(1)}, bf16[192,384]{1,0:T(8,128)(2,1)S(1)}, u32[]{:S(2)}, u32[]{:S(2)}) collective-permute-start(bf16[192,384]{1,0:T(8,128)(2,1)S(1)} %get-tuple-element.206), channel_id=1, source_target_pairs={{0,24},{8,16},{16,8},{24,0},{1,25},{9,17},{17,9},{25,1},{2,26},{10... | collective-permute-start | bytes 442376 | tf_op jit(solution)/shard_map/ppermute | solution.py:44
  175.3 8.3 %collective-permute-start.50 = (f32[32,384]{1,0:T(8,128)S(1)}, f32[32,384]{1,0:T(8,128)S(1)}, u32[]{:S(2)}, u32[]{:S(2)}) collective-permute-start(f32[32,384]{1,0:T(8,128)S(1)} %get-tuple-element.207.refs_1_), channel_id=1, source_target_pairs={{0,1},{1,0},{2,3},{3,2},{4,5},{5,4},{6,7},{7,6},{8,9},{9,8},{10,11... | collective-permute-start | bytes 147464 | tf_op jit(solution)/shard_map/ppermute | solution.py:44
  (24 other events, 338.7 us)

commit v5 on v4

--- a/solution.py
+++ b/solution.py
@@ -401,10 +401,7 @@
                 else:
                     cross[z, r] = grad[start : start + S, :]
     hand_out(where, room, handed)
-    for k, mask in enumerate([0, 2]):
-        rows = slice(k * ROWS, (k + 1) * ROWS)
-        cross_own[rows] = cross[where[1] ^ mask]
-        cross_send[rows] = cross[where[1] ^ mask ^ 1]
+    hand_cross(where, cross, cross_own, cross_send)
 
 
 def hidden_back_kernel(where, low, slope, wd, wu, grad_pre, part, sums, back):
@@ -423,13 +420,22 @@
     part[...] = dot(grad_pre[...], wu[...], NT).astype(BF16)
 
 
+def hand_cross(where, cross, own, send):
+    for k, mask in enumerate([0, 2]):
+        rows = slice(k * ROWS, (k + 1) * ROWS)
+        own[rows] = cross[where[1] ^ mask]
+        send[rows] = cross[where[1] ^ mask ^ 1]
+
+
 def up_grad_kernel(where, low, grad_pre, *refs):
-    handed, room = refs[:5], refs[5]
+    handed, (cross_own, cross_send, room, cross) = refs[:5], refs[5:]
     for z in range(QUADS):
         grad = dot(low[...], grad_pre[:, z * COLS : (z + 1) * COLS], TN).astype(BF16)
         for r in range(ROWS):
-            room[r, z] = grad[r * W : (r + 1) * W, :]
+            room[r, z] = grad[r * W : r * W + PART[0], :]
+            cross[z, r] = grad[r * W + PART[0] : (r + 1) * W, :]
     hand_out(where, room, handed)
+    hand_cross(where, cross, cross_own, cross_send)
 
 
 def first_norm_kernel(
@@ -531,8 +537,8 @@
 
 def token_sum_kernel(where, result, grad_one, p0, p1, *refs):
     total, room = refs[-2:]
-    cross = [*refs[:2], refs[6]] if len(refs) > 6 else []
-    outs = refs[2:6] if cross else refs[:4]
+    count = (len(refs) - 6) // 3
+    sums, outs, owns = refs[: 2 * count], refs[2 * count : 2 * count + 4], refs[2 * count + 4 : -2]
 
     def body(i):
         at = strip(i)
@@ -544,12 +550,11 @@
     for m, out in enumerate(outs):
         row = where[0] ^ m
         out[0:LEN, :] = room[row]
-        if cross:
-            kept, got, own = cross
-            sums = kept[row] + got[row].astype(F32)
-            out[LEN:, :] = sums.astype(BF16)
+        for i, own in enumerate(owns):
+            block = sums[2 * i][row] + sums[2 * i + 1][row].astype(F32)
+            out[LEN + i * S : LEN + (i + 1) * S, :] = block.astype(BF16)
             if m == 0:
-                own[...] = sums
+                own[...] = block
 
 
 def token_out_kernel(where, t0, t1, t2, t3, result, total):
@@ -691,8 +696,15 @@
         out[...] = value
 
 
-def up_adam_kernel(where, kept, r2, r1, r3, w, f, s, *outs):
+def sum_rows(own, r1, r2, r3, start):
+    rows = slice(start, start + S)
+    far = r2[rows, :].astype(F32) + r3[rows, :].astype(F32)
+    return (own[...] + r1[rows, :].astype(F32)) + far
+
+
+def up_adam_kernel(where, kept, r2, r1, r3, own, c1, c2, c3, w, f, s, *outs):
     grad = (kept[...] + r1[...].astype(F32)) + (r2[...].astype(F32) + r3[...].astype(F32))
+    grad = jnp.concatenate([grad, sum_rows(own, c1, c2, c3, LEN + S)], axis=0)
     for q in range(3):
         at = (pl.ds(q, W, stride=3), slice(None))
         cut = grad[:, q * 128 : (q + 1) * 128]
@@ -701,8 +713,7 @@
 
 
 def down_adam_kernel(where, kept, got, own, r1, r2, r3, w, f, s, *outs):
-    far = r2[LEN:, :].astype(F32) + r3[LEN:, :].astype(F32)
-    cross = (own[...] + r1[LEN:, :].astype(F32)) + far
+    cross = sum_rows(own, r1, r2, r3, LEN)
     most = kept[...] + got[...].astype(F32)
     for q in range(4):
         at = (slice(None), slice(q * COLS, (q + 1) * COLS))
@@ -923,13 +934,18 @@
         [pltpu.VMEM((LEN, FFC), F32)],
     )
     third_passed = scatter_pass(where, third_handed, third_got)
-    second_handed = run(
+    rooms = [
+        pltpu.VMEM((ROWS, QUADS) + PART, BF16),
+        pltpu.VMEM((QUADS, ROWS) + CROSS, BF16),
+    ]
+    out = run(
         up_grad_kernel,
         where,
         [hidden_low, grad_pre],
-        HANDED,
-        [pltpu.VMEM((ROWS, QUADS) + CHUNK, BF16)],
-    )
+        handed_shapes(PART) + [PLANES] * 2,
+        rooms,
+    )
+    second_handed, cross_up = out[:5], out[5:]
     grad_one, grad_mixed, low, sums_one = run(
         first_norm_kernel,
         where,
@@ -978,21 +994,22 @@
     def sums(dims, split):
         return [shape(*dims, dtype=F32), shape(*split)]
 
+    cross_sum = []
     if direct:
         plane = (ROWS,) + CROSS
-        cross = run(cross_far_kernel, where, cross[:1] + cross_got, sums(plane, plane))
-        cross_sum = [cross[0], swap(cross[1], "dp", 2)]
-    else:
-        cross_sum = []
+        for own, got in [(cross[0], cross_got[0]), (cross_up[0], swap(cross_up[1], "dp", 1))]:
+            near = run(cross_far_kernel, where, [own, got], sums(plane, plane))
+            cross_sum += [near[0], swap(near[1], "dp", 2)]
     (part,) = run(
-        token_back_kernel, where, [grad_mixed, wj], [shape(LEN, D)], after=first_handed[:1]
-    )
-    own = [shape(*CROSS, dtype=F32)] if direct else []
+        token_back_kernel, where, [grad_mixed, wj], [shape(LEN, D)], after=first_got
+    )
+    other = swap(part, "col", 1)
+    own = [shape(*CROSS, dtype=F32)] * 2 if direct else []
     pieces = run(
         token_sum_kernel,
         where,
-        [result, grad_one, part, swap(part, "col", 1)] + cross_sum,
-        blocks_out + own,
+        [result, grad_one, part, other] + cross_sum,
+        [shape(LEN + 2 * S if direct else LEN, 2 * W)] * ROWS + own,
         [pltpu.VMEM((LEN, D), F32), pltpu.VMEM((ROWS, LEN, 2 * W), BF16)],
     )
     first_passed = run(
@@ -1000,7 +1017,7 @@
         where,
         first_handed[2:4] + first_handed[:1] + first_got,
         [PAIR, shape(*CARRIED)],
-        after=pieces[:1],
+        after=cross_sum[1:2],
     )
     first_last = scatter_second(first_passed)
 
@@ -1017,7 +1034,7 @@
         got = swap(third_sum[1], "dp", 1)
         third_sum = run(far_line_kernel, where, [third_sum[0], got], sums(PART, PART))
         third_sum[1] = swap(third_sum[1], "dp", 2)
-        ready = third_sum[1:] + pieces[:1]
+        ready = third_sum[1:] + cross_sum[3:4]
     else:
         ready = pieces[:1]
     second_got = scatter_first(second_handed)
@@ -1035,8 +1052,8 @@
         line_kernel,
         where,
         second_handed[-1:] + second_got + second_last,
-        sums(CHUNK, CHUNK) + [shape(*CHUNK)] * 2 if direct else wide,
-        lines,
+        sums(PART, PART) + [shape(*PART)] * 2 if direct else [shape(4, *PART, dtype=F32)],
+        [pltpu.VMEM((4,) + PART, F32)],
     )
     if direct:
         got = swap(first_sum[1], "dp", 1)
@@ -1074,19 +1091,24 @@
 
     if direct:
         down_new = run(
-            down_adam_kernel, where, third_sum + pieces[ROWS:] + got[1:] + down, like(down)
+            down_adam_kernel, where, third_sum + pieces[ROWS : ROWS + 1] + got[1:] + down, like(down)
         )
         vector_new = step_vectors(vector)
+        rows_got = pieces[ROWS + 1 :] + got[1:]
         got = [swap(v, "dp", mask) for v, mask in zip(second_sum[1:], ORDER[1:])]
         after = out[:1] + vector_new[:1] + down_new[:1]
-        up_new = run(up_adam_kernel, where, second_sum[:1] + got + up, like(up), after=after)
+        up_new = run(up_adam_kernel, where, second_sum[:1] + got + rows_got + up, like(up), after=after)
         up_new = [v.reshape(up_weight.shape) for v in up_new]
     else:
-        kept, sent = [v.reshape(2, ROWS, *CROSS) for v in cross]
-        cross = jnp.stack([kept, sent], axis=1).reshape(QUADS, ROWS, *CROSS)
-        cross = lax.psum_scatter(cross.astype(F32), "row", scatter_dimension=1)
-        third = jnp.concatenate([third_sum[0], cross], axis=1)
-        grads = wide_sums(first_sum[0], second_sum[0], third)
+
+        def sum_cross(pair):
+            kept, sent = [v.reshape(2, ROWS, *CROSS) for v in pair]
+            both = jnp.stack([kept, sent], axis=1).reshape(QUADS, ROWS, *CROSS)
+            return lax.psum_scatter(both.astype(F32), "row", scatter_dimension=1)
+
+        second = jnp.concatenate([second_sum[0], sum_cross(cross_up)], axis=1)
+        third = jnp.concatenate([third_sum[0], sum_cross(cross)], axis=1)
+        grads = wide_sums(first_sum[0], second, third)
         joint_new = adamw(*joint, grads[0], JOINT_RATE, DECAY)
         output_new = adamw(*output, grads[1], OUTPUT_RATE, DECAY)
         up_new = adamw(*up, grads[2][:, None], JOINT_RATE, DECAY)

time: 189 us -> 190 us (level); the launches traced: 188 us -> 187 us
  waiting for transfers between devices: 66.4 us -> 55.8 us
  starting transfers between devices: 62.8 us -> 71.2 us
    ppermute x51 -> x53, waiting for transfers between devices: 66.4 us -> 55.8 us  [swap(): return lax.ppermute(value, axis, [(i, i ^ mask) for i in range(n)])]
    ppermute x51 -> x53, starting transfers between devices: 62.8 us -> 71.2 us  [swap(): return lax.ppermute(value, axis, [(i, i ^ mask) for i in range(n)])]
    pallas_call x38 -> x39, Pallas kernels: 53.2 us -> 53.7 us  [run(): pl.pallas_call(body, out_shape=outs, in_specs=[pl.BlockSpec(memory_space=...]
  transfers between devices with their start and end apart: 51 -> 53, of which waited for: 23 -> 21; matrix products, arithmetic and copies ran while one was open for 0% -> 0% of each run, Pallas kernels for 22% -> 23%
where the time goes in v5:
time: 190 us; the launch traced here: 187 us
  starting transfers between devices  71.2 us (37%)
  waiting for transfers between devices  55.8 us (29%)
  Pallas kernels  53.7 us (28%)
  local copies, waits for them, and re-layouts  3.38 us (2%)
    ppermute x53, starting transfers between devices, swap(): return lax.ppermute(value, axis, [(i, i ^ mask) for i in range(n)])  71.2 us
    ppermute x53, waiting for transfers between devices, swap(): return lax.ppermute(value, axis, [(i, i ^ mask) for i in range(n)])  55.8 us
    pallas_call x39, Pallas kernels, run(): pl.pallas_call(body, out_shape=outs, in_specs=[pl.BlockSpec(memory_space=...  53.7 us
  transfers between devices with their start and end apart: 53, of which 21 were waited for; matrix products, arithmetic and copies ran while one was open for 0% of the time, Pallas kernels for 23%

profile of v5, /device:TPU:1, one launch (start us, length us, event | category | flops | bytes accessed | tf_op | source)
XLA Modules:
  0.0 186.6 jit_solution(14064355842476993706)
XLA Ops:
  1.9 3.0 %shard_map.305 = (bf16[304,384]{1,0:T(8,128)(2,1)}, bf16[304,384]{1,0:T(8,128)(2,1)}, bf16[304,384]{1,0:T(8,128)(2,1)}, bf16[304,384]{1,0:T(8,128)(2,1)}, bf16[192,384]{1,0:T(8,128)(2,1)}) custom-call(s32[4]{0:T(128)} %pad_add_fusion.refs_0_, bf16[4,128,384]{2,1,0:T(8,128)(2,1)} %bitcast.89, bf16[4,128,384]{2,1,0:T(8,128)(2,1)} %bitcast.90, ...), custom_call_target="tpu_custom_call" | custom-call | tf_op jit(solution)/shard_map/pallas_call | solution.py:58
  5.0 4.2 %collective-permute-start.5 = (bf16[192,384]{1,0:T(8,128)(2,1)}, bf16[192,384]{1,0:T(8,128)(2,1)S(1)}, u32[]{:S(2)}, u32[]{:S(2)}) collective-permute-start(bf16[192,384]{1,0:T(8,128)(2,1)} %get-tuple-element.127.refs_1_), channel_id=1, source_target_pairs={{0,24},{8,16},{16,8},{24,0},{1,25},{9,17},{17,9},{25,1},{2,26},{10... | collective-permute-start | bytes 442376 | tf_op jit(solution)/shard_map/ppermute | solution.py:44
  10.4 1.2 collective-permute-start.1
  13.0 1.5 collective-permute-start.3
  14.5 1.8 collective-permute-done.4.refs_3_
  16.3 1.9 %collective-permute-done.3.refs_2_ = bf16[192,384]{1,0:T(8,128)(2,1)S(1)} collective-permute-done((bf16[192,384]{1,0:T(8,128)(2,1)}, bf16[192,384]{1,0:T(8,128)(2,1)S(1)}, u32[]{:S(2)}, u32[]{:S(2)}) %collective-permute-start.3) | collective-permute-done | bytes 147488 | tf_op jit(solution)/shard_map/ppermute | solution.py:44
  18.2 3.4 %collective-permute-done.2.refs_7_.refs_4_ = bf16[304,384]{1,0:T(8,128)(2,1)S(1)} collective-permute-done((bf16[304,384]{1,0:T(8,128)(2,1)}, bf16[304,384]{1,0:T(8,128)(2,1)S(1)}, u32[]{:S(2)}, u32[]{:S(2)}) %collective-permute-start.2) | collective-permute-done | bytes 233504 | tf_op jit(solution)/shard_map/ppermute | solution.py:44
  26.3 6.1 %collective-permute-done.11.refs_2_ = bf16[192,384]{1,0:T(8,128)(2,1)S(1)} collective-permute-done((bf16[192,384]{1,0:T(8,128)(2,1)S(1)}, bf16[192,384]{1,0:T(8,128)(2,1)S(1)}, u32[]{:S(2)}, u32[]{:S(2)}) %collective-permute-start.11) | collective-permute-done | bytes 147488 | tf_op jit(solution)/shard_map/ppermute | solution.py:44
  33.7 1.6 collective-permute-start.17
  35.2 5.1 %collective-permute-done.17.refs_2_ = bf16[4,48,384]{2,1,0:T(8,128)(2,1)S(1)} collective-permute-done((bf16[4,48,384]{2,1,0:T(8,128)(2,1)S(1)}, bf16[4,48,384]{2,1,0:T(8,128)(2,1)S(1)}, u32[]{:S(2)}, u32[]{:S(2)}) %collective-permute-start.17) | collective-permute-done | bytes 147488 | tf_op jit(solution)/shard_map/ppermute | solution.py:44
  45.5 2.4 %collective-permute-done.19.refs_2_ = bf16[144,384]{1,0:T(8,128)(2,1)S(1)} collective-permute-done((bf16[144,384]{1,0:T(8,128)(2,1)S(1)}, bf16[144,384]{1,0:T(8,128)(2,1)S(1)}, u32[]{:S(2)}, u32[]{:S(2)}) %collective-permute-start.19) | collective-permute-done | bytes 110624 | tf_op jit(solution)/shard_map/ppermute | solution.py:44
  49.1 5.7 %collective-permute-done.20.refs_2_ = bf16[2,144,384]{2,1,0:T(8,128)(2,1)S(1)} collective-permute-done((bf16[2,144,384]{2,1,0:T(8,128)(2,1)S(1)}, bf16[2,144,384]{2,1,0:T(8,128)(2,1)S(1)}, u32[]{:S(2)}, u32[]{:S(2)}) %collective-permute-start.20) | collective-permute-done | bytes 221216 | tf_op jit(solution)/shard_map/ppermute | solution.py:44
  56.5 5.2 %shard_map.308 = (bf16[256,768]{1,0:T(8,128)(2,1)S(1)}, bf16[256,768]{1,0:T(8,128)(2,1)S(1)}, bf16[4,1152,192]{2,1,0:T(8,128)(2,1)S(1)}, bf16[768,384]{1,0:T(8,1...) custom-call(s32[4]{0:T(128)S(1)} %copy-done.5, ...), custom_call_target="tpu_custom_call" | custom-call | tf_op jit(solution)/shard_map/pallas_call | solution.py:58
  61.6 9.2 %collective-permute-start.10 = (bf16[256,768]{1,0:T(8,128)(2,1)S(1)}, bf16[256,768]{1,0:T(8,128)(2,1)S(1)}, u32[]{:S(2)}, u32[]{:S(2)}) collective-permute-start(bf16[256,768]{1,0:T(8,128)(2,1)S(1)} %get-tuple-element.131.refs_2_), channel_id=1, source_target_pairs={{0,1},{1,0},{2,3},{3,2},{4,5},{5,4},{6,7},{7,6},{8,9},{9,8},{10,11... | collective-permute-start | bytes 1179656 | tf_op jit(solution)/shard_map/ppermute | solution.py:44
  71.4 1.3 collective-permute-start.15
  75.1 5.5 %collective-permute-done.15.refs_8_ = bf16[2,192,384]{2,1,0:T(8,128)(2,1)S(1)} collective-permute-done((bf16[2,192,384]{2,1,0:T(8,128)(2,1)S(1)}, bf16[2,192,384]{2,1,0:T(8,128)(2,1)S(1)}, u32[]{:S(2)}, u32[]{:S(2)}) %collective-permute-start.15) | collective-permute-done | bytes 294944 | tf_op jit(solution)/shard_map/ppermute | solution.py:44
  80.6 3.8 %shard_map.315 = (f32[256,768]{1,0:T(8,128)S(1)}, bf16[256,768]{1,0:T(8,128)(2,1)S(1)}, f32[256,768]{1,0:T(8,128)S(1)}, f32[256,1]{1,0:T(8,128)S(1)}, bf16[256,1...) custom-call(s32[4]{0:T(128)S(1)} %copy-done.5, ...), custom_call_target="tpu_custom_call" | custom-call | tf_op jit(solution)/shard_map/pallas_call | solution.py:58
  85.3 1.5 shard_map.320
  86.9 4.2 %collective-permute-start.25 = (bf16[256,768]{1,0:T(8,128)(2,1)S(1)}, bf16[256,768]{1,0:T(8,128)(2,1)S(1)}, u32[]{:S(2)}, u32[]{:S(2)}) collective-permute-start(bf16[256,768]{1,0:T(8,128)(2,1)S(1)} %get-tuple-element.138.refs_2_), channel_id=1, source_target_pairs={{0,1},{1,0},{2,3},{3,2},{4,5},{5,4},{6,7},{7,6},{8,9},{9,8},{10,11... | collective-permute-start | bytes 1179656 | tf_op jit(solution)/shard_map/ppermute | solution.py:44
  91.1 1.3 collective-permute-done.25.refs_3_
  92.4 3.7 %shard_map.321 = (f32[256,768]{1,0:T(8,128)S(1)}, bf16[256,768]{1,0:T(8,128)(2,1)S(1)}, f32[256,768]{1,0:T(8,128)S(1)}, f32[8,768]{1,0:T(8,128)S(1)}, bf16[4,144...) custom-call(s32[4]{0:T(128)S(1)} %copy-done.5, ...), custom_call_target="tpu_custom_call" | custom-call | tf_op jit(solution)/shard_map/pallas_call | solution.py:58
  96.6 3.3 %shard_map.322 = (bf16[256,1536]{1,0:T(8,128)(2,1)S(1)}, bf16[256,768]{1,0:T(8,128)(2,1)S(1)}, f32[8,1536]{1,0:T(8,128)S(1)}) custom-call(s32[4]{0:T(128)S(1)} %copy-done.5, bf16[256,768]{1,0:T(8,128)(2,1)S(1)} %get-tuple-element.142.refs_1_, f32[256,1536]{1,0:T(8,128)S(1)} %get-tuple-element.143.refs_2_, bf16[768,1536]{1,0:T(8,128)(2,1)S(1)} %get-tuple-element.144.refs_3_, ...), custom_call_target="tpu_custom_call" | custom-call | tf_op jit(solution)/shard_map/pallas_call | solution.py:58
  100.7 1.7 collective-permute-start.29
  102.4 4.4 %shard_map.323 = (f32[256,768]{1,0:T(8,128)S(1)}, bf16[1152,256]{1,0:T(8,128)(2,1)S(1)}, bf16[256,768]{1,0:T(8,128)(2,1)S(1)}, f32[8,768]{1,0:T(8,128)S(1)}) custom-call(s32[4]{0:T(128)S(1)} %copy-done.5, f32[256,768]{1,0:T(8,128)S(1)} %get-tuple-element.141.refs_1_, bf16[256,768]{1,0:T(8,128)(2,1)S(1)} %get-tuple-element.146.refs_2_, ...), custom_call_target="tpu_custom_call" | custom-call | tf_op jit(solution)/shard_map/pallas_call | solution.py:58
  106.8 1.7 shard_map.324
  110.4 1.3 collective-permute-start.31
  112.8 1.7 shard_map.329
  117.7 6.1 %collective-permute-done.34.refs_2_ = bf16[8,48,384]{2,1,0:T(8,128)(2,1)S(1)} collective-permute-done((bf16[8,48,384]{2,1,0:T(8,128)(2,1)S(1)}, bf16[8,48,384]{2,1,0:T(8,128)(2,1)S(1)}, u32[]{:S(2)}, u32[]{:S(2)}) %collective-permute-start.34) | collective-permute-done | bytes 294944 | tf_op jit(solution)/shard_map/ppermute | solution.py:44
  124.9 4.5 %collective-permute-done.31.refs_4_.refs_5_.refs_3_ = bf16[1056,384]{1,0:T(8,128)(2,1)S(1)} collective-permute-done((bf16[1056,384]{1,0:T(8,128)(2,1)S(1)}, bf16[1056,384]{1,0:T(8,128)(2,1)S(1)}, u32[]{:S(2)}, u32[]{:S(2)}) %collective-permute-start.31) | collective-permute-done | bytes 811040 | tf_op jit(solution)/shard_map/ppermute | solution.py:44
  129.4 1.7 collective-permute-start.35
  134.4 1.6 collective-permute-done.35.refs_8_.refs_6_
  137.1 1.5 shard_map.327.refs_3_
  138.6 1.6 collective-permute-done.43.refs_2_
  140.2 2.1 %collective-permute-start.32 = (bf16[256,768]{1,0:T(8,128)(2,1)S(1)}, bf16[256,768]{1,0:T(8,128)(2,1)S(1)}, u32[]{:S(2)}, u32[]{:S(2)}) collective-permute-start(bf16[256,768]{1,0:T(8,128)(2,1)S(1)} %shard_map.327.refs_3_), channel_id=1, source_target_pairs={{0,1},{1,0},{2,3},{3,2},{4,5},{5,4},{6,7},{7,6},{8,9},{9,8},{10,11... | collective-permute-start | bytes 1179656 | tf_op jit(solution)/shard_map/ppermute | solution.py:44
  142.9 1.8 collective-permute-start.44
  144.7 2.7 %collective-permute-done.44.refs_5_.refs_2_ = bf16[144,384]{1,0:T(8,128)(2,1)S(1)} collective-permute-done((bf16[144,384]{1,0:T(8,128)(2,1)S(1)}, bf16[144,384]{1,0:T(8,128)(2,1)S(1)}, u32[]{:S(2)}, u32[]{:S(2)}) %collective-permute-start.44) | collective-permute-done | bytes 110624 | tf_op jit(solution)/shard_map/ppermute | solution.py:44
  149.0 1.6 collective-permute-start.45
  151.3 1.2 shard_map.331
  153.4 4.0 %collective-permute-start.48 = (bf16[2,144,384]{2,1,0:T(8,128)(2,1)S(1)}, bf16[2,144,384]{2,1,0:T(8,128)(2,1)S(1)}, u32[]{:S(2)}, u32[]{:S(2)}) collective-permute-start(bf16[2,144,384]{2,1,0:T(8,128)(2,1)S(1)} %get-tuple-element.200.refs_8_), channel_id=1, source_target_pairs={{0,4},{2,6},{4,0},{6,2},{1,5},{3,7},{5,1},{7,3},{8,12},{10,14},{12... | collective-permute-start | bytes 663560 | tf_op jit(solution)/shard_map/ppermute | solution.py:44
  158.1 2.2 %collective-permute-start.46 = (bf16[256,384]{1,0:T(8,128)(2,1)S(1)}, bf16[256,384]{1,0:T(8,128)(2,1)S(1)}, u32[]{:S(2)}, u32[]{:S(2)}) collective-permute-start(bf16[256,384]{1,0:T(8,128)(2,1)S(1)} %get-tuple-element.204), channel_id=1, source_target_pairs={{0,16},{8,24},{16,0},{24,8},{1,17},{9,25},{17,1},{25,9},{2,18},{10... | collective-permute-start | bytes 589832 | tf_op jit(solution)/shard_map/ppermute | solution.py:44
  160.3 4.2 %collective-permute-start.38 = (bf16[352,384]{1,0:T(8,128)(2,1)S(1)}, bf16[352,384]{1,0:T(8,128)(2,1)S(1)}, u32[]{:S(2)}, u32[]{:S(2)}) collective-permute-start(bf16[352,384]{1,0:T(8,128)(2,1)S(1)} %get-tuple-element.183), channel_id=1, source_target_pairs={{0,6},{2,4},{4,2},{6,0},{1,7},{3,5},{5,3},{7,1},{8,14},{10,12},{12... | collective-permute-start | bytes 811016 | tf_op jit(solution)/shard_map/ppermute | solution.py:44
  165.2 2.0 %collective-permute-start.49 = (bf16[144,384]{1,0:T(8,128)(2,1)S(1)}, bf16[144,384]{1,0:T(8,128)(2,1)S(1)}, u32[]{:S(2)}, u32[]{:S(2)}) collective-permute-start(bf16[144,384]{1,0:T(8,128)(2,1)S(1)} %get-tuple-element.213), channel_id=1, source_target_pairs={{0,16},{8,24},{16,0},{24,8},{1,17},{9,25},{17,1},{25,9},{2,18},{10... | collective-permute-start | bytes 331784 | tf_op jit(solution)/shard_map/ppermute | solution.py:44
  168.6 2.0 %collective-permute-start.51 = (bf16[144,384]{1,0:T(8,128)(2,1)S(1)}, bf16[144,384]{1,0:T(8,128)(2,1)S(1)}, u32[]{:S(2)}, u32[]{:S(2)}) collective-permute-start(bf16[144,384]{1,0:T(8,128)(2,1)S(1)} %get-tuple-element.215), channel_id=1, source_target_pairs={{0,24},{8,16},{16,8},{24,0},{1,25},{9,17},{17,9},{25,1},{2,26},{10... | collective-permute-start | bytes 331784 | tf_op jit(solution)/shard_map/ppermute | solution.py:44
  170.8 1.7 shard_map.339
  173.6 4.9 %collective-permute-start.52 = (f32[32,384]{1,0:T(8,128)S(1)}, f32[32,384]{1,0:T(8,128)S(1)}, u32[]{:S(2)}, u32[]{:S(2)}) collective-permute-start(f32[32,384]{1,0:T(8,128)S(1)} %get-tuple-element.217.refs_1_), channel_id=1, source_target_pairs={{0,1},{1,0},{2,3},{3,2},{4,5},{5,4},{6,7},{7,6},{8,9},{9,8},{10,11... | collective-permute-start | bytes 147464 | tf_op jit(solution)/shard_map/ppermute | solution.py:44
  178.5 1.8 shard_map.332
  180.3 1.6 shard_map.342
  184.9 1.7 shard_map.343
  (140 shorter events, 44.4 us)
Async XLA Ops:
  5.0 8.0 %collective-permute-start.5 = (bf16[192,384]{1,0:T(8,128)(2,1)}, bf16[192,384]{1,0:T(8,128)(2,1)S(1)}, u32[]{:S(2)}, u32[]{:S(2)}) collective-permute-start(bf16[192,384]{1,0:T(8,128)(2,1)} %get-tuple-element.127.refs_1_), channel_id=1, source_target_pairs={{0,24},{8,16},{16,8},{24,0},{1,25},{9,17},{17,9},{25,1},{2,26},{10... | collective-permute-start | bytes 442376 | tf_op jit(solution)/shard_map/ppermute | solution.py:44
  9.2 9.0 %collective-permute-start = (bf16[304,384]{1,0:T(8,128)(2,1)}, bf16[304,384]{1,0:T(8,128)(2,1)S(1)}, u32[]{:S(2)}, u32[]{:S(2)}) collective-permute-start(bf16[304,384]{1,0:T(8,128)(2,1)} %get-tuple-element.124), channel_id=1, source_target_pairs={{0,2},{2,0},{4,6},{6,4},{1,3},{3,1},{5,7},{7,5},{8,10},{10,8},{12,... | collective-permute-start | bytes 700424 | tf_op jit(solution)/shard_map/ppermute | solution.py:44
  10.4 7.8 %collective-permute-start.1 = (bf16[304,384]{1,0:T(8,128)(2,1)}, bf16[304,384]{1,0:T(8,128)(2,1)S(1)}, u32[]{:S(2)}, u32[]{:S(2)}) collective-permute-start(bf16[304,384]{1,0:T(8,128)(2,1)} %get-tuple-element.125), channel_id=1, source_target_pairs={{0,4},{2,6},{4,0},{6,2},{1,5},{3,7},{5,1},{7,3},{8,12},{10,14},{12... | collective-permute-start | bytes 700424 | tf_op jit(solution)/shard_map/ppermute | solution.py:44
  11.6 10.0 %collective-permute-start.2 = (bf16[304,384]{1,0:T(8,128)(2,1)}, bf16[304,384]{1,0:T(8,128)(2,1)S(1)}, u32[]{:S(2)}, u32[]{:S(2)}) collective-permute-start(bf16[304,384]{1,0:T(8,128)(2,1)} %get-tuple-element.126), channel_id=1, source_target_pairs={{0,6},{2,4},{4,2},{6,0},{1,7},{3,5},{5,3},{7,1},{8,14},{10,12},{12... | collective-permute-start | bytes 700424 | tf_op jit(solution)/shard_map/ppermute | solution.py:44
  23.8 19.3 %collective-permute-start.7 = (bf16[4,192,384]{2,1,0:T(8,128)(2,1)S(1)}, bf16[4,192,384]{2,1,0:T(8,128)(2,1)S(1)}, u32[]{:S(2)}, u32[]{:S(2)}) collective-permute-start(bf16[4,192,384]{2,1,0:T(8,128)(2,1)S(1)} %shard_map.306.refs_6_), channel_id=1, source_target_pairs={{0,4},{2,6},{4,0},{6,2},{1,5},{3,7},{5,1},{7,3},{8,12},{10,14},{12... | collective-permute-start | bytes 1769480 | tf_op jit(solution)/shard_map/ppermute | solution.py:44
  24.1 19.0 %collective-permute-start.6 = (bf16[4,192,384]{2,1,0:T(8,128)(2,1)S(1)}, bf16[4,192,384]{2,1,0:T(8,128)(2,1)S(1)}, u32[]{:S(2)}, u32[]{:S(2)}) collective-permute-start(bf16[4,192,384]{2,1,0:T(8,128)(2,1)S(1)} %shard_map.306.refs_6_), channel_id=1, source_target_pairs={{0,2},{2,0},{4,6},{6,4},{1,3},{3,1},{5,7},{7,5},{8,10},{10,8},{12,... | collective-permute-start | bytes 1769480 | tf_op jit(solution)/shard_map/ppermute | solution.py:44
  25.9 6.5 %collective-permute-start.11 = (bf16[192,384]{1,0:T(8,128)(2,1)S(1)}, bf16[192,384]{1,0:T(8,128)(2,1)S(1)}, u32[]{:S(2)}, u32[]{:S(2)}) collective-permute-start(bf16[192,384]{1,0:T(8,128)(2,1)S(1)} %shard_map.309.refs_1_), channel_id=1, source_target_pairs={{0,16},{8,24},{16,0},{24,8},{1,17},{9,25},{17,1},{25,9},{2,18},{10... | collective-permute-start | bytes 442376 | tf_op jit(solution)/shard_map/ppermute | solution.py:44
  33.0 8.8 %collective-permute-start.12 = (bf16[2,192,384]{2,1,0:T(8,128)(2,1)S(1)}, bf16[2,192,384]{2,1,0:T(8,128)(2,1)S(1)}, u32[]{:S(2)}, u32[]{:S(2)}) collective-permute-start(bf16[2,192,384]{2,1,0:T(8,128)(2,1)S(1)} %shard_map.310.refs_1_), channel_id=1, source_target_pairs={{0,8},{8,0},{16,24},{24,16},{1,9},{9,1},{17,25},{25,17},{2,10},{10... | collective-permute-start | bytes 884744 | tf_op jit(solution)/shard_map/ppermute | solution.py:44
  33.7 6.7 %collective-permute-start.17 = (bf16[4,48,384]{2,1,0:T(8,128)(2,1)S(1)}, bf16[4,48,384]{2,1,0:T(8,128)(2,1)S(1)}, u32[]{:S(2)}, u32[]{:S(2)}) collective-permute-start(bf16[4,48,384]{2,1,0:T(8,128)(2,1)S(1)} %shard_map.313.refs_1_), channel_id=1, source_target_pairs={{0,16},{8,24},{16,0},{24,8},{1,17},{9,25},{17,1},{25,9},{2,18},{10... | collective-permute-start | bytes 442376 | tf_op jit(solution)/shard_map/ppermute | solution.py:44
  43.7 11.1 %collective-permute-start.8 = (bf16[2,192,384]{2,1,0:T(8,128)(2,1)S(1)}, bf16[2,192,384]{2,1,0:T(8,128)(2,1)S(1)}, u32[]{:S(2)}, u32[]{:S(2)}) collective-permute-start(bf16[2,192,384]{2,1,0:T(8,128)(2,1)S(1)} %get-tuple-element.128), channel_id=1, source_target_pairs={{0,2},{2,0},{4,6},{6,4},{1,3},{3,1},{5,7},{7,5},{8,10},{10,8},{12,... | collective-permute-start | bytes 884744 | tf_op jit(solution)/shard_map/ppermute | solution.py:44
  44.0 10.7 %collective-permute-start.9 = (bf16[2,192,384]{2,1,0:T(8,128)(2,1)S(1)}, bf16[2,192,384]{2,1,0:T(8,128)(2,1)S(1)}, u32[]{:S(2)}, u32[]{:S(2)}) collective-permute-start(bf16[2,192,384]{2,1,0:T(8,128)(2,1)S(1)} %get-tuple-element.129), channel_id=1, source_target_pairs={{0,4},{2,6},{4,0},{6,2},{1,5},{3,7},{5,1},{7,3},{8,12},{10,14},{12... | collective-permute-start | bytes 884744 | tf_op jit(solution)/shard_map/ppermute | solution.py:44
  44.3 17.4 %collective-permute-start.14 = (bf16[4,192,384]{2,1,0:T(8,128)(2,1)S(1)}, bf16[4,192,384]{2,1,0:T(8,128)(2,1)S(1)}, u32[]{:S(2)}, u32[]{:S(2)}) collective-permute-start(bf16[4,192,384]{2,1,0:T(8,128)(2,1)S(1)} %shard_map.311.refs_5_.refs_2_), channel_id=1, source_target_pairs={{0,4},{2,6},{4,0},{6,2},{1,5},{3,7},{5,1},{7,3},{8,12},{10,14},{12... | collective-permute-start | bytes 1769480 | tf_op jit(solution)/shard_map/ppermute | solution.py:44
  48.4 6.3 %collective-permute-start.20 = (bf16[2,144,384]{2,1,0:T(8,128)(2,1)S(1)}, bf16[2,144,384]{2,1,0:T(8,128)(2,1)S(1)}, u32[]{:S(2)}, u32[]{:S(2)}) collective-permute-start(bf16[2,144,384]{2,1,0:T(8,128)(2,1)S(1)} %shard_map.317.refs_1_), channel_id=1, source_target_pairs={{0,8},{8,0},{16,24},{24,16},{1,9},{9,1},{17,25},{25,17},{2,10},{10... | collective-permute-start | bytes 663560 | tf_op jit(solution)/shard_map/ppermute | solution.py:44
  48.5 22.3 %collective-permute-start.13 = (bf16[4,192,384]{2,1,0:T(8,128)(2,1)S(1)}, bf16[4,192,384]{2,1,0:T(8,128)(2,1)S(1)}, u32[]{:S(2)}, u32[]{:S(2)}) collective-permute-start(bf16[4,192,384]{2,1,0:T(8,128)(2,1)S(1)} %shard_map.311.refs_5_.refs_2_), channel_id=1, source_target_pairs={{0,2},{2,0},{4,6},{6,4},{1,3},{3,1},{5,7},{7,5},{8,10},{10,8},{12,... | collective-permute-start | bytes 1769480 | tf_op jit(solution)/shard_map/ppermute | solution.py:44
  55.4 17.4 %collective-permute-start.22 = (bf16[4,144,384]{2,1,0:T(8,128)(2,1)S(1)}, bf16[4,144,384]{2,1,0:T(8,128)(2,1)S(1)}, u32[]{:S(2)}, u32[]{:S(2)}) collective-permute-start(bf16[4,144,384]{2,1,0:T(8,128)(2,1)S(1)} %shard_map.318.refs_2_), channel_id=1, source_target_pairs={{0,4},{2,6},{4,0},{6,2},{1,5},{3,7},{5,1},{7,3},{8,12},{10,14},{12... | collective-permute-start | bytes 1327112 | tf_op jit(solution)/shard_map/ppermute | solution.py:44
  56.1 17.8 %collective-permute-start.21 = (bf16[4,144,384]{2,1,0:T(8,128)(2,1)S(1)}, bf16[4,144,384]{2,1,0:T(8,128)(2,1)S(1)}, u32[]{:S(2)}, u32[]{:S(2)}) collective-permute-start(bf16[4,144,384]{2,1,0:T(8,128)(2,1)S(1)} %shard_map.318.refs_2_), channel_id=1, source_target_pairs={{0,2},{2,0},{4,6},{6,4},{1,3},{3,1},{5,7},{7,5},{8,10},{10,8},{12,... | collective-permute-start | bytes 1327112 | tf_op jit(solution)/shard_map/ppermute | solution.py:44
  56.5 18.2 %collective-permute-start.18 = (bf16[8,48,384]{2,1,0:T(8,128)(2,1)S(1)}, bf16[8,48,384]{2,1,0:T(8,128)(2,1)S(1)}, u32[]{:S(2)}, u32[]{:S(2)}) collective-permute-start(bf16[8,48,384]{2,1,0:T(8,128)(2,1)S(1)} %shard_map.314.refs_3_.refs_7_), channel_id=1, source_target_pairs={{0,8},{8,0},{16,24},{24,16},{1,9},{9,1},{17,25},{25,17},{2,10},{10... | collective-permute-start | bytes 884744 | tf_op jit(solution)/shard_map/ppermute | solution.py:44
  61.6 19.0 %collective-permute-start.10 = (bf16[256,768]{1,0:T(8,128)(2,1)S(1)}, bf16[256,768]{1,0:T(8,128)(2,1)S(1)}, u32[]{:S(2)}, u32[]{:S(2)}) collective-permute-start(bf16[256,768]{1,0:T(8,128)(2,1)S(1)} %get-tuple-element.131.refs_2_), channel_id=1, source_target_pairs={{0,1},{1,0},{2,3},{3,2},{4,5},{5,4},{6,7},{7,6},{8,9},{9,8},{10,11... | collective-permute-start | bytes 1179656 | tf_op jit(solution)/shard_map/ppermute | solution.py:44
  71.4 9.2 %collective-permute-start.15 = (bf16[2,192,384]{2,1,0:T(8,128)(2,1)S(1)}, bf16[2,192,384]{2,1,0:T(8,128)(2,1)S(1)}, u32[]{:S(2)}, u32[]{:S(2)}) collective-permute-start(bf16[2,192,384]{2,1,0:T(8,128)(2,1)S(1)} %get-tuple-element.132), channel_id=1, source_target_pairs={{0,2},{2,0},{4,6},{6,4},{1,3},{3,1},{5,7},{7,5},{8,10},{10,8},{12,... | collective-permute-start | bytes 884744 | tf_op jit(solution)/shard_map/ppermute | solution.py:44
  72.7 7.9 %collective-permute-start.16 = (bf16[2,192,384]{2,1,0:T(8,128)(2,1)S(1)}, bf16[2,192,384]{2,1,0:T(8,128)(2,1)S(1)}, u32[]{:S(2)}, u32[]{:S(2)}) collective-permute-start(bf16[2,192,384]{2,1,0:T(8,128)(2,1)S(1)} %get-tuple-element.133), channel_id=1, source_target_pairs={{0,4},{2,6},{4,0},{6,2},{1,5},{3,7},{5,1},{7,3},{8,12},{10,14},{12... | collective-permute-start | bytes 884744 | tf_op jit(solution)/shard_map/ppermute | solution.py:44
  74.5 10.8 %collective-permute-start.23 = (bf16[2,144,384]{2,1,0:T(8,128)(2,1)S(1)}, bf16[2,144,384]{2,1,0:T(8,128)(2,1)S(1)}, u32[]{:S(2)}, u32[]{:S(2)}) collective-permute-start(bf16[2,144,384]{2,1,0:T(8,128)(2,1)S(1)} %get-tuple-element.136), channel_id=1, source_target_pairs={{0,2},{2,0},{4,6},{6,4},{1,3},{3,1},{5,7},{7,5},{8,10},{10,8},{12,... | collective-permute-start | bytes 663560 | tf_op jit(solution)/shard_map/ppermute | solution.py:44
  74.6 10.7 %collective-permute-start.24 = (bf16[2,144,384]{2,1,0:T(8,128)(2,1)S(1)}, bf16[2,144,384]{2,1,0:T(8,128)(2,1)S(1)}, u32[]{:S(2)}, u32[]{:S(2)}) collective-permute-start(bf16[2,144,384]{2,1,0:T(8,128)(2,1)S(1)} %get-tuple-element.137), channel_id=1, source_target_pairs={{0,4},{2,6},{4,0},{6,2},{1,5},{3,7},{5,1},{7,3},{8,12},{10,14},{12... | collective-permute-start | bytes 663560 | tf_op jit(solution)/shard_map/ppermute | solution.py:44
  86.9 5.5 %collective-permute-start.25 = (bf16[256,768]{1,0:T(8,128)(2,1)S(1)}, bf16[256,768]{1,0:T(8,128)(2,1)S(1)}, u32[]{:S(2)}, u32[]{:S(2)}) collective-permute-start(bf16[256,768]{1,0:T(8,128)(2,1)S(1)} %get-tuple-element.138.refs_2_), channel_id=1, source_target_pairs={{0,1},{1,0},{2,3},{3,2},{4,5},{5,4},{6,7},{7,6},{8,9},{9,8},{10,11... | collective-permute-start | bytes 1179656 | tf_op jit(solution)/shard_map/ppermute | solution.py:44
  96.1 12.4 %collective-permute-start.27 = (bf16[4,144,384]{2,1,0:T(8,128)(2,1)S(1)}, bf16[4,144,384]{2,1,0:T(8,128)(2,1)S(1)}, u32[]{:S(2)}, u32[]{:S(2)}) collective-permute-start(bf16[4,144,384]{2,1,0:T(8,128)(2,1)S(1)} %get-tuple-element.164), channel_id=1, source_target_pairs={{0,2},{2,0},{4,6},{6,4},{1,3},{3,1},{5,7},{7,5},{8,10},{10,8},{12,... | collective-permute-start | bytes 1327112 | tf_op jit(solution)/shard_map/ppermute | solution.py:44
  96.2 12.3 %collective-permute-start.28 = (bf16[4,144,384]{2,1,0:T(8,128)(2,1)S(1)}, bf16[4,144,384]{2,1,0:T(8,128)(2,1)S(1)}, u32[]{:S(2)}, u32[]{:S(2)}) collective-permute-start(bf16[4,144,384]{2,1,0:T(8,128)(2,1)S(1)} %get-tuple-element.165), channel_id=1, source_target_pairs={{0,4},{2,6},{4,0},{6,2},{1,5},{3,7},{5,1},{7,3},{8,12},{10,14},{12... | collective-permute-start | bytes 1327112 | tf_op jit(solution)/shard_map/ppermute | solution.py:44
  100.7 9.0 %collective-permute-start.29 = (bf16[8,48,384]{2,1,0:T(8,128)(2,1)S(1)}, bf16[8,48,384]{2,1,0:T(8,128)(2,1)S(1)}, u32[]{:S(2)}, u32[]{:S(2)}) collective-permute-start(bf16[8,48,384]{2,1,0:T(8,128)(2,1)S(1)} %get-tuple-element.168), channel_id=1, source_target_pairs={{0,8},{8,0},{16,24},{24,16},{1,9},{9,1},{17,25},{25,17},{2,10},{10... | collective-permute-start | bytes 884744 | tf_op jit(solution)/shard_map/ppermute | solution.py:44
  110.4 19.0 %collective-permute-start.31 = (bf16[1056,384]{1,0:T(8,128)(2,1)S(1)}, bf16[1056,384]{1,0:T(8,128)(2,1)S(1)}, u32[]{:S(2)}, u32[]{:S(2)}) collective-permute-start(bf16[1056,384]{1,0:T(8,128)(2,1)S(1)} %get-tuple-element.170), channel_id=1, source_target_pairs={{0,4},{2,6},{4,0},{6,2},{1,5},{3,7},{5,1},{7,3},{8,12},{10,14},{12... | collective-permute-start | bytes 2433032 | tf_op jit(solution)/shard_map/ppermute | solution.py:44
  111.7 19.7 %collective-permute-start.30 = (bf16[1120,384]{1,0:T(8,128)(2,1)S(1)}, bf16[1120,384]{1,0:T(8,128)(2,1)S(1)}, u32[]{:S(2)}, u32[]{:S(2)}) collective-permute-start(bf16[1120,384]{1,0:T(8,128)(2,1)S(1)} %get-tuple-element.169.refs_3_), channel_id=1, source_target_pairs={{0,2},{2,0},{4,6},{6,4},{1,3},{3,1},{5,7},{7,5},{8,10},{10,8},{12,... | collective-permute-start | bytes 2580488 | tf_op jit(solution)/shard_map/ppermute | solution.py:44
  114.6 9.2 %collective-permute-start.34 = (bf16[8,48,384]{2,1,0:T(8,128)(2,1)S(1)}, bf16[8,48,384]{2,1,0:T(8,128)(2,1)S(1)}, u32[]{:S(2)}, u32[]{:S(2)}) collective-permute-start(bf16[8,48,384]{2,1,0:T(8,128)(2,1)S(1)} %get-tuple-element.177), channel_id=1, source_target_pairs={{0,8},{8,0},{16,24},{24,16},{1,9},{9,1},{17,25},{25,17},{2,10},{10... | collective-permute-start | bytes 884744 | tf_op jit(solution)/shard_map/ppermute | solution.py:44
  115.7 27.2 %collective-permute-start.41 = (bf16[4,144,384]{2,1,0:T(8,128)(2,1)S(1)}, bf16[4,144,384]{2,1,0:T(8,128)(2,1)S(1)}, u32[]{:S(2)}, u32[]{:S(2)}) collective-permute-start(bf16[4,144,384]{2,1,0:T(8,128)(2,1)S(1)} %get-tuple-element.193), channel_id=1, source_target_pairs={{0,2},{2,0},{4,6},{6,4},{1,3},{3,1},{5,7},{7,5},{8,10},{10,8},{12,... | collective-permute-start | bytes 1327112 | tf_op jit(solution)/shard_map/ppermute | solution.py:44
  116.9 16.4 %collective-permute-start.33 = (bf16[4,48,384]{2,1,0:T(8,128)(2,1)S(1)}, bf16[4,48,384]{2,1,0:T(8,128)(2,1)S(1)}, u32[]{:S(2)}, u32[]{:S(2)}) collective-permute-start(bf16[4,48,384]{2,1,0:T(8,128)(2,1)S(1)} %get-tuple-element.173), channel_id=1, source_target_pairs={{0,16},{8,24},{16,0},{24,8},{1,17},{9,25},{17,1},{25,9},{2,18},{10... | collective-permute-start | bytes 442376 | tf_op jit(solution)/shard_map/ppermute | solution.py:44
  123.8 20.9 %collective-permute-start.42 = (bf16[4,144,384]{2,1,0:T(8,128)(2,1)S(1)}, bf16[4,144,384]{2,1,0:T(8,128)(2,1)S(1)}, u32[]{:S(2)}, u32[]{:S(2)}) collective-permute-start(bf16[4,144,384]{2,1,0:T(8,128)(2,1)S(1)} %get-tuple-element.194), channel_id=1, source_target_pairs={{0,4},{2,6},{4,0},{6,2},{1,5},{3,7},{5,1},{7,3},{8,12},{10,14},{12... | collective-permute-start | bytes 1327112 | tf_op jit(solution)/shard_map/ppermute | solution.py:44
  129.4 6.6 %collective-permute-start.35 = (bf16[4,48,384]{2,1,0:T(8,128)(2,1)S(1)}, bf16[4,48,384]{2,1,0:T(8,128)(2,1)S(1)}, u32[]{:S(2)}, u32[]{:S(2)}) collective-permute-start(bf16[4,48,384]{2,1,0:T(8,128)(2,1)S(1)} %get-tuple-element.179), channel_id=1, source_target_pairs={{0,16},{8,24},{16,0},{24,8},{1,17},{9,25},{17,1},{25,9},{2,18},{10... | collective-permute-start | bytes 442376 | tf_op jit(solution)/shard_map/ppermute | solution.py:44
  132.2 8.0 %collective-permute-start.43 = (bf16[2,144,384]{2,1,0:T(8,128)(2,1)S(1)}, bf16[2,144,384]{2,1,0:T(8,128)(2,1)S(1)}, u32[]{:S(2)}, u32[]{:S(2)}) collective-permute-start(bf16[2,144,384]{2,1,0:T(8,128)(2,1)S(1)} %get-tuple-element.197), channel_id=1, source_target_pairs={{0,8},{8,0},{16,24},{24,16},{1,9},{9,1},{17,25},{25,17},{2,10},{10... | collective-permute-start | bytes 663560 | tf_op jit(solution)/shard_map/ppermute | solution.py:44
  134.1 14.1 %collective-permute-start.40 = (bf16[448,384]{1,0:T(8,128)(2,1)S(1)}, bf16[448,384]{1,0:T(8,128)(2,1)S(1)}, u32[]{:S(2)}, u32[]{:S(2)}) collective-permute-start(bf16[448,384]{1,0:T(8,128)(2,1)S(1)} %get-tuple-element.190.refs_6_), channel_id=1, source_target_pairs={{0,4},{2,6},{4,0},{6,2},{1,5},{3,7},{5,1},{7,3},{8,12},{10,14},{12... | collective-permute-start | bytes 1032200 | tf_op jit(solution)/shard_map/ppermute | solution.py:44
  136.0 12.1 %collective-permute-start.39 = (bf16[2,192,384]{2,1,0:T(8,128)(2,1)S(1)}, bf16[2,192,384]{2,1,0:T(8,128)(2,1)S(1)}, u32[]{:S(2)}, u32[]{:S(2)}) collective-permute-start(bf16[2,192,384]{2,1,0:T(8,128)(2,1)S(1)} %get-tuple-element.189), channel_id=1, source_target_pairs={{0,2},{2,0},{4,6},{6,4},{1,3},{3,1},{5,7},{7,5},{8,10},{10,8},{12,... | collective-permute-start | bytes 884744 | tf_op jit(solution)/shard_map/ppermute | solution.py:44
  140.2 11.0 %collective-permute-start.32 = (bf16[256,768]{1,0:T(8,128)(2,1)S(1)}, bf16[256,768]{1,0:T(8,128)(2,1)S(1)}, u32[]{:S(2)}, u32[]{:S(2)}) collective-permute-start(bf16[256,768]{1,0:T(8,128)(2,1)S(1)} %shard_map.327.refs_3_), channel_id=1, source_target_pairs={{0,1},{1,0},{2,3},{3,2},{4,5},{5,4},{6,7},{7,6},{8,9},{9,8},{10,11... | collective-permute-start | bytes 1179656 | tf_op jit(solution)/shard_map/ppermute | solution.py:44
  149.0 8.4 %collective-permute-start.45 = (bf16[448,384]{1,0:T(8,128)(2,1)S(1)}, bf16[448,384]{1,0:T(8,128)(2,1)S(1)}, u32[]{:S(2)}, u32[]{:S(2)}) collective-permute-start(bf16[448,384]{1,0:T(8,128)(2,1)S(1)} %get-tuple-element.202), channel_id=1, source_target_pairs={{0,8},{8,0},{16,24},{24,16},{1,9},{9,1},{17,25},{25,17},{2,10},{10... | collective-permute-start | bytes 1032200 | tf_op jit(solution)/shard_map/ppermute | solution.py:44
  150.6 9.6 %collective-permute-start.47 = (bf16[2,144,384]{2,1,0:T(8,128)(2,1)S(1)}, bf16[2,144,384]{2,1,0:T(8,128)(2,1)S(1)}, u32[]{:S(2)}, u32[]{:S(2)}) collective-permute-start(bf16[2,144,384]{2,1,0:T(8,128)(2,1)S(1)} %get-tuple-element.199.refs_7_), channel_id=1, source_target_pairs={{0,2},{2,0},{4,6},{6,4},{1,3},{3,1},{5,7},{7,5},{8,10},{10,8},{12,... | collective-permute-start | bytes 663560 | tf_op jit(solution)/shard_map/ppermute | solution.py:44
  152.5 14.7 %collective-permute-start.36 = (bf16[352,384]{1,0:T(8,128)(2,1)S(1)}, bf16[352,384]{1,0:T(8,128)(2,1)S(1)}, u32[]{:S(2)}, u32[]{:S(2)}) collective-permute-start(bf16[352,384]{1,0:T(8,128)(2,1)S(1)} %get-tuple-element.181), channel_id=1, source_target_pairs={{0,2},{2,0},{4,6},{6,4},{1,3},{3,1},{5,7},{7,5},{8,10},{10,8},{12,... | collective-permute-start | bytes 811016 | tf_op jit(solution)/shard_map/ppermute | solution.py:44
  153.4 11.0 %collective-permute-start.48 = (bf16[2,144,384]{2,1,0:T(8,128)(2,1)S(1)}, bf16[2,144,384]{2,1,0:T(8,128)(2,1)S(1)}, u32[]{:S(2)}, u32[]{:S(2)}) collective-permute-start(bf16[2,144,384]{2,1,0:T(8,128)(2,1)S(1)} %get-tuple-element.200.refs_8_), channel_id=1, source_target_pairs={{0,4},{2,6},{4,0},{6,2},{1,5},{3,7},{5,1},{7,3},{8,12},{10,14},{12... | collective-permute-start | bytes 663560 | tf_op jit(solution)/shard_map/ppermute | solution.py:44
  157.4 16.2 %collective-permute-start.37 = (bf16[352,384]{1,0:T(8,128)(2,1)S(1)}, bf16[352,384]{1,0:T(8,128)(2,1)S(1)}, u32[]{:S(2)}, u32[]{:S(2)}) collective-permute-start(bf16[352,384]{1,0:T(8,128)(2,1)S(1)} %get-tuple-element.182), channel_id=1, source_target_pairs={{0,4},{2,6},{4,0},{6,2},{1,5},{3,7},{5,1},{7,3},{8,12},{10,14},{12... | collective-permute-start | bytes 811016 | tf_op jit(solution)/shard_map/ppermute | solution.py:44
  158.1 10.5 %collective-permute-start.46 = (bf16[256,384]{1,0:T(8,128)(2,1)S(1)}, bf16[256,384]{1,0:T(8,128)(2,1)S(1)}, u32[]{:S(2)}, u32[]{:S(2)}) collective-permute-start(bf16[256,384]{1,0:T(8,128)(2,1)S(1)} %get-tuple-element.204), channel_id=1, source_target_pairs={{0,16},{8,24},{16,0},{24,8},{1,17},{9,25},{17,1},{25,9},{2,18},{10... | collective-permute-start | bytes 589832 | tf_op jit(solution)/shard_map/ppermute | solution.py:44
  160.3 18.2 %collective-permute-start.38 = (bf16[352,384]{1,0:T(8,128)(2,1)S(1)}, bf16[352,384]{1,0:T(8,128)(2,1)S(1)}, u32[]{:S(2)}, u32[]{:S(2)}) collective-permute-start(bf16[352,384]{1,0:T(8,128)(2,1)S(1)} %get-tuple-element.183), channel_id=1, source_target_pairs={{0,6},{2,4},{4,2},{6,0},{1,7},{3,5},{5,3},{7,1},{8,14},{10,12},{12... | collective-permute-start | bytes 811016 | tf_op jit(solution)/shard_map/ppermute | solution.py:44
  165.2 17.9 %collective-permute-start.49 = (bf16[144,384]{1,0:T(8,128)(2,1)S(1)}, bf16[144,384]{1,0:T(8,128)(2,1)S(1)}, u32[]{:S(2)}, u32[]{:S(2)}) collective-permute-start(bf16[144,384]{1,0:T(8,128)(2,1)S(1)} %get-tuple-element.213), channel_id=1, source_target_pairs={{0,16},{8,24},{16,0},{24,8},{1,17},{9,25},{17,1},{25,9},{2,18},{10... | collective-permute-start | bytes 331784 | tf_op jit(solution)/shard_map/ppermute | solution.py:44
  167.2 16.0 %collective-permute-start.50 = (bf16[144,384]{1,0:T(8,128)(2,1)S(1)}, bf16[144,384]{1,0:T(8,128)(2,1)S(1)}, u32[]{:S(2)}, u32[]{:S(2)}) collective-permute-start(bf16[144,384]{1,0:T(8,128)(2,1)S(1)} %get-tuple-element.214), channel_id=1, source_target_pairs={{0,8},{8,0},{16,24},{24,16},{1,9},{9,1},{17,25},{25,17},{2,10},{10... | collective-permute-start | bytes 331784 | tf_op jit(solution)/shard_map/ppermute | solution.py:44
  168.6 14.5 %collective-permute-start.51 = (bf16[144,384]{1,0:T(8,128)(2,1)S(1)}, bf16[144,384]{1,0:T(8,128)(2,1)S(1)}, u32[]{:S(2)}, u32[]{:S(2)}) collective-permute-start(bf16[144,384]{1,0:T(8,128)(2,1)S(1)} %get-tuple-element.215), channel_id=1, source_target_pairs={{0,24},{8,16},{16,8},{24,0},{1,25},{9,17},{17,9},{25,1},{2,26},{10... | collective-permute-start | bytes 331784 | tf_op jit(solution)/shard_map/ppermute | solution.py:44
  173.6 8.3 %collective-permute-start.52 = (f32[32,384]{1,0:T(8,128)S(1)}, f32[32,384]{1,0:T(8,128)S(1)}, u32[]{:S(2)}, u32[]{:S(2)}) collective-permute-start(f32[32,384]{1,0:T(8,128)S(1)} %get-tuple-element.217.refs_1_), channel_id=1, source_target_pairs={{0,1},{1,0},{2,3},{3,2},{4,5},{5,4},{6,7},{7,6},{8,9},{9,8},{10,11... | collective-permute-start | bytes 147464 | tf_op jit(solution)/shard_map/ppermute | solution.py:44
  (26 other events, 321.7 us)

commit v6 on v5

--- a/solution.py
+++ b/solution.py
@@ -1004,14 +1004,6 @@
         token_back_kernel, where, [grad_mixed, wj], [shape(LEN, D)], after=first_got
     )
     other = swap(part, "col", 1)
-    own = [shape(*CROSS, dtype=F32)] * 2 if direct else []
-    pieces = run(
-        token_sum_kernel,
-        where,
-        [result, grad_one, part, other] + cross_sum,
-        [shape(LEN + 2 * S if direct else LEN, 2 * W)] * ROWS + own,
-        [pltpu.VMEM((LEN, D), F32), pltpu.VMEM((ROWS, LEN, 2 * W), BF16)],
-    )
     first_passed = run(
         carry_pass_kernel,
         where,
@@ -1034,19 +1026,28 @@
         got = swap(third_sum[1], "dp", 1)
         third_sum = run(far_line_kernel, where, [third_sum[0], got], sums(PART, PART))
         third_sum[1] = swap(third_sum[1], "dp", 2)
-        ready = third_sum[1:] + cross_sum[3:4]
+        ready = third_sum[:1] + cross_sum[3:4]
     else:
-        ready = pieces[:1]
+        ready = []
     second_got = scatter_first(second_handed)
     second_passed = scatter_pass(where, second_handed, second_got, ready)
     second_last = scatter_second(second_passed)
+    own = [shape(*CROSS, dtype=F32)] * 2 if direct else []
+    pieces = run(
+        token_sum_kernel,
+        where,
+        [result, grad_one, part, other] + cross_sum,
+        [shape(LEN + 2 * S if direct else LEN, 2 * W)] * ROWS + own,
+        [pltpu.VMEM((LEN, D), F32), pltpu.VMEM((ROWS, LEN, 2 * W), BF16)],
+        after=second_last,
+    )
     first_sum = run(
         carry_near_kernel,
         where,
         first_handed[-1:] + first_got + first_last + first_passed[1:],
         sums((2 * W + VROWS, COLS), CARRIED) if direct else wide + [shape(*VECTOR, dtype=F32)],
         lines,
-        after=second_passed,
+        after=second_passed + third_sum[1:],
     )
     second_sum = run(
         line_kernel,

time: 190 us -> 192 us (1.011); the launches traced: 187 us -> 192 us
  waiting for transfers between devices: 55.8 us -> 66 us
  starting transfers between devices: 71.2 us -> 66 us
    ppermute x53, waiting for transfers between devices: 55.8 us -> 66 us  [swap(): return lax.ppermute(value, axis, [(i, i ^ mask) for i in range(n)])]
    ppermute x53, starting transfers between devices: 71.2 us -> 66 us  [swap(): return lax.ppermute(value, axis, [(i, i ^ mask) for i in range(n)])]
  transfers between devices with their start and end apart: 53 -> 53, of which waited for: 21 -> 23; matrix products, arithmetic and copies ran while one was open for 0% -> 0% of each run, Pallas kernels for 23% -> 22%
where the time goes in v6:
time: 192 us
  starting transfers between devices  66 us (34%)
  waiting for transfers between devices  66 us (34%)
  Pallas kernels  53.7 us (28%)
  local copies, waits for them, and re-layouts  3.38 us (2%)
    ppermute x53, starting transfers between devices, swap(): return lax.ppermute(value, axis, [(i, i ^ mask) for i in range(n)])  66 us
    ppermute x53, waiting for transfers between devices, swap(): return lax.ppermute(value, axis, [(i, i ^ mask) for i in range(n)])  66 us
    pallas_call x39, Pallas kernels, run(): pl.pallas_call(body, out_shape=outs, in_specs=[pl.BlockSpec(memory_space=...  53.7 us
  transfers between devices with their start and end apart: 53, of which 23 were waited for; matrix products, arithmetic and copies ran while one was open for 0% of the time, Pallas kernels for 22%

profile of v6, /device:TPU:1, one launch (start us, length us, event | category | flops | bytes accessed | tf_op | source)
XLA Modules:
  0.0 191.5 jit_solution(4408033612895207564)
XLA Ops:
  1.9 3.0 %shard_map.305 = (bf16[304,384]{1,0:T(8,128)(2,1)}, bf16[304,384]{1,0:T(8,128)(2,1)}, bf16[304,384]{1,0:T(8,128)(2,1)}, bf16[304,384]{1,0:T(8,128)(2,1)}, bf16[192,384]{1,0:T(8,128)(2,1)}) custom-call(s32[4]{0:T(128)} %pad_add_fusion.refs_0_, bf16[4,128,384]{2,1,0:T(8,128)(2,1)} %bitcast.89, bf16[4,128,384]{2,1,0:T(8,128)(2,1)} %bitcast.90, ...), custom_call_target="tpu_custom_call" | custom-call | tf_op jit(solution)/shard_map/pallas_call | solution.py:58
  5.0 4.2 %collective-permute-start.5 = (bf16[192,384]{1,0:T(8,128)(2,1)}, bf16[192,384]{1,0:T(8,128)(2,1)S(1)}, u32[]{:S(2)}, u32[]{:S(2)}) collective-permute-start(bf16[192,384]{1,0:T(8,128)(2,1)} %get-tuple-element.127.refs_1_), channel_id=1, source_target_pairs={{0,24},{8,16},{16,8},{24,0},{1,25},{9,17},{17,9},{25,1},{2,26},{10... | collective-permute-start | bytes 442376 | tf_op jit(solution)/shard_map/ppermute | solution.py:44
  13.0 1.5 collective-permute-start.3
  14.5 1.8 collective-permute-done.4.refs_3_
  16.3 1.9 collective-permute-done.3.refs_2_
  18.2 3.4 %collective-permute-done.2.refs_7_.refs_4_ = bf16[304,384]{1,0:T(8,128)(2,1)S(1)} collective-permute-done((bf16[304,384]{1,0:T(8,128)(2,1)}, bf16[304,384]{1,0:T(8,128)(2,1)S(1)}, u32[]{:S(2)}, u32[]{:S(2)}) %collective-permute-start.2) | collective-permute-done | bytes 233504 | tf_op jit(solution)/shard_map/ppermute | solution.py:44
  26.3 6.1 %collective-permute-done.11.refs_2_ = bf16[192,384]{1,0:T(8,128)(2,1)S(1)} collective-permute-done((bf16[192,384]{1,0:T(8,128)(2,1)S(1)}, bf16[192,384]{1,0:T(8,128)(2,1)S(1)}, u32[]{:S(2)}, u32[]{:S(2)}) %collective-permute-start.11) | collective-permute-done | bytes 147488 | tf_op jit(solution)/shard_map/ppermute | solution.py:44
  33.7 1.6 collective-permute-start.17
  35.2 5.1 %collective-permute-done.17.refs_2_ = bf16[4,48,384]{2,1,0:T(8,128)(2,1)S(1)} collective-permute-done((bf16[4,48,384]{2,1,0:T(8,128)(2,1)S(1)}, bf16[4,48,384]{2,1,0:T(8,128)(2,1)S(1)}, u32[]{:S(2)}, u32[]{:S(2)}) %collective-permute-start.17) | collective-permute-done | bytes 147488 | tf_op jit(solution)/shard_map/ppermute | solution.py:44
  45.5 2.4 %collective-permute-done.19.refs_2_ = bf16[144,384]{1,0:T(8,128)(2,1)S(1)} collective-permute-done((bf16[144,384]{1,0:T(8,128)(2,1)S(1)}, bf16[144,384]{1,0:T(8,128)(2,1)S(1)}, u32[]{:S(2)}, u32[]{:S(2)}) %collective-permute-start.19) | collective-permute-done | bytes 110624 | tf_op jit(solution)/shard_map/ppermute | solution.py:44
  49.1 5.7 %collective-permute-done.20.refs_2_ = bf16[2,144,384]{2,1,0:T(8,128)(2,1)S(1)} collective-permute-done((bf16[2,144,384]{2,1,0:T(8,128)(2,1)S(1)}, bf16[2,144,384]{2,1,0:T(8,128)(2,1)S(1)}, u32[]{:S(2)}, u32[]{:S(2)}) %collective-permute-start.20) | collective-permute-done | bytes 221216 | tf_op jit(solution)/shard_map/ppermute | solution.py:44
  56.5 5.2 %shard_map.308 = (bf16[256,768]{1,0:T(8,128)(2,1)S(1)}, bf16[256,768]{1,0:T(8,128)(2,1)S(1)}, bf16[4,1152,192]{2,1,0:T(8,128)(2,1)S(1)}, bf16[768,384]{1,0:T(8,1...) custom-call(s32[4]{0:T(128)S(1)} %copy-done.5, ...), custom_call_target="tpu_custom_call" | custom-call | tf_op jit(solution)/shard_map/pallas_call | solution.py:58
  61.6 9.2 %collective-permute-start.10 = (bf16[256,768]{1,0:T(8,128)(2,1)S(1)}, bf16[256,768]{1,0:T(8,128)(2,1)S(1)}, u32[]{:S(2)}, u32[]{:S(2)}) collective-permute-start(bf16[256,768]{1,0:T(8,128)(2,1)S(1)} %get-tuple-element.131.refs_2_), channel_id=1, source_target_pairs={{0,1},{1,0},{2,3},{3,2},{4,5},{5,4},{6,7},{7,6},{8,9},{9,8},{10,11... | collective-permute-start | bytes 1179656 | tf_op jit(solution)/shard_map/ppermute | solution.py:44
  71.4 1.3 collective-permute-start.15
  75.1 5.5 %collective-permute-done.15.refs_8_ = bf16[2,192,384]{2,1,0:T(8,128)(2,1)S(1)} collective-permute-done((bf16[2,192,384]{2,1,0:T(8,128)(2,1)S(1)}, bf16[2,192,384]{2,1,0:T(8,128)(2,1)S(1)}, u32[]{:S(2)}, u32[]{:S(2)}) %collective-permute-start.15) | collective-permute-done | bytes 294944 | tf_op jit(solution)/shard_map/ppermute | solution.py:44
  80.6 3.8 %shard_map.315 = (f32[256,768]{1,0:T(8,128)S(1)}, bf16[256,768]{1,0:T(8,128)(2,1)S(1)}, f32[256,768]{1,0:T(8,128)S(1)}, f32[256,1]{1,0:T(8,128)S(1)}, bf16[256,1...) custom-call(s32[4]{0:T(128)S(1)} %copy-done.5, ...), custom_call_target="tpu_custom_call" | custom-call | tf_op jit(solution)/shard_map/pallas_call | solution.py:58
  85.3 1.6 shard_map.320
  86.9 4.2 %collective-permute-start.25 = (bf16[256,768]{1,0:T(8,128)(2,1)S(1)}, bf16[256,768]{1,0:T(8,128)(2,1)S(1)}, u32[]{:S(2)}, u32[]{:S(2)}) collective-permute-start(bf16[256,768]{1,0:T(8,128)(2,1)S(1)} %get-tuple-element.138.refs_2_), channel_id=1, source_target_pairs={{0,1},{1,0},{2,3},{3,2},{4,5},{5,4},{6,7},{7,6},{8,9},{9,8},{10,11... | collective-permute-start | bytes 1179656 | tf_op jit(solution)/shard_map/ppermute | solution.py:44
  91.1 1.3 collective-permute-done.25.refs_3_
  92.4 3.7 %shard_map.321 = (f32[256,768]{1,0:T(8,128)S(1)}, bf16[256,768]{1,0:T(8,128)(2,1)S(1)}, f32[256,768]{1,0:T(8,128)S(1)}, f32[8,768]{1,0:T(8,128)S(1)}, bf16[4,144...) custom-call(s32[4]{0:T(128)S(1)} %copy-done.5, ...), custom_call_target="tpu_custom_call" | custom-call | tf_op jit(solution)/shard_map/pallas_call | solution.py:58
  96.6 3.3 %shard_map.322 = (bf16[256,1536]{1,0:T(8,128)(2,1)S(1)}, bf16[256,768]{1,0:T(8,128)(2,1)S(1)}, f32[8,1536]{1,0:T(8,128)S(1)}) custom-call(s32[4]{0:T(128)S(1)} %copy-done.5, bf16[256,768]{1,0:T(8,128)(2,1)S(1)} %get-tuple-element.142.refs_1_, f32[256,1536]{1,0:T(8,128)S(1)} %get-tuple-element.143.refs_2_, bf16[768,1536]{1,0:T(8,128)(2,1)S(1)} %get-tuple-element.144.refs_3_, ...), custom_call_target="tpu_custom_call" | custom-call | tf_op jit(solution)/shard_map/pallas_call | solution.py:58
  100.7 1.7 collective-permute-start.29
  102.4 4.4 %shard_map.323 = (f32[256,768]{1,0:T(8,128)S(1)}, bf16[1152,256]{1,0:T(8,128)(2,1)S(1)}, bf16[256,768]{1,0:T(8,128)(2,1)S(1)}, f32[8,768]{1,0:T(8,128)S(1)}) custom-call(s32[4]{0:T(128)S(1)} %copy-done.5, f32[256,768]{1,0:T(8,128)S(1)} %get-tuple-element.141.refs_1_, bf16[256,768]{1,0:T(8,128)(2,1)S(1)} %get-tuple-element.146.refs_2_, ...), custom_call_target="tpu_custom_call" | custom-call | tf_op jit(solution)/shard_map/pallas_call | solution.py:58
  106.8 1.7 shard_map.324
  110.4 1.3 collective-permute-start.31
  112.8 1.7 shard_map.329
  117.7 6.1 %collective-permute-done.34.refs_2_ = bf16[8,48,384]{2,1,0:T(8,128)(2,1)S(1)} collective-permute-done((bf16[8,48,384]{2,1,0:T(8,128)(2,1)S(1)}, bf16[8,48,384]{2,1,0:T(8,128)(2,1)S(1)}, u32[]{:S(2)}, u32[]{:S(2)}) %collective-permute-start.34) | collective-permute-done | bytes 294944 | tf_op jit(solution)/shard_map/ppermute | solution.py:44
  124.9 4.4 %collective-permute-done.31.refs_4_.refs_5_.refs_3_ = bf16[1056,384]{1,0:T(8,128)(2,1)S(1)} collective-permute-done((bf16[1056,384]{1,0:T(8,128)(2,1)S(1)}, bf16[1056,384]{1,0:T(8,128)(2,1)S(1)}, u32[]{:S(2)}, u32[]{:S(2)}) %collective-permute-start.31) | collective-permute-done | bytes 811040 | tf_op jit(solution)/shard_map/ppermute | solution.py:44
  129.4 1.8 collective-permute-start.35
  134.4 1.6 collective-permute-done.35.refs_6_.refs_8_
  137.1 1.5 shard_map.327.refs_3_
  138.6 1.6 collective-permute-done.38.refs_2_
  140.2 2.1 %collective-permute-start.32 = (bf16[256,768]{1,0:T(8,128)(2,1)S(1)}, bf16[256,768]{1,0:T(8,128)(2,1)S(1)}, u32[]{:S(2)}, u32[]{:S(2)}) collective-permute-start(bf16[256,768]{1,0:T(8,128)(2,1)S(1)} %shard_map.327.refs_3_), channel_id=1, source_target_pairs={{0,1},{1,0},{2,3},{3,2},{4,5},{5,4},{6,7},{7,6},{8,9},{9,8},{10,11... | collective-permute-start | bytes 1179656 | tf_op jit(solution)/shard_map/ppermute | solution.py:44
  142.8 1.8 collective-permute-start.46
  145.4 1.8 collective-permute-done.44.refs_4_
  148.3 1.6 collective-permute-start.47
  150.5 3.4 %collective-permute-start.40 = (bf16[2,144,384]{2,1,0:T(8,128)(2,1)S(1)}, bf16[2,144,384]{2,1,0:T(8,128)(2,1)S(1)}, u32[]{:S(2)}, u32[]{:S(2)}) collective-permute-start(bf16[2,144,384]{2,1,0:T(8,128)(2,1)S(1)} %get-tuple-element.189.refs_8_), channel_id=1, source_target_pairs={{0,4},{2,6},{4,0},{6,2},{1,5},{3,7},{5,1},{7,3},{8,12},{10,14},{12... | collective-permute-start | bytes 663560 | tf_op jit(solution)/shard_map/ppermute | solution.py:44
  154.7 3.4 %collective-permute-done.40.refs_10_.refs_5_ = bf16[2,144,384]{2,1,0:T(8,128)(2,1)S(1)} collective-permute-done((bf16[2,144,384]{2,1,0:T(8,128)(2,1)S(1)}, bf16[2,144,384]{2,1,0:T(8,128)(2,1)S(1)}, u32[]{:S(2)}, u32[]{:S(2)}) %collective-permute-start.40) | collective-permute-done | bytes 221216 | tf_op jit(solution)/shard_map/ppermute | solution.py:44
  159.4 2.3 %collective-permute-start.41 = (bf16[352,384]{1,0:T(8,128)(2,1)S(1)}, bf16[352,384]{1,0:T(8,128)(2,1)S(1)}, u32[]{:S(2)}, u32[]{:S(2)}) collective-permute-start(bf16[352,384]{1,0:T(8,128)(2,1)S(1)} %get-tuple-element.191), channel_id=1, source_target_pairs={{0,2},{2,0},{4,6},{6,4},{1,3},{3,1},{5,7},{7,5},{8,10},{10,8},{12,... | collective-permute-start | bytes 811016 | tf_op jit(solution)/shard_map/ppermute | solution.py:44
  161.6 1.3 collective-permute-start.42
  163.6 1.8 collective-permute-start.48
  168.0 9.1 %collective-permute-done.48.refs_2_ = bf16[256,384]{1,0:T(8,128)(2,1)S(1)} collective-permute-done((bf16[256,384]{1,0:T(8,128)(2,1)S(1)}, bf16[256,384]{1,0:T(8,128)(2,1)S(1)}, u32[]{:S(2)}, u32[]{:S(2)}) %collective-permute-start.48) | collective-permute-done | bytes 196640 | tf_op jit(solution)/shard_map/ppermute | solution.py:44
  177.1 1.9 collective-permute-start.51
  179.1 1.7 shard_map.339
  180.8 2.6 %collective-permute-start.52 = (f32[32,384]{1,0:T(8,128)S(1)}, f32[32,384]{1,0:T(8,128)S(1)}, u32[]{:S(2)}, u32[]{:S(2)}) collective-permute-start(f32[32,384]{1,0:T(8,128)S(1)} %get-tuple-element.218.refs_1_), channel_id=1, source_target_pairs={{0,1},{1,0},{2,3},{3,2},{4,5},{5,4},{6,7},{7,6},{8,9},{9,8},{10,11... | collective-permute-start | bytes 147464 | tf_op jit(solution)/shard_map/ppermute | solution.py:44
  183.4 1.8 shard_map.335
  185.2 1.6 shard_map.342
  189.8 1.7 shard_map.343
  (140 shorter events, 46.1 us)
Async XLA Ops:
  5.0 8.0 %collective-permute-start.5 = (bf16[192,384]{1,0:T(8,128)(2,1)}, bf16[192,384]{1,0:T(8,128)(2,1)S(1)}, u32[]{:S(2)}, u32[]{:S(2)}) collective-permute-start(bf16[192,384]{1,0:T(8,128)(2,1)} %get-tuple-element.127.refs_1_), channel_id=1, source_target_pairs={{0,24},{8,16},{16,8},{24,0},{1,25},{9,17},{17,9},{25,1},{2,26},{10... | collective-permute-start | bytes 442376 | tf_op jit(solution)/shard_map/ppermute | solution.py:44
  9.2 9.0 %collective-permute-start = (bf16[304,384]{1,0:T(8,128)(2,1)}, bf16[304,384]{1,0:T(8,128)(2,1)S(1)}, u32[]{:S(2)}, u32[]{:S(2)}) collective-permute-start(bf16[304,384]{1,0:T(8,128)(2,1)} %get-tuple-element.124), channel_id=1, source_target_pairs={{0,2},{2,0},{4,6},{6,4},{1,3},{3,1},{5,7},{7,5},{8,10},{10,8},{12,... | collective-permute-start | bytes 700424 | tf_op jit(solution)/shard_map/ppermute | solution.py:44
  10.4 7.8 %collective-permute-start.1 = (bf16[304,384]{1,0:T(8,128)(2,1)}, bf16[304,384]{1,0:T(8,128)(2,1)S(1)}, u32[]{:S(2)}, u32[]{:S(2)}) collective-permute-start(bf16[304,384]{1,0:T(8,128)(2,1)} %get-tuple-element.125), channel_id=1, source_target_pairs={{0,4},{2,6},{4,0},{6,2},{1,5},{3,7},{5,1},{7,3},{8,12},{10,14},{12... | collective-permute-start | bytes 700424 | tf_op jit(solution)/shard_map/ppermute | solution.py:44
  11.6 10.0 %collective-permute-start.2 = (bf16[304,384]{1,0:T(8,128)(2,1)}, bf16[304,384]{1,0:T(8,128)(2,1)S(1)}, u32[]{:S(2)}, u32[]{:S(2)}) collective-permute-start(bf16[304,384]{1,0:T(8,128)(2,1)} %get-tuple-element.126), channel_id=1, source_target_pairs={{0,6},{2,4},{4,2},{6,0},{1,7},{3,5},{5,3},{7,1},{8,14},{10,12},{12... | collective-permute-start | bytes 700424 | tf_op jit(solution)/shard_map/ppermute | solution.py:44
  13.0 5.2 %collective-permute-start.3 = (bf16[192,384]{1,0:T(8,128)(2,1)}, bf16[192,384]{1,0:T(8,128)(2,1)S(1)}, u32[]{:S(2)}, u32[]{:S(2)}) collective-permute-start(bf16[192,384]{1,0:T(8,128)(2,1)} %get-tuple-element.127.refs_1_), channel_id=1, source_target_pairs={{0,16},{8,24},{16,0},{24,8},{1,17},{9,25},{17,1},{25,9},{2,18},{10... | collective-permute-start | bytes 442376 | tf_op jit(solution)/shard_map/ppermute | solution.py:44
  23.8 19.3 %collective-permute-start.7 = (bf16[4,192,384]{2,1,0:T(8,128)(2,1)S(1)}, bf16[4,192,384]{2,1,0:T(8,128)(2,1)S(1)}, u32[]{:S(2)}, u32[]{:S(2)}) collective-permute-start(bf16[4,192,384]{2,1,0:T(8,128)(2,1)S(1)} %shard_map.306.refs_6_), channel_id=1, source_target_pairs={{0,4},{2,6},{4,0},{6,2},{1,5},{3,7},{5,1},{7,3},{8,12},{10,14},{12... | collective-permute-start | bytes 1769480 | tf_op jit(solution)/shard_map/ppermute | solution.py:44
  24.1 19.0 %collective-permute-start.6 = (bf16[4,192,384]{2,1,0:T(8,128)(2,1)S(1)}, bf16[4,192,384]{2,1,0:T(8,128)(2,1)S(1)}, u32[]{:S(2)}, u32[]{:S(2)}) collective-permute-start(bf16[4,192,384]{2,1,0:T(8,128)(2,1)S(1)} %shard_map.306.refs_6_), channel_id=1, source_target_pairs={{0,2},{2,0},{4,6},{6,4},{1,3},{3,1},{5,7},{7,5},{8,10},{10,8},{12,... | collective-permute-start | bytes 1769480 | tf_op jit(solution)/shard_map/ppermute | solution.py:44
  25.9 6.5 %collective-permute-start.11 = (bf16[192,384]{1,0:T(8,128)(2,1)S(1)}, bf16[192,384]{1,0:T(8,128)(2,1)S(1)}, u32[]{:S(2)}, u32[]{:S(2)}) collective-permute-start(bf16[192,384]{1,0:T(8,128)(2,1)S(1)} %shard_map.309.refs_1_), channel_id=1, source_target_pairs={{0,16},{8,24},{16,0},{24,8},{1,17},{9,25},{17,1},{25,9},{2,18},{10... | collective-permute-start | bytes 442376 | tf_op jit(solution)/shard_map/ppermute | solution.py:44
  33.0 8.8 %collective-permute-start.12 = (bf16[2,192,384]{2,1,0:T(8,128)(2,1)S(1)}, bf16[2,192,384]{2,1,0:T(8,128)(2,1)S(1)}, u32[]{:S(2)}, u32[]{:S(2)}) collective-permute-start(bf16[2,192,384]{2,1,0:T(8,128)(2,1)S(1)} %shard_map.310.refs_1_), channel_id=1, source_target_pairs={{0,8},{8,0},{16,24},{24,16},{1,9},{9,1},{17,25},{25,17},{2,10},{10... | collective-permute-start | bytes 884744 | tf_op jit(solution)/shard_map/ppermute | solution.py:44
  33.7 6.7 %collective-permute-start.17 = (bf16[4,48,384]{2,1,0:T(8,128)(2,1)S(1)}, bf16[4,48,384]{2,1,0:T(8,128)(2,1)S(1)}, u32[]{:S(2)}, u32[]{:S(2)}) collective-permute-start(bf16[4,48,384]{2,1,0:T(8,128)(2,1)S(1)} %shard_map.313.refs_1_), channel_id=1, source_target_pairs={{0,16},{8,24},{16,0},{24,8},{1,17},{9,25},{17,1},{25,9},{2,18},{10... | collective-permute-start | bytes 442376 | tf_op jit(solution)/shard_map/ppermute | solution.py:44
  43.7 11.1 %collective-permute-start.8 = (bf16[2,192,384]{2,1,0:T(8,128)(2,1)S(1)}, bf16[2,192,384]{2,1,0:T(8,128)(2,1)S(1)}, u32[]{:S(2)}, u32[]{:S(2)}) collective-permute-start(bf16[2,192,384]{2,1,0:T(8,128)(2,1)S(1)} %get-tuple-element.128), channel_id=1, source_target_pairs={{0,2},{2,0},{4,6},{6,4},{1,3},{3,1},{5,7},{7,5},{8,10},{10,8},{12,... | collective-permute-start | bytes 884744 | tf_op jit(solution)/shard_map/ppermute | solution.py:44
  44.0 10.7 %collective-permute-start.9 = (bf16[2,192,384]{2,1,0:T(8,128)(2,1)S(1)}, bf16[2,192,384]{2,1,0:T(8,128)(2,1)S(1)}, u32[]{:S(2)}, u32[]{:S(2)}) collective-permute-start(bf16[2,192,384]{2,1,0:T(8,128)(2,1)S(1)} %get-tuple-element.129), channel_id=1, source_target_pairs={{0,4},{2,6},{4,0},{6,2},{1,5},{3,7},{5,1},{7,3},{8,12},{10,14},{12... | collective-permute-start | bytes 884744 | tf_op jit(solution)/shard_map/ppermute | solution.py:44
  44.3 17.4 %collective-permute-start.14 = (bf16[4,192,384]{2,1,0:T(8,128)(2,1)S(1)}, bf16[4,192,384]{2,1,0:T(8,128)(2,1)S(1)}, u32[]{:S(2)}, u32[]{:S(2)}) collective-permute-start(bf16[4,192,384]{2,1,0:T(8,128)(2,1)S(1)} %shard_map.311.refs_5_.refs_2_), channel_id=1, source_target_pairs={{0,4},{2,6},{4,0},{6,2},{1,5},{3,7},{5,1},{7,3},{8,12},{10,14},{12... | collective-permute-start | bytes 1769480 | tf_op jit(solution)/shard_map/ppermute | solution.py:44
  48.4 6.3 %collective-permute-start.20 = (bf16[2,144,384]{2,1,0:T(8,128)(2,1)S(1)}, bf16[2,144,384]{2,1,0:T(8,128)(2,1)S(1)}, u32[]{:S(2)}, u32[]{:S(2)}) collective-permute-start(bf16[2,144,384]{2,1,0:T(8,128)(2,1)S(1)} %shard_map.317.refs_1_), channel_id=1, source_target_pairs={{0,8},{8,0},{16,24},{24,16},{1,9},{9,1},{17,25},{25,17},{2,10},{10... | collective-permute-start | bytes 663560 | tf_op jit(solution)/shard_map/ppermute | solution.py:44
  48.5 22.3 %collective-permute-start.13 = (bf16[4,192,384]{2,1,0:T(8,128)(2,1)S(1)}, bf16[4,192,384]{2,1,0:T(8,128)(2,1)S(1)}, u32[]{:S(2)}, u32[]{:S(2)}) collective-permute-start(bf16[4,192,384]{2,1,0:T(8,128)(2,1)S(1)} %shard_map.311.refs_5_.refs_2_), channel_id=1, source_target_pairs={{0,2},{2,0},{4,6},{6,4},{1,3},{3,1},{5,7},{7,5},{8,10},{10,8},{12,... | collective-permute-start | bytes 1769480 | tf_op jit(solution)/shard_map/ppermute | solution.py:44
  55.4 17.4 %collective-permute-start.22 = (bf16[4,144,384]{2,1,0:T(8,128)(2,1)S(1)}, bf16[4,144,384]{2,1,0:T(8,128)(2,1)S(1)}, u32[]{:S(2)}, u32[]{:S(2)}) collective-permute-start(bf16[4,144,384]{2,1,0:T(8,128)(2,1)S(1)} %shard_map.318.refs_2_), channel_id=1, source_target_pairs={{0,4},{2,6},{4,0},{6,2},{1,5},{3,7},{5,1},{7,3},{8,12},{10,14},{12... | collective-permute-start | bytes 1327112 | tf_op jit(solution)/shard_map/ppermute | solution.py:44
  56.1 17.8 %collective-permute-start.21 = (bf16[4,144,384]{2,1,0:T(8,128)(2,1)S(1)}, bf16[4,144,384]{2,1,0:T(8,128)(2,1)S(1)}, u32[]{:S(2)}, u32[]{:S(2)}) collective-permute-start(bf16[4,144,384]{2,1,0:T(8,128)(2,1)S(1)} %shard_map.318.refs_2_), channel_id=1, source_target_pairs={{0,2},{2,0},{4,6},{6,4},{1,3},{3,1},{5,7},{7,5},{8,10},{10,8},{12,... | collective-permute-start | bytes 1327112 | tf_op jit(solution)/shard_map/ppermute | solution.py:44
  56.5 18.2 %collective-permute-start.18 = (bf16[8,48,384]{2,1,0:T(8,128)(2,1)S(1)}, bf16[8,48,384]{2,1,0:T(8,128)(2,1)S(1)}, u32[]{:S(2)}, u32[]{:S(2)}) collective-permute-start(bf16[8,48,384]{2,1,0:T(8,128)(2,1)S(1)} %shard_map.314.refs_3_.refs_7_), channel_id=1, source_target_pairs={{0,8},{8,0},{16,24},{24,16},{1,9},{9,1},{17,25},{25,17},{2,10},{10... | collective-permute-start | bytes 884744 | tf_op jit(solution)/shard_map/ppermute | solution.py:44
  61.6 19.0 %collective-permute-start.10 = (bf16[256,768]{1,0:T(8,128)(2,1)S(1)}, bf16[256,768]{1,0:T(8,128)(2,1)S(1)}, u32[]{:S(2)}, u32[]{:S(2)}) collective-permute-start(bf16[256,768]{1,0:T(8,128)(2,1)S(1)} %get-tuple-element.131.refs_2_), channel_id=1, source_target_pairs={{0,1},{1,0},{2,3},{3,2},{4,5},{5,4},{6,7},{7,6},{8,9},{9,8},{10,11... | collective-permute-start | bytes 1179656 | tf_op jit(solution)/shard_map/ppermute | solution.py:44
  71.4 9.2 %collective-permute-start.15 = (bf16[2,192,384]{2,1,0:T(8,128)(2,1)S(1)}, bf16[2,192,384]{2,1,0:T(8,128)(2,1)S(1)}, u32[]{:S(2)}, u32[]{:S(2)}) collective-permute-start(bf16[2,192,384]{2,1,0:T(8,128)(2,1)S(1)} %get-tuple-element.132), channel_id=1, source_target_pairs={{0,2},{2,0},{4,6},{6,4},{1,3},{3,1},{5,7},{7,5},{8,10},{10,8},{12,... | collective-permute-start | bytes 884744 | tf_op jit(solution)/shard_map/ppermute | solution.py:44
  72.7 7.9 %collective-permute-start.16 = (bf16[2,192,384]{2,1,0:T(8,128)(2,1)S(1)}, bf16[2,192,384]{2,1,0:T(8,128)(2,1)S(1)}, u32[]{:S(2)}, u32[]{:S(2)}) collective-permute-start(bf16[2,192,384]{2,1,0:T(8,128)(2,1)S(1)} %get-tuple-element.133), channel_id=1, source_target_pairs={{0,4},{2,6},{4,0},{6,2},{1,5},{3,7},{5,1},{7,3},{8,12},{10,14},{12... | collective-permute-start | bytes 884744 | tf_op jit(solution)/shard_map/ppermute | solution.py:44
  74.5 10.8 %collective-permute-start.23 = (bf16[2,144,384]{2,1,0:T(8,128)(2,1)S(1)}, bf16[2,144,384]{2,1,0:T(8,128)(2,1)S(1)}, u32[]{:S(2)}, u32[]{:S(2)}) collective-permute-start(bf16[2,144,384]{2,1,0:T(8,128)(2,1)S(1)} %get-tuple-element.136), channel_id=1, source_target_pairs={{0,2},{2,0},{4,6},{6,4},{1,3},{3,1},{5,7},{7,5},{8,10},{10,8},{12,... | collective-permute-start | bytes 663560 | tf_op jit(solution)/shard_map/ppermute | solution.py:44
  74.6 10.7 %collective-permute-start.24 = (bf16[2,144,384]{2,1,0:T(8,128)(2,1)S(1)}, bf16[2,144,384]{2,1,0:T(8,128)(2,1)S(1)}, u32[]{:S(2)}, u32[]{:S(2)}) collective-permute-start(bf16[2,144,384]{2,1,0:T(8,128)(2,1)S(1)} %get-tuple-element.137), channel_id=1, source_target_pairs={{0,4},{2,6},{4,0},{6,2},{1,5},{3,7},{5,1},{7,3},{8,12},{10,14},{12... | collective-permute-start | bytes 663560 | tf_op jit(solution)/shard_map/ppermute | solution.py:44
  86.9 5.5 %collective-permute-start.25 = (bf16[256,768]{1,0:T(8,128)(2,1)S(1)}, bf16[256,768]{1,0:T(8,128)(2,1)S(1)}, u32[]{:S(2)}, u32[]{:S(2)}) collective-permute-start(bf16[256,768]{1,0:T(8,128)(2,1)S(1)} %get-tuple-element.138.refs_2_), channel_id=1, source_target_pairs={{0,1},{1,0},{2,3},{3,2},{4,5},{5,4},{6,7},{7,6},{8,9},{9,8},{10,11... | collective-permute-start | bytes 1179656 | tf_op jit(solution)/shard_map/ppermute | solution.py:44
  96.1 12.4 %collective-permute-start.27 = (bf16[4,144,384]{2,1,0:T(8,128)(2,1)S(1)}, bf16[4,144,384]{2,1,0:T(8,128)(2,1)S(1)}, u32[]{:S(2)}, u32[]{:S(2)}) collective-permute-start(bf16[4,144,384]{2,1,0:T(8,128)(2,1)S(1)} %get-tuple-element.164), channel_id=1, source_target_pairs={{0,2},{2,0},{4,6},{6,4},{1,3},{3,1},{5,7},{7,5},{8,10},{10,8},{12,... | collective-permute-start | bytes 1327112 | tf_op jit(solution)/shard_map/ppermute | solution.py:44
  96.2 12.4 %collective-permute-start.28 = (bf16[4,144,384]{2,1,0:T(8,128)(2,1)S(1)}, bf16[4,144,384]{2,1,0:T(8,128)(2,1)S(1)}, u32[]{:S(2)}, u32[]{:S(2)}) collective-permute-start(bf16[4,144,384]{2,1,0:T(8,128)(2,1)S(1)} %get-tuple-element.165), channel_id=1, source_target_pairs={{0,4},{2,6},{4,0},{6,2},{1,5},{3,7},{5,1},{7,3},{8,12},{10,14},{12... | collective-permute-start | bytes 1327112 | tf_op jit(solution)/shard_map/ppermute | solution.py:44
  100.7 8.9 %collective-permute-start.29 = (bf16[8,48,384]{2,1,0:T(8,128)(2,1)S(1)}, bf16[8,48,384]{2,1,0:T(8,128)(2,1)S(1)}, u32[]{:S(2)}, u32[]{:S(2)}) collective-permute-start(bf16[8,48,384]{2,1,0:T(8,128)(2,1)S(1)} %get-tuple-element.168), channel_id=1, source_target_pairs={{0,8},{8,0},{16,24},{24,16},{1,9},{9,1},{17,25},{25,17},{2,10},{10... | collective-permute-start | bytes 884744 | tf_op jit(solution)/shard_map/ppermute | solution.py:44
  110.4 19.0 %collective-permute-start.31 = (bf16[1056,384]{1,0:T(8,128)(2,1)S(1)}, bf16[1056,384]{1,0:T(8,128)(2,1)S(1)}, u32[]{:S(2)}, u32[]{:S(2)}) collective-permute-start(bf16[1056,384]{1,0:T(8,128)(2,1)S(1)} %get-tuple-element.170), channel_id=1, source_target_pairs={{0,4},{2,6},{4,0},{6,2},{1,5},{3,7},{5,1},{7,3},{8,12},{10,14},{12... | collective-permute-start | bytes 2433032 | tf_op jit(solution)/shard_map/ppermute | solution.py:44
  111.7 19.7 %collective-permute-start.30 = (bf16[1120,384]{1,0:T(8,128)(2,1)S(1)}, bf16[1120,384]{1,0:T(8,128)(2,1)S(1)}, u32[]{:S(2)}, u32[]{:S(2)}) collective-permute-start(bf16[1120,384]{1,0:T(8,128)(2,1)S(1)} %get-tuple-element.169.refs_3_), channel_id=1, source_target_pairs={{0,2},{2,0},{4,6},{6,4},{1,3},{3,1},{5,7},{7,5},{8,10},{10,8},{12,... | collective-permute-start | bytes 2580488 | tf_op jit(solution)/shard_map/ppermute | solution.py:44
  114.6 9.2 %collective-permute-start.34 = (bf16[8,48,384]{2,1,0:T(8,128)(2,1)S(1)}, bf16[8,48,384]{2,1,0:T(8,128)(2,1)S(1)}, u32[]{:S(2)}, u32[]{:S(2)}) collective-permute-start(bf16[8,48,384]{2,1,0:T(8,128)(2,1)S(1)} %get-tuple-element.177), channel_id=1, source_target_pairs={{0,8},{8,0},{16,24},{24,16},{1,9},{9,1},{17,25},{25,17},{2,10},{10... | collective-permute-start | bytes 884744 | tf_op jit(solution)/shard_map/ppermute | solution.py:44
  115.7 27.1 %collective-permute-start.36 = (bf16[4,144,384]{2,1,0:T(8,128)(2,1)S(1)}, bf16[4,144,384]{2,1,0:T(8,128)(2,1)S(1)}, u32[]{:S(2)}, u32[]{:S(2)}) collective-permute-start(bf16[4,144,384]{2,1,0:T(8,128)(2,1)S(1)} %get-tuple-element.182), channel_id=1, source_target_pairs={{0,2},{2,0},{4,6},{6,4},{1,3},{3,1},{5,7},{7,5},{8,10},{10,8},{12,... | collective-permute-start | bytes 1327112 | tf_op jit(solution)/shard_map/ppermute | solution.py:44
  116.9 16.4 %collective-permute-start.33 = (bf16[4,48,384]{2,1,0:T(8,128)(2,1)S(1)}, bf16[4,48,384]{2,1,0:T(8,128)(2,1)S(1)}, u32[]{:S(2)}, u32[]{:S(2)}) collective-permute-start(bf16[4,48,384]{2,1,0:T(8,128)(2,1)S(1)} %get-tuple-element.173), channel_id=1, source_target_pairs={{0,16},{8,24},{16,0},{24,8},{1,17},{9,25},{17,1},{25,9},{2,18},{10... | collective-permute-start | bytes 442376 | tf_op jit(solution)/shard_map/ppermute | solution.py:44
  123.8 20.9 %collective-permute-start.37 = (bf16[4,144,384]{2,1,0:T(8,128)(2,1)S(1)}, bf16[4,144,384]{2,1,0:T(8,128)(2,1)S(1)}, u32[]{:S(2)}, u32[]{:S(2)}) collective-permute-start(bf16[4,144,384]{2,1,0:T(8,128)(2,1)S(1)} %get-tuple-element.183), channel_id=1, source_target_pairs={{0,4},{2,6},{4,0},{6,2},{1,5},{3,7},{5,1},{7,3},{8,12},{10,14},{12... | collective-permute-start | bytes 1327112 | tf_op jit(solution)/shard_map/ppermute | solution.py:44
  129.4 6.6 %collective-permute-start.35 = (bf16[4,48,384]{2,1,0:T(8,128)(2,1)S(1)}, bf16[4,48,384]{2,1,0:T(8,128)(2,1)S(1)}, u32[]{:S(2)}, u32[]{:S(2)}) collective-permute-start(bf16[4,48,384]{2,1,0:T(8,128)(2,1)S(1)} %get-tuple-element.179), channel_id=1, source_target_pairs={{0,16},{8,24},{16,0},{24,8},{1,17},{9,25},{17,1},{25,9},{2,18},{10... | collective-permute-start | bytes 442376 | tf_op jit(solution)/shard_map/ppermute | solution.py:44
  132.2 8.0 %collective-permute-start.38 = (bf16[2,144,384]{2,1,0:T(8,128)(2,1)S(1)}, bf16[2,144,384]{2,1,0:T(8,128)(2,1)S(1)}, u32[]{:S(2)}, u32[]{:S(2)}) collective-permute-start(bf16[2,144,384]{2,1,0:T(8,128)(2,1)S(1)} %get-tuple-element.186), channel_id=1, source_target_pairs={{0,8},{8,0},{16,24},{24,16},{1,9},{9,1},{17,25},{25,17},{2,10},{10... | collective-permute-start | bytes 663560 | tf_op jit(solution)/shard_map/ppermute | solution.py:44
  134.1 13.4 %collective-permute-start.45 = (bf16[448,384]{1,0:T(8,128)(2,1)S(1)}, bf16[448,384]{1,0:T(8,128)(2,1)S(1)}, u32[]{:S(2)}, u32[]{:S(2)}) collective-permute-start(bf16[448,384]{1,0:T(8,128)(2,1)S(1)} %get-tuple-element.200.refs_6_), channel_id=1, source_target_pairs={{0,4},{2,6},{4,0},{6,2},{1,5},{3,7},{5,1},{7,3},{8,12},{10,14},{12... | collective-permute-start | bytes 1032200 | tf_op jit(solution)/shard_map/ppermute | solution.py:44
  135.9 11.2 %collective-permute-start.44 = (bf16[2,192,384]{2,1,0:T(8,128)(2,1)S(1)}, bf16[2,192,384]{2,1,0:T(8,128)(2,1)S(1)}, u32[]{:S(2)}, u32[]{:S(2)}) collective-permute-start(bf16[2,192,384]{2,1,0:T(8,128)(2,1)S(1)} %get-tuple-element.199), channel_id=1, source_target_pairs={{0,2},{2,0},{4,6},{6,4},{1,3},{3,1},{5,7},{7,5},{8,10},{10,8},{12,... | collective-permute-start | bytes 884744 | tf_op jit(solution)/shard_map/ppermute | solution.py:44
  140.2 13.8 %collective-permute-start.32 = (bf16[256,768]{1,0:T(8,128)(2,1)S(1)}, bf16[256,768]{1,0:T(8,128)(2,1)S(1)}, u32[]{:S(2)}, u32[]{:S(2)}) collective-permute-start(bf16[256,768]{1,0:T(8,128)(2,1)S(1)} %shard_map.327.refs_3_), channel_id=1, source_target_pairs={{0,1},{1,0},{2,3},{3,2},{4,5},{5,4},{6,7},{7,6},{8,9},{9,8},{10,11... | collective-permute-start | bytes 1179656 | tf_op jit(solution)/shard_map/ppermute | solution.py:44
  148.3 14.7 %collective-permute-start.47 = (bf16[448,384]{1,0:T(8,128)(2,1)S(1)}, bf16[448,384]{1,0:T(8,128)(2,1)S(1)}, u32[]{:S(2)}, u32[]{:S(2)}) collective-permute-start(bf16[448,384]{1,0:T(8,128)(2,1)S(1)} %get-tuple-element.203), channel_id=1, source_target_pairs={{0,8},{8,0},{16,24},{24,16},{1,9},{9,1},{17,25},{25,17},{2,10},{10... | collective-permute-start | bytes 1032200 | tf_op jit(solution)/shard_map/ppermute | solution.py:44
  150.5 7.5 %collective-permute-start.40 = (bf16[2,144,384]{2,1,0:T(8,128)(2,1)S(1)}, bf16[2,144,384]{2,1,0:T(8,128)(2,1)S(1)}, u32[]{:S(2)}, u32[]{:S(2)}) collective-permute-start(bf16[2,144,384]{2,1,0:T(8,128)(2,1)S(1)} %get-tuple-element.189.refs_8_), channel_id=1, source_target_pairs={{0,4},{2,6},{4,0},{6,2},{1,5},{3,7},{5,1},{7,3},{8,12},{10,14},{12... | collective-permute-start | bytes 663560 | tf_op jit(solution)/shard_map/ppermute | solution.py:44
  159.4 7.6 %collective-permute-start.41 = (bf16[352,384]{1,0:T(8,128)(2,1)S(1)}, bf16[352,384]{1,0:T(8,128)(2,1)S(1)}, u32[]{:S(2)}, u32[]{:S(2)}) collective-permute-start(bf16[352,384]{1,0:T(8,128)(2,1)S(1)} %get-tuple-element.191), channel_id=1, source_target_pairs={{0,2},{2,0},{4,6},{6,4},{1,3},{3,1},{5,7},{7,5},{8,10},{10,8},{12,... | collective-permute-start | bytes 811016 | tf_op jit(solution)/shard_map/ppermute | solution.py:44
  161.6 19.2 %collective-permute-start.42 = (bf16[352,384]{1,0:T(8,128)(2,1)S(1)}, bf16[352,384]{1,0:T(8,128)(2,1)S(1)}, u32[]{:S(2)}, u32[]{:S(2)}) collective-permute-start(bf16[352,384]{1,0:T(8,128)(2,1)S(1)} %get-tuple-element.192), channel_id=1, source_target_pairs={{0,4},{2,6},{4,0},{6,2},{1,5},{3,7},{5,1},{7,3},{8,12},{10,14},{12... | collective-permute-start | bytes 811016 | tf_op jit(solution)/shard_map/ppermute | solution.py:44
  163.6 13.5 %collective-permute-start.48 = (bf16[256,384]{1,0:T(8,128)(2,1)S(1)}, bf16[256,384]{1,0:T(8,128)(2,1)S(1)}, u32[]{:S(2)}, u32[]{:S(2)}) collective-permute-start(bf16[256,384]{1,0:T(8,128)(2,1)S(1)} %get-tuple-element.205), channel_id=1, source_target_pairs={{0,16},{8,24},{16,0},{24,8},{1,17},{9,25},{17,1},{25,9},{2,18},{10... | collective-permute-start | bytes 589832 | tf_op jit(solution)/shard_map/ppermute | solution.py:44
  165.4 18.0 %collective-permute-start.43 = (bf16[352,384]{1,0:T(8,128)(2,1)S(1)}, bf16[352,384]{1,0:T(8,128)(2,1)S(1)}, u32[]{:S(2)}, u32[]{:S(2)}) collective-permute-start(bf16[352,384]{1,0:T(8,128)(2,1)S(1)} %get-tuple-element.193), channel_id=1, source_target_pairs={{0,6},{2,4},{4,2},{6,0},{1,7},{3,5},{5,3},{7,1},{8,14},{10,12},{12... | collective-permute-start | bytes 811016 | tf_op jit(solution)/shard_map/ppermute | solution.py:44
  166.3 21.7 %collective-permute-start.49 = (bf16[144,384]{1,0:T(8,128)(2,1)S(1)}, bf16[144,384]{1,0:T(8,128)(2,1)S(1)}, u32[]{:S(2)}, u32[]{:S(2)}) collective-permute-start(bf16[144,384]{1,0:T(8,128)(2,1)S(1)} %get-tuple-element.214), channel_id=1, source_target_pairs={{0,16},{8,24},{16,0},{24,8},{1,17},{9,25},{17,1},{25,9},{2,18},{10... | collective-permute-start | bytes 331784 | tf_op jit(solution)/shard_map/ppermute | solution.py:44
  166.9 21.1 %collective-permute-start.50 = (bf16[144,384]{1,0:T(8,128)(2,1)S(1)}, bf16[144,384]{1,0:T(8,128)(2,1)S(1)}, u32[]{:S(2)}, u32[]{:S(2)}) collective-permute-start(bf16[144,384]{1,0:T(8,128)(2,1)S(1)} %get-tuple-element.215), channel_id=1, source_target_pairs={{0,8},{8,0},{16,24},{24,16},{1,9},{9,1},{17,25},{25,17},{2,10},{10... | collective-permute-start | bytes 331784 | tf_op jit(solution)/shard_map/ppermute | solution.py:44
  177.1 10.9 %collective-permute-start.51 = (bf16[144,384]{1,0:T(8,128)(2,1)S(1)}, bf16[144,384]{1,0:T(8,128)(2,1)S(1)}, u32[]{:S(2)}, u32[]{:S(2)}) collective-permute-start(bf16[144,384]{1,0:T(8,128)(2,1)S(1)} %get-tuple-element.216), channel_id=1, source_target_pairs={{0,24},{8,16},{16,8},{24,0},{1,25},{9,17},{17,9},{25,1},{2,26},{10... | collective-permute-start | bytes 331784 | tf_op jit(solution)/shard_map/ppermute | solution.py:44
  180.8 6.0 %collective-permute-start.52 = (f32[32,384]{1,0:T(8,128)S(1)}, f32[32,384]{1,0:T(8,128)S(1)}, u32[]{:S(2)}, u32[]{:S(2)}) collective-permute-start(f32[32,384]{1,0:T(8,128)S(1)} %get-tuple-element.218.refs_1_), channel_id=1, source_target_pairs={{0,1},{1,0},{2,3},{3,2},{4,5},{5,4},{6,7},{7,6},{8,9},{9,8},{10,11... | collective-permute-start | bytes 147464 | tf_op jit(solution)/shard_map/ppermute | solution.py:44
  (26 other events, 315.2 us)

commit v7 on v4

--- a/solution.py
+++ b/solution.py
@@ -1069,12 +1069,17 @@
             [vector, swap(vector, "col", 1)] + state,
             like(state),
             [pltpu.VMEM((72, 128), F32)],
+            limit=48,
         )
         return [v.reshape(vectors.shape) for v in new]
 
     if direct:
         down_new = run(
-            down_adam_kernel, where, third_sum + pieces[ROWS:] + got[1:] + down, like(down)
+            down_adam_kernel,
+            where,
+            third_sum + pieces[ROWS:] + got[1:] + down,
+            like(down),
+            limit=48,
         )
         vector_new = step_vectors(vector)
         got = [swap(v, "dp", mask) for v, mask in zip(second_sum[1:], ORDER[1:])]

time: 189 us -> 189 us (level)
  no operation moved by 1% of the time
where the time goes in v7:
time: 189 us; the launch traced here: 188 us
  waiting for transfers between devices  66.4 us (35%)
  starting transfers between devices  62.9 us (33%)
  Pallas kernels  53.2 us (28%)
  local copies, waits for them, and re-layouts  3.39 us (2%)
    ppermute x51, waiting for transfers between devices, swap(): return lax.ppermute(value, axis, [(i, i ^ mask) for i in range(n)])  66.4 us
    ppermute x51, starting transfers between devices, swap(): return lax.ppermute(value, axis, [(i, i ^ mask) for i in range(n)])  62.9 us
    pallas_call x38, Pallas kernels, run(): pl.pallas_call(body, out_shape=outs, in_specs=[pl.BlockSpec(memory_space=...  53.2 us
  transfers between devices with their start and end apart: 51, of which 23 were waited for; matrix products, arithmetic and copies ran while one was open for 0% of the time, Pallas kernels for 22%

profile of v7, /device:TPU:1, one launch (start us, length us, event | category | flops | bytes accessed | tf_op | source)
XLA Modules:
  0.0 188.3 jit_solution(4078163841517958605)
XLA Ops:
  1.9 3.0 %shard_map.305 = (bf16[304,384]{1,0:T(8,128)(2,1)}, bf16[304,384]{1,0:T(8,128)(2,1)}, bf16[304,384]{1,0:T(8,128)(2,1)}, bf16[304,384]{1,0:T(8,128)(2,1)}, bf16[192,384]{1,0:T(8,128)(2,1)}) custom-call(s32[4]{0:T(128)} %pad_add_fusion.refs_0_, bf16[4,128,384]{2,1,0:T(8,128)(2,1)} %bitcast.89, bf16[4,128,384]{2,1,0:T(8,128)(2,1)} %bitcast.90, ...), custom_call_target="tpu_custom_call" | custom-call | tf_op jit(solution)/shard_map/pallas_call | solution.py:58
  5.0 4.2 %collective-permute-start.5 = (bf16[192,384]{1,0:T(8,128)(2,1)}, bf16[192,384]{1,0:T(8,128)(2,1)S(1)}, u32[]{:S(2)}, u32[]{:S(2)}) collective-permute-start(bf16[192,384]{1,0:T(8,128)(2,1)} %get-tuple-element.122.refs_1_), channel_id=1, source_target_pairs={{0,24},{8,16},{16,8},{24,0},{1,25},{9,17},{17,9},{25,1},{2,26},{10... | collective-permute-start | bytes 442376 | tf_op jit(solution)/shard_map/ppermute | solution.py:44
  10.4 1.2 collective-permute-start.1
  13.0 1.5 collective-permute-start.3
  14.5 1.8 collective-permute-done.4.refs_3_
  16.3 1.9 %collective-permute-done.3.refs_2_ = bf16[192,384]{1,0:T(8,128)(2,1)S(1)} collective-permute-done((bf16[192,384]{1,0:T(8,128)(2,1)}, bf16[192,384]{1,0:T(8,128)(2,1)S(1)}, u32[]{:S(2)}, u32[]{:S(2)}) %collective-permute-start.3) | collective-permute-done | bytes 147488 | tf_op jit(solution)/shard_map/ppermute | solution.py:44
  18.2 3.4 %collective-permute-done.2.refs_7_.refs_4_ = bf16[304,384]{1,0:T(8,128)(2,1)S(1)} collective-permute-done((bf16[304,384]{1,0:T(8,128)(2,1)}, bf16[304,384]{1,0:T(8,128)(2,1)S(1)}, u32[]{:S(2)}, u32[]{:S(2)}) %collective-permute-start.2) | collective-permute-done | bytes 233504 | tf_op jit(solution)/shard_map/ppermute | solution.py:44
  26.3 6.1 %collective-permute-done.11.refs_2_ = bf16[192,384]{1,0:T(8,128)(2,1)S(1)} collective-permute-done((bf16[192,384]{1,0:T(8,128)(2,1)S(1)}, bf16[192,384]{1,0:T(8,128)(2,1)S(1)}, u32[]{:S(2)}, u32[]{:S(2)}) %collective-permute-start.11) | collective-permute-done | bytes 147488 | tf_op jit(solution)/shard_map/ppermute | solution.py:44
  33.7 1.6 collective-permute-start.17
  35.2 5.1 %collective-permute-done.17.refs_2_ = bf16[4,48,384]{2,1,0:T(8,128)(2,1)S(1)} collective-permute-done((bf16[4,48,384]{2,1,0:T(8,128)(2,1)S(1)}, bf16[4,48,384]{2,1,0:T(8,128)(2,1)S(1)}, u32[]{:S(2)}, u32[]{:S(2)}) %collective-permute-start.17) | collective-permute-done | bytes 147488 | tf_op jit(solution)/shard_map/ppermute | solution.py:44
  45.5 2.4 %collective-permute-done.19.refs_2_ = bf16[144,384]{1,0:T(8,128)(2,1)S(1)} collective-permute-done((bf16[144,384]{1,0:T(8,128)(2,1)S(1)}, bf16[144,384]{1,0:T(8,128)(2,1)S(1)}, u32[]{:S(2)}, u32[]{:S(2)}) %collective-permute-start.19) | collective-permute-done | bytes 110624 | tf_op jit(solution)/shard_map/ppermute | solution.py:44
  49.1 5.7 %collective-permute-done.20.refs_2_ = bf16[2,144,384]{2,1,0:T(8,128)(2,1)S(1)} collective-permute-done((bf16[2,144,384]{2,1,0:T(8,128)(2,1)S(1)}, bf16[2,144,384]{2,1,0:T(8,128)(2,1)S(1)}, u32[]{:S(2)}, u32[]{:S(2)}) %collective-permute-start.20) | collective-permute-done | bytes 221216 | tf_op jit(solution)/shard_map/ppermute | solution.py:44
  56.5 5.2 %shard_map.308 = (bf16[256,768]{1,0:T(8,128)(2,1)S(1)}, bf16[256,768]{1,0:T(8,128)(2,1)S(1)}, bf16[4,1152,192]{2,1,0:T(8,128)(2,1)S(1)}, bf16[768,384]{1,0:T(8,1...) custom-call(s32[4]{0:T(128)S(1)} %copy-done.6, ...), custom_call_target="tpu_custom_call" | custom-call | tf_op jit(solution)/shard_map/pallas_call | solution.py:58
  61.6 9.2 %collective-permute-start.10 = (bf16[256,768]{1,0:T(8,128)(2,1)S(1)}, bf16[256,768]{1,0:T(8,128)(2,1)S(1)}, u32[]{:S(2)}, u32[]{:S(2)}) collective-permute-start(bf16[256,768]{1,0:T(8,128)(2,1)S(1)} %get-tuple-element.126.refs_2_), channel_id=1, source_target_pairs={{0,1},{1,0},{2,3},{3,2},{4,5},{5,4},{6,7},{7,6},{8,9},{9,8},{10,11... | collective-permute-start | bytes 1179656 | tf_op jit(solution)/shard_map/ppermute | solution.py:44
  71.4 1.3 collective-permute-start.15
  75.1 5.5 %collective-permute-done.15.refs_8_ = bf16[2,192,384]{2,1,0:T(8,128)(2,1)S(1)} collective-permute-done((bf16[2,192,384]{2,1,0:T(8,128)(2,1)S(1)}, bf16[2,192,384]{2,1,0:T(8,128)(2,1)S(1)}, u32[]{:S(2)}, u32[]{:S(2)}) %collective-permute-start.15) | collective-permute-done | bytes 294944 | tf_op jit(solution)/shard_map/ppermute | solution.py:44
  80.6 3.8 %shard_map.315 = (f32[256,768]{1,0:T(8,128)S(1)}, bf16[256,768]{1,0:T(8,128)(2,1)S(1)}, f32[256,768]{1,0:T(8,128)S(1)}, f32[256,1]{1,0:T(8,128)S(1)}, bf16[256,1...) custom-call(s32[4]{0:T(128)S(1)} %copy-done.6, ...), custom_call_target="tpu_custom_call" | custom-call | tf_op jit(solution)/shard_map/pallas_call | solution.py:58
  85.3 1.5 shard_map.320
  86.9 4.2 %collective-permute-start.25 = (bf16[256,768]{1,0:T(8,128)(2,1)S(1)}, bf16[256,768]{1,0:T(8,128)(2,1)S(1)}, u32[]{:S(2)}, u32[]{:S(2)}) collective-permute-start(bf16[256,768]{1,0:T(8,128)(2,1)S(1)} %get-tuple-element.133.refs_2_), channel_id=1, source_target_pairs={{0,1},{1,0},{2,3},{3,2},{4,5},{5,4},{6,7},{7,6},{8,9},{9,8},{10,11... | collective-permute-start | bytes 1179656 | tf_op jit(solution)/shard_map/ppermute | solution.py:44
  91.1 1.3 collective-permute-done.25.refs_3_
  92.4 3.7 %shard_map.321 = (f32[256,768]{1,0:T(8,128)S(1)}, bf16[256,768]{1,0:T(8,128)(2,1)S(1)}, f32[256,768]{1,0:T(8,128)S(1)}, f32[8,768]{1,0:T(8,128)S(1)}, bf16[4,144...) custom-call(s32[4]{0:T(128)S(1)} %copy-done.6, ...), custom_call_target="tpu_custom_call" | custom-call | tf_op jit(solution)/shard_map/pallas_call | solution.py:58
  96.6 3.3 %shard_map.322 = (bf16[256,1536]{1,0:T(8,128)(2,1)S(1)}, bf16[256,768]{1,0:T(8,128)(2,1)S(1)}, f32[8,1536]{1,0:T(8,128)S(1)}) custom-call(s32[4]{0:T(128)S(1)} %copy-done.6, bf16[256,768]{1,0:T(8,128)(2,1)S(1)} %get-tuple-element.137.refs_1_, f32[256,1536]{1,0:T(8,128)S(1)} %get-tuple-element.138.refs_2_, bf16[768,1536]{1,0:T(8,128)(2,1)S(1)} %get-tuple-element.139.refs_3_, ...), custom_call_target="tpu_custom_call" | custom-call | tf_op jit(solution)/shard_map/pallas_call | solution.py:58
  100.7 1.7 collective-permute-start.29
  102.4 4.4 %shard_map.323 = (f32[256,768]{1,0:T(8,128)S(1)}, bf16[1152,256]{1,0:T(8,128)(2,1)S(1)}, bf16[256,768]{1,0:T(8,128)(2,1)S(1)}, f32[8,768]{1,0:T(8,128)S(1)}) custom-call(s32[4]{0:T(128)S(1)} %copy-done.6, f32[256,768]{1,0:T(8,128)S(1)} %get-tuple-element.136.refs_1_, bf16[256,768]{1,0:T(8,128)(2,1)S(1)} %get-tuple-element.141.refs_2_, ...), custom_call_target="tpu_custom_call" | custom-call | tf_op jit(solution)/shard_map/pallas_call | solution.py:58
  106.8 1.7 shard_map.324
  110.4 1.4 collective-permute-start.35
  112.8 1.5 shard_map.327.refs_3_
  114.3 1.5 collective-permute-start.30
  116.4 1.7 collective-permute-start.31
  118.1 1.8 shard_map.332
  120.6 5.5 %collective-permute-done.31.refs_6_ = bf16[4,48,384]{2,1,0:T(8,128)(2,1)S(1)} collective-permute-done((bf16[4,48,384]{2,1,0:T(8,128)(2,1)S(1)}, bf16[4,48,384]{2,1,0:T(8,128)(2,1)S(1)}, u32[]{:S(2)}, u32[]{:S(2)}) %collective-permute-start.31) | collective-permute-done | bytes 147488 | tf_op jit(solution)/shard_map/ppermute | solution.py:44
  127.6 2.6 %collective-permute-done.36.refs_5_.refs_3_ = bf16[1056,384]{1,0:T(8,128)(2,1)S(1)} collective-permute-done((bf16[1056,384]{1,0:T(8,128)(2,1)S(1)}, bf16[1056,384]{1,0:T(8,128)(2,1)S(1)}, u32[]{:S(2)}, u32[]{:S(2)}) %collective-permute-start.36) | collective-permute-done | bytes 811040 | tf_op jit(solution)/shard_map/ppermute | solution.py:44
  131.1 1.3 collective-permute-start.38
  135.3 3.0 %collective-permute-done.41.refs_2_ = bf16[2,144,384]{2,1,0:T(8,128)(2,1)S(1)} collective-permute-done((bf16[2,144,384]{2,1,0:T(8,128)(2,1)S(1)}, bf16[2,144,384]{2,1,0:T(8,128)(2,1)S(1)}, u32[]{:S(2)}, u32[]{:S(2)}) %collective-permute-start.41) | collective-permute-done | bytes 221216 | tf_op jit(solution)/shard_map/ppermute | solution.py:44
  139.0 1.8 collective-permute-start.42
  140.8 2.3 %collective-permute-done.39.refs_3_.refs_2_ = bf16[4,192,384]{2,1,0:T(8,128)(2,1)S(1)} collective-permute-done((bf16[4,192,384]{2,1,0:T(8,128)(2,1)S(1)}, bf16[4,192,384]{2,1,0:T(8,128)(2,1)S(1)}, u32[]{:S(2)}, u32[]{:S(2)}) %collective-permute-start.39) | collective-permute-done | bytes 589856 | tf_op jit(solution)/shard_map/ppermute | solution.py:44
  144.5 4.9 %collective-permute-done.37.refs_4_ = bf16[2,192,384]{2,1,0:T(8,128)(2,1)S(1)} collective-permute-done((bf16[2,192,384]{2,1,0:T(8,128)(2,1)S(1)}, bf16[2,192,384]{2,1,0:T(8,128)(2,1)S(1)}, u32[]{:S(2)}, u32[]{:S(2)}) %collective-permute-start.37) | collective-permute-done | bytes 294944 | tf_op jit(solution)/shard_map/ppermute | solution.py:44
  151.2 1.4 collective-permute-start.43
  154.8 3.9 %collective-permute-done.43.refs_2_ = bf16[448,384]{1,0:T(8,128)(2,1)S(1)} collective-permute-done((bf16[448,384]{1,0:T(8,128)(2,1)S(1)}, bf16[448,384]{1,0:T(8,128)(2,1)S(1)}, u32[]{:S(2)}, u32[]{:S(2)}) %collective-permute-start.43) | collective-permute-done | bytes 344096 | tf_op jit(solution)/shard_map/ppermute | solution.py:44
  159.4 1.6 collective-permute-start.44
  164.5 1.4 collective-permute-start.48
  165.9 5.6 %collective-permute-done.44.refs_2_ = bf16[256,384]{1,0:T(8,128)(2,1)S(1)} collective-permute-done((bf16[256,384]{1,0:T(8,128)(2,1)S(1)}, bf16[256,384]{1,0:T(8,128)(2,1)S(1)}, u32[]{:S(2)}, u32[]{:S(2)}) %collective-permute-start.44) | collective-permute-done | bytes 196640 | tf_op jit(solution)/shard_map/ppermute | solution.py:44
  171.5 2.1 %collective-permute-start.49 = (bf16[192,384]{1,0:T(8,128)(2,1)S(1)}, bf16[192,384]{1,0:T(8,128)(2,1)S(1)}, u32[]{:S(2)}, u32[]{:S(2)}) collective-permute-start(bf16[192,384]{1,0:T(8,128)(2,1)S(1)} %get-tuple-element.206), channel_id=1, source_target_pairs={{0,24},{8,16},{16,8},{24,0},{1,25},{9,17},{17,9},{25,1},{2,26},{10... | collective-permute-start | bytes 442376 | tf_op jit(solution)/shard_map/ppermute | solution.py:44
  173.7 1.7 shard_map.338
  175.4 4.8 %collective-permute-start.50 = (f32[32,384]{1,0:T(8,128)S(1)}, f32[32,384]{1,0:T(8,128)S(1)}, u32[]{:S(2)}, u32[]{:S(2)}) collective-permute-start(f32[32,384]{1,0:T(8,128)S(1)} %get-tuple-element.207.refs_1_), channel_id=1, source_target_pairs={{0,1},{1,0},{2,3},{3,2},{4,5},{5,4},{6,7},{7,6},{8,9},{9,8},{10,11... | collective-permute-start | bytes 147464 | tf_op jit(solution)/shard_map/ppermute | solution.py:44
  180.2 1.8 shard_map.330
  182.0 1.6 shard_map.341
  186.6 1.7 shard_map.342
  (137 shorter events, 44.8 us)
Async XLA Ops:
  5.0 8.0 %collective-permute-start.5 = (bf16[192,384]{1,0:T(8,128)(2,1)}, bf16[192,384]{1,0:T(8,128)(2,1)S(1)}, u32[]{:S(2)}, u32[]{:S(2)}) collective-permute-start(bf16[192,384]{1,0:T(8,128)(2,1)} %get-tuple-element.122.refs_1_), channel_id=1, source_target_pairs={{0,24},{8,16},{16,8},{24,0},{1,25},{9,17},{17,9},{25,1},{2,26},{10... | collective-permute-start | bytes 442376 | tf_op jit(solution)/shard_map/ppermute | solution.py:44
  9.2 9.0 %collective-permute-start = (bf16[304,384]{1,0:T(8,128)(2,1)}, bf16[304,384]{1,0:T(8,128)(2,1)S(1)}, u32[]{:S(2)}, u32[]{:S(2)}) collective-permute-start(bf16[304,384]{1,0:T(8,128)(2,1)} %get-tuple-element.119), channel_id=1, source_target_pairs={{0,2},{2,0},{4,6},{6,4},{1,3},{3,1},{5,7},{7,5},{8,10},{10,8},{12,... | collective-permute-start | bytes 700424 | tf_op jit(solution)/shard_map/ppermute | solution.py:44
  10.4 7.8 %collective-permute-start.1 = (bf16[304,384]{1,0:T(8,128)(2,1)}, bf16[304,384]{1,0:T(8,128)(2,1)S(1)}, u32[]{:S(2)}, u32[]{:S(2)}) collective-permute-start(bf16[304,384]{1,0:T(8,128)(2,1)} %get-tuple-element.120), channel_id=1, source_target_pairs={{0,4},{2,6},{4,0},{6,2},{1,5},{3,7},{5,1},{7,3},{8,12},{10,14},{12... | collective-permute-start | bytes 700424 | tf_op jit(solution)/shard_map/ppermute | solution.py:44
  11.6 10.0 %collective-permute-start.2 = (bf16[304,384]{1,0:T(8,128)(2,1)}, bf16[304,384]{1,0:T(8,128)(2,1)S(1)}, u32[]{:S(2)}, u32[]{:S(2)}) collective-permute-start(bf16[304,384]{1,0:T(8,128)(2,1)} %get-tuple-element.121), channel_id=1, source_target_pairs={{0,6},{2,4},{4,2},{6,0},{1,7},{3,5},{5,3},{7,1},{8,14},{10,12},{12... | collective-permute-start | bytes 700424 | tf_op jit(solution)/shard_map/ppermute | solution.py:44
  13.0 5.2 %collective-permute-start.3 = (bf16[192,384]{1,0:T(8,128)(2,1)}, bf16[192,384]{1,0:T(8,128)(2,1)S(1)}, u32[]{:S(2)}, u32[]{:S(2)}) collective-permute-start(bf16[192,384]{1,0:T(8,128)(2,1)} %get-tuple-element.122.refs_1_), channel_id=1, source_target_pairs={{0,16},{8,24},{16,0},{24,8},{1,17},{9,25},{17,1},{25,9},{2,18},{10... | collective-permute-start | bytes 442376 | tf_op jit(solution)/shard_map/ppermute | solution.py:44
  23.8 19.3 %collective-permute-start.7 = (bf16[4,192,384]{2,1,0:T(8,128)(2,1)S(1)}, bf16[4,192,384]{2,1,0:T(8,128)(2,1)S(1)}, u32[]{:S(2)}, u32[]{:S(2)}) collective-permute-start(bf16[4,192,384]{2,1,0:T(8,128)(2,1)S(1)} %shard_map.306.refs_6_), channel_id=1, source_target_pairs={{0,4},{2,6},{4,0},{6,2},{1,5},{3,7},{5,1},{7,3},{8,12},{10,14},{12... | collective-permute-start | bytes 1769480 | tf_op jit(solution)/shard_map/ppermute | solution.py:44
  24.1 19.0 %collective-permute-start.6 = (bf16[4,192,384]{2,1,0:T(8,128)(2,1)S(1)}, bf16[4,192,384]{2,1,0:T(8,128)(2,1)S(1)}, u32[]{:S(2)}, u32[]{:S(2)}) collective-permute-start(bf16[4,192,384]{2,1,0:T(8,128)(2,1)S(1)} %shard_map.306.refs_6_), channel_id=1, source_target_pairs={{0,2},{2,0},{4,6},{6,4},{1,3},{3,1},{5,7},{7,5},{8,10},{10,8},{12,... | collective-permute-start | bytes 1769480 | tf_op jit(solution)/shard_map/ppermute | solution.py:44
  25.9 6.5 %collective-permute-start.11 = (bf16[192,384]{1,0:T(8,128)(2,1)S(1)}, bf16[192,384]{1,0:T(8,128)(2,1)S(1)}, u32[]{:S(2)}, u32[]{:S(2)}) collective-permute-start(bf16[192,384]{1,0:T(8,128)(2,1)S(1)} %shard_map.309.refs_1_), channel_id=1, source_target_pairs={{0,16},{8,24},{16,0},{24,8},{1,17},{9,25},{17,1},{25,9},{2,18},{10... | collective-permute-start | bytes 442376 | tf_op jit(solution)/shard_map/ppermute | solution.py:44
  33.0 8.8 %collective-permute-start.12 = (bf16[2,192,384]{2,1,0:T(8,128)(2,1)S(1)}, bf16[2,192,384]{2,1,0:T(8,128)(2,1)S(1)}, u32[]{:S(2)}, u32[]{:S(2)}) collective-permute-start(bf16[2,192,384]{2,1,0:T(8,128)(2,1)S(1)} %shard_map.310.refs_1_), channel_id=1, source_target_pairs={{0,8},{8,0},{16,24},{24,16},{1,9},{9,1},{17,25},{25,17},{2,10},{10... | collective-permute-start | bytes 884744 | tf_op jit(solution)/shard_map/ppermute | solution.py:44
  33.7 6.7 %collective-permute-start.17 = (bf16[4,48,384]{2,1,0:T(8,128)(2,1)S(1)}, bf16[4,48,384]{2,1,0:T(8,128)(2,1)S(1)}, u32[]{:S(2)}, u32[]{:S(2)}) collective-permute-start(bf16[4,48,384]{2,1,0:T(8,128)(2,1)S(1)} %shard_map.313.refs_1_), channel_id=1, source_target_pairs={{0,16},{8,24},{16,0},{24,8},{1,17},{9,25},{17,1},{25,9},{2,18},{10... | collective-permute-start | bytes 442376 | tf_op jit(solution)/shard_map/ppermute | solution.py:44
  43.0 4.9 %collective-permute-start.19 = (bf16[144,384]{1,0:T(8,128)(2,1)S(1)}, bf16[144,384]{1,0:T(8,128)(2,1)S(1)}, u32[]{:S(2)}, u32[]{:S(2)}) collective-permute-start(bf16[144,384]{1,0:T(8,128)(2,1)S(1)} %shard_map.316.refs_1_), channel_id=1, source_target_pairs={{0,16},{8,24},{16,0},{24,8},{1,17},{9,25},{17,1},{25,9},{2,18},{10... | collective-permute-start | bytes 331784 | tf_op jit(solution)/shard_map/ppermute | solution.py:44
  43.7 11.1 %collective-permute-start.8 = (bf16[2,192,384]{2,1,0:T(8,128)(2,1)S(1)}, bf16[2,192,384]{2,1,0:T(8,128)(2,1)S(1)}, u32[]{:S(2)}, u32[]{:S(2)}) collective-permute-start(bf16[2,192,384]{2,1,0:T(8,128)(2,1)S(1)} %get-tuple-element.123), channel_id=1, source_target_pairs={{0,2},{2,0},{4,6},{6,4},{1,3},{3,1},{5,7},{7,5},{8,10},{10,8},{12,... | collective-permute-start | bytes 884744 | tf_op jit(solution)/shard_map/ppermute | solution.py:44
  44.0 10.7 %collective-permute-start.9 = (bf16[2,192,384]{2,1,0:T(8,128)(2,1)S(1)}, bf16[2,192,384]{2,1,0:T(8,128)(2,1)S(1)}, u32[]{:S(2)}, u32[]{:S(2)}) collective-permute-start(bf16[2,192,384]{2,1,0:T(8,128)(2,1)S(1)} %get-tuple-element.124), channel_id=1, source_target_pairs={{0,4},{2,6},{4,0},{6,2},{1,5},{3,7},{5,1},{7,3},{8,12},{10,14},{12... | collective-permute-start | bytes 884744 | tf_op jit(solution)/shard_map/ppermute | solution.py:44
  44.3 17.4 %collective-permute-start.14 = (bf16[4,192,384]{2,1,0:T(8,128)(2,1)S(1)}, bf16[4,192,384]{2,1,0:T(8,128)(2,1)S(1)}, u32[]{:S(2)}, u32[]{:S(2)}) collective-permute-start(bf16[4,192,384]{2,1,0:T(8,128)(2,1)S(1)} %shard_map.311.refs_5_.refs_2_), channel_id=1, source_target_pairs={{0,4},{2,6},{4,0},{6,2},{1,5},{3,7},{5,1},{7,3},{8,12},{10,14},{12... | collective-permute-start | bytes 1769480 | tf_op jit(solution)/shard_map/ppermute | solution.py:44
  48.4 6.3 %collective-permute-start.20 = (bf16[2,144,384]{2,1,0:T(8,128)(2,1)S(1)}, bf16[2,144,384]{2,1,0:T(8,128)(2,1)S(1)}, u32[]{:S(2)}, u32[]{:S(2)}) collective-permute-start(bf16[2,144,384]{2,1,0:T(8,128)(2,1)S(1)} %shard_map.317.refs_1_), channel_id=1, source_target_pairs={{0,8},{8,0},{16,24},{24,16},{1,9},{9,1},{17,25},{25,17},{2,10},{10... | collective-permute-start | bytes 663560 | tf_op jit(solution)/shard_map/ppermute | solution.py:44
  48.5 22.3 %collective-permute-start.13 = (bf16[4,192,384]{2,1,0:T(8,128)(2,1)S(1)}, bf16[4,192,384]{2,1,0:T(8,128)(2,1)S(1)}, u32[]{:S(2)}, u32[]{:S(2)}) collective-permute-start(bf16[4,192,384]{2,1,0:T(8,128)(2,1)S(1)} %shard_map.311.refs_5_.refs_2_), channel_id=1, source_target_pairs={{0,2},{2,0},{4,6},{6,4},{1,3},{3,1},{5,7},{7,5},{8,10},{10,8},{12,... | collective-permute-start | bytes 1769480 | tf_op jit(solution)/shard_map/ppermute | solution.py:44
  55.4 17.4 %collective-permute-start.22 = (bf16[4,144,384]{2,1,0:T(8,128)(2,1)S(1)}, bf16[4,144,384]{2,1,0:T(8,128)(2,1)S(1)}, u32[]{:S(2)}, u32[]{:S(2)}) collective-permute-start(bf16[4,144,384]{2,1,0:T(8,128)(2,1)S(1)} %shard_map.318.refs_2_), channel_id=1, source_target_pairs={{0,4},{2,6},{4,0},{6,2},{1,5},{3,7},{5,1},{7,3},{8,12},{10,14},{12... | collective-permute-start | bytes 1327112 | tf_op jit(solution)/shard_map/ppermute | solution.py:44
  56.1 17.8 %collective-permute-start.21 = (bf16[4,144,384]{2,1,0:T(8,128)(2,1)S(1)}, bf16[4,144,384]{2,1,0:T(8,128)(2,1)S(1)}, u32[]{:S(2)}, u32[]{:S(2)}) collective-permute-start(bf16[4,144,384]{2,1,0:T(8,128)(2,1)S(1)} %shard_map.318.refs_2_), channel_id=1, source_target_pairs={{0,2},{2,0},{4,6},{6,4},{1,3},{3,1},{5,7},{7,5},{8,10},{10,8},{12,... | collective-permute-start | bytes 1327112 | tf_op jit(solution)/shard_map/ppermute | solution.py:44
  56.5 18.2 %collective-permute-start.18 = (bf16[8,48,384]{2,1,0:T(8,128)(2,1)S(1)}, bf16[8,48,384]{2,1,0:T(8,128)(2,1)S(1)}, u32[]{:S(2)}, u32[]{:S(2)}) collective-permute-start(bf16[8,48,384]{2,1,0:T(8,128)(2,1)S(1)} %shard_map.314.refs_3_.refs_7_), channel_id=1, source_target_pairs={{0,8},{8,0},{16,24},{24,16},{1,9},{9,1},{17,25},{25,17},{2,10},{10... | collective-permute-start | bytes 884744 | tf_op jit(solution)/shard_map/ppermute | solution.py:44
  61.6 19.0 %collective-permute-start.10 = (bf16[256,768]{1,0:T(8,128)(2,1)S(1)}, bf16[256,768]{1,0:T(8,128)(2,1)S(1)}, u32[]{:S(2)}, u32[]{:S(2)}) collective-permute-start(bf16[256,768]{1,0:T(8,128)(2,1)S(1)} %get-tuple-element.126.refs_2_), channel_id=1, source_target_pairs={{0,1},{1,0},{2,3},{3,2},{4,5},{5,4},{6,7},{7,6},{8,9},{9,8},{10,11... | collective-permute-start | bytes 1179656 | tf_op jit(solution)/shard_map/ppermute | solution.py:44
  71.4 9.2 %collective-permute-start.15 = (bf16[2,192,384]{2,1,0:T(8,128)(2,1)S(1)}, bf16[2,192,384]{2,1,0:T(8,128)(2,1)S(1)}, u32[]{:S(2)}, u32[]{:S(2)}) collective-permute-start(bf16[2,192,384]{2,1,0:T(8,128)(2,1)S(1)} %get-tuple-element.127), channel_id=1, source_target_pairs={{0,2},{2,0},{4,6},{6,4},{1,3},{3,1},{5,7},{7,5},{8,10},{10,8},{12,... | collective-permute-start | bytes 884744 | tf_op jit(solution)/shard_map/ppermute | solution.py:44
  72.7 7.9 %collective-permute-start.16 = (bf16[2,192,384]{2,1,0:T(8,128)(2,1)S(1)}, bf16[2,192,384]{2,1,0:T(8,128)(2,1)S(1)}, u32[]{:S(2)}, u32[]{:S(2)}) collective-permute-start(bf16[2,192,384]{2,1,0:T(8,128)(2,1)S(1)} %get-tuple-element.128), channel_id=1, source_target_pairs={{0,4},{2,6},{4,0},{6,2},{1,5},{3,7},{5,1},{7,3},{8,12},{10,14},{12... | collective-permute-start | bytes 884744 | tf_op jit(solution)/shard_map/ppermute | solution.py:44
  74.5 10.8 %collective-permute-start.23 = (bf16[2,144,384]{2,1,0:T(8,128)(2,1)S(1)}, bf16[2,144,384]{2,1,0:T(8,128)(2,1)S(1)}, u32[]{:S(2)}, u32[]{:S(2)}) collective-permute-start(bf16[2,144,384]{2,1,0:T(8,128)(2,1)S(1)} %get-tuple-element.131), channel_id=1, source_target_pairs={{0,2},{2,0},{4,6},{6,4},{1,3},{3,1},{5,7},{7,5},{8,10},{10,8},{12,... | collective-permute-start | bytes 663560 | tf_op jit(solution)/shard_map/ppermute | solution.py:44
  74.6 10.7 %collective-permute-start.24 = (bf16[2,144,384]{2,1,0:T(8,128)(2,1)S(1)}, bf16[2,144,384]{2,1,0:T(8,128)(2,1)S(1)}, u32[]{:S(2)}, u32[]{:S(2)}) collective-permute-start(bf16[2,144,384]{2,1,0:T(8,128)(2,1)S(1)} %get-tuple-element.132), channel_id=1, source_target_pairs={{0,4},{2,6},{4,0},{6,2},{1,5},{3,7},{5,1},{7,3},{8,12},{10,14},{12... | collective-permute-start | bytes 663560 | tf_op jit(solution)/shard_map/ppermute | solution.py:44
  86.9 5.5 %collective-permute-start.25 = (bf16[256,768]{1,0:T(8,128)(2,1)S(1)}, bf16[256,768]{1,0:T(8,128)(2,1)S(1)}, u32[]{:S(2)}, u32[]{:S(2)}) collective-permute-start(bf16[256,768]{1,0:T(8,128)(2,1)S(1)} %get-tuple-element.133.refs_2_), channel_id=1, source_target_pairs={{0,1},{1,0},{2,3},{3,2},{4,5},{5,4},{6,7},{7,6},{8,9},{9,8},{10,11... | collective-permute-start | bytes 1179656 | tf_op jit(solution)/shard_map/ppermute | solution.py:44
  96.1 12.4 %collective-permute-start.27 = (bf16[4,144,384]{2,1,0:T(8,128)(2,1)S(1)}, bf16[4,144,384]{2,1,0:T(8,128)(2,1)S(1)}, u32[]{:S(2)}, u32[]{:S(2)}) collective-permute-start(bf16[4,144,384]{2,1,0:T(8,128)(2,1)S(1)} %get-tuple-element.159), channel_id=1, source_target_pairs={{0,2},{2,0},{4,6},{6,4},{1,3},{3,1},{5,7},{7,5},{8,10},{10,8},{12,... | collective-permute-start | bytes 1327112 | tf_op jit(solution)/shard_map/ppermute | solution.py:44
  96.2 12.3 %collective-permute-start.28 = (bf16[4,144,384]{2,1,0:T(8,128)(2,1)S(1)}, bf16[4,144,384]{2,1,0:T(8,128)(2,1)S(1)}, u32[]{:S(2)}, u32[]{:S(2)}) collective-permute-start(bf16[4,144,384]{2,1,0:T(8,128)(2,1)S(1)} %get-tuple-element.160), channel_id=1, source_target_pairs={{0,4},{2,6},{4,0},{6,2},{1,5},{3,7},{5,1},{7,3},{8,12},{10,14},{12... | collective-permute-start | bytes 1327112 | tf_op jit(solution)/shard_map/ppermute | solution.py:44
  100.7 9.0 %collective-permute-start.29 = (bf16[8,48,384]{2,1,0:T(8,128)(2,1)S(1)}, bf16[8,48,384]{2,1,0:T(8,128)(2,1)S(1)}, u32[]{:S(2)}, u32[]{:S(2)}) collective-permute-start(bf16[8,48,384]{2,1,0:T(8,128)(2,1)S(1)} %get-tuple-element.163), channel_id=1, source_target_pairs={{0,8},{8,0},{16,24},{24,16},{1,9},{9,1},{17,25},{25,17},{2,10},{10... | collective-permute-start | bytes 884744 | tf_op jit(solution)/shard_map/ppermute | solution.py:44
  110.4 20.0 %collective-permute-start.35 = (bf16[1120,384]{1,0:T(8,128)(2,1)S(1)}, bf16[1120,384]{1,0:T(8,128)(2,1)S(1)}, u32[]{:S(2)}, u32[]{:S(2)}) collective-permute-start(bf16[1120,384]{1,0:T(8,128)(2,1)S(1)} %get-tuple-element.164.refs_3_), channel_id=1, source_target_pairs={{0,2},{2,0},{4,6},{6,4},{1,3},{3,1},{5,7},{7,5},{8,10},{10,8},{12,... | collective-permute-start | bytes 2580488 | tf_op jit(solution)/shard_map/ppermute | solution.py:44
  111.8 18.4 %collective-permute-start.36 = (bf16[1056,384]{1,0:T(8,128)(2,1)S(1)}, bf16[1056,384]{1,0:T(8,128)(2,1)S(1)}, u32[]{:S(2)}, u32[]{:S(2)}) collective-permute-start(bf16[1056,384]{1,0:T(8,128)(2,1)S(1)} %get-tuple-element.175), channel_id=1, source_target_pairs={{0,4},{2,6},{4,0},{6,2},{1,5},{3,7},{5,1},{7,3},{8,12},{10,14},{12... | collective-permute-start | bytes 2433032 | tf_op jit(solution)/shard_map/ppermute | solution.py:44
  114.3 12.1 %collective-permute-start.30 = (bf16[256,768]{1,0:T(8,128)(2,1)S(1)}, bf16[256,768]{1,0:T(8,128)(2,1)S(1)}, u32[]{:S(2)}, u32[]{:S(2)}) collective-permute-start(bf16[256,768]{1,0:T(8,128)(2,1)S(1)} %shard_map.327.refs_3_), channel_id=1, source_target_pairs={{0,1},{1,0},{2,3},{3,2},{4,5},{5,4},{6,7},{7,6},{8,9},{9,8},{10,11... | collective-permute-start | bytes 1179656 | tf_op jit(solution)/shard_map/ppermute | solution.py:44
  116.4 9.6 %collective-permute-start.31 = (bf16[4,48,384]{2,1,0:T(8,128)(2,1)S(1)}, bf16[4,48,384]{2,1,0:T(8,128)(2,1)S(1)}, u32[]{:S(2)}, u32[]{:S(2)}) collective-permute-start(bf16[4,48,384]{2,1,0:T(8,128)(2,1)S(1)} %get-tuple-element.167), channel_id=1, source_target_pairs={{0,16},{8,24},{16,0},{24,8},{1,17},{9,25},{17,1},{25,9},{2,18},{10... | collective-permute-start | bytes 442376 | tf_op jit(solution)/shard_map/ppermute | solution.py:44
  119.9 23.2 %collective-permute-start.39 = (bf16[4,192,384]{2,1,0:T(8,128)(2,1)S(1)}, bf16[4,192,384]{2,1,0:T(8,128)(2,1)S(1)}, u32[]{:S(2)}, u32[]{:S(2)}) collective-permute-start(bf16[4,192,384]{2,1,0:T(8,128)(2,1)S(1)} %get-tuple-element.184), channel_id=1, source_target_pairs={{0,2},{2,0},{4,6},{6,4},{1,3},{3,1},{5,7},{7,5},{8,10},{10,8},{12,... | collective-permute-start | bytes 1769480 | tf_op jit(solution)/shard_map/ppermute | solution.py:44
  126.0 17.1 %collective-permute-start.40 = (bf16[4,192,384]{2,1,0:T(8,128)(2,1)S(1)}, bf16[4,192,384]{2,1,0:T(8,128)(2,1)S(1)}, u32[]{:S(2)}, u32[]{:S(2)}) collective-permute-start(bf16[4,192,384]{2,1,0:T(8,128)(2,1)S(1)} %get-tuple-element.185), channel_id=1, source_target_pairs={{0,4},{2,6},{4,0},{6,2},{1,5},{3,7},{5,1},{7,3},{8,12},{10,14},{12... | collective-permute-start | bytes 1769480 | tf_op jit(solution)/shard_map/ppermute | solution.py:44
  131.1 19.1 %collective-permute-start.38 = (bf16[448,384]{1,0:T(8,128)(2,1)S(1)}, bf16[448,384]{1,0:T(8,128)(2,1)S(1)}, u32[]{:S(2)}, u32[]{:S(2)}) collective-permute-start(bf16[448,384]{1,0:T(8,128)(2,1)S(1)} %get-tuple-element.179.refs_6_), channel_id=1, source_target_pairs={{0,4},{2,6},{4,0},{6,2},{1,5},{3,7},{5,1},{7,3},{8,12},{10,14},{12... | collective-permute-start | bytes 1032200 | tf_op jit(solution)/shard_map/ppermute | solution.py:44
  133.2 5.1 %collective-permute-start.41 = (bf16[2,144,384]{2,1,0:T(8,128)(2,1)S(1)}, bf16[2,144,384]{2,1,0:T(8,128)(2,1)S(1)}, u32[]{:S(2)}, u32[]{:S(2)}) collective-permute-start(bf16[2,144,384]{2,1,0:T(8,128)(2,1)S(1)} %get-tuple-element.188), channel_id=1, source_target_pairs={{0,8},{8,0},{16,24},{24,16},{1,9},{9,1},{17,25},{25,17},{2,10},{10... | collective-permute-start | bytes 663560 | tf_op jit(solution)/shard_map/ppermute | solution.py:44
  134.4 15.0 %collective-permute-start.37 = (bf16[2,192,384]{2,1,0:T(8,128)(2,1)S(1)}, bf16[2,192,384]{2,1,0:T(8,128)(2,1)S(1)}, u32[]{:S(2)}, u32[]{:S(2)}) collective-permute-start(bf16[2,192,384]{2,1,0:T(8,128)(2,1)S(1)} %get-tuple-element.178), channel_id=1, source_target_pairs={{0,2},{2,0},{4,6},{6,4},{1,3},{3,1},{5,7},{7,5},{8,10},{10,8},{12,... | collective-permute-start | bytes 884744 | tf_op jit(solution)/shard_map/ppermute | solution.py:44
  151.2 7.6 %collective-permute-start.43 = (bf16[448,384]{1,0:T(8,128)(2,1)S(1)}, bf16[448,384]{1,0:T(8,128)(2,1)S(1)}, u32[]{:S(2)}, u32[]{:S(2)}) collective-permute-start(bf16[448,384]{1,0:T(8,128)(2,1)S(1)} %get-tuple-element.193), channel_id=1, source_target_pairs={{0,8},{8,0},{16,24},{24,16},{1,9},{9,1},{17,25},{25,17},{2,10},{10... | collective-permute-start | bytes 1032200 | tf_op jit(solution)/shard_map/ppermute | solution.py:44
  152.6 9.5 %collective-permute-start.45 = (bf16[2,192,384]{2,1,0:T(8,128)(2,1)S(1)}, bf16[2,192,384]{2,1,0:T(8,128)(2,1)S(1)}, u32[]{:S(2)}, u32[]{:S(2)}) collective-permute-start(bf16[2,192,384]{2,1,0:T(8,128)(2,1)S(1)} %get-tuple-element.190.refs_7_), channel_id=1, source_target_pairs={{0,2},{2,0},{4,6},{6,4},{1,3},{3,1},{5,7},{7,5},{8,10},{10,8},{12,... | collective-permute-start | bytes 884744 | tf_op jit(solution)/shard_map/ppermute | solution.py:44
  152.9 9.8 %collective-permute-start.46 = (bf16[2,192,384]{2,1,0:T(8,128)(2,1)S(1)}, bf16[2,192,384]{2,1,0:T(8,128)(2,1)S(1)}, u32[]{:S(2)}, u32[]{:S(2)}) collective-permute-start(bf16[2,192,384]{2,1,0:T(8,128)(2,1)S(1)} %get-tuple-element.191.refs_8_), channel_id=1, source_target_pairs={{0,4},{2,6},{4,0},{6,2},{1,5},{3,7},{5,1},{7,3},{8,12},{10,14},{12... | collective-permute-start | bytes 884744 | tf_op jit(solution)/shard_map/ppermute | solution.py:44
  153.9 10.5 %collective-permute-start.32 = (bf16[304,384]{1,0:T(8,128)(2,1)S(1)}, bf16[304,384]{1,0:T(8,128)(2,1)S(1)}, u32[]{:S(2)}, u32[]{:S(2)}) collective-permute-start(bf16[304,384]{1,0:T(8,128)(2,1)S(1)} %get-tuple-element.169), channel_id=1, source_target_pairs={{0,2},{2,0},{4,6},{6,4},{1,3},{3,1},{5,7},{7,5},{8,10},{10,8},{12,... | collective-permute-start | bytes 700424 | tf_op jit(solution)/shard_map/ppermute | solution.py:44
  159.4 12.1 %collective-permute-start.44 = (bf16[256,384]{1,0:T(8,128)(2,1)S(1)}, bf16[256,384]{1,0:T(8,128)(2,1)S(1)}, u32[]{:S(2)}, u32[]{:S(2)}) collective-permute-start(bf16[256,384]{1,0:T(8,128)(2,1)S(1)} %get-tuple-element.195), channel_id=1, source_target_pairs={{0,16},{8,24},{16,0},{24,8},{1,17},{9,25},{17,1},{25,9},{2,18},{10... | collective-permute-start | bytes 589832 | tf_op jit(solution)/shard_map/ppermute | solution.py:44
  161.0 14.4 %collective-permute-start.33 = (bf16[304,384]{1,0:T(8,128)(2,1)S(1)}, bf16[304,384]{1,0:T(8,128)(2,1)S(1)}, u32[]{:S(2)}, u32[]{:S(2)}) collective-permute-start(bf16[304,384]{1,0:T(8,128)(2,1)S(1)} %get-tuple-element.170), channel_id=1, source_target_pairs={{0,4},{2,6},{4,0},{6,2},{1,5},{3,7},{5,1},{7,3},{8,12},{10,14},{12... | collective-permute-start | bytes 700424 | tf_op jit(solution)/shard_map/ppermute | solution.py:44
  162.2 18.0 %collective-permute-start.34 = (bf16[304,384]{1,0:T(8,128)(2,1)S(1)}, bf16[304,384]{1,0:T(8,128)(2,1)S(1)}, u32[]{:S(2)}, u32[]{:S(2)}) collective-permute-start(bf16[304,384]{1,0:T(8,128)(2,1)S(1)} %get-tuple-element.171), channel_id=1, source_target_pairs={{0,6},{2,4},{4,2},{6,0},{1,7},{3,5},{5,3},{7,1},{8,14},{10,12},{12... | collective-permute-start | bytes 700424 | tf_op jit(solution)/shard_map/ppermute | solution.py:44
  163.6 21.2 %collective-permute-start.47 = (bf16[192,384]{1,0:T(8,128)(2,1)S(1)}, bf16[192,384]{1,0:T(8,128)(2,1)S(1)}, u32[]{:S(2)}, u32[]{:S(2)}) collective-permute-start(bf16[192,384]{1,0:T(8,128)(2,1)S(1)} %get-tuple-element.204), channel_id=1, source_target_pairs={{0,16},{8,24},{16,0},{24,8},{1,17},{9,25},{17,1},{25,9},{2,18},{10... | collective-permute-start | bytes 442376 | tf_op jit(solution)/shard_map/ppermute | solution.py:44
  164.5 20.4 %collective-permute-start.48 = (bf16[192,384]{1,0:T(8,128)(2,1)S(1)}, bf16[192,384]{1,0:T(8,128)(2,1)S(1)}, u32[]{:S(2)}, u32[]{:S(2)}) collective-permute-start(bf16[192,384]{1,0:T(8,128)(2,1)S(1)} %get-tuple-element.205), channel_id=1, source_target_pairs={{0,8},{8,0},{16,24},{24,16},{1,9},{9,1},{17,25},{25,17},{2,10},{10... | collective-permute-start | bytes 442376 | tf_op jit(solution)/shard_map/ppermute | solution.py:44
  171.5 13.3 %collective-permute-start.49 = (bf16[192,384]{1,0:T(8,128)(2,1)S(1)}, bf16[192,384]{1,0:T(8,128)(2,1)S(1)}, u32[]{:S(2)}, u32[]{:S(2)}) collective-permute-start(bf16[192,384]{1,0:T(8,128)(2,1)S(1)} %get-tuple-element.206), channel_id=1, source_target_pairs={{0,24},{8,16},{16,8},{24,0},{1,25},{9,17},{17,9},{25,1},{2,26},{10... | collective-permute-start | bytes 442376 | tf_op jit(solution)/shard_map/ppermute | solution.py:44
  175.4 8.2 %collective-permute-start.50 = (f32[32,384]{1,0:T(8,128)S(1)}, f32[32,384]{1,0:T(8,128)S(1)}, u32[]{:S(2)}, u32[]{:S(2)}) collective-permute-start(f32[32,384]{1,0:T(8,128)S(1)} %get-tuple-element.207.refs_1_), channel_id=1, source_target_pairs={{0,1},{1,0},{2,3},{3,2},{4,5},{5,4},{6,7},{7,6},{8,9},{9,8},{10,11... | collective-permute-start | bytes 147464 | tf_op jit(solution)/shard_map/ppermute | solution.py:44
  (25 other events, 358.5 us)
